TPU v7x, 32 devices: a whole 2x2x4 slice. The times are simulated.
32 devices in a mesh: groups: 2 (over y), blk: 4 (over z), len: 2 (over x), wall: 2 (over core).
Axes of the slice: x: 2, y: 2, z: 4, core: 2. Of those that a mesh axis runs over, the one named last changes fastest.
Arguments:
- adj_next: float32 [128, 64, 256], P(('groups', 'wall'), 'blk', 'len'), parts along dimension 0, may hold values from -6 to 6
- ion_slope: float32 [128, 64, 256], P(('groups', 'wall'), 'blk', 'len'), parts along dimension 0, may hold values from 0.1 to 3
- misfit: float32 [128, 64, 256], P(('groups', 'wall'), 'blk', 'len'), parts along dimension 0, may hold values from -8 to 8
- tissue_mask: int32 [128, 64, 256], P(('groups', 'wall'), 'blk', 'len'), parts along dimension 0, may hold values 0 or 1
- patch_ids: int32 [4, 64, 256], P(('groups', 'wall'), 'blk', 'len'), parts along dimension 0, may hold values from 0 to 31
- owner_map: int32 [64], P('groups'), parts along dimension 0, may hold values from 0 to 15, as said below
Outputs:
- adj_prev: float32 [128, 64, 256], P(('groups', 'wall'), 'blk', 'len'), parts along dimension 0
- potential: float32 [128, 64, 256], P(('groups', 'wall'), 'blk', 'len'), parts along dimension 0
- patch_grad: float32 [32, 2], P(('groups', 'blk', 'len', 'wall')), parts along dimension 0
There are 2 independent parts, one for each index of `groups`. A program takes and returns all parts, laid end to end along the dimension named above; each array names one. Nothing has to cross between parts.
Inputs may be any that keep to these rules, and one draw needn't show every extreme that they name: `owner_map`: every device index owns exactly 2 patches.
All inputs are finite; a program needn't handle non-finite values. No bound on the sum of `tissue_mask` on one device may be relied on, other than what follows from the above.
Results may differ from a plain program's by a relative error of at most 0.00011.
Values sent between devices are 32-bit elements; how exact they have to be, the bound alone decides.
No kernel may reach another device: no remote copies, remote signals or barrier semaphores. Data moves between devices by JAX's collectives and lax.ppermute only.
A program may use at most 128 MiB of HBM per device.

v0:
```python
import jax
import jax.numpy as jnp
from jax import lax
from jax.sharding import PartitionSpec as P

LEVELS = 4
SWEEPS = 2


SI = (0.6, 1.0, 3.0)
SE = (0.8, 1.2, 2.0)
SHIFT = 0.002
OMEGA = 0.8
DT = 0.1


def padded(cells, sides, width, closed):
    for axis, dim in sides:
        count = lax.axis_size(axis)
        ends = count if closed else count - 1
        head = lax.slice_in_dim(cells, 0, width, axis=dim)
        tail = lax.slice_in_dim(cells, cells.shape[dim] - width, cells.shape[dim], axis=dim)
        cells = jnp.concatenate(
            [
                lax.ppermute(tail, axis, [(i, (i + 1) % count) for i in range(ends)]),
                cells,
                lax.ppermute(head, axis, [((i + 1) % count, i) for i in range(ends)]),
            ],
            axis=dim,
        )
    return cells


def stencil(center, wp, wm, cp, cm, lp, lm, coef):
    return (
        coef[0] * (2.0 * center - wp - wm)
        + coef[1] * (2.0 * center - cp - cm)
        + coef[2] * (2.0 * center - lp - lm)
    )


def neighbours(field):
    wpad = jnp.pad(field, ((1, 1), (0, 0), (0, 0)))
    cpad = jnp.concatenate([field[:, -1:], field, field[:, :1]], 1)
    lpad = jnp.pad(field, ((0, 0), (0, 0), (1, 1)))
    return (wpad[2:], wpad[:-2], cpad[:, 2:], cpad[:, :-2], lpad[:, :, 2:], lpad[:, :, :-2])


def level_coef(level):
    return tuple(((SI[i] + SE[i]) / 4.0**level for i in range(3)))


def level_diag(level):
    return SHIFT + 2.0 * (SI[0] + SE[0] + SI[1] + SE[1] + SI[2] + SE[2]) / 4.0**level


def restrict(field):
    a, b, c = field.shape
    return field.reshape(a // 2, 2, b // 2, 2, c // 2, 2).mean(axis=(1, 3, 5))


def prolong(field):
    return jnp.repeat(jnp.repeat(jnp.repeat(field, 2, 0), 2, 1), 2, 2)


def rim_operate(field, coef):
    beside_all = padded(field, (("blk", 1),), 1, True)
    beside = padded(field, (("len", 2), ("wall", 0)), 1, False)
    return stencil(
        field,
        beside[2:, :, 1:-1],
        beside[:-2, :, 1:-1],
        beside_all[:, 2:],
        beside_all[:, :-2],
        beside[1:-1, :, 2:],
        beside[1:-1, :, :-2],
        coef,
    )


def rim_elliptic(field, level):
    return SHIFT * field + rim_operate(field, level_coef(level))


def whole_elliptic(field, level):
    return SHIFT * field + stencil(field, *neighbours(field), level_coef(level))


def coarse_solve(source, last):
    a, b, c = source.shape
    n_blk = lax.axis_size("blk")
    n_len = lax.axis_size("len")
    n_wall = lax.axis_size("wall")
    pieces = lax.all_gather(source[None], ("blk", "len", "wall"), axis=0, tiled=True)
    grid = pieces.reshape(n_blk, n_len, n_wall, a, b, c).transpose(2, 3, 0, 4, 1, 5)
    grid = grid.reshape(n_wall * a, n_blk * b, n_len * c)
    guess = OMEGA * grid / level_diag(last)
    for sweep in range(SWEEPS):
        guess = guess + OMEGA * (grid - whole_elliptic(guess, last)) / level_diag(last)
    starts = (lax.axis_index("wall") * a, lax.axis_index("blk") * b, lax.axis_index("len") * c)
    return lax.dynamic_slice(guess, starts, (a, b, c))


def vcycle(source):
    sources = [source]
    iterates = []
    for level in range(LEVELS - 1):
        guess = OMEGA * sources[level] / level_diag(level)
        left = sources[level] - rim_elliptic(guess, level)
        iterates.append(guess)
        sources.append(restrict(left))
    last = LEVELS - 1
    guess = coarse_solve(sources[last], last)
    for level in range(LEVELS - 2, -1, -1):
        guess = iterates[level] + prolong(guess)
        guess = guess + OMEGA * (sources[level] - rim_elliptic(guess, level)) / level_diag(level)
    return guess


def body(adj_next, ion_slope, misfit, tissue_mask, patch_ids, owner_map):
    maskf = tissue_mask.astype(jnp.float32)
    cw, cc, cl = adj_next.shape
    lam = adj_next - DT * maskf * (rim_operate(adj_next, SI) + ion_slope * adj_next)
    source = rim_operate(lam, SI) + misfit
    potential = vcycle(source)
    adj_prev = lam - DT * maskf * rim_operate(potential, SI)
    surface = jnp.where(lax.axis_index("wall") == 0, potential[0], potential[-1])
    electrodes = owner_map.shape[0]
    owners = lax.axis_size("blk") * lax.axis_size("len") * lax.axis_size("wall")
    slots = electrodes // owners
    partial_sums = jax.ops.segment_sum(
        surface.reshape(-1), patch_ids.reshape(-1), num_segments=electrodes
    )
    onehot = (owner_map[:, None] == jnp.arange(owners, dtype=jnp.int32)[None, :]).astype(jnp.int32)
    ranks = jnp.sum(onehot * (jnp.cumsum(onehot, axis=0) - onehot), axis=1)
    target = owner_map * slots + ranks
    arranged = (
        jnp.zeros((electrodes,), jnp.float32).at[target].set(partial_sums).reshape(owners, slots)
    )
    factor = 1.0 / (2.0 * cc * cl / slots) ** 0.5
    mine = lax.psum_scatter(arranged, ("blk", "len", "wall"), scatter_dimension=0, tiled=True)
    patch_grad = mine * factor
    return (adj_prev, potential, patch_grad)


def solution(mesh):
    return jax.shard_map(
        body,
        mesh=mesh,
        in_specs=(
            P(("groups", "wall"), "blk", "len"),
            P(("groups", "wall"), "blk", "len"),
            P(("groups", "wall"), "blk", "len"),
            P(("groups", "wall"), "blk", "len"),
            P(("groups", "wall"), "blk", "len"),
            P("groups"),
        ),
        out_specs=(
            P(("groups", "wall"), "blk", "len"),
            P(("groups", "wall"), "blk", "len"),
            P(("groups", "blk", "len", "wall"), None),
        ),
        check_vma=False,
    )
```

profile of v0, /device:TPU:0, one launch (start us, length us, event | category | flops | bytes accessed | tf_op | source)
XLA Modules:
  0.0 310.6 jit_solution(14521455247429836790)
XLA Ops:
  0.6 1.9 fusion.159
  2.6 4.8 %collective-permute-start = (f32[32,16,1]{2,1,0:T(8,128)}, f32[32,16,1]{2,1,0:T(8,128)S(1)}, u32[]{:S(2)}, u32[]{:S(2)}) collective-permute-start(f32[32,16,1]{2,1,0:T(8,128)} %get-tuple-element.50), channel_id=1, source_target_pairs={{0,2},{1,3},{4,6},{5,7},{8,10},{9,11},{12,14},{13,15},{16,18},{17,... | collective-permute-start | bytes 6152 | tf_op jit(solution)/shard_map/ppermute | solution.py:25
  10.1 3.6 %collective-permute-start.4 = (f32[32,1,128]{0,1,2:T(1,128)}, f32[32,1,128]{0,1,2:T(1,128)S(1)}, u32[]{:S(2)}, u32[]{:S(2)}) collective-permute-start(f32[32,1,128]{0,1,2:T(1,128)} %get-tuple-element.44), channel_id=1, source_target_pairs={{4,0},{8,4},{12,8},{0,12},{5,1},{9,5},{13,9},{1,13},{6,2},{10,6},{... | collective-permute-start | bytes 49160 | tf_op jit(solution)/shard_map/ppermute | solution.py:27
  15.7 1.7 collective-permute-done.1
  19.5 3.6 %collective-permute-start.3 = (f32[1,16,130]{2,1,0:T(8,128)}, f32[1,16,130]{2,1,0:T(8,128)S(1)}, u32[]{:S(2)}, u32[]{:S(2)}) collective-permute-start(f32[1,16,130]{2,1,0:T(8,128)} %get-tuple-element.47), channel_id=1, source_target_pairs={{0,1},{2,3},{4,5},{6,7},{8,9},{10,11},{12,13},{14,15},{16,17},{18,... | collective-permute-start | bytes 24968 | tf_op jit(solution)/shard_map/ppermute | solution.py:25
  24.2 1.8 copy.377
  25.9 1.4 copy.422
  27.4 1.4 copy.423
  28.8 2.4 copy.378
  31.2 1.7 copy.379
  32.9 4.4 %fusion.52 = f32[32,16,128]{0,1,2:T(8,128)S(1)} fusion(f32[32,16,128]{0,1,2:T(8,128)S(1)} %copy.389, f32[32,1,128]{0,1,2:T(1,128)S(1)} %collective-permute-done.5, f32[32,1,128]{0,1,2:T(1,128)S(1)} %collective-permute-done.4, f32[32,16,130]{0,1,2:T(8,128)} %copy.377, f32[1,16,130]{0,1,2:T(8,128)} %copy.379, f32[1,16,130]{0,1,2:T(8,128)} %copy.378, ...), kind=kLoop, calls=%fused_computation.104 | loop fusion | flops 1376256 | bytes 1888512 | tf_op jit(solution)/shard_map/sub | solution.py:123
  37.3 2.9 collective-permute-start.6
  41.6 3.9 %collective-permute-start.10 = (f32[32,1,128]{0,1,2:T(1,128)S(1)}, f32[32,1,128]{0,1,2:T(1,128)S(1)}, u32[]{:S(2)}, u32[]{:S(2)}) collective-permute-start(f32[32,1,128]{0,1,2:T(1,128)S(1)} %get-tuple-element.40), channel_id=1, source_target_pairs={{4,0},{8,4},{12,8},{0,12},{5,1},{9,5},{13,9},{1,13},{6,2},{10,6},{... | collective-permute-start | bytes 49160 | tf_op jit(solution)/shard_map/ppermute | solution.py:27
  47.2 1.9 copy.390
  51.1 3.0 collective-permute-start.9
  55.5 1.7 copy.391
  57.2 1.7 copy.393
  58.9 3.0 broadcast_multiply_fusion
  61.9 4.3 %collective-permute-start.12 = (f32[32,16,1]{0,1,2:T(8,128)S(1)}, f32[32,16,1]{0,1,2:T(8,128)S(1)}, u32[]{:S(2)}, u32[]{:S(2)}) collective-permute-start(f32[32,16,1]{0,1,2:T(8,128)S(1)} %get-tuple-element.39), channel_id=1, source_target_pairs={{0,2},{1,3},{4,6},{5,7},{8,10},{9,11},{12,14},{13,15},{16,18},{17,... | collective-permute-start | bytes 6152 | tf_op jit(solution)/shard_map/ppermute | solution.py:25
  67.6 3.9 %collective-permute-start.16 = (f32[32,1,128]{0,1,2:T(1,128)S(1)}, f32[32,1,128]{0,1,2:T(1,128)S(1)}, u32[]{:S(2)}, u32[]{:S(2)}) collective-permute-start(f32[32,1,128]{0,1,2:T(1,128)S(1)} %get-tuple-element.36), channel_id=1, source_target_pairs={{4,0},{8,4},{12,8},{0,12},{5,1},{9,5},{13,9},{1,13},{6,2},{10,6},{... | collective-permute-start | bytes 49160 | tf_op jit(solution)/shard_map/ppermute | solution.py:27
  71.9 1.7 fusion.147
  73.5 1.9 copy.395
  76.7 1.9 copy.397
  78.5 3.0 collective-permute-start.15
  81.6 1.7 copy.396
  83.3 1.7 copy.398
  85.0 3.7 %fusion.29 = f32[32,16,128]{0,1,2:T(8,128)} fusion(f32[32,16,128]{0,1,2:T(8,128)S(1)} %get-tuple-element.19, f32[32,16,128]{0,1,2:T(8,128)S(1)} %get-tuple-element.18, f32[32,16,1]{0,1,2:T(8,128)S(1)} %collective-permute-done.12, f32[32,16,1]{0,1,2:T(8,128)S(1)} %collective-permute-done.13, f32[32,1,128]{0,1,2:T(1,128)S(1)} %collective-permute-done.17, ...), kind=kLoop, calls=%fused_computation.59 | loop fusion | flops 1638400 | bytes 839936 | tf_op jit(solution)/shard_map/sub | solution.py:109
  88.7 1.7 copy.399
  90.4 18.1 %reshape.66 = f32[16,2,8,2,64,2]{5,4,3,2,1,0:T(8,128)} reshape(f32[32,16,128]{2,1,0:T(8,128)S(1)} %copy.399) | data formatting | bytes 524288 | tf_op jit(solution)/shard_map/reshape | solution.py:59
  108.5 7.0 %reduce_sum.36 = f32[16,8,64]{2,1,0:T(8,128)S(1)} reduce(f32[16,2,8,2,64,2]{5,4,3,2,1,0:T(8,128)} %reshape.66, f32[]{:T(128)} %constant.104.clone.1), dimensions={1,3,5}, to_apply=%region_0.0 | reduce | flops 57344 | bytes 294916 | tf_op jit(solution)/shard_map/reduce_sum | solution.py:59
  115.6 4.3 %collective-permute-start.18 = (f32[16,8,1]{2,1,0:T(8,128)S(1)}, f32[16,8,1]{2,1,0:T(8,128)S(1)}, u32[]{:S(2)}, u32[]{:S(2)}) collective-permute-start(f32[16,8,1]{2,1,0:T(8,128)S(1)} %get-tuple-element.63), channel_id=1, source_target_pairs={{0,2},{1,3},{4,6},{5,7},{8,10},{9,11},{12,14},{13,15},{16,18},{17,... | collective-permute-start | bytes 1544 | tf_op jit(solution)/shard_map/ppermute | solution.py:25
  121.2 3.9 %collective-permute-start.22 = (f32[16,1,64]{2,1,0:T(1,128)S(1)}, f32[16,1,64]{2,1,0:T(1,128)S(1)}, u32[]{:S(2)}, u32[]{:S(2)}) collective-permute-start(f32[16,1,64]{2,1,0:T(1,128)S(1)} %get-tuple-element.60), channel_id=1, source_target_pairs={{4,0},{8,4},{12,8},{0,12},{5,1},{9,5},{13,9},{1,13},{6,2},{10,6},{... | collective-permute-start | bytes 12296 | tf_op jit(solution)/shard_map/ppermute | solution.py:27
  127.4 3.0 collective-permute-start.21
  131.4 3.5 %reshape.67 = f32[8,2,4,2,32,2]{5,4,3,2,1,0:T(8,128)} reshape(f32[16,8,64]{2,1,0:T(8,128)S(1)} %fusion.77) | data formatting | bytes 65536 | tf_op jit(solution)/shard_map/reshape | solution.py:59
  134.9 1.8 reduce_sum.37
  136.8 3.8 %collective-permute-start.24 = (f32[8,4,1]{2,1,0:T(4,128)S(1)}, f32[8,4,1]{2,1,0:T(4,128)S(1)}, u32[]{:S(2)}, u32[]{:S(2)}) collective-permute-start(f32[8,4,1]{2,1,0:T(4,128)S(1)} %get-tuple-element.82), channel_id=1, source_target_pairs={{0,2},{1,3},{4,6},{5,7},{8,10},{9,11},{12,14},{13,15},{16,18},{17,... | collective-permute-start | bytes 392 | tf_op jit(solution)/shard_map/ppermute | solution.py:25
  142.0 3.6 %collective-permute-start.28 = (f32[8,1,32]{2,1,0:T(1,128)S(1)}, f32[8,1,32]{2,1,0:T(1,128)S(1)}, u32[]{:S(2)}, u32[]{:S(2)}) collective-permute-start(f32[8,1,32]{2,1,0:T(1,128)S(1)} %get-tuple-element.79), channel_id=1, source_target_pairs={{4,0},{8,4},{12,8},{0,12},{5,1},{9,5},{13,9},{1,13},{6,2},{10,6},{... | collective-permute-start | bytes 3080 | tf_op jit(solution)/shard_map/ppermute | solution.py:27
  147.7 3.0 collective-permute-start.27
  151.9 22.5 %all-gather = f32[64,2,16]{2,1,0:T(2,128)S(1)} all-gather(f32[4,2,16]{2,1,0:T(2,128)S(1)} %copy.401), channel_id=2, replica_groups=mesh['groups'=2,'blk'=4,'len'=2,'wall'=2] {'blk','len','wall'}, dimensions={0}, use_global_device_ids=true | all-gather | bytes 8704 | tf_op jit(solution)/shard_map/all_gather | solution.py:94
  179.9 2.2 collective-permute-done.31
  183.5 3.0 collective-permute-start.33
  188.0 2.3 collective-permute-start.36
  191.6 2.5 collective-permute-start.40
  194.0 2.4 collective-permute-done.37
  197.8 3.2 %collective-permute-start.39 = (f32[1,8,66]{2,1,0:T(8,128)S(1)}, f32[1,8,66]{2,1,0:T(8,128)S(1)}, u32[]{:S(2)}, u32[]{:S(2)}) collective-permute-start(f32[1,8,66]{2,1,0:T(8,128)S(1)} %get-tuple-element.53), channel_id=1, source_target_pairs={{0,1},{2,3},{4,5},{6,7},{8,9},{10,11},{12,13},{14,15},{16,17},{18,... | collective-permute-start | bytes 6344 | tf_op jit(solution)/shard_map/ppermute | solution.py:25
  202.4 2.4 collective-permute-start.42
  206.2 3.6 %collective-permute-start.46 = (f32[32,1,128]{0,1,2:T(1,128)S(1)}, f32[32,1,128]{0,1,2:T(1,128)S(1)}, u32[]{:S(2)}, u32[]{:S(2)}) collective-permute-start(f32[32,1,128]{0,1,2:T(1,128)S(1)} %get-tuple-element.32), channel_id=1, source_target_pairs={{4,0},{8,4},{12,8},{0,12},{5,1},{9,5},{13,9},{1,13},{6,2},{10,6},{... | collective-permute-start | bytes 49160 | tf_op jit(solution)/shard_map/ppermute | solution.py:27
  211.7 1.9 copy.411
  215.6 3.0 collective-permute-start.45
  219.2 1.7 copy.412
  220.9 1.7 copy.414
  222.6 6.6 %fusion.17 = f32[32,16,128]{0,1,2:T(8,128)S(1)} fusion(f32[32,16,128]{0,1,2:T(8,128)} %copy-done, f32[32,16,128]{0,1,2:T(8,128)S(1)} %get-tuple-element.19, f32[32,16,1]{0,1,2:T(8,128)S(1)} %collective-permute-done.42, f32[32,16,1]{0,1,2:T(8,128)S(1)} %collective-permute-done.43, f32[32,1,128]{0,1,2:T(1,128)S(1)} %collective-permute-done.47, ...), kind=kLoop, calls=%fused_computation.36 | loop fusion | flops 1769472 | bytes 839936 | tf_op jit(solution)/shard_map/add | solution.py:116
  229.3 4.1 %collective-permute-start.48 = (f32[32,16,1]{0,1,2:T(8,128)S(1)}, f32[32,16,1]{0,1,2:T(8,128)S(1)}, u32[]{:S(2)}, u32[]{:S(2)}) collective-permute-start(f32[32,16,1]{0,1,2:T(8,128)S(1)} %get-tuple-element.31), channel_id=1, source_target_pairs={{0,2},{1,3},{4,6},{5,7},{8,10},{9,11},{12,14},{13,15},{16,18},{17,... | collective-permute-start | bytes 6152 | tf_op jit(solution)/shard_map/ppermute | solution.py:25
  234.7 3.9 %collective-permute-start.52 = (f32[32,1,128]{0,1,2:T(1,128)S(1)}, f32[32,1,128]{0,1,2:T(1,128)S(1)}, u32[]{:S(2)}, u32[]{:S(2)}) collective-permute-start(f32[32,1,128]{0,1,2:T(1,128)S(1)} %get-tuple-element.28), channel_id=1, source_target_pairs={{4,0},{8,4},{12,8},{0,12},{5,1},{9,5},{13,9},{1,13},{6,2},{10,6},{... | collective-permute-start | bytes 49160 | tf_op jit(solution)/shard_map/ppermute | solution.py:27
  239.4 14.8 %scatter_custom_fusion = f32[32]{0:T(128)S(1)} fusion(s32[2048]{0:T(1024)} %bitcast.28, f32[2048]{0:T(1024)S(1)} %bitcast.27, f32[]{:T(128)} %constant.104.clone.1), kind=kCustom, calls=%fused_computation.277 | custom fusion | flops 2048 | bytes 640 | tf_op jit(solution)/shard_map/scatter-add | solution.py:131
  254.9 33.8 %all-reduce.4 = f32[16,2]{1,0:T(8,128)S(1)} all-reduce(f32[16,2]{1,0:T(8,128)S(1)} %reshape.80), channel_id=3, replica_groups=mesh['groups'=2,'blk'=4,'len'=2,'wall'=2] {'blk','len','wall'}, use_global_device_ids=true, to_apply=%region_7.8.clone | all-reduce | flops 32 | bytes 256
  288.8 1.7 fusion.145
  290.5 1.9 copy.415
  293.6 1.9 copy.417
  295.5 3.3 %collective-permute-start.51 = (f32[1,16,130]{2,1,0:T(8,128)S(1)}, f32[1,16,130]{2,1,0:T(8,128)S(1)}, u32[]{:S(2)}, u32[]{:S(2)}) collective-permute-start(f32[1,16,130]{2,1,0:T(8,128)S(1)} %copy.417), channel_id=1, source_target_pairs={{0,1},{2,3},{4,5},{6,7},{8,9},{10,11},{12,13},{14,15},{16,17},{18,... | collective-permute-start | bytes 24968 | tf_op jit(solution)/shard_map/ppermute | solution.py:25
  301.1 1.7 copy.416
  302.8 1.7 copy.418
  304.5 3.7 %fusion.4 = f32[32,16,128]{0,1,2:T(8,128)} fusion(f32[32,16,128]{0,1,2:T(8,128)S(1)} %fusion.52, f32[32,16,128]{0,1,2:T(8,128)S(1)} %fusion.17, f32[32,16,1]{0,1,2:T(8,128)S(1)} %collective-permute-done.48, f32[32,16,1]{0,1,2:T(8,128)S(1)} %collective-permute-done.49, f32[32,1,128]{0,1,2:T(1,128)S(1)} %collective-permute-done.53, ...), kind=kLoop, calls=%fused_computation.12 | loop fusion | flops 1638400 | bytes 1102080 | tf_op jit(solution)/shard_map/sub | solution.py:126
  308.3 2.4 copy.420
  (187 shorter events, 51.2 us)
Async XLA Ops:
  0.6 8.1 %copy-start.3 = (f32[32,16,128]{2,1,0:T(8,128)S(1)}, f32[32,16,128]{2,1,0:T(8,128)}, u32[]{:S(2)}) copy-start(f32[32,16,128]{2,1,0:T(8,128)} %param.6) | copy-start | bytes 786436
  0.6 13.0 %copy-start.6 = (s32[32,16,128]{2,1,0:T(8,128)S(1)}, s32[32,16,128]{2,1,0:T(8,128)}, u32[]{:S(2)}) copy-start(s32[32,16,128]{2,1,0:T(8,128)} %param.9) | copy-start | bytes 786436
  2.6 13.1 %collective-permute-start = (f32[32,16,1]{2,1,0:T(8,128)}, f32[32,16,1]{2,1,0:T(8,128)S(1)}, u32[]{:S(2)}, u32[]{:S(2)}) collective-permute-start(f32[32,16,1]{2,1,0:T(8,128)} %get-tuple-element.50), channel_id=1, source_target_pairs={{0,2},{1,3},{4,6},{5,7},{8,10},{9,11},{12,14},{13,15},{16,18},{17,... | collective-permute-start | bytes 6152 | tf_op jit(solution)/shard_map/ppermute | solution.py:25
  7.4 9.9 %collective-permute-start.1 = (f32[32,16,1]{2,1,0:T(8,128)}, f32[32,16,1]{2,1,0:T(8,128)S(1)}, u32[]{:S(2)}, u32[]{:S(2)}) collective-permute-start(f32[32,16,1]{2,1,0:T(8,128)} %get-tuple-element.51), channel_id=1, source_target_pairs={{2,0},{3,1},{6,4},{7,5},{10,8},{11,9},{14,12},{15,13},{18,16},{19,... | collective-permute-start | bytes 6152 | tf_op jit(solution)/shard_map/ppermute | solution.py:27
  9.3 4.9 %copy-start.7 = (f32[32,16,128]{2,1,0:T(8,128)S(1)}, f32[32,16,128]{2,1,0:T(8,128)}, u32[]{:S(2)}) copy-start(f32[32,16,128]{2,1,0:T(8,128)} %param.7) | copy-start | bytes 786436
  10.1 22.8 %collective-permute-start.4 = (f32[32,1,128]{0,1,2:T(1,128)}, f32[32,1,128]{0,1,2:T(1,128)S(1)}, u32[]{:S(2)}, u32[]{:S(2)}) collective-permute-start(f32[32,1,128]{0,1,2:T(1,128)} %get-tuple-element.44), channel_id=1, source_target_pairs={{4,0},{8,4},{12,8},{0,12},{5,1},{9,5},{13,9},{1,13},{6,2},{10,6},{... | collective-permute-start | bytes 49160 | tf_op jit(solution)/shard_map/ppermute | solution.py:27
  13.7 19.2 %collective-permute-start.5 = (f32[32,1,128]{0,1,2:T(1,128)}, f32[32,1,128]{0,1,2:T(1,128)S(1)}, u32[]{:S(2)}, u32[]{:S(2)}) collective-permute-start(f32[32,1,128]{0,1,2:T(1,128)} %get-tuple-element.45), channel_id=1, source_target_pairs={{0,4},{4,8},{8,12},{12,0},{1,5},{5,9},{9,13},{13,1},{2,6},{6,10},{... | collective-permute-start | bytes 49160 | tf_op jit(solution)/shard_map/ppermute | solution.py:25
  14.2 18.7 %copy-start.1 = (s32[32,16,128]{0,1,2:T(8,128)}, s32[32,16,128]{0,1,2:T(8,128)S(1)}, u32[]{:S(2)}) copy-start(s32[32,16,128]{0,1,2:T(8,128)S(1)} %copy.375) | copy-start | bytes 786436
  18.2 10.6 %collective-permute-start.2 = (f32[1,16,130]{2,1,0:T(8,128)}, f32[1,16,130]{2,1,0:T(8,128)}, u32[]{:S(2)}, u32[]{:S(2)}) collective-permute-start(f32[1,16,130]{2,1,0:T(8,128)} %get-tuple-element.46), channel_id=1, source_target_pairs={{1,0},{3,2},{5,4},{7,6},{9,8},{11,10},{13,12},{15,14},{17,16},{19,... | collective-permute-start | bytes 24968 | tf_op jit(solution)/shard_map/ppermute | solution.py:27
  19.5 11.7 %collective-permute-start.3 = (f32[1,16,130]{2,1,0:T(8,128)}, f32[1,16,130]{2,1,0:T(8,128)S(1)}, u32[]{:S(2)}, u32[]{:S(2)}) collective-permute-start(f32[1,16,130]{2,1,0:T(8,128)} %get-tuple-element.47), channel_id=1, source_target_pairs={{0,1},{2,3},{4,5},{6,7},{8,9},{10,11},{12,13},{14,15},{16,17},{18,... | collective-permute-start | bytes 24968 | tf_op jit(solution)/shard_map/ppermute | solution.py:25
  24.2 3.2 %copy-start.4 = (f32[32,16,128]{2,1,0:T(8,128)S(1)}, f32[32,16,128]{2,1,0:T(8,128)}, u32[]{:S(2)}) copy-start(f32[32,16,128]{2,1,0:T(8,128)} %get-tuple-element.49) | copy-start | bytes 786436
  37.3 8.2 %collective-permute-start.6 = (f32[32,16,1]{0,1,2:T(8,128)S(1)}, f32[32,16,1]{0,1,2:T(8,128)S(1)}, u32[]{:S(2)}, u32[]{:S(2)}) collective-permute-start(f32[32,16,1]{0,1,2:T(8,128)S(1)} %get-tuple-element.43), channel_id=1, source_target_pairs={{0,2},{1,3},{4,6},{5,7},{8,10},{9,11},{12,14},{13,15},{16,18},{17,... | collective-permute-start | bytes 6152 | tf_op jit(solution)/shard_map/ppermute | solution.py:25
  40.2 5.5 %collective-permute-start.7 = (f32[32,16,1]{0,1,2:T(8,128)S(1)}, f32[32,16,1]{0,1,2:T(8,128)S(1)}, u32[]{:S(2)}, u32[]{:S(2)}) collective-permute-start(f32[32,16,1]{0,1,2:T(8,128)S(1)} %get-tuple-element.42), channel_id=1, source_target_pairs={{2,0},{3,1},{6,4},{7,5},{10,8},{11,9},{14,12},{15,13},{18,16},{19,... | collective-permute-start | bytes 6152 | tf_op jit(solution)/shard_map/ppermute | solution.py:27
  41.6 17.3 %collective-permute-start.10 = (f32[32,1,128]{0,1,2:T(1,128)S(1)}, f32[32,1,128]{0,1,2:T(1,128)S(1)}, u32[]{:S(2)}, u32[]{:S(2)}) collective-permute-start(f32[32,1,128]{0,1,2:T(1,128)S(1)} %get-tuple-element.40), channel_id=1, source_target_pairs={{4,0},{8,4},{12,8},{0,12},{5,1},{9,5},{13,9},{1,13},{6,2},{10,6},{... | collective-permute-start | bytes 49160 | tf_op jit(solution)/shard_map/ppermute | solution.py:27
  45.5 13.4 %collective-permute-start.11 = (f32[32,1,128]{0,1,2:T(1,128)S(1)}, f32[32,1,128]{0,1,2:T(1,128)S(1)}, u32[]{:S(2)}, u32[]{:S(2)}) collective-permute-start(f32[32,1,128]{0,1,2:T(1,128)S(1)} %get-tuple-element.41), channel_id=1, source_target_pairs={{0,4},{4,8},{8,12},{12,0},{1,5},{5,9},{9,13},{13,1},{2,6},{6,10},{... | collective-permute-start | bytes 49160 | tf_op jit(solution)/shard_map/ppermute | solution.py:25
  47.2 6.9 %copy-start.8 = (f32[32,16,128]{2,1,0:T(8,128)S(1)}, f32[32,16,128]{2,1,0:T(8,128)}, u32[]{:S(2)}) copy-start(f32[32,16,128]{2,1,0:T(8,128)} %param.8) | copy-start | bytes 786436
  49.1 6.5 %collective-permute-start.8 = (f32[1,16,130]{2,1,0:T(8,128)S(1)}, f32[1,16,130]{2,1,0:T(8,128)S(1)}, u32[]{:S(2)}, u32[]{:S(2)}) collective-permute-start(f32[1,16,130]{2,1,0:T(8,128)S(1)} %copy.390), channel_id=1, source_target_pairs={{1,0},{3,2},{5,4},{7,6},{9,8},{11,10},{13,12},{15,14},{17,16},{19,... | collective-permute-start | bytes 24968 | tf_op jit(solution)/shard_map/ppermute | solution.py:27
  51.1 6.2 %collective-permute-start.9 = (f32[1,16,130]{2,1,0:T(8,128)S(1)}, f32[1,16,130]{2,1,0:T(8,128)S(1)}, u32[]{:S(2)}, u32[]{:S(2)}) collective-permute-start(f32[1,16,130]{2,1,0:T(8,128)S(1)} %copy.392), channel_id=1, source_target_pairs={{0,1},{2,3},{4,5},{6,7},{8,9},{10,11},{12,13},{14,15},{16,17},{18,... | collective-permute-start | bytes 24968 | tf_op jit(solution)/shard_map/ppermute | solution.py:25
  61.9 9.6 %collective-permute-start.12 = (f32[32,16,1]{0,1,2:T(8,128)S(1)}, f32[32,16,1]{0,1,2:T(8,128)S(1)}, u32[]{:S(2)}, u32[]{:S(2)}) collective-permute-start(f32[32,16,1]{0,1,2:T(8,128)S(1)} %get-tuple-element.39), channel_id=1, source_target_pairs={{0,2},{1,3},{4,6},{5,7},{8,10},{9,11},{12,14},{13,15},{16,18},{17,... | collective-permute-start | bytes 6152 | tf_op jit(solution)/shard_map/ppermute | solution.py:25
  66.2 5.5 %collective-permute-start.13 = (f32[32,16,1]{0,1,2:T(8,128)S(1)}, f32[32,16,1]{0,1,2:T(8,128)S(1)}, u32[]{:S(2)}, u32[]{:S(2)}) collective-permute-start(f32[32,16,1]{0,1,2:T(8,128)S(1)} %get-tuple-element.38), channel_id=1, source_target_pairs={{2,0},{3,1},{6,4},{7,5},{10,8},{11,9},{14,12},{15,13},{18,16},{19,... | collective-permute-start | bytes 6152 | tf_op jit(solution)/shard_map/ppermute | solution.py:27
  67.6 17.3 %collective-permute-start.16 = (f32[32,1,128]{0,1,2:T(1,128)S(1)}, f32[32,1,128]{0,1,2:T(1,128)S(1)}, u32[]{:S(2)}, u32[]{:S(2)}) collective-permute-start(f32[32,1,128]{0,1,2:T(1,128)S(1)} %get-tuple-element.36), channel_id=1, source_target_pairs={{4,0},{8,4},{12,8},{0,12},{5,1},{9,5},{13,9},{1,13},{6,2},{10,6},{... | collective-permute-start | bytes 49160 | tf_op jit(solution)/shard_map/ppermute | solution.py:27
  71.5 13.5 %collective-permute-start.17 = (f32[32,1,128]{0,1,2:T(1,128)S(1)}, f32[32,1,128]{0,1,2:T(1,128)S(1)}, u32[]{:S(2)}, u32[]{:S(2)}) collective-permute-start(f32[32,1,128]{0,1,2:T(1,128)S(1)} %get-tuple-element.37), channel_id=1, source_target_pairs={{0,4},{4,8},{8,12},{12,0},{1,5},{5,9},{9,13},{13,1},{2,6},{6,10},{... | collective-permute-start | bytes 49160 | tf_op jit(solution)/shard_map/ppermute | solution.py:25
  75.4 6.2 %collective-permute-start.14 = (f32[1,16,130]{2,1,0:T(8,128)S(1)}, f32[1,16,130]{2,1,0:T(8,128)S(1)}, u32[]{:S(2)}, u32[]{:S(2)}) collective-permute-start(f32[1,16,130]{2,1,0:T(8,128)S(1)} %copy.395), channel_id=1, source_target_pairs={{1,0},{3,2},{5,4},{7,6},{9,8},{11,10},{13,12},{15,14},{17,16},{19,... | collective-permute-start | bytes 24968 | tf_op jit(solution)/shard_map/ppermute | solution.py:27
  78.5 4.7 %collective-permute-start.15 = (f32[1,16,130]{2,1,0:T(8,128)S(1)}, f32[1,16,130]{2,1,0:T(8,128)S(1)}, u32[]{:S(2)}, u32[]{:S(2)}) collective-permute-start(f32[1,16,130]{2,1,0:T(8,128)S(1)} %copy.397), channel_id=1, source_target_pairs={{0,1},{2,3},{4,5},{6,7},{8,9},{10,11},{12,13},{14,15},{16,17},{18,... | collective-permute-start | bytes 24968 | tf_op jit(solution)/shard_map/ppermute | solution.py:25
  115.6 9.5 %collective-permute-start.18 = (f32[16,8,1]{2,1,0:T(8,128)S(1)}, f32[16,8,1]{2,1,0:T(8,128)S(1)}, u32[]{:S(2)}, u32[]{:S(2)}) collective-permute-start(f32[16,8,1]{2,1,0:T(8,128)S(1)} %get-tuple-element.63), channel_id=1, source_target_pairs={{0,2},{1,3},{4,6},{5,7},{8,10},{9,11},{12,14},{13,15},{16,18},{17,... | collective-permute-start | bytes 1544 | tf_op jit(solution)/shard_map/ppermute | solution.py:25
  119.8 6.2 %collective-permute-start.19 = (f32[16,8,1]{2,1,0:T(8,128)S(1)}, f32[16,8,1]{2,1,0:T(8,128)S(1)}, u32[]{:S(2)}, u32[]{:S(2)}) collective-permute-start(f32[16,8,1]{2,1,0:T(8,128)S(1)} %get-tuple-element.62), channel_id=1, source_target_pairs={{2,0},{3,1},{6,4},{7,5},{10,8},{11,9},{14,12},{15,13},{18,16},{19,... | collective-permute-start | bytes 1544 | tf_op jit(solution)/shard_map/ppermute | solution.py:27
  121.2 10.0 %collective-permute-start.22 = (f32[16,1,64]{2,1,0:T(1,128)S(1)}, f32[16,1,64]{2,1,0:T(1,128)S(1)}, u32[]{:S(2)}, u32[]{:S(2)}) collective-permute-start(f32[16,1,64]{2,1,0:T(1,128)S(1)} %get-tuple-element.60), channel_id=1, source_target_pairs={{4,0},{8,4},{12,8},{0,12},{5,1},{9,5},{13,9},{1,13},{6,2},{10,6},{... | collective-permute-start | bytes 12296 | tf_op jit(solution)/shard_map/ppermute | solution.py:27
  125.0 6.2 %collective-permute-start.23 = (f32[16,1,64]{2,1,0:T(1,128)S(1)}, f32[16,1,64]{2,1,0:T(1,128)S(1)}, u32[]{:S(2)}, u32[]{:S(2)}) collective-permute-start(f32[16,1,64]{2,1,0:T(1,128)S(1)} %get-tuple-element.61), channel_id=1, source_target_pairs={{0,4},{4,8},{8,12},{12,0},{1,5},{5,9},{9,13},{13,1},{2,6},{6,10},{... | collective-permute-start | bytes 12296 | tf_op jit(solution)/shard_map/ppermute | solution.py:25
  126.1 4.3 %collective-permute-start.20 = (f32[1,8,66]{2,1,0:T(8,128)S(1)}, f32[1,8,66]{2,1,0:T(8,128)S(1)}, u32[]{:S(2)}, u32[]{:S(2)}) collective-permute-start(f32[1,8,66]{2,1,0:T(8,128)S(1)} %get-tuple-element.54), channel_id=1, source_target_pairs={{1,0},{3,2},{5,4},{7,6},{9,8},{11,10},{13,12},{15,14},{17,16},{19,... | collective-permute-start | bytes 6344 | tf_op jit(solution)/shard_map/ppermute | solution.py:27
  127.4 3.8 %collective-permute-start.21 = (f32[1,8,66]{2,1,0:T(8,128)S(1)}, f32[1,8,66]{2,1,0:T(8,128)S(1)}, u32[]{:S(2)}, u32[]{:S(2)}) collective-permute-start(f32[1,8,66]{2,1,0:T(8,128)S(1)} %get-tuple-element.55), channel_id=1, source_target_pairs={{0,1},{2,3},{4,5},{6,7},{8,9},{10,11},{12,13},{14,15},{16,17},{18,... | collective-permute-start | bytes 6344 | tf_op jit(solution)/shard_map/ppermute | solution.py:25
  136.7 49.8 %copy-start.9 = (s32[32]{0:T(128)S(1)}, s32[32]{0:T(128)}, u32[]{:S(2)}) copy-start(s32[32]{0:T(128)} %param.11) | copy-start | bytes 388
  136.8 8.8 %collective-permute-start.24 = (f32[8,4,1]{2,1,0:T(4,128)S(1)}, f32[8,4,1]{2,1,0:T(4,128)S(1)}, u32[]{:S(2)}, u32[]{:S(2)}) collective-permute-start(f32[8,4,1]{2,1,0:T(4,128)S(1)} %get-tuple-element.82), channel_id=1, source_target_pairs={{0,2},{1,3},{4,6},{5,7},{8,10},{9,11},{12,14},{13,15},{16,18},{17,... | collective-permute-start | bytes 392 | tf_op jit(solution)/shard_map/ppermute | solution.py:25
  140.7 5.6 %collective-permute-start.25 = (f32[8,4,1]{2,1,0:T(4,128)S(1)}, f32[8,4,1]{2,1,0:T(4,128)S(1)}, u32[]{:S(2)}, u32[]{:S(2)}) collective-permute-start(f32[8,4,1]{2,1,0:T(4,128)S(1)} %get-tuple-element.81), channel_id=1, source_target_pairs={{2,0},{3,1},{6,4},{7,5},{10,8},{11,9},{14,12},{15,13},{18,16},{19,... | collective-permute-start | bytes 392 | tf_op jit(solution)/shard_map/ppermute | solution.py:27
  142.0 9.5 %collective-permute-start.28 = (f32[8,1,32]{2,1,0:T(1,128)S(1)}, f32[8,1,32]{2,1,0:T(1,128)S(1)}, u32[]{:S(2)}, u32[]{:S(2)}) collective-permute-start(f32[8,1,32]{2,1,0:T(1,128)S(1)} %get-tuple-element.79), channel_id=1, source_target_pairs={{4,0},{8,4},{12,8},{0,12},{5,1},{9,5},{13,9},{1,13},{6,2},{10,6},{... | collective-permute-start | bytes 3080 | tf_op jit(solution)/shard_map/ppermute | solution.py:27
  145.6 5.9 %collective-permute-start.29 = (f32[8,1,32]{2,1,0:T(1,128)S(1)}, f32[8,1,32]{2,1,0:T(1,128)S(1)}, u32[]{:S(2)}, u32[]{:S(2)}) collective-permute-start(f32[8,1,32]{2,1,0:T(1,128)S(1)} %get-tuple-element.80), channel_id=1, source_target_pairs={{0,4},{4,8},{8,12},{12,0},{1,5},{5,9},{9,13},{13,1},{2,6},{6,10},{... | collective-permute-start | bytes 3080 | tf_op jit(solution)/shard_map/ppermute | solution.py:25
  146.4 4.3 %collective-permute-start.26 = (f32[1,4,34]{2,1,0:T(4,128)S(1)}, f32[1,4,34]{2,1,0:T(4,128)S(1)}, u32[]{:S(2)}, u32[]{:S(2)}) collective-permute-start(f32[1,4,34]{2,1,0:T(4,128)S(1)} %get-tuple-element.66), channel_id=1, source_target_pairs={{1,0},{3,2},{5,4},{7,6},{9,8},{11,10},{13,12},{15,14},{17,16},{19,... | collective-permute-start | bytes 1640 | tf_op jit(solution)/shard_map/ppermute | solution.py:27
  147.7 3.8 %collective-permute-start.27 = (f32[1,4,34]{2,1,0:T(4,128)S(1)}, f32[1,4,34]{2,1,0:T(4,128)S(1)}, u32[]{:S(2)}, u32[]{:S(2)}) collective-permute-start(f32[1,4,34]{2,1,0:T(4,128)S(1)} %get-tuple-element.67), channel_id=1, source_target_pairs={{0,1},{2,3},{4,5},{6,7},{8,9},{10,11},{12,13},{14,15},{16,17},{18,... | collective-permute-start | bytes 1640 | tf_op jit(solution)/shard_map/ppermute | solution.py:25
  175.2 4.7 %collective-permute-start.30 = (f32[8,4,1]{2,1,0:T(4,128)S(1)}, f32[8,4,1]{2,1,0:T(4,128)S(1)}, u32[]{:S(2)}, u32[]{:S(2)}) collective-permute-start(f32[8,4,1]{2,1,0:T(4,128)S(1)} %get-tuple-element.78), channel_id=1, source_target_pairs={{0,2},{1,3},{4,6},{5,7},{8,10},{9,11},{12,14},{13,15},{16,18},{17,... | collective-permute-start | bytes 392 | tf_op jit(solution)/shard_map/ppermute | solution.py:25
  176.5 5.6 %collective-permute-start.31 = (f32[8,4,1]{2,1,0:T(4,128)S(1)}, f32[8,4,1]{2,1,0:T(4,128)S(1)}, u32[]{:S(2)}, u32[]{:S(2)}) collective-permute-start(f32[8,4,1]{2,1,0:T(4,128)S(1)} %get-tuple-element.77), channel_id=1, source_target_pairs={{2,0},{3,1},{6,4},{7,5},{10,8},{11,9},{14,12},{15,13},{18,16},{19,... | collective-permute-start | bytes 392 | tf_op jit(solution)/shard_map/ppermute | solution.py:27
  177.8 9.5 %collective-permute-start.34 = (f32[8,1,32]{2,1,0:T(1,128)S(1)}, f32[8,1,32]{2,1,0:T(1,128)S(1)}, u32[]{:S(2)}, u32[]{:S(2)}) collective-permute-start(f32[8,1,32]{2,1,0:T(1,128)S(1)} %get-tuple-element.75), channel_id=1, source_target_pairs={{4,0},{8,4},{12,8},{0,12},{5,1},{9,5},{13,9},{1,13},{6,2},{10,6},{... | collective-permute-start | bytes 3080 | tf_op jit(solution)/shard_map/ppermute | solution.py:27
  178.5 8.9 %collective-permute-start.35 = (f32[8,1,32]{2,1,0:T(1,128)S(1)}, f32[8,1,32]{2,1,0:T(1,128)S(1)}, u32[]{:S(2)}, u32[]{:S(2)}) collective-permute-start(f32[8,1,32]{2,1,0:T(1,128)S(1)} %get-tuple-element.76), channel_id=1, source_target_pairs={{0,4},{4,8},{8,12},{12,0},{1,5},{5,9},{9,13},{13,1},{2,6},{6,10},{... | collective-permute-start | bytes 3080 | tf_op jit(solution)/shard_map/ppermute | solution.py:25
  182.2 4.5 %collective-permute-start.32 = (f32[1,4,34]{2,1,0:T(4,128)S(1)}, f32[1,4,34]{2,1,0:T(4,128)S(1)}, u32[]{:S(2)}, u32[]{:S(2)}) collective-permute-start(f32[1,4,34]{2,1,0:T(4,128)S(1)} %get-tuple-element.64), channel_id=1, source_target_pairs={{1,0},{3,2},{5,4},{7,6},{9,8},{11,10},{13,12},{15,14},{17,16},{19,... | collective-permute-start | bytes 1640 | tf_op jit(solution)/shard_map/ppermute | solution.py:27
  183.5 3.8 %collective-permute-start.33 = (f32[1,4,34]{2,1,0:T(4,128)S(1)}, f32[1,4,34]{2,1,0:T(4,128)S(1)}, u32[]{:S(2)}, u32[]{:S(2)}) collective-permute-start(f32[1,4,34]{2,1,0:T(4,128)S(1)} %get-tuple-element.65), channel_id=1, source_target_pairs={{0,1},{2,3},{4,5},{6,7},{8,9},{10,11},{12,13},{14,15},{16,17},{18,... | collective-permute-start | bytes 1640 | tf_op jit(solution)/shard_map/ppermute | solution.py:25
  188.0 6.1 %collective-permute-start.36 = (f32[16,8,1]{2,1,0:T(8,128)S(1)}, f32[16,8,1]{2,1,0:T(8,128)S(1)}, u32[]{:S(2)}, u32[]{:S(2)}) collective-permute-start(f32[16,8,1]{2,1,0:T(8,128)S(1)} %get-tuple-element.59), channel_id=1, source_target_pairs={{0,2},{1,3},{4,6},{5,7},{8,10},{9,11},{12,14},{13,15},{16,18},{17,... | collective-permute-start | bytes 1544 | tf_op jit(solution)/shard_map/ppermute | solution.py:25
  190.3 6.2 %collective-permute-start.37 = (f32[16,8,1]{2,1,0:T(8,128)S(1)}, f32[16,8,1]{2,1,0:T(8,128)S(1)}, u32[]{:S(2)}, u32[]{:S(2)}) collective-permute-start(f32[16,8,1]{2,1,0:T(8,128)S(1)} %get-tuple-element.58), channel_id=1, source_target_pairs={{2,0},{3,1},{6,4},{7,5},{10,8},{11,9},{14,12},{15,13},{18,16},{19,... | collective-permute-start | bytes 1544 | tf_op jit(solution)/shard_map/ppermute | solution.py:27
  191.6 10.0 %collective-permute-start.40 = (f32[16,1,64]{2,1,0:T(1,128)S(1)}, f32[16,1,64]{2,1,0:T(1,128)S(1)}, u32[]{:S(2)}, u32[]{:S(2)}) collective-permute-start(f32[16,1,64]{2,1,0:T(1,128)S(1)} %get-tuple-element.56), channel_id=1, source_target_pairs={{4,0},{8,4},{12,8},{0,12},{5,1},{9,5},{13,9},{1,13},{6,2},{10,6},{... | collective-permute-start | bytes 12296 | tf_op jit(solution)/shard_map/ppermute | solution.py:27
  194.0 7.6 %collective-permute-start.41 = (f32[16,1,64]{2,1,0:T(1,128)S(1)}, f32[16,1,64]{2,1,0:T(1,128)S(1)}, u32[]{:S(2)}, u32[]{:S(2)}) collective-permute-start(f32[16,1,64]{2,1,0:T(1,128)S(1)} %get-tuple-element.57), channel_id=1, source_target_pairs={{0,4},{4,8},{8,12},{12,0},{1,5},{5,9},{9,13},{13,1},{2,6},{6,10},{... | collective-permute-start | bytes 12296 | tf_op jit(solution)/shard_map/ppermute | solution.py:25
  196.5 4.7 %collective-permute-start.38 = (f32[1,8,66]{2,1,0:T(8,128)S(1)}, f32[1,8,66]{2,1,0:T(8,128)S(1)}, u32[]{:S(2)}, u32[]{:S(2)}) collective-permute-start(f32[1,8,66]{2,1,0:T(8,128)S(1)} %get-tuple-element.52), channel_id=1, source_target_pairs={{1,0},{3,2},{5,4},{7,6},{9,8},{11,10},{13,12},{15,14},{17,16},{19,... | collective-permute-start | bytes 6344 | tf_op jit(solution)/shard_map/ppermute | solution.py:27
  197.8 3.8 %collective-permute-start.39 = (f32[1,8,66]{2,1,0:T(8,128)S(1)}, f32[1,8,66]{2,1,0:T(8,128)S(1)}, u32[]{:S(2)}, u32[]{:S(2)}) collective-permute-start(f32[1,8,66]{2,1,0:T(8,128)S(1)} %get-tuple-element.53), channel_id=1, source_target_pairs={{0,1},{2,3},{4,5},{6,7},{8,9},{10,11},{12,13},{14,15},{16,17},{18,... | collective-permute-start | bytes 6344 | tf_op jit(solution)/shard_map/ppermute | solution.py:25
  202.3 8.0 %copy-start = (f32[32,16,128]{0,1,2:T(8,128)}, f32[32,16,128]{0,1,2:T(8,128)S(1)}, u32[]{:S(2)}) copy-start(f32[32,16,128]{0,1,2:T(8,128)S(1)} %bitcast_add_fusion) | copy-start | bytes 786436
  202.4 7.5 %collective-permute-start.42 = (f32[32,16,1]{0,1,2:T(8,128)S(1)}, f32[32,16,1]{0,1,2:T(8,128)S(1)}, u32[]{:S(2)}, u32[]{:S(2)}) collective-permute-start(f32[32,16,1]{0,1,2:T(8,128)S(1)} %get-tuple-element.35), channel_id=1, source_target_pairs={{0,2},{1,3},{4,6},{5,7},{8,10},{9,11},{12,14},{13,15},{16,18},{17,... | collective-permute-start | bytes 6152 | tf_op jit(solution)/shard_map/ppermute | solution.py:25
  204.8 5.5 %collective-permute-start.43 = (f32[32,16,1]{0,1,2:T(8,128)S(1)}, f32[32,16,1]{0,1,2:T(8,128)S(1)}, u32[]{:S(2)}, u32[]{:S(2)}) collective-permute-start(f32[32,16,1]{0,1,2:T(8,128)S(1)} %get-tuple-element.34), channel_id=1, source_target_pairs={{2,0},{3,1},{6,4},{7,5},{10,8},{11,9},{14,12},{15,13},{18,16},{19,... | collective-permute-start | bytes 6152 | tf_op jit(solution)/shard_map/ppermute | solution.py:27
  206.2 16.5 %collective-permute-start.46 = (f32[32,1,128]{0,1,2:T(1,128)S(1)}, f32[32,1,128]{0,1,2:T(1,128)S(1)}, u32[]{:S(2)}, u32[]{:S(2)}) collective-permute-start(f32[32,1,128]{0,1,2:T(1,128)S(1)} %get-tuple-element.32), channel_id=1, source_target_pairs={{4,0},{8,4},{12,8},{0,12},{5,1},{9,5},{13,9},{1,13},{6,2},{10,6},{... | collective-permute-start | bytes 49160 | tf_op jit(solution)/shard_map/ppermute | solution.py:27
  209.8 12.8 %collective-permute-start.47 = (f32[32,1,128]{0,1,2:T(1,128)S(1)}, f32[32,1,128]{0,1,2:T(1,128)S(1)}, u32[]{:S(2)}, u32[]{:S(2)}) collective-permute-start(f32[32,1,128]{0,1,2:T(1,128)S(1)} %get-tuple-element.33), channel_id=1, source_target_pairs={{0,4},{4,8},{8,12},{12,0},{1,5},{5,9},{9,13},{13,1},{2,6},{6,10},{... | collective-permute-start | bytes 49160 | tf_op jit(solution)/shard_map/ppermute | solution.py:25
  211.7 6.9 %copy-start.10 = (u32[32]{0:T(128)S(1)}, u32[32]{0:T(128)}, u32[]{:S(2)}) copy-start(u32[32]{0:T(128)} %constant.148) | copy-start | bytes 388
  213.6 5.6 %collective-permute-start.44 = (f32[1,16,130]{2,1,0:T(8,128)S(1)}, f32[1,16,130]{2,1,0:T(8,128)S(1)}, u32[]{:S(2)}, u32[]{:S(2)}) collective-permute-start(f32[1,16,130]{2,1,0:T(8,128)S(1)} %copy.411), channel_id=1, source_target_pairs={{1,0},{3,2},{5,4},{7,6},{9,8},{11,10},{13,12},{15,14},{17,16},{19,... | collective-permute-start | bytes 24968 | tf_op jit(solution)/shard_map/ppermute | solution.py:27
  215.6 5.3 %collective-permute-start.45 = (f32[1,16,130]{2,1,0:T(8,128)S(1)}, f32[1,16,130]{2,1,0:T(8,128)S(1)}, u32[]{:S(2)}, u32[]{:S(2)}) collective-permute-start(f32[1,16,130]{2,1,0:T(8,128)S(1)} %copy.413), channel_id=1, source_target_pairs={{0,1},{2,3},{4,5},{6,7},{8,9},{10,11},{12,13},{14,15},{16,17},{18,... | collective-permute-start | bytes 24968 | tf_op jit(solution)/shard_map/ppermute | solution.py:25
  229.3 59.4 %collective-permute-start.48 = (f32[32,16,1]{0,1,2:T(8,128)S(1)}, f32[32,16,1]{0,1,2:T(8,128)S(1)}, u32[]{:S(2)}, u32[]{:S(2)}) collective-permute-start(f32[32,16,1]{0,1,2:T(8,128)S(1)} %get-tuple-element.31), channel_id=1, source_target_pairs={{0,2},{1,3},{4,6},{5,7},{8,10},{9,11},{12,14},{13,15},{16,18},{17,... | collective-permute-start | bytes 6152 | tf_op jit(solution)/shard_map/ppermute | solution.py:25
  233.4 55.3 %collective-permute-start.49 = (f32[32,16,1]{0,1,2:T(8,128)S(1)}, f32[32,16,1]{0,1,2:T(8,128)S(1)}, u32[]{:S(2)}, u32[]{:S(2)}) collective-permute-start(f32[32,16,1]{0,1,2:T(8,128)S(1)} %get-tuple-element.30), channel_id=1, source_target_pairs={{2,0},{3,1},{6,4},{7,5},{10,8},{11,9},{14,12},{15,13},{18,16},{19,... | collective-permute-start | bytes 6152 | tf_op jit(solution)/shard_map/ppermute | solution.py:27
  234.7 69.8 %collective-permute-start.52 = (f32[32,1,128]{0,1,2:T(1,128)S(1)}, f32[32,1,128]{0,1,2:T(1,128)S(1)}, u32[]{:S(2)}, u32[]{:S(2)}) collective-permute-start(f32[32,1,128]{0,1,2:T(1,128)S(1)} %get-tuple-element.28), channel_id=1, source_target_pairs={{4,0},{8,4},{12,8},{0,12},{5,1},{9,5},{13,9},{1,13},{6,2},{10,6},{... | collective-permute-start | bytes 49160 | tf_op jit(solution)/shard_map/ppermute | solution.py:27
  238.6 65.9 %collective-permute-start.53 = (f32[32,1,128]{0,1,2:T(1,128)S(1)}, f32[32,1,128]{0,1,2:T(1,128)S(1)}, u32[]{:S(2)}, u32[]{:S(2)}) collective-permute-start(f32[32,1,128]{0,1,2:T(1,128)S(1)} %get-tuple-element.29), channel_id=1, source_target_pairs={{0,4},{4,8},{8,12},{12,0},{1,5},{5,9},{9,13},{13,1},{2,6},{6,10},{... | collective-permute-start | bytes 49160 | tf_op jit(solution)/shard_map/ppermute | solution.py:25
  292.3 8.8 %collective-permute-start.50 = (f32[1,16,130]{2,1,0:T(8,128)S(1)}, f32[1,16,130]{2,1,0:T(8,128)S(1)}, u32[]{:S(2)}, u32[]{:S(2)}) collective-permute-start(f32[1,16,130]{2,1,0:T(8,128)S(1)} %copy.415), channel_id=1, source_target_pairs={{1,0},{3,2},{5,4},{7,6},{9,8},{11,10},{13,12},{15,14},{17,16},{19,... | collective-permute-start | bytes 24968 | tf_op jit(solution)/shard_map/ppermute | solution.py:27
  295.5 7.3 %collective-permute-start.51 = (f32[1,16,130]{2,1,0:T(8,128)S(1)}, f32[1,16,130]{2,1,0:T(8,128)S(1)}, u32[]{:S(2)}, u32[]{:S(2)}) collective-permute-start(f32[1,16,130]{2,1,0:T(8,128)S(1)} %copy.417), channel_id=1, source_target_pairs={{0,1},{2,3},{4,5},{6,7},{8,9},{10,11},{12,13},{14,15},{16,17},{18,... | collective-permute-start | bytes 24968 | tf_op jit(solution)/shard_map/ppermute | solution.py:25
  301.1 3.4 %copy-start.2 = (s32[32,16,128]{0,1,2:T(8,128)S(1)}, s32[32,16,128]{0,1,2:T(8,128)}, u32[]{:S(2)}) copy-start(s32[32,16,128]{0,1,2:T(8,128)} %copy-done.1) | copy-start | bytes 786436
  (1 other events, 1.8 us)
where the time goes:
time: 312 us; the launch traced here: 311 us
  starting transfers between devices  113 us (36%)
  local copies, waits for them, and re-layouts  78.4 us (25%)
  blocking collectives  56.2 us (18%)
  other arithmetic  50.1 us (16%)
  waiting for transfers between devices  11.7 us (4%)
    ppermute x27, starting transfers between devices, padded(): lax.ppermute(tail, axis, [(i, (i + 1) % count) for i in range(ends)])  59.9 us
    ppermute x27, starting transfers between devices, padded(): lax.ppermute(head, axis, [((i + 1) % count, i) for i in range(ends)])  52.7 us
    unnamed x1, blocking collectives  33.8 us
    all_gather x1, blocking collectives, coarse_solve(): lax.all_gather(source[None], ('blk', 'len', 'wall'), axis=0, tiled=True)  22.5 us
    reshape x3, local copies, waits for them, and re-layouts, restrict(): return field.reshape(a // 2, 2, b // 2, 2, c // 2, 2).mean(axis=(1, 3, 5))  21.7 us
    slice x26, local copies, waits for them, and re-layouts, padded(): head = lax.slice_in_dim(cells, 0, width, axis=dim)  15.6 us
    scatter-add x1, other arithmetic, body(): jax.ops.segment_sum(surface.reshape(-1), patch_ids.reshape(-1), num_segme...  14.8 us
    unnamed x31, local copies, waits for them, and re-layouts  11 us
  transfers between devices with their start and end apart: 54, of which 12 were waited for; matrix products, arithmetic and copies ran while one was open for 22% of the time, Pallas kernels for 0%

commit v1 on v0

v1 whole, which is shorter than its diff:
```python
import functools

import jax
import jax.numpy as jnp
from jax import lax
from jax.experimental import pallas as pl
from jax.experimental.pallas import tpu as pltpu
from jax.sharding import PartitionSpec as P

SWEEPS = 2
SI = (0.6, 1.0, 3.0)
SE = (0.8, 1.2, 2.0)
SHIFT = 0.002
OMEGA = 0.8
DT = 0.1
H = 4
LANES = 128
HIGHEST = lax.Precision.HIGHEST
F32 = jnp.float32


def level_coef(level):
    return tuple((SI[i] + SE[i]) / 4.0**level for i in range(3))


def level_diag(level):
    return SHIFT + 2.0 * sum(level_coef(level))


def level_step(level):
    return OMEGA / level_diag(level)


def lane_of(shape):
    return lax.broadcasted_iota(jnp.int32, shape, len(shape) - 1)


def before(m, e):
    first = lane_of(m.shape) == 0
    rm, re = pltpu.roll(m, 1, 1), pltpu.roll(e, 1, 1)
    return jnp.where(first, re, rm), jnp.where(first, rm, re)


def after(m, e):
    last = lane_of(m.shape) == LANES - 1
    rm, re = pltpu.roll(m, LANES - 1, 1), pltpu.roll(e, LANES - 1, 1)
    return jnp.where(last, re, rm), jnp.where(last, rm, re)


def beside_lanes(m, e):
    bm, be = before(m, e)
    am, ae = after(m, e)
    return bm + am, be + ae


def beside_lanes_main(m, e):
    lane = lane_of(m.shape)
    left = jnp.where(lane == 0, pltpu.roll(e, 1, 1), pltpu.roll(m, 1, 1))
    right = jnp.where(lane == LANES - 1, pltpu.roll(e, LANES - 1, 1), pltpu.roll(m, LANES - 1, 1))
    return left + right


def beside_rows(x, row_before, row_after):
    rows = x.shape[0]
    row = lax.broadcasted_iota(jnp.int32, x.shape, 0)
    low = jnp.where(row == 0, row_before, pltpu.roll(x, 1, 0))
    high = jnp.where(row == rows - 1, row_after, pltpu.roll(x, rows - 1, 0))
    return low + high


def beside_dense(x):
    return pltpu.roll(x, 1, 0) + pltpu.roll(x, x.shape[0] - 1, 0)


def plane(ref, i, rows):
    return ref[pl.ds(pl.multiple_of(i * rows, rows), rows), :]


def set_plane(ref, i, rows, value):
    ref[pl.ds(pl.multiple_of(i * rows, rows), rows), :] = value


def loop(low, high, step, unroll):
    def wrapped(i, carry):
        step(i)
        return carry

    lax.fori_loop(low, high, wrapped, 0, unroll=min(unroll, high - low))


def pack_faces(n_len, adj, ion, mask, mis, wall_out, *outs):
    W, C, L = adj.shape
    arrays = (adj, ion, mask, mis)
    wall, length = lax.axis_index("wall"), lax.axis_index("len")
    base = jnp.where(wall == 0, W - H, 0)
    group = lane_of((C, LANES)) // H
    n_dir = 1 if n_len == 2 else 2
    strips, corners = outs[:n_dir], outs[n_dir:]
    turns = [jnp.where(length == 0, H, 0)] if n_dir == 1 else [H, 0]
    for d in range(n_dir):
        corner = jnp.zeros((C, LANES), F32)
        for a, ref in enumerate(arrays):
            strip = jnp.zeros((C, LANES), F32)
            for w in range(W):
                turned = pltpu.roll(ref[w].astype(F32), lax.rem(H * w + turns[d], LANES), 1)
                strip = jnp.where(group == w, turned, strip)
            strips[d][a] = strip
            for p in range(H):
                face = ref[base + p].astype(F32)
                if d == 0:
                    wall_out[a, p] = face
                slot = a * H + p
                turned = pltpu.roll(face, lax.rem(H * slot + turns[d], LANES), 1)
                corner = jnp.where(group == slot, turned, corner)
        corners[d][...] = corner


def spots(m_ref, e_ref, i, rows, coef):
    m, e = plane(m_ref, i, rows), plane(e_ref, i, rows)
    wm = plane(m_ref, i - 1, rows) + plane(m_ref, i + 1, rows)
    we = plane(e_ref, i - 1, rows) + plane(e_ref, i + 1, rows)
    lm, le = beside_lanes(m, e)
    cm, ce = beside_rows(m, 0.0, 0.0), beside_rows(e, 0.0, 0.0)
    double = 2.0 * sum(coef)
    dm = double * m - coef[0] * wm - coef[1] * cm - coef[2] * lm
    de = double * e - coef[0] * we - coef[1] * ce - coef[2] * le
    return m, e, dm, de


def sector(n_len, adj, ion, mask, mis, wall_in, *rest):
    W, C, L = adj.shape
    N = W + 2 * H
    n_dir = 1 if n_len == 2 else 2
    strips, corners, rest = rest[:n_dir], rest[n_dir : 2 * n_dir], rest[2 * n_dir :]
    qm, pm, pe, to_next, to_prev = rest[:5]
    xm, xe, qe = rest[5:9], rest[9:13], rest[13]
    wall, length = lax.axis_index("wall"), lax.axis_index("len")
    lane = lane_of((C, LANES))
    if n_dir == 1:
        offs, valid = [jnp.where(length == 0, 0, LANES - H)], [True]
    else:
        offs, valid = [0, LANES - H], [length < n_len - 1, length > 0]
    seen = [jnp.logical_and(lax.rem(lane - off + LANES, LANES) < H, ok) for off, ok in zip(offs, valid)]

    def rim(packed, base):
        out = jnp.zeros((C, LANES), F32)
        for d in range(n_dir):
            out = jnp.where(seen[d], pltpu.roll(packed[d], lax.rem(offs[d] - base + LANES, LANES), 1), out)
        return out

    here = jnp.where(wall == 0, N - H, 0)
    none = N - H - here
    zero = jnp.zeros((C, LANES), F32)
    for a, ref in enumerate((adj, ion, mask, mis)):
        packed = [strip[a] for strip in strips]
        for w in range(W):
            set_plane(xm[a], w + H, C, ref[w].astype(F32))
            set_plane(xe[a], w + H, C, rim(packed, H * w))
        packed = [corner[...] for corner in corners]
        for p in range(H):
            set_plane(xm[a], here + p, C, wall_in[a, p])
            set_plane(xe[a], here + p, C, rim(packed, H * (a * H + p)))
            set_plane(xm[a], none + p, C, zero)
            set_plane(xe[a], none + p, C, zero)
    for i in (0, N - 1):
        set_plane(qm, i, C, zero)
        set_plane(qe, i, C, zero)
    for i in (0, 1, N - 2, N - 1):
        set_plane(pm, i, C, zero)
        set_plane(pe, i, C, zero)

    def parabolic(i):
        m, e, dm, de = spots(xm[0], xe[0], i, C, SI)
        set_plane(qm, i, C, m - DT * plane(xm[2], i, C) * (dm + plane(xm[1], i, C) * m))
        set_plane(qe, i, C, e - DT * plane(xe[2], i, C) * (de + plane(xe[1], i, C) * e))

    loop(1, N - 1, parabolic, 2)

    def elliptic_source(i):
        m, e, dm, de = spots(qm, qe, i, C, SI)
        set_plane(pm, i, C, plane(xm[3], i, C) + dm)
        set_plane(pe, i, C, plane(xe[3], i, C) + de)

    loop(2, N - 2, elliptic_source, 2)

    pos_of = lane_of((8, LANES)) // 8
    tiles = N // 8
    for out, near, second in ((to_next, C - 1, C - 2), (to_prev, 0, 1)):
        for q, (m, r) in enumerate(((xm[0], near), (xm[2], near), (qm, near), (pm, near), (pm, second))):
            out[q * N : (q + 1) * N, :] = m[pl.ds(r, N, stride=C), :]
        packs = [jnp.zeros((8, LANES), F32), jnp.zeros((8, LANES), F32)]
        for q, e in enumerate((xe[0], xe[2], qe, pe)):
            dense = e[pl.ds(near, N, stride=C), :]
            for s in range(tiles):
                t = q * tiles + s
                turned = pltpu.roll(dense[8 * s : 8 * s + 8], (H + 8 * (t % 16)) % LANES, 1)
                packs[t // 16] = jnp.where(pos_of == t % 16, turned, packs[t // 16])
        out[5 * N : 5 * N + 8, :] = packs[0]
        out[5 * N + 8 : 5 * N + 16, :] = packs[1]


def unpacked(ref, N):
    lane = lane_of((8, LANES))
    rim = jnp.logical_or(lane < H, lane >= LANES - H)
    tiles = N // 8
    mains = [ref[q * N : (q + 1) * N, :] for q in range(5)]
    packs = [ref[5 * N : 5 * N + 8, :], ref[5 * N + 8 : 5 * N + 16, :]]
    rims = []
    for q in range(4):
        parts = []
        for s in range(tiles):
            t = q * tiles + s
            turned = pltpu.roll(packs[t // 16], (2 * LANES - H - 8 * (t % 16)) % LANES, 1)
            parts.append(jnp.where(rim, turned, 0.0))
        rims.append(jnp.concatenate(parts, 0))
    return [(mains[q], rims[q]) for q in range(4)] + [mains[4]]


def lateral(pair):
    m, e = pair
    lm, le = beside_lanes(m, e)
    double = 2.0 * sum(SI)
    return (
        double * m - SI[0] * beside_dense(m) - SI[2] * lm,
        double * e - SI[0] * beside_dense(e) - SI[2] * le,
    )


def rim_lanes(lane, length, n_len):
    return jnp.logical_or(
        jnp.logical_and(lane < H, length < n_len - 1),
        jnp.logical_and(lane >= LANES - H, length > 0),
    )


def source_rows(own, other):
    adj_o, mask_o, q_o, _, _ = own
    adj_n, mask_n, q_n, p_n, second_n = other
    step = DT * SI[1]
    delta_o = [step * mask_o[k] * adj_n[k] for k in range(2)]
    delta_n = [step * mask_n[k] * adj_o[k] for k in range(2)]
    lat_o, lat_n = lateral(delta_o), lateral(delta_n)
    near = [lat_o[k] - SI[1] * (q_n[k] + delta_n[k]) for k in range(2)]
    second = [-SI[1] * delta_o[k] for k in range(2)]
    halo = [p_n[k] + lat_n[k] - SI[1] * (q_o[k] + delta_o[k]) for k in range(2)]
    halo_second = second_n - SI[1] * delta_n[0]
    return near, second, halo, halo_second, delta_o[0]


def residual(electrodes, n_len, n_wall, pm, pe, ids, own_next, own_prev, from_next, from_prev, *rest):
    bm, be, rows_n, rows_p, message = rest[:5]
    surf, pairs, sums = rest[5:]
    _, C, L = ids.shape
    N = pm.shape[0] // C
    W = N - 2 * H
    wall, length = lax.axis_index("wall"), lax.axis_index("len")
    lane = lane_of((C, LANES))
    rim = rim_lanes(lane, length, n_len)

    def inside(i):
        w = wall * W + i - H
        return jnp.logical_and(w >= 0, w < n_wall * W)

    def clear(i):
        ok = inside(i)
        set_plane(bm, i, C, jnp.where(ok, plane(pm, i, C), 0.0))
        set_plane(be, i, C, jnp.where(jnp.logical_and(rim, ok), plane(pe, i, C), 0.0))

    loop(0, N, clear, 4)

    dense_lane = lane_of((N, LANES))
    ok_m = inside(lax.broadcasted_iota(jnp.int32, (N, LANES), 0))
    ok_e = jnp.logical_and(ok_m, rim_lanes(dense_lane, length, n_len))
    for own, other, out, near_at, second_at in (
        (own_next, from_next, rows_n, C - 1, C - 2),
        (own_prev, from_prev, rows_p, 0, 1),
    ):
        near, second, halo, halo_second, delta = source_rows(unpacked(own, N), unpacked(other, N))
        for k, (ref, ok) in enumerate(((bm, ok_m), (be, ok_e))):
            for at, extra in ((near_at, near[k]), (second_at, second[k])):
                spot = pl.ds(at, N, stride=C)
                ref[spot, :] = ref[spot, :] + jnp.where(ok, extra, 0.0)
        out[0] = jnp.where(ok_m, halo[0], 0.0)
        out[1] = jnp.where(ok_e, halo[1], 0.0)
        out[2] = jnp.where(ok_m, halo_second, 0.0)
        out[3] = delta

    coef, k0 = level_coef(0), level_step(0)

    def left(i):
        m, e = plane(bm, i, C), plane(be, i, C)
        wm = plane(bm, i - 1, C) + plane(bm, i + 1, C)
        cm = beside_rows(m, rows_p[0, pl.ds(i, 1), :], rows_n[0, pl.ds(i, 1), :])
        lm = beside_lanes_main(m, e)
        return (1.0 - OMEGA) * m + k0 * (coef[0] * wm + coef[1] * cm + coef[2] * lm)

    def pair(q):
        i = 2 * q + H
        first, second = left(i), left(i + 1)
        set_plane(pairs, q, C, first + second)

        @pl.when(q == 0)
        def _():
            surf[0] = first

        @pl.when(q == W // 2 - 1)
        def _():
            surf[1] = second

    loop(0, W // 2, pair, 2)

    half = W * C // 8
    z = pairs[pl.ds(0, 2 * half, stride=2), :] + pairs[pl.ds(1, 2 * half, stride=2), :]
    src = lax.broadcasted_iota(jnp.int32, (LANES, LANES), 0) // 2
    dst = lax.broadcasted_iota(jnp.int32, (LANES, LANES), 1)
    low = jnp.where(src == dst, 0.125, 0.0).astype(F32)
    high = jnp.where(src == dst - LANES // 2, 0.125, 0.0).astype(F32)
    message[0:half, :] = jnp.dot(z[:half], low, precision=HIGHEST, preferred_element_type=F32) + jnp.dot(
        z[half:], high, precision=HIGHEST, preferred_element_type=F32
    )
    patch = ids[0]
    message[half : half + C, :] = patch.astype(F32)

    b_surf = plane(bm, jnp.where(wall == 0, H, W + H - 1), C)
    y = k0 * (b_surf + jnp.where(wall == 0, surf[0], surf[1]))
    wide = sums.shape[0]
    sums[...] = jnp.zeros(sums.shape, F32)

    def one(e):
        sums[pl.ds(e, 1), :] = jnp.sum(jnp.where(patch == e, y, 0.0), axis=0, keepdims=True)

    loop(0, electrodes, one, 8)
    totals = lax.dot_general(
        jnp.ones((8, LANES), F32), sums[...], (((1,), (1,)), ((), ())), precision=HIGHEST, preferred_element_type=F32
    )
    message[half + C : half + C + 8, :] = jnp.zeros((8, LANES), F32)
    for t in range(wide // LANES):
        message[half + C + t : half + C + t + 1, :] = totals[0:1, t * LANES : (t + 1) * LANES]


def around(x, by):
    rows, lanes = x.shape
    lane = lane_of(x.shape)
    c = pltpu.roll(x, by, 0) + pltpu.roll(x, rows - by, 0)
    l = jnp.where(lane < by, 0.0, pltpu.roll(x, by, 1)) + jnp.where(
        lane >= lanes - by, 0.0, pltpu.roll(x, lanes - by, 1)
    )
    return c, l


def twins(x, by):
    rows, lanes = x.shape
    row = lax.broadcasted_iota(jnp.int32, x.shape, 0)
    lane = lane_of(x.shape)
    x = x + jnp.where((row & by) == 0, pltpu.roll(x, rows - by, 0), pltpu.roll(x, by, 0))
    return x + jnp.where((lane & by) == 0, pltpu.roll(x, lanes - by, 1), pltpu.roll(x, by, 1))


def solve(sizes, relative, electrodes, *refs):
    n_blk, n_len, n_wall = sizes
    count = n_len * n_wall
    blocks, refs = refs[:count], refs[count:]
    bm, be, rows_n, rows_p, qm, mask, owner, adj_prev, potential, patch_grad = refs[:10]
    b1, x1, b2, x2, b3, x3, wide_m, wide_e, thin, hx, xm, xe, hp, tm, te, sheet = refs[10:]
    W, C, L = mask.shape
    N = W + 2 * H
    W1, C1 = W // 2, C // 2
    planes, NC1, NL1 = b1.shape
    planes -= 2
    blk, length, wall = lax.axis_index("blk"), lax.axis_index("len"), lax.axis_index("wall")
    half = W1 // 2
    middle = LANES // 2
    lane8 = lane_of((C1, LANES))

    def blk_of(d):
        return lax.rem(blk - d + n_blk, n_blk) if relative else d

    def length_of(j):
        return (length + j) % n_len if n_len == 2 else j

    zero1 = jnp.zeros((NC1, NL1), F32)
    for ref in (b1, x1, b2, x2, b3, x3):
        ref[0] = zero1
        ref[ref.shape[0] - 1] = zero1

    for v in range(n_wall):
        wall_s = (wall + v) % n_wall
        mine = blocks[v * n_len : (v + 1) * n_len]

        def unpack(d):
            at = pl.ds(pl.multiple_of(C1 * blk_of(d), C1), C1)
            for t in range(n_len // 2):
                one, two = mine[2 * t], mine[2 * t + 1]
                for i in range(half):
                    a, b = one[d, i * C1 : (i + 1) * C1, :], two[d, i * C1 : (i + 1) * C1, :]
                    if n_len == 2:
                        a, b = jnp.where(length == 0, a, b), jnp.where(length == 0, b, a)
                    spot = 1 + wall_s * W1 + i
                    lanes = slice(t * LANES, (t + 1) * LANES)
                    b1[spot, at, lanes] = jnp.where(lane8 < middle, a, pltpu.roll(b, middle, 1))
                    b1[spot + half, at, lanes] = jnp.where(lane8 < middle, pltpu.roll(a, middle, 1), b)

        loop(0, n_blk, unpack, 4)

    def swept(x, wsum, b, level):
        coef, k = level_coef(level), level_step(level)
        c, l = around(x, 2 ** (level - 1))
        total = coef[0] * wsum + coef[1] * c + coef[2] * l
        return total, k

    def left(ref, i, level):
        b = ref[i]
        total, k = swept(b, ref[i - 1] + ref[i + 1], b, level)
        return (1.0 - OMEGA) * b + k * total

    def sweep(x_ref, b_ref, i, level):
        x = x_ref[i]
        total, k = swept(x, x_ref[i - 1] + x_ref[i + 1], None, level)
        return (1.0 - OMEGA) * x + k * (b_ref[i] + total)

    def down1(q):
        b2[1 + q] = 0.125 * twins(left(b1, 2 * q + 1, 1) + left(b1, 2 * q + 2, 1), 1)

    loop(0, planes // 2, down1, 4)

    def down2(q):
        b3[1 + q] = 0.125 * twins(left(b2, 2 * q + 1, 2) + left(b2, 2 * q + 2, 2), 2)

    loop(0, planes // 4, down2, 4)

    deep = planes // 8 * 2
    k3 = level_step(3)

    def start3(q):
        x3[1 + q] = k3 * b3[1 + q]

    loop(0, deep, start3, 8)
    for _ in range(SWEEPS):

        def sweep3(q):
            x2[1 + q] = sweep(x3, b3, 1 + q, 3)

        loop(0, deep, sweep3, 4)

        def back3(q):
            x3[1 + q] = x2[1 + q]

        loop(0, deep, back3, 8)

    k2 = level_step(2)

    def up2(q):
        coarse = x3[1 + q]
        x2[1 + 2 * q] = k2 * b2[1 + 2 * q] + coarse
        x2[2 + 2 * q] = k2 * b2[2 + 2 * q] + coarse

    loop(0, planes // 4, up2, 4)

    k1 = level_step(1)

    def up1(q):
        fine = sweep(x2, b2, 1 + q, 2)
        x1[1 + 2 * q] = k1 * b1[1 + 2 * q] + fine
        x1[2 + 2 * q] = k1 * b1[2 + 2 * q] + fine

    loop(0, planes // 2, up1, 4)

    def finish1(i):
        b1[1 + i] = sweep(x1, b1, 1 + i, 1)

    loop(0, planes, finish1, 4)

    lane = lane_of((NL1, LANES))
    source = lax.broadcasted_iota(jnp.int32, (NL1, LANES), 0)
    first = length * middle
    take_m = jnp.where(source == first + lane // 2, 1.0, 0.0).astype(F32)
    at_e = jnp.where(lane < H, middle + lane // 2, jnp.where(lane >= LANES - H, lane // 2 - middle, 4 * NL1))
    take_e = jnp.where(source == first + at_e, 1.0, 0.0).astype(F32)
    Q = W1 + 2

    def taken(sector_index, sel):
        rows = b1[pl.ds(wall * W1, Q), pl.ds(pl.multiple_of(sector_index * C1, C1), C1), :]
        return jnp.dot(rows.reshape(Q * C1, NL1), sel, precision=HIGHEST, preferred_element_type=F32)

    for wide, sel in ((wide_m, take_m), (wide_e, take_e)):
        value = taken(blk, sel)
        wide[pl.ds(0, Q * C1, stride=2), :] = value
        wide[pl.ds(1, Q * C1, stride=2), :] = value
    padded = 8 * ((Q + 7) // 8)
    thin[...] = jnp.zeros(thin.shape, F32)
    k0 = level_step(0)
    for side, (other, at, rows) in enumerate(
        ((lax.rem(blk + 1, n_blk), 0, rows_n), (lax.rem(blk + n_blk - 1, n_blk), C1 - 1, rows_p))
    ):
        for k, sel in enumerate((take_m, take_e)):
            thin[0 : Q * C1, :] = taken(other, sel)
            dense = thin[pl.ds(at, padded, stride=C1), :]
            hx[side, k] = jnp.zeros(hx.shape[2:], F32)
            hx[side, k, pl.ds(H - 2, padded, stride=2), :] = dense
            hx[side, k, pl.ds(H - 1, padded, stride=2), :] = dense

    def start0(i):
        q = (i - 2) // 2
        set_plane(xm, i, C, k0 * plane(bm, i, C) + plane(wide_m, q, C))
        set_plane(xe, i, C, k0 * plane(be, i, C) + plane(wide_e, q, C))

    loop(2, N - 2, start0, 4)
    for i in (0, 1, N - 2, N - 1):
        set_plane(xm, i, C, jnp.zeros((C, LANES), F32))
        set_plane(xe, i, C, jnp.zeros((C, LANES), F32))
    coef = level_coef(0)
    for side, (rows, at) in enumerate(((rows_n, C - 1), (rows_p, 0))):
        coarse = hx[side, 0, 0:N, :]
        near_m = k0 * rows[0] + coarse
        near_e = k0 * rows[1] + hx[side, 1, 0:N, :]
        far_m = k0 * rows[2] + coarse
        own = xm[pl.ds(at, N, stride=C), :]
        total = (
            coef[0] * beside_dense(near_m) + coef[1] * (far_m + own) + coef[2] * beside_lanes_main(near_m, near_e)
        )
        hp[side, 0] = near_m
        hp[side, 1] = near_e
        hp[side, 2] = (1.0 - OMEGA) * near_m + k0 * (rows[0] + total)

    rim = rim_lanes(lane_of((C, LANES)), length, n_len)

    def last(i):
        m, e = plane(xm, i, C), plane(xe, i, C)
        wm = plane(xm, i - 1, C) + plane(xm, i + 1, C)
        we = plane(xe, i - 1, C) + plane(xe, i + 1, C)
        lm, le = beside_lanes(m, e)
        at = pl.ds(i, 1)
        cm = beside_rows(m, hp[1, 0, at, :], hp[0, 0, at, :])
        ce = beside_rows(e, hp[1, 1, at, :], hp[0, 1, at, :])
        pm = (1.0 - OMEGA) * m + k0 * (plane(bm, i, C) + coef[0] * wm + coef[1] * cm + coef[2] * lm)
        pe = (1.0 - OMEGA) * e + k0 * (plane(be, i, C) + coef[0] * we + coef[1] * ce + coef[2] * le)
        w = wall * W + i - H
        ok = jnp.logical_and(w >= 0, w < n_wall * W)
        set_plane(tm, i, C, jnp.where(ok, pm, 0.0))
        set_plane(te, i, C, jnp.where(rim, pe, 0.0))

    loop(H - 1, N - H + 1, last, 2)

    row = lax.broadcasted_iota(jnp.int32, (C, LANES), 0)

    def finish0(w):
        i = w + H
        m, e = plane(tm, i, C), plane(te, i, C)
        at = pl.ds(i, 1)
        wm = plane(tm, i - 1, C) + plane(tm, i + 1, C)
        cm = beside_rows(m, hp[1, 2, at, :], hp[0, 2, at, :])
        lm = beside_lanes_main(m, e)
        lam = plane(qm, i, C)
        lam = lam + jnp.where(row == C - 1, rows_n[3, at, :], 0.0) + jnp.where(row == 0, rows_p[3, at, :], 0.0)
        moved = 2.0 * sum(SI) * m - SI[0] * wm - SI[1] * cm - SI[2] * lm
        adj_prev[w] = lam - DT * mask[w].astype(F32) * moved
        potential[w] = m

    loop(0, W, finish0, 2)

    NC, NL = sheet.shape[1:]
    twice_c = jnp.where(
        lax.broadcasted_iota(jnp.int32, (NC, NC1), 0) // 2 == lax.broadcasted_iota(jnp.int32, (NC, NC1), 1), 1.0, 0.0
    ).astype(F32)
    twice_l = jnp.where(
        lax.broadcasted_iota(jnp.int32, (NL1, NL), 1) // 2 == lax.broadcasted_iota(jnp.int32, (NL1, NL), 0), 1.0, 0.0
    ).astype(F32)
    for s, i in enumerate((1, planes)):
        p = jnp.dot(twice_c, b1[i], precision=HIGHEST, preferred_element_type=F32)
        p = jnp.dot(p, twice_l, precision=HIGHEST, preferred_element_type=F32)
        c, l = around(p, 1)
        sheet[s] = (1.0 - OMEGA) * p + k0 * (coef[0] * p + coef[1] * c + coef[2] * l)

    me = (blk * n_len + length) * n_wall + wall
    which = lax.broadcasted_iota(jnp.int32, (1, electrodes), 1).astype(F32)
    mine = owner[...] == me
    patches = (
        jnp.min(jnp.where(mine, which, float(electrodes))),
        jnp.max(jnp.where(mine, which, -1.0)),
    )
    spot = lax.broadcasted_iota(jnp.int32, (8, LANES), 0) * LANES + lane_of((8, LANES))
    spot = spot.astype(F32)
    start = half * C1
    totals = [jnp.zeros((C, LANES), F32) for _ in patches]
    small = [jnp.zeros((8, LANES), F32) for _ in patches]
    for v in range(n_wall):
        wall_s = (wall + v) % n_wall
        for j in range(n_len):
            ref = blocks[v * n_len + j]
            at_l = pl.ds(pl.multiple_of(length_of(j) * L, L), L)

            def add(d, carry):
                big, little = carry
                values = sheet[wall_s, pl.ds(pl.multiple_of(blk_of(d) * C, C), C), at_l]
                ids = ref[d, start : start + C, :]
                parts = ref[d, start + C : start + C + 8, :]
                big = [x + jnp.where(ids == e, values, 0.0) for x, e in zip(big, patches)]
                little = [x + jnp.where(spot == e, parts, 0.0) for x, e in zip(little, patches)]
                return big, little

            totals, small = lax.fori_loop(0, n_blk, add, (totals, small), unroll=min(4, n_blk))
    factor = 1.0 / (2.0 * C * L / 2) ** 0.5
    for r in range(2):
        patch_grad[0, r] = (jnp.sum(totals[r]) + jnp.sum(small[r])) * factor


def ring(x, axis, by):
    count = lax.axis_size(axis)
    return lax.ppermute(x, axis, [(i, (i + by) % count) for i in range(count)])


def call(kernel, outs, scratch, smem=(), **kwargs):
    specs = [pl.BlockSpec(memory_space=pltpu.SMEM if k in smem else pltpu.VMEM) for k in range(len(outs))]
    return pl.pallas_call(
        kernel,
        out_shape=[jax.ShapeDtypeStruct(shape, F32) for shape in outs],
        out_specs=specs,
        scratch_shapes=[pltpu.VMEM(shape, F32) for shape in scratch],
        compiler_params=pltpu.CompilerParams(vmem_limit_bytes=48 * 2**20),
        **kwargs,
    )


def body(adj_next, ion_slope, misfit, tissue_mask, patch_ids, owner_map):
    W, C, L = adj_next.shape
    n_blk, n_len, n_wall = lax.axis_size("blk"), lax.axis_size("len"), lax.axis_size("wall")
    electrodes = owner_map.shape[0]
    assert L == LANES and H * W == LANES and n_wall == 2 and electrodes == 2 * n_blk * n_len * n_wall
    N = W + 2 * H
    n_dir = 1 if n_len == 2 else 2
    raw = (adj_next, ion_slope, tissue_mask, misfit)

    faces = call(
        functools.partial(pack_faces, n_len), [(4, H, C, L)] + [(4, C, L)] * n_dir + [(C, L)] * n_dir, [], name="faces"
    )(*raw)
    wall_in = ring(faces[0], "wall", 1)
    if n_dir == 1:
        strips = [ring(faces[1], "len", 1)]
        corners = [across(faces[2])]
    else:
        strips = [ring(faces[2], "len", -1), ring(faces[1], "len", 1)]
        corners = [ring(ring(faces[4], "wall", 1), "len", -1), ring(ring(faces[3], "wall", 1), "len", 1)]

    field = (N * C, L)
    near = (5 * N + 16, L)
    qm, pm, pe, to_next, to_prev = call(
        functools.partial(sector, n_len), [field] * 3 + [near] * 2, [field] * 9, name="sector"
    )(*raw, wall_in, *strips, *corners)
    from_next = ring(to_prev, "blk", -1)
    from_prev = ring(to_next, "blk", 1)

    rows = (4, N, L)
    wide = LANES * ((electrodes + LANES - 1) // LANES)
    message = (W * C // 8 + C + 8, L)
    bm, be, rows_n, rows_p, mine = call(
        functools.partial(residual, electrodes, n_len, n_wall),
        [field, field, rows, rows, message],
        [(2, C, L), (W // 2 * C, L), (wide, L)],
        name="residual",
    )(pm, pe, patch_ids, to_next, to_prev, from_next, from_prev)

    relative = n_blk <= 4
    if relative:
        sector_blocks = jnp.stack([mine] + [ring(mine, "blk", d) for d in range(1, n_blk)])
    else:
        sector_blocks = lax.all_gather(mine, "blk")
    if n_len == 2:
        here = [sector_blocks, ring(sector_blocks, "len", 1)]
    else:
        gathered = lax.all_gather(sector_blocks, "len")
        here = [gathered[j] for j in range(n_len)]
    blocks = here + [ring(x, "wall", 1) for x in here]

    NC1, NL1 = n_blk * C // 2, n_len * L // 2
    planes = n_wall * W // 2
    grid1 = (planes + 2, NC1, NL1)
    grid2 = (planes // 2 + 2, NC1, NL1)
    grid3 = (planes // 4 + 2, NC1, NL1)
    Q = W // 2 + 2
    padded = 8 * ((Q + 7) // 8)
    scratch = [grid1, grid1, grid2, grid2, grid3, grid3]
    scratch += [(Q * C, L), (Q * C, L), (padded * C // 2, L), (2, 2, 2 * padded + 8, L)]
    scratch += [field, field, (2, 3, N, L), field, field, (2, n_blk * C, n_len * L)]
    adj_prev, potential, patch_grad = call(
        functools.partial(solve, (n_blk, n_len, n_wall), relative, electrodes),
        [(W, C, L), (W, C, L), (1, 2)],
        scratch,
        smem=(2,),
        name="solve",
    )(*blocks, bm, be, rows_n, rows_p, qm, tissue_mask, owner_map.reshape(1, electrodes))
    return adj_prev, potential, patch_grad


def across(x):
    n_wall = lax.axis_size("wall")
    pairs = [(l * n_wall + w, (1 - l) * n_wall + (w + 1) % n_wall) for l in range(2) for w in range(n_wall)]
    return lax.ppermute(x, ("len", "wall"), pairs)


def solution(mesh):
    field = P(("groups", "wall"), "blk", "len")
    return jax.shard_map(
        body,
        mesh=mesh,
        in_specs=(field, field, field, field, field, P("groups")),
        out_specs=(field, field, P(("groups", "blk", "len", "wall"), None)),
        check_vma=False,
    )
```

time: 312 us -> 51.5 us (0.17)
  starting transfers between devices: 113 us -> 11.3 us
  local copies, waits for them, and re-layouts: 78.4 us -> 4.45 us
  blocking collectives: 56.2 us -> 0 us
  other arithmetic: 50.1 us -> 0.02 us
  Pallas kernels: 0 us -> 15.7 us
  waiting for transfers between devices: 11.7 us -> 19.2 us
    ppermute x54 -> x11, starting transfers between devices: 113 us -> 11.3 us  [the longest x10 11.2 us: ring(): return lax.ppermute(x, axis, [(i, (i + by) % count) for i in range(count)])]
    unnamed x1 -> x0, blocking collectives: 33.8 us -> none
    slice x33 -> x0, local copies, waits for them, and re-layouts: 22.6 us -> none  [the longest x26 15.6 us: padded(): head = lax.slice_in_dim(cells, 0, width, axis=dim)]
    all_gather x1 -> x0, blocking collectives: 22.5 us -> none  [coarse_solve(): lax.all_gather(source[None], ('blk', 'len', 'wall'), axis=0, tiled=True)]
    reshape x10 -> x0, local copies, waits for them, and re-layouts: 22.4 us -> none  [the longest x3 21.7 us: restrict(): return field.reshape(a // 2, 2, b // 2, 2, c // 2, 2).mean(axis=(1, 3, 5))]
    ppermute x10 -> x0, local copies, waits for them, and re-layouts: 17.5 us -> none  [the longest x5 9.04 us: padded(): lax.ppermute(head, axis, [((i + 1) % count, i) for i in range(ends)])]
    pallas_call x0 -> x4, Pallas kernels: none -> 15.7 us  [the longest x1 8.66 us: body(): call(functools.partial(solve, (n_blk, n_len, n_wall), relative, electrode...]
    scatter-add x1 -> x0, other arithmetic: 14.8 us -> none  [body(): jax.ops.segment_sum(surface.reshape(-1), patch_ids.reshape(-1), num_segme...]
  transfers between devices with their start and end apart: 54 -> 11, of which waited for: 12 -> 8; matrix products, arithmetic and copies ran while one was open for 22% -> 0% of each run, Pallas kernels for 0% -> 0%
where the time goes in v1:
time: 51.5 us; the launch traced here: 51.3 us
  waiting for transfers between devices  19.2 us (37%)
  Pallas kernels  15.7 us (30%)
  starting transfers between devices  11.3 us (22%)
  local copies, waits for them, and re-layouts  4.45 us (9%)
  between operations  0.67 us (1%)
    ppermute x10, waiting for transfers between devices, ring(): return lax.ppermute(x, axis, [(i, (i + by) % count) for i in range(count)])  16.1 us
    ppermute x10, starting transfers between devices, ring(): return lax.ppermute(x, axis, [(i, (i + by) % count) for i in range(count)])  11.2 us
    pallas_call x1, Pallas kernels, body(): call(functools.partial(solve, (n_blk, n_len, n_wall), relative, electrode...  8.66 us
    unnamed x14, local copies, waits for them, and re-layouts  4.45 us
    pallas_call x1, Pallas kernels, body(): call(functools.partial(sector, n_len), [field] * 3 + [near] * 2, [field]...  3.88 us
    ppermute x1, waiting for transfers between devices, across(): return lax.ppermute(x, ('len', 'wall'), pairs)  3.01 us
    pallas_call x1, Pallas kernels, body(): call(functools.partial(residual, electrodes, n_len, n_wall), [field, fiel...  2.74 us
  transfers between devices with their start and end apart: 11, of which 8 were waited for; matrix products, arithmetic and copies ran while one was open for 0% of the time, Pallas kernels for 0%

profile of v1, /device:TPU:0, one launch (start us, length us, event | category | flops | bytes accessed | tf_op | source)
XLA Modules:
  0.0 51.3 jit_solution(10696470260155190359)
XLA Ops:
  0.6 0.0 copy-start
  0.6 0.9 %copy-done = s32[32,16,128]{2,1,0:T(8,128)S(1)} copy-done((s32[32,16,128]{2,1,0:T(8,128)S(1)}, s32[32,16,128]{2,1,0:T(8,128)}, u32[]{:S(2)}) %copy-start) | copy-done | bytes 262168
  1.6 0.0 copy-start.2
  1.6 0.9 %copy-done.2 = f32[32,16,128]{2,1,0:T(8,128)S(1)} copy-done((f32[32,16,128]{2,1,0:T(8,128)S(1)}, f32[32,16,128]{2,1,0:T(8,128)}, u32[]{:S(2)}) %copy-start.2) | copy-done | bytes 262168
  2.5 0.0 copy-start.3
  2.5 0.9 %copy-done.3 = f32[32,16,128]{2,1,0:T(8,128)S(1)} copy-done((f32[32,16,128]{2,1,0:T(8,128)S(1)}, f32[32,16,128]{2,1,0:T(8,128)}, u32[]{:S(2)}) %copy-start.3) | copy-done | bytes 262168
  3.5 0.0 copy-start.4
  3.5 0.9 %copy-done.4 = f32[32,16,128]{2,1,0:T(8,128)S(1)} copy-done((f32[32,16,128]{2,1,0:T(8,128)S(1)}, f32[32,16,128]{2,1,0:T(8,128)}, u32[]{:S(2)}) %copy-start.4) | copy-done | bytes 262168
  4.4 0.4 faces.1
  4.8 0.5 %collective-permute-start = (f32[4,4,16,128]{3,2,1,0:T(8,128)S(1)}, f32[4,4,16,128]{3,2,1,0:T(8,128)S(1)}, u32[]{:S(2)}, u32[]{:S(2)}) collective-permute-start(f32[4,4,16,128]{3,2,1,0:T(8,128)S(1)} %get-tuple-element.16), channel_id=1, source_target_pairs={{0,1},{1,0},{2,3},{3,2},{4,5},{5,4},{6,7},{7,6},{8,9},{9,8},{10,11... | collective-permute-start | bytes 393224 | tf_op jit(solution)/shard_map/ppermute | solution.py:609
  5.3 2.6 %collective-permute-start.1 = (f32[4,16,128]{2,1,0:T(8,128)S(1)}, f32[4,16,128]{2,1,0:T(8,128)S(1)}, u32[]{:S(2)}, u32[]{:S(2)}) collective-permute-start(f32[4,16,128]{2,1,0:T(8,128)S(1)} %get-tuple-element.17), channel_id=1, source_target_pairs={{0,2},{2,0},{1,3},{3,1},{4,6},{6,4},{5,7},{7,5},{8,10},{10,8},{9,1... | collective-permute-start | bytes 98312 | tf_op jit(solution)/shard_map/ppermute | solution.py:609
  7.9 0.1 collective-permute-start.2
  8.0 3.0 %collective-permute-done.2.rest_1_ = f32[16,128]{1,0:T(8,128)S(1)} collective-permute-done((f32[16,128]{1,0:T(8,128)S(1)}, f32[16,128]{1,0:T(8,128)S(1)}, u32[]{:S(2)}, u32[]{:S(2)}) %collective-permute-start.2) | collective-permute-done | bytes 8224 | tf_op jit(solution)/shard_map/ppermute | solution.py:697
  11.0 0.0 collective-permute-done.1.rest_0_
  11.0 0.0 collective-permute-done.wall_in
  11.0 0.0 copy-start.5
  11.0 3.9 %sector.1 = (f32[640,128]{1,0:T(8,128)S(1)}, f32[640,128]{1,0:T(8,128)S(1)}, f32[640,128]{1,0:T(8,128)S(1)}, f32[216,128]{1,0:T(8,128)S(1)}, f32[216,128]{1,0:T(8,128)S(1)}) custom-call(f32[32,16,128]{2,1,0:T(8,128)S(1)} %copy-done.2, f32[32,16,128]{2,1,0:T(8,128)S(1)} %copy-done.3, s32[32,16,128]{2,1,0:T(8,128)S(1)} %copy-done, ...), custom_call_target="tpu_custom_call" | custom-call | tf_op jit(solution)/shard_map/sector/pallas_call | solution.py:646
  14.9 1.6 %collective-permute-start.4 = (f32[216,128]{1,0:T(8,128)S(1)}, f32[216,128]{1,0:T(8,128)S(1)}, u32[]{:S(2)}, u32[]{:S(2)}) collective-permute-start(f32[216,128]{1,0:T(8,128)S(1)} %get-tuple-element.21.own_next), channel_id=1, source_target_pairs={{0,4},{4,8},{8,12},{12,0},{1,5},{5,9},{9,13},{13,1},{2,6},{6,10},{... | collective-permute-start | bytes 331784 | tf_op jit(solution)/shard_map/ppermute | solution.py:609
  16.5 2.2 %collective-permute-start.3 = (f32[216,128]{1,0:T(8,128)S(1)}, f32[216,128]{1,0:T(8,128)S(1)}, u32[]{:S(2)}, u32[]{:S(2)}) collective-permute-start(f32[216,128]{1,0:T(8,128)S(1)} %get-tuple-element.22.own_prev), channel_id=1, source_target_pairs={{0,12},{4,0},{8,4},{12,8},{1,13},{5,1},{9,5},{13,9},{2,14},{6,2},{... | collective-permute-start | bytes 331784 | tf_op jit(solution)/shard_map/ppermute | solution.py:609
  18.8 3.9 %collective-permute-done.4.from_prev = f32[216,128]{1,0:T(8,128)S(1)} collective-permute-done((f32[216,128]{1,0:T(8,128)S(1)}, f32[216,128]{1,0:T(8,128)S(1)}, u32[]{:S(2)}, u32[]{:S(2)}) %collective-permute-start.4) | collective-permute-done | bytes 110624 | tf_op jit(solution)/shard_map/ppermute | solution.py:609
  22.6 1.1 %collective-permute-done.3.from_next = f32[216,128]{1,0:T(8,128)S(1)} collective-permute-done((f32[216,128]{1,0:T(8,128)S(1)}, f32[216,128]{1,0:T(8,128)S(1)}, u32[]{:S(2)}, u32[]{:S(2)}) %collective-permute-start.3) | collective-permute-done | bytes 110624 | tf_op jit(solution)/shard_map/ppermute | solution.py:609
  23.7 0.0 copy-done.5
  23.7 2.7 %residual.1 = (f32[640,128]{1,0:T(8,128)S(1)}, f32[640,128]{1,0:T(8,128)S(1)}, f32[4,40,128]{2,1,0:T(8,128)S(1)}, f32[4,40,128]{2,1,0:T(8,128)S(1)}, f32[88,128]{1,0:T(8,128)S(1)}) custom-call(f32[640,128]{1,0:T(8,128)S(1)} %get-tuple-element.19.pm, f32[640,128]{1,0:T(8,128)S(1)} %get-tuple-element.20.pe, s32[1,16,128]{2,1,0:T(8,128)S(1)} %copy-done.5, ...), custom_call_target="tpu_custom_call" | custom-call | tf_op jit(solution)/shard_map/residual/pallas_call | solution.py:655
  26.5 0.0 copy-start.1
  26.5 2.4 %collective-permute-start.7 = (f32[88,128]{1,0:T(8,128)S(1)}, f32[88,128]{1,0:T(8,128)S(1)}, u32[]{:S(2)}, u32[]{:S(2)}) collective-permute-start(f32[88,128]{1,0:T(8,128)S(1)} %get-tuple-element.23), channel_id=1, source_target_pairs={{0,12},{4,0},{8,4},{12,8},{1,13},{5,1},{9,5},{13,9},{2,14},{6,2},{... | collective-permute-start | bytes 135176 | tf_op jit(solution)/shard_map/ppermute | solution.py:609
  28.8 0.3 collective-permute-start.6
  29.1 0.7 %collective-permute-start.5 = (f32[88,128]{1,0:T(8,128)S(1)}, f32[88,128]{1,0:T(8,128)S(1)}, u32[]{:S(2)}, u32[]{:S(2)}) collective-permute-start(f32[88,128]{1,0:T(8,128)S(1)} %get-tuple-element.23), channel_id=1, source_target_pairs={{0,4},{4,8},{8,12},{12,0},{1,5},{5,9},{9,13},{13,1},{2,6},{6,10},{... | collective-permute-start | bytes 135176 | tf_op jit(solution)/shard_map/ppermute | solution.py:609
  29.8 0.7 %collective-permute-done.7 = f32[88,128]{1,0:T(8,128)S(1)} collective-permute-done((f32[88,128]{1,0:T(8,128)S(1)}, f32[88,128]{1,0:T(8,128)S(1)}, u32[]{:S(2)}, u32[]{:S(2)}) %collective-permute-start.7) | collective-permute-done | bytes 45088 | tf_op jit(solution)/shard_map/ppermute | solution.py:609
  30.6 3.4 %collective-permute-done.6 = f32[88,128]{1,0:T(8,128)S(1)} collective-permute-done((f32[88,128]{1,0:T(8,128)S(1)}, f32[88,128]{1,0:T(8,128)S(1)}, u32[]{:S(2)}, u32[]{:S(2)}) %collective-permute-start.6) | collective-permute-done | bytes 45088 | tf_op jit(solution)/shard_map/ppermute | solution.py:609
  33.9 1.0 %collective-permute-done.5 = f32[88,128]{1,0:T(8,128)S(1)} collective-permute-done((f32[88,128]{1,0:T(8,128)S(1)}, f32[88,128]{1,0:T(8,128)S(1)}, u32[]{:S(2)}, u32[]{:S(2)}) %collective-permute-start.5) | collective-permute-done | bytes 45088 | tf_op jit(solution)/shard_map/ppermute | solution.py:609
  35.0 0.9 %collective-permute-start.8 = (f32[4,88,128]{2,1,0:T(8,128)S(1)}, f32[4,88,128]{2,1,0:T(8,128)S(1)}, u32[]{:S(2)}, u32[]{:S(2)}) collective-permute-start(f32[4,88,128]{2,1,0:T(8,128)S(1)} %pad_maximum_fusion.refs_0_), channel_id=1, source_target_pairs={{0,2},{2,0},{1,3},{3,1},{4,6},{6,4},{5,7},{7,5},{8,10},{10,8},{9,1... | collective-permute-start | bytes 540680 | tf_op jit(solution)/shard_map/ppermute | solution.py:609
  35.9 0.0 collective-permute-start.9
  35.9 4.7 %collective-permute-done.8.refs_1_ = f32[4,88,128]{2,1,0:T(8,128)S(1)} collective-permute-done((f32[4,88,128]{2,1,0:T(8,128)S(1)}, f32[4,88,128]{2,1,0:T(8,128)S(1)}, u32[]{:S(2)}, u32[]{:S(2)}) %collective-permute-start.8) | collective-permute-done | bytes 180256 | tf_op jit(solution)/shard_map/ppermute | solution.py:609
  40.5 0.0 collective-permute-start.10
  40.5 0.0 collective-permute-done.9.refs_2_
  40.5 1.4 %collective-permute-done.10.refs_3_ = f32[4,88,128]{2,1,0:T(8,128)S(1)} collective-permute-done((f32[4,88,128]{2,1,0:T(8,128)S(1)}, f32[4,88,128]{2,1,0:T(8,128)S(1)}, u32[]{:S(2)}, u32[]{:S(2)}) %collective-permute-start.10) | collective-permute-done | bytes 180256 | tf_op jit(solution)/shard_map/ppermute | solution.py:609
  41.9 0.0 copy-start.6
  41.9 0.0 copy-done.1
  41.9 0.7 %copy-done.6 = s32[32]{0:T(128)S(1)} copy-done((s32[32]{0:T(128)S(1)}, s32[32]{0:T(128)}, u32[]{:S(2)}) %copy-start.6) | copy-done | bytes 152
  42.6 8.7 %solve.1 = (f32[32,16,128]{2,1,0:T(8,128)}, f32[32,16,128]{2,1,0:T(8,128)}, f32[1,2]{1,0:T(1,128)}) custom-call(f32[4,88,128]{2,1,0:T(8,128)S(1)} %pad_maximum_fusion.refs_0_, f32[4,88,128]{2,1,0:T(8,128)S(1)} %collective-permute-done.8.refs_1_, f32[4,88,128]{2,1,0:T(8,128)S(1)} %collective-permute-done.9.refs_2_, ...), custom_call_target="tpu_custom_call" | custom-call | tf_op jit(solution)/shard_map/solve/pallas_call | solution.py:684
  (1 shorter events, 0.0 us)
Async XLA Ops:
  0.6 1.0 %copy-start = (s32[32,16,128]{2,1,0:T(8,128)S(1)}, s32[32,16,128]{2,1,0:T(8,128)}, u32[]{:S(2)}) copy-start(s32[32,16,128]{2,1,0:T(8,128)} %refs_9_.1) | copy-start | bytes 786436
  1.6 0.9 %copy-start.2 = (f32[32,16,128]{2,1,0:T(8,128)S(1)}, f32[32,16,128]{2,1,0:T(8,128)}, u32[]{:S(2)}) copy-start(f32[32,16,128]{2,1,0:T(8,128)} %adj.3) | copy-start | bytes 786436
  2.5 0.9 %copy-start.3 = (f32[32,16,128]{2,1,0:T(8,128)S(1)}, f32[32,16,128]{2,1,0:T(8,128)}, u32[]{:S(2)}) copy-start(f32[32,16,128]{2,1,0:T(8,128)} %ion.3) | copy-start | bytes 786436
  3.5 0.9 %copy-start.4 = (f32[32,16,128]{2,1,0:T(8,128)S(1)}, f32[32,16,128]{2,1,0:T(8,128)}, u32[]{:S(2)}) copy-start(f32[32,16,128]{2,1,0:T(8,128)} %mis.3) | copy-start | bytes 786436
  4.8 6.2 %collective-permute-start = (f32[4,4,16,128]{3,2,1,0:T(8,128)S(1)}, f32[4,4,16,128]{3,2,1,0:T(8,128)S(1)}, u32[]{:S(2)}, u32[]{:S(2)}) collective-permute-start(f32[4,4,16,128]{3,2,1,0:T(8,128)S(1)} %get-tuple-element.16), channel_id=1, source_target_pairs={{0,1},{1,0},{2,3},{3,2},{4,5},{5,4},{6,7},{7,6},{8,9},{9,8},{10,11... | collective-permute-start | bytes 393224 | tf_op jit(solution)/shard_map/ppermute | solution.py:609
  5.3 5.6 %collective-permute-start.1 = (f32[4,16,128]{2,1,0:T(8,128)S(1)}, f32[4,16,128]{2,1,0:T(8,128)S(1)}, u32[]{:S(2)}, u32[]{:S(2)}) collective-permute-start(f32[4,16,128]{2,1,0:T(8,128)S(1)} %get-tuple-element.17), channel_id=1, source_target_pairs={{0,2},{2,0},{1,3},{3,1},{4,6},{6,4},{5,7},{7,5},{8,10},{10,8},{9,1... | collective-permute-start | bytes 98312 | tf_op jit(solution)/shard_map/ppermute | solution.py:609
  7.9 3.1 %collective-permute-start.2 = (f32[16,128]{1,0:T(8,128)S(1)}, f32[16,128]{1,0:T(8,128)S(1)}, u32[]{:S(2)}, u32[]{:S(2)}) collective-permute-start(f32[16,128]{1,0:T(8,128)S(1)} %get-tuple-element.18), channel_id=1, source_target_pairs={{0,3},{1,2},{2,1},{3,0},{4,7},{5,6},{6,5},{7,4},{8,11},{9,10},{10,... | collective-permute-start | bytes 24584 | tf_op jit(solution)/shard_map/ppermute | solution.py:697
  11.0 12.7 %copy-start.5 = (s32[1,16,128]{2,1,0:T(8,128)S(1)}, s32[1,16,128]{2,1,0:T(8,128)}, u32[]{:S(2)}) copy-start(s32[1,16,128]{2,1,0:T(8,128)} %ids.1) | copy-start | bytes 24580
  14.9 7.7 %collective-permute-start.4 = (f32[216,128]{1,0:T(8,128)S(1)}, f32[216,128]{1,0:T(8,128)S(1)}, u32[]{:S(2)}, u32[]{:S(2)}) collective-permute-start(f32[216,128]{1,0:T(8,128)S(1)} %get-tuple-element.21.own_next), channel_id=1, source_target_pairs={{0,4},{4,8},{8,12},{12,0},{1,5},{5,9},{9,13},{13,1},{2,6},{6,10},{... | collective-permute-start | bytes 331784 | tf_op jit(solution)/shard_map/ppermute | solution.py:609
  16.5 7.2 %collective-permute-start.3 = (f32[216,128]{1,0:T(8,128)S(1)}, f32[216,128]{1,0:T(8,128)S(1)}, u32[]{:S(2)}, u32[]{:S(2)}) collective-permute-start(f32[216,128]{1,0:T(8,128)S(1)} %get-tuple-element.22.own_prev), channel_id=1, source_target_pairs={{0,12},{4,0},{8,4},{12,8},{1,13},{5,1},{9,5},{13,9},{2,14},{6,2},{... | collective-permute-start | bytes 331784 | tf_op jit(solution)/shard_map/ppermute | solution.py:609
  26.5 15.5 %copy-start.1 = (s32[32,16,128]{2,1,0:T(8,128)S(1)}, s32[32,16,128]{2,1,0:T(8,128)}, u32[]{:S(2)}) copy-start(s32[32,16,128]{2,1,0:T(8,128)} %refs_9_.1) | copy-start | bytes 786436
  26.5 4.1 %collective-permute-start.7 = (f32[88,128]{1,0:T(8,128)S(1)}, f32[88,128]{1,0:T(8,128)S(1)}, u32[]{:S(2)}, u32[]{:S(2)}) collective-permute-start(f32[88,128]{1,0:T(8,128)S(1)} %get-tuple-element.23), channel_id=1, source_target_pairs={{0,12},{4,0},{8,4},{12,8},{1,13},{5,1},{9,5},{13,9},{2,14},{6,2},{... | collective-permute-start | bytes 135176 | tf_op jit(solution)/shard_map/ppermute | solution.py:609
  28.8 5.1 %collective-permute-start.6 = (f32[88,128]{1,0:T(8,128)S(1)}, f32[88,128]{1,0:T(8,128)S(1)}, u32[]{:S(2)}, u32[]{:S(2)}) collective-permute-start(f32[88,128]{1,0:T(8,128)S(1)} %get-tuple-element.23), channel_id=1, source_target_pairs={{0,8},{4,12},{8,0},{12,4},{1,9},{5,13},{9,1},{13,5},{2,10},{6,14},... | collective-permute-start | bytes 135176 | tf_op jit(solution)/shard_map/ppermute | solution.py:609
  29.1 5.8 %collective-permute-start.5 = (f32[88,128]{1,0:T(8,128)S(1)}, f32[88,128]{1,0:T(8,128)S(1)}, u32[]{:S(2)}, u32[]{:S(2)}) collective-permute-start(f32[88,128]{1,0:T(8,128)S(1)} %get-tuple-element.23), channel_id=1, source_target_pairs={{0,4},{4,8},{8,12},{12,0},{1,5},{5,9},{9,13},{13,1},{2,6},{6,10},{... | collective-permute-start | bytes 135176 | tf_op jit(solution)/shard_map/ppermute | solution.py:609
  35.0 5.6 %collective-permute-start.8 = (f32[4,88,128]{2,1,0:T(8,128)S(1)}, f32[4,88,128]{2,1,0:T(8,128)S(1)}, u32[]{:S(2)}, u32[]{:S(2)}) collective-permute-start(f32[4,88,128]{2,1,0:T(8,128)S(1)} %pad_maximum_fusion.refs_0_), channel_id=1, source_target_pairs={{0,2},{2,0},{1,3},{3,1},{4,6},{6,4},{5,7},{7,5},{8,10},{10,8},{9,1... | collective-permute-start | bytes 540680 | tf_op jit(solution)/shard_map/ppermute | solution.py:609
  35.9 4.7 %collective-permute-start.9 = (f32[4,88,128]{2,1,0:T(8,128)S(1)}, f32[4,88,128]{2,1,0:T(8,128)S(1)}, u32[]{:S(2)}, u32[]{:S(2)}) collective-permute-start(f32[4,88,128]{2,1,0:T(8,128)S(1)} %pad_maximum_fusion.refs_0_), channel_id=1, source_target_pairs={{0,1},{1,0},{2,3},{3,2},{4,5},{5,4},{6,7},{7,6},{8,9},{9,8},{10,11... | collective-permute-start | bytes 540680 | tf_op jit(solution)/shard_map/ppermute | solution.py:609
  40.5 1.4 %collective-permute-start.10 = (f32[4,88,128]{2,1,0:T(8,128)S(1)}, f32[4,88,128]{2,1,0:T(8,128)S(1)}, u32[]{:S(2)}, u32[]{:S(2)}) collective-permute-start(f32[4,88,128]{2,1,0:T(8,128)S(1)} %collective-permute-done.8.refs_1_), channel_id=1, source_target_pairs={{0,1},{1,0},{2,3},{3,2},{4,5},{5,4},{6,7},{7,6},{8,9},{9,8},{10,11... | collective-permute-start | bytes 540680 | tf_op jit(solution)/shard_map/ppermute | solution.py:609
  41.9 0.7 %copy-start.6 = (s32[32]{0:T(128)S(1)}, s32[32]{0:T(128)}, u32[]{:S(2)}) copy-start(s32[32]{0:T(128)} %param.11) | copy-start | bytes 388

commit v2 on v1

v2 whole, which is shorter than its diff:
```python
import functools

import jax
import jax.numpy as jnp
from jax import lax
from jax.experimental import pallas as pl
from jax.experimental.pallas import tpu as pltpu
from jax.sharding import PartitionSpec as P

SWEEPS = 2
SI = (0.6, 1.0, 3.0)
SE = (0.8, 1.2, 2.0)
SHIFT = 0.002
OMEGA = 0.8
DT = 0.1
H = 4
LANES = 128
HIGHEST = lax.Precision.HIGHEST
F32 = jnp.float32


def level_coef(level):
    return tuple((SI[i] + SE[i]) / 4.0**level for i in range(3))


def level_diag(level):
    return SHIFT + 2.0 * sum(level_coef(level))


def level_step(level):
    return OMEGA / level_diag(level)


def lane_of(shape):
    return lax.broadcasted_iota(jnp.int32, shape, len(shape) - 1)


def before(m, e):
    first = lane_of(m.shape) == 0
    rm, re = pltpu.roll(m, 1, 1), pltpu.roll(e, 1, 1)
    return jnp.where(first, re, rm), jnp.where(first, rm, re)


def after(m, e):
    last = lane_of(m.shape) == LANES - 1
    rm, re = pltpu.roll(m, LANES - 1, 1), pltpu.roll(e, LANES - 1, 1)
    return jnp.where(last, re, rm), jnp.where(last, rm, re)


def beside_lanes(m, e):
    bm, be = before(m, e)
    am, ae = after(m, e)
    return bm + am, be + ae


def beside_lanes_main(m, e):
    lane = lane_of(m.shape)
    left = jnp.where(lane == 0, pltpu.roll(e, 1, 1), pltpu.roll(m, 1, 1))
    right = jnp.where(lane == LANES - 1, pltpu.roll(e, LANES - 1, 1), pltpu.roll(m, LANES - 1, 1))
    return left + right


def beside_rows(x, row_before, row_after):
    rows = x.shape[0]
    row = lax.broadcasted_iota(jnp.int32, x.shape, 0)
    low = jnp.where(row == 0, row_before, pltpu.roll(x, 1, 0))
    high = jnp.where(row == rows - 1, row_after, pltpu.roll(x, rows - 1, 0))
    return low + high


def beside_dense(x):
    return pltpu.roll(x, 1, 0) + pltpu.roll(x, x.shape[0] - 1, 0)


def plane(ref, i, rows):
    return ref[pl.ds(pl.multiple_of(i * rows, rows), rows), :]


def set_plane(ref, i, rows, value):
    ref[pl.ds(pl.multiple_of(i * rows, rows), rows), :] = value


def loop(low, high, step, unroll):
    def wrapped(i, carry):
        step(i)
        return carry

    lax.fori_loop(low, high, wrapped, 0, unroll=min(unroll, high - low))


FACES = (H, H - 1, H - 1, H - 2)


def face_planes(array):
    return FACES[array], sum(FACES[:array])


def pack_faces(n_len, adj, ion, mask, mis, *rest):
    n_dir = 1 if n_len == 2 else 2
    fields, wall_out, rest = rest[:4], rest[4], rest[5:]
    strips, corners = rest[:n_dir], rest[n_dir : 2 * n_dir]
    whole_mask, sems = rest[2 * n_dir :]
    cells = adj.shape[0]
    C = wall_out.shape[1]
    W = cells // C
    wall, length = lax.axis_index("wall"), lax.axis_index("len")
    targets = (fields[0], fields[1], whole_mask, fields[3])
    copies = []
    for a, (src, dst) in enumerate(zip((adj, ion, mask, mis), targets)):
        part = cells // 2
        for k in range(2):
            spot = pl.ds(k * part, part)
            copies.append(pltpu.make_async_copy(src.at[spot], dst.at[spot], sems.at[a, k]))
            copies[-1].start()

    base = jnp.where(wall == 0, W - H, 0)
    group = lane_of((C, LANES)) // H
    turns = [jnp.where(length == 0, H, 0)] if n_dir == 1 else [H, 0]
    corner = [jnp.zeros((C, LANES), F32) for _ in range(n_dir)]
    for a in (0, 1, 3, 2):
        copies[2 * a].wait()
        copies[2 * a + 1].wait()
        if a == 2:
            fields[2][...] = whole_mask[...].astype(F32)
        ref = fields[a]
        strip = [jnp.zeros((C, LANES), F32) for _ in range(n_dir)]
        for w in range(W):
            value = ref[w * C : (w + 1) * C, :]
            for d in range(n_dir):
                turned = pltpu.roll(value, lax.rem(H * w + turns[d], LANES), 1)
                strip[d] = jnp.where(group == w, turned, strip[d])
        for d in range(n_dir):
            strips[d][a] = strip[d]
        count, first = face_planes(a)
        for p in range(count):
            face = plane(ref, base + jnp.where(wall == 0, H - count, 0) + p, C)
            wall_out[first + p] = face
            slot = first + p
            for d in range(n_dir):
                turned = pltpu.roll(face, lax.rem(H * slot + turns[d], LANES), 1)
                corner[d] = jnp.where(group == slot, turned, corner[d])
    for d in range(n_dir):
        corners[d][...] = corner[d]


def dense(ref, row, N, C):
    return ref[pl.ds(row, N, stride=C), :]


def dense_pair(m, e, row, N, C):
    return dense(m, row, N, C), dense(e, row, N, C)


def dense_apply(pair, inner, outer, coef):
    m, e = pair
    lm, le = beside_lanes(m, e)
    double = 2.0 * sum(coef)
    out = [double * m - coef[0] * beside_dense(m) - coef[2] * lm, double * e - coef[0] * beside_dense(e) - coef[2] * le]
    for row in (inner, outer):
        if row is not None:
            out = [out[k] - coef[1] * row[k] for k in range(2)]
    return out


def boundary(n_len, C, xm0, xm1, xm2, xm3, wall_in, *rest):
    n_dir = 1 if n_len == 2 else 2
    strips, corners, rest = rest[:n_dir], rest[n_dir : 2 * n_dir], rest[2 * n_dir :]
    xm, xe, to_next, to_prev, own_rows = rest[:4], rest[4:8], rest[8], rest[9], rest[10]
    N = xm[0].shape[0] // C
    W = N - 2 * H
    wall, length = lax.axis_index("wall"), lax.axis_index("len")
    lane = lane_of((C, LANES))
    if n_dir == 1:
        offs, valid = [jnp.where(length == 0, 0, LANES - H)], [True]
    else:
        offs, valid = [0, LANES - H], [length < n_len - 1, length > 0]
    seen = [jnp.logical_and(lax.rem(lane - off + LANES, LANES) < H, ok) for off, ok in zip(offs, valid)]

    def rim(packed, base):
        out = jnp.zeros((C, LANES), F32)
        for d in range(n_dir):
            out = jnp.where(seen[d], pltpu.roll(packed[d], lax.rem(offs[d] - base + LANES, LANES), 1), out)
        return out

    zero = jnp.zeros((C, LANES), F32)
    last = N - H
    for a, own in enumerate((xm0, xm1, xm2, xm3)):
        packed = [strip[a] for strip in strips]
        for w in range(W):
            set_plane(xm[a], w + H, C, plane(own, w, C))
            set_plane(xe[a], w + H, C, rim(packed, H * w))
        packed = [corner[...] for corner in corners]
        for i in range(H):
            set_plane(xm[a], i, C, zero)
            set_plane(xe[a], i, C, zero)
            set_plane(xm[a], last + i, C, zero)
            set_plane(xe[a], last + i, C, zero)
        count, first = face_planes(a)
        here = jnp.where(wall == 0, last, H - count)
        for p in range(count):
            set_plane(xm[a], here + p, C, wall_in[first + p])
            set_plane(xe[a], here + p, C, rim(packed, H * (first + p)))

    pos_of = lane_of((8, LANES)) // 8
    tiles = N // 8
    for side, (out, order) in enumerate(((to_next, (C - 1, C - 2, C - 3, C - 4)), (to_prev, (0, 1, 2, 3)))):
        adj = [dense_pair(xm[0], xe[0], r, N, C) for r in order]
        mask = [dense_pair(xm[2], xe[2], r, N, C) for r in order[:3]]
        q = []
        for k in range(3):
            ion = dense_pair(xm[1], xe[1], order[k], N, C)
            moved = dense_apply(adj[k], adj[k + 1], adj[k - 1] if k else None, SI)
            q.append([adj[k][j] - DT * mask[k][j] * (moved[j] + ion[j] * adj[k][j]) for j in range(2)])
        near = dense_apply(q[0], q[1], None, SI)
        mis = dense_pair(xm[3], xe[3], order[0], N, C)
        near = [near[j] + mis[j] for j in range(2)]
        second = dense_apply(q[1], q[2], q[0], SI)[0] + dense(xm[3], order[1], N, C)
        mains = (adj[0][0], mask[0][0], q[0][0], near[0], second)
        for k, value in enumerate(mains):
            out[k * N : (k + 1) * N, :] = value
        packs = [jnp.zeros((8, LANES), F32), jnp.zeros((8, LANES), F32)]
        for k, value in enumerate((adj[0][1], mask[0][1], q[0][1], near[1])):
            for s in range(tiles):
                t = k * tiles + s
                turned = pltpu.roll(value[8 * s : 8 * s + 8], (H + 8 * (t % 16)) % LANES, 1)
                packs[t // 16] = jnp.where(pos_of == t % 16, turned, packs[t // 16])
        out[5 * N : 5 * N + 8, :] = packs[0]
        out[5 * N + 8 : 5 * N + 16, :] = packs[1]
        for k, pair in enumerate((adj[0], mask[0], q[0])):
            own_rows[side, 2 * k] = pair[0]
            own_rows[side, 2 * k + 1] = pair[1]


def spots(m_ref, e_ref, i, rows, coef):
    m, e = plane(m_ref, i, rows), plane(e_ref, i, rows)
    wm = plane(m_ref, i - 1, rows) + plane(m_ref, i + 1, rows)
    we = plane(e_ref, i - 1, rows) + plane(e_ref, i + 1, rows)
    lm, le = beside_lanes(m, e)
    cm, ce = beside_rows(m, 0.0, 0.0), beside_rows(e, 0.0, 0.0)
    double = 2.0 * sum(coef)
    dm = double * m - coef[0] * wm - coef[1] * cm - coef[2] * lm
    de = double * e - coef[0] * we - coef[1] * ce - coef[2] * le
    return m, e, dm, de


def rim_lanes(lane, length, n_len):
    return jnp.logical_or(
        jnp.logical_and(lane < H, length < n_len - 1),
        jnp.logical_and(lane >= LANES - H, length > 0),
    )


def inside(i, wall, W, n_wall):
    w = wall * W + i - H
    return jnp.logical_and(w >= 0, w < n_wall * W)


def halving():
    src = lax.broadcasted_iota(jnp.int32, (LANES, LANES), 0) // 2
    dst = lax.broadcasted_iota(jnp.int32, (LANES, LANES), 1)
    low = jnp.where(src == dst, 0.125, 0.0).astype(F32)
    high = jnp.where(src == dst - LANES // 2, 0.125, 0.0).astype(F32)
    return low, high


def precise(a, b):
    return jnp.dot(a, b, precision=HIGHEST, preferred_element_type=F32)


def sector(n_len, n_wall, C, xm0, xm1, xm2, xm3, xe0, xe1, xe2, xe3, qm, bm, be, coarse, surface, qe, pairs):
    xm, xe = (xm0, xm1, xm2, xm3), (xe0, xe1, xe2, xe3)
    N = qm.shape[0] // C
    W = N - 2 * H
    wall, length = lax.axis_index("wall"), lax.axis_index("len")
    rim = rim_lanes(lane_of((C, LANES)), length, n_len)
    zero = jnp.zeros((C, LANES), F32)
    for i in (0, N - 1):
        set_plane(qm, i, C, zero)
        set_plane(qe, i, C, zero)
    for i in (0, 1, N - 2, N - 1):
        set_plane(bm, i, C, zero)
        set_plane(be, i, C, zero)

    def parabolic(i):
        m, e, dm, de = spots(xm[0], xe[0], i, C, SI)
        set_plane(qm, i, C, m - DT * plane(xm[2], i, C) * (dm + plane(xm[1], i, C) * m))
        set_plane(qe, i, C, e - DT * plane(xe[2], i, C) * (de + plane(xe[1], i, C) * e))

    loop(1, N - 1, parabolic, 2)

    def elliptic_source(i):
        m, e, dm, de = spots(qm, qe, i, C, SI)
        ok = inside(i, wall, W, n_wall)
        set_plane(bm, i, C, jnp.where(ok, plane(xm[3], i, C) + dm, 0.0))
        set_plane(be, i, C, jnp.where(jnp.logical_and(rim, ok), plane(xe[3], i, C) + de, 0.0))

    loop(2, N - 2, elliptic_source, 2)

    coef, k0 = level_coef(0), level_step(0)

    def left(i):
        m, e = plane(bm, i, C), plane(be, i, C)
        wm = plane(bm, i - 1, C) + plane(bm, i + 1, C)
        cm = beside_rows(m, 0.0, 0.0)
        lm = beside_lanes_main(m, e)
        return m, (1.0 - OMEGA) * m + k0 * (coef[0] * wm + coef[1] * cm + coef[2] * lm)

    def pair(q):
        i = 2 * q + H
        m, first = left(i)
        n, second = left(i + 1)
        set_plane(pairs, q, C, first + second)

        @pl.when(jnp.logical_and(q == 0, wall == 0))
        def _():
            surface[...] = k0 * (m + first)

        @pl.when(jnp.logical_and(q == W // 2 - 1, wall == n_wall - 1))
        def _():
            surface[...] = k0 * (n + second)

    loop(0, W // 2, pair, 2)

    half = W * C // 8
    z = pairs[pl.ds(0, 2 * half, stride=2), :] + pairs[pl.ds(1, 2 * half, stride=2), :]
    low, high = halving()
    coarse[...] = precise(z[:half], low) + precise(z[half:], high)


def unpacked(ref, N):
    lane = lane_of((8, LANES))
    rim = jnp.logical_or(lane < H, lane >= LANES - H)
    tiles = N // 8
    mains = [ref[q * N : (q + 1) * N, :] for q in range(5)]
    packs = [ref[5 * N : 5 * N + 8, :], ref[5 * N + 8 : 5 * N + 16, :]]
    rims = []
    for q in range(4):
        parts = []
        for s in range(tiles):
            t = q * tiles + s
            turned = pltpu.roll(packs[t // 16], (2 * LANES - H - 8 * (t % 16)) % LANES, 1)
            parts.append(jnp.where(rim, turned, 0.0))
        rims.append(jnp.concatenate(parts, 0))
    return [(mains[q], rims[q]) for q in range(4)] + [mains[4]]


def lateral(pair):
    return dense_apply(pair, None, None, SI)


def source_rows(own, other):
    adj_o, mask_o, q_o = own
    adj_n, mask_n, q_n, p_n, second_n = other
    step = DT * SI[1]
    delta_o = [step * mask_o[k] * adj_n[k] for k in range(2)]
    delta_n = [step * mask_n[k] * adj_o[k] for k in range(2)]
    lat_o, lat_n = lateral(delta_o), lateral(delta_n)
    near = [lat_o[k] - SI[1] * (q_n[k] + delta_n[k]) for k in range(2)]
    second = [-SI[1] * delta_o[k] for k in range(2)]
    halo = [p_n[k] + lat_n[k] - SI[1] * (q_o[k] + delta_o[k]) for k in range(2)]
    halo_second = second_n - SI[1] * delta_n[0]
    return near, second, halo, halo_second, delta_o[0]


def correct(electrodes, n_len, n_wall, own_rows, from_next, from_prev, coarse, surface, ids, *rest):
    rows_n, rows_p, message = rest[:3]
    lines, sums = rest[3:]
    _, C, L = ids.shape
    N = own_rows.shape[2]
    W = N - 2 * H
    wall, length = lax.axis_index("wall"), lax.axis_index("len")
    ok_m = inside(lax.broadcasted_iota(jnp.int32, (N, LANES), 0), wall, W, n_wall)
    ok_e = jnp.logical_and(ok_m, rim_lanes(lane_of((N, LANES)), length, n_len))
    coef, k0 = level_coef(0), level_step(0)
    y = surface[...]
    row = lax.broadcasted_iota(jnp.int32, (C, LANES), 0)
    at = pl.ds(jnp.where(wall == 0, H, W + H - 1), 1)
    lows, highs = [], []
    W1, C1 = W // 2, C // 2
    for side, (other, out, order) in enumerate(
        ((from_next, rows_n, (C - 1, C - 2, C - 3)), (from_prev, rows_p, (0, 1, 2)))
    ):
        own = [(own_rows[side, 2 * k], own_rows[side, 2 * k + 1]) for k in range(3)]
        near, second, halo, halo_second, delta = source_rows(own, unpacked(other, N))
        near = [jnp.where(ok_m, near[0], 0.0), jnp.where(ok_e, near[1], 0.0)]
        second = [jnp.where(ok_m, second[0], 0.0), jnp.where(ok_e, second[1], 0.0)]
        out[0] = halo_m = jnp.where(ok_m, halo[0], 0.0)
        out[1] = jnp.where(ok_e, halo[1], 0.0)
        out[2] = jnp.where(ok_m, halo_second, 0.0)
        out[3] = delta
        out[4], out[5] = near
        out[6], out[7] = second

        def turned(pair, beside):
            m, e = pair
            return (1.0 - OMEGA) * m + k0 * (
                coef[0] * beside_dense(m) + coef[2] * beside_lanes_main(m, e) + coef[1] * beside
            )

        first = turned(near, second[0] + halo_m)
        next_one = turned(second, near[0])
        third = k0 * coef[1] * second[0]
        for k, change in enumerate((near[0] + first, second[0] + next_one, third)):
            lines[0] = change
            y = y + jnp.where(row == order[k], k0 * lines[0, at, :], 0.0)
        for change in (first + next_one, third):
            lines[0] = change
            both = lines[0, pl.ds(H, W1, stride=2), :] + lines[0, pl.ds(H + 1, W1, stride=2), :]
            lows.append(both[: W1 // 2])
            highs.append(both[W1 // 2 :])
    low, high = halving()
    add = precise(jnp.concatenate(lows, 0), low) + precise(jnp.concatenate(highs, 0), high)
    half = W * C // 8
    message[0:half, :] = coarse[...]
    for k, c1 in enumerate((C1 - 1, C1 - 2, 0, 1)):
        spot = pl.ds(c1, W1 // 2, stride=C1)
        message[spot, :] = message[spot, :] + add[k * (W1 // 2) : (k + 1) * (W1 // 2)]
    patch = ids[0]
    message[half : half + C, :] = patch.astype(F32)
    wide = sums.shape[0]
    if wide > electrodes:
        sums[...] = jnp.zeros(sums.shape, F32)

    def one(e):
        sums[pl.ds(e, 1), :] = jnp.sum(jnp.where(patch == e, y, 0.0), axis=0, keepdims=True)

    loop(0, electrodes, one, 8)
    totals = lax.dot_general(
        jnp.ones((8, LANES), F32), sums[...], (((1,), (1,)), ((), ())), precision=HIGHEST, preferred_element_type=F32
    )
    message[half + C : half + C + 8, :] = jnp.zeros((8, LANES), F32)
    for t in range(wide // LANES):
        message[half + C + t : half + C + t + 1, :] = totals[0:1, t * LANES : (t + 1) * LANES]


def source_part(n_blk, n_len, n_wall, C, electrodes, bm, be, rows_n, rows_p, qm, mask, owner, base_adj, base_pot, *rest):
    patches, fm, fe, tm, te, hp = rest
    N = bm.shape[0] // C
    W = N - 2 * H
    blk, length, wall = lax.axis_index("blk"), lax.axis_index("len"), lax.axis_index("wall")
    fm[...] = bm[...]
    fe[...] = be[...]
    for rows, near, second in ((rows_n, C - 1, C - 2), (rows_p, 0, 1)):
        for k, at in ((4, near), (6, second)):
            spot = pl.ds(at, N, stride=C)
            fm[spot, :] = fm[spot, :] + rows[k]
            fe[spot, :] = fe[spot, :] + rows[k + 1]
    coef, k0 = level_coef(0), level_step(0)
    rim = rim_lanes(lane_of((C, LANES)), length, n_len)

    def part(i):
        m, e = plane(fm, i, C), plane(fe, i, C)
        wm = plane(fm, i - 1, C) + plane(fm, i + 1, C)
        we = plane(fe, i - 1, C) + plane(fe, i + 1, C)
        lm, le = beside_lanes(m, e)
        at = pl.ds(i, 1)
        cm = beside_rows(m, rows_p[0, at, :], rows_n[0, at, :])
        ce = beside_rows(e, rows_p[1, at, :], rows_n[1, at, :])
        pm = k0 * ((2.0 - OMEGA) * m + k0 * (coef[0] * wm + coef[1] * cm + coef[2] * lm))
        pe = k0 * ((2.0 - OMEGA) * e + k0 * (coef[0] * we + coef[1] * ce + coef[2] * le))
        set_plane(tm, i, C, jnp.where(inside(i, wall, W, n_wall), pm, 0.0))
        set_plane(te, i, C, jnp.where(rim, pe, 0.0))

    loop(H - 1, N - H + 1, part, 2)
    for side, (rows, at) in enumerate(((rows_n, C - 1), (rows_p, 0))):
        m = rows[0]
        total = (
            coef[0] * beside_dense(m)
            + coef[1] * (rows[2] + dense(fm, at, N, C))
            + coef[2] * beside_lanes_main(m, rows[1])
        )
        hp[side] = k0 * ((2.0 - OMEGA) * m + k0 * total)
    row = lax.broadcasted_iota(jnp.int32, (C, LANES), 0)

    def finish(w):
        i = w + H
        m, e = plane(tm, i, C), plane(te, i, C)
        at = pl.ds(i, 1)
        wm = plane(tm, i - 1, C) + plane(tm, i + 1, C)
        cm = beside_rows(m, hp[1, at, :], hp[0, at, :])
        lm = beside_lanes_main(m, e)
        lam = plane(qm, i, C)
        lam = lam + jnp.where(row == C - 1, rows_n[3, at, :], 0.0) + jnp.where(row == 0, rows_p[3, at, :], 0.0)
        moved = 2.0 * sum(SI) * m - SI[0] * wm - SI[1] * cm - SI[2] * lm
        set_plane(base_adj, w, C, lam - DT * plane(mask, i, C) * moved)
        set_plane(base_pot, w, C, m)

    loop(0, W, finish, 2)

    me = (blk * n_len + length) * n_wall + wall
    which = lax.broadcasted_iota(jnp.int32, (1, electrodes), 1).astype(F32)
    mine = owner[...] == me
    patches[0:1, :] = jnp.full((1, LANES), jnp.min(jnp.where(mine, which, float(electrodes))))
    patches[1:2, :] = jnp.full((1, LANES), jnp.max(jnp.where(mine, which, -1.0)))
    patches[2:8, :] = jnp.zeros((6, LANES), F32)


def around(x, by):
    rows, lanes = x.shape
    lane = lane_of(x.shape)
    c = pltpu.roll(x, by, 0) + pltpu.roll(x, rows - by, 0)
    l = jnp.where(lane < by, 0.0, pltpu.roll(x, by, 1)) + jnp.where(
        lane >= lanes - by, 0.0, pltpu.roll(x, lanes - by, 1)
    )
    return c, l


def twins(x, by):
    rows, lanes = x.shape
    row = lax.broadcasted_iota(jnp.int32, x.shape, 0)
    lane = lane_of(x.shape)
    x = x + jnp.where((row & by) == 0, pltpu.roll(x, rows - by, 0), pltpu.roll(x, by, 0))
    return x + jnp.where((lane & by) == 0, pltpu.roll(x, lanes - by, 1), pltpu.roll(x, by, 1))


def solve(sizes, relative, C, W, *refs):
    n_blk, n_len, n_wall = sizes
    count = n_len * n_wall
    blocks, refs = refs[:count], refs[count:]
    base_adj, base_pot, mask, patches, adj_prev, potential, patch_grad = refs[:7]
    b1, x1, b2, x2, b3, x3, near, wide, pm, pe, tm, te, adj_out, pot_out, sheet, sems = refs[7:]
    L = LANES
    W1, C1 = W // 2, C // 2
    planes, NC1, NL1 = b1.shape
    planes -= 2
    blk, length, wall = lax.axis_index("blk"), lax.axis_index("len"), lax.axis_index("wall")
    half = W1 // 2
    middle = LANES // 2
    lane8 = lane_of((C1, LANES))
    often = 8 if NC1 * NL1 <= 4096 else 1

    def blk_of(d):
        return lax.rem(blk - d + n_blk, n_blk) if relative else d

    def length_of(j):
        return (length + j) % n_len if n_len == 2 else j

    zero1 = jnp.zeros((NC1, NL1), F32)
    for ref in (b1, x1, b2, x2, b3, x3):
        ref[0] = zero1
        ref[ref.shape[0] - 1] = zero1

    for v in range(n_wall):
        wall_s = (wall + v) % n_wall
        mine = blocks[v * n_len : (v + 1) * n_len]

        def unpack(d):
            at = pl.ds(pl.multiple_of(C1 * blk_of(d), C1), C1)
            for t in range(n_len // 2):
                one, two = mine[2 * t], mine[2 * t + 1]
                for i in range(half):
                    a, b = one[d, i * C1 : (i + 1) * C1, :], two[d, i * C1 : (i + 1) * C1, :]
                    if n_len == 2:
                        a, b = jnp.where(length == 0, a, b), jnp.where(length == 0, b, a)
                    spot = 1 + wall_s * W1 + i
                    lanes = slice(t * LANES, (t + 1) * LANES)
                    b1[spot, at, lanes] = jnp.where(lane8 < middle, a, pltpu.roll(b, middle, 1))
                    b1[spot + half, at, lanes] = jnp.where(lane8 < middle, pltpu.roll(a, middle, 1), b)

        loop(0, n_blk, unpack, 4)

    def total_of(x, wsum, level, by):
        coef = level_coef(level)
        c, l = around(x, by)
        return level_step(level) * (coef[0] * wsum + coef[1] * c + coef[2] * l)

    def left(ref, i, level):
        b = ref[i]
        return (1.0 - OMEGA) * b + total_of(b, ref[i - 1] + ref[i + 1], level, 2 ** (level - 1))

    def sweep(x_ref, b_ref, i, level):
        x = x_ref[i]
        total = total_of(x, x_ref[i - 1] + x_ref[i + 1], level, 2 ** (level - 1))
        return (1.0 - OMEGA) * x + level_step(level) * b_ref[i] + total

    def down1(q):
        b2[1 + q] = 0.125 * twins(left(b1, 2 * q + 1, 1) + left(b1, 2 * q + 2, 1), 1)

    loop(0, planes // 2, down1, often)

    def down2(q):
        b3[1 + q] = 0.125 * twins(left(b2, 2 * q + 1, 2) + left(b2, 2 * q + 2, 2), 2)

    loop(0, planes // 4, down2, often)

    deep = planes // 4
    k3 = level_step(3)

    def start3(q):
        x3[1 + q] = k3 * b3[1 + q]

    loop(0, deep, start3, often)
    for k in range(SWEEPS):
        from_ref, to_ref = (x3, x2) if k % 2 == 0 else (x2, x3)

        if k == 1:
            x2[1 + deep] = zero1

        def sweep3(q):
            to_ref[1 + q] = sweep(from_ref, b3, 1 + q, 3)

        loop(0, deep, sweep3, often)
    deepest = x3 if SWEEPS % 2 == 0 else x2
    assert deepest is x3
    k2 = level_step(2)

    def up2(q):
        coarse = x3[1 + q]
        x2[1 + 2 * q] = k2 * b2[1 + 2 * q] + coarse
        x2[2 + 2 * q] = k2 * b2[2 + 2 * q] + coarse

    loop(0, planes // 4, up2, often)

    k1 = level_step(1)

    def up1(q):
        fine = sweep(x2, b2, 1 + q, 2)
        x1[1 + 2 * q] = k1 * b1[1 + 2 * q] + fine
        x1[2 + 2 * q] = k1 * b1[2 + 2 * q] + fine

    loop(0, planes // 2, up1, often)

    Q = W1 + 2
    sectors = (blk, lax.rem(blk + 1, n_blk), lax.rem(blk + n_blk - 1, n_blk))
    spots3 = [pl.ds(pl.multiple_of(s * C1, C1), C1) for s in sectors]
    row8 = lax.broadcasted_iota(jnp.int32, (C1, NL1), 0)
    NR = 2 * C1

    def three(ref, i):
        return jnp.concatenate([ref[i, s, :] for s in spots3], 0)

    def finish1(q):
        i = wall * W1 + q
        x = three(x1, i)
        wsum = three(x1, jnp.maximum(i - 1, 0)) + three(x1, jnp.minimum(i + 1, planes + 1))
        value = (1.0 - OMEGA) * x + k1 * three(b1, i) + total_of(x, wsum, 1, 1)
        value = jnp.where(jnp.logical_and(i >= 1, i <= planes), value, 0.0)
        set_plane(near, 2 * q, C1, value[:C1])
        set_plane(near, 2 * q + 1, C1, jnp.where(row8 < 2, value[C1 : 2 * C1], value[2 * C1 :]))

    loop(0, Q, finish1, min(often, 6))

    lane = lane_of((NL1, LANES))
    source = lax.broadcasted_iota(jnp.int32, (NL1, LANES), 0)
    first = length * middle
    take_m = jnp.where(source == first + lane // 2, 1.0, 0.0).astype(F32)
    at_e = jnp.where(lane < H, middle + lane // 2, jnp.where(lane >= LANES - H, lane // 2 - middle, 4 * NL1))
    take_e = jnp.where(source == first + at_e, 1.0, 0.0).astype(F32)
    R = C + 8
    row8 = lax.broadcasted_iota(jnp.int32, (8, LANES), 0)
    for out, sel in ((pm, take_m), (pe, take_e)):
        value = precise(near[...], sel)
        wide[pl.ds(0, Q * NR, stride=2), :] = value
        wide[pl.ds(1, Q * NR, stride=2), :] = value
        for q in range(Q):
            base = 2 * NR * q
            out[R * q : R * q + C, :] = wide[base : base + C, :]
            out[R * q + C : R * (q + 1), :] = jnp.where(
                row8 < H, wide[base + C : base + C + 8, :], wide[base + 2 * NR - 8 : base + 2 * NR, :]
            )
    coef, k0 = level_coef(0), level_step(0)
    rim = rim_lanes(lane_of((R, LANES)), length, n_len)

    def rows_beside(x):
        return pltpu.roll(x, 1, 0) + pltpu.roll(x, x.shape[0] - 1, 0)

    def coarse_terms(q):
        m, e = plane(pm, q, R), plane(pe, q, R)
        lm, le = beside_lanes(m, e)
        gm = (1.0 - OMEGA) * m + k0 * (coef[0] * m + coef[1] * rows_beside(m) + coef[2] * lm)
        ge = (1.0 - OMEGA) * e + k0 * (coef[0] * e + coef[1] * rows_beside(e) + coef[2] * le)
        return gm, ge

    ks = k0 * coef[0]

    def put(t, gm, ge, other, ok):
        m = gm + ks * plane(pm, other, R)
        e = jnp.where(rim, ge + ks * plane(pe, other, R), 0.0)
        if ok is not None:
            m, e = jnp.where(ok, m, 0.0), jnp.where(ok, e, 0.0)
        set_plane(tm, t, R, m)
        set_plane(te, t, R, e)

    put(0, *coarse_terms(0), 1, wall > 0)
    put(W + 1, *coarse_terms(Q - 1), Q - 2, wall < n_wall - 1)

    def level0(q):
        gm, ge = coarse_terms(q)
        put(2 * q - 1, gm, ge, q - 1, None)
        put(2 * q, gm, ge, q + 1, None)
        for w in (2 * q - 2, 2 * q - 1):
            set_plane(pot_out, w, C, plane(base_pot, w, C) + plane(tm, w + 1, R)[:C])

    def finish0(w):
        m, e = plane(tm, w + 1, R), plane(te, w + 1, R)[:C]
        cm = rows_beside(m)[:C]
        m = m[:C]
        wm = plane(tm, w, R)[:C] + plane(tm, w + 2, R)[:C]
        lm = beside_lanes_main(m, e)
        moved = 2.0 * sum(SI) * m - SI[0] * wm - SI[1] * cm - SI[2] * lm
        set_plane(adj_out, w, C, plane(base_adj, w, C) - DT * plane(mask, w + H, C) * moved)

    parts = 2
    size = W // parts
    copies = []

    def send(src, dst, k, sem):
        spot = pl.ds(k * size * C, size * C)
        copies.append(pltpu.make_async_copy(src.at[spot], dst.at[spot], sem))
        copies[-1].start()

    for k in range(parts):
        loop(1 + k * W1 // parts, 1 + (k + 1) * W1 // parts, level0, 4)
        send(pot_out, potential, k, sems.at[0, k])
    for k in range(parts):
        loop(k * size, (k + 1) * size, finish0, 4)
        send(adj_out, adj_prev, k, sems.at[1, k])

    NC, NL = sheet.shape[1:]
    twice_c = jnp.where(
        lax.broadcasted_iota(jnp.int32, (NC, NC1), 0) // 2 == lax.broadcasted_iota(jnp.int32, (NC, NC1), 1), 1.0, 0.0
    ).astype(F32)
    twice_l = jnp.where(
        lax.broadcasted_iota(jnp.int32, (NL1, NL), 1) // 2 == lax.broadcasted_iota(jnp.int32, (NL1, NL), 0), 1.0, 0.0
    ).astype(F32)
    for s, i in enumerate((1, planes)):
        p = precise(precise(twice_c, sweep(x1, b1, i, 1)), twice_l)
        c, l = around(p, 1)
        sheet[s] = (1.0 - OMEGA) * p + k0 * (coef[0] * p + coef[1] * c + coef[2] * l)

    owned = [patches[r : r + 1, :] for r in range(2)]
    spot = lax.broadcasted_iota(jnp.int32, (8, LANES), 0) * LANES + lane_of((8, LANES))
    spot = spot.astype(F32)
    start = half * C1
    totals = [jnp.zeros((C, LANES), F32) for _ in owned]
    small = [jnp.zeros((8, LANES), F32) for _ in owned]
    for v in range(n_wall):
        wall_s = (wall + v) % n_wall
        for j in range(n_len):
            ref = blocks[v * n_len + j]
            at_l = pl.ds(pl.multiple_of(length_of(j) * L, L), L)

            def add(d, carry):
                big, little = carry
                values = sheet[wall_s, pl.ds(pl.multiple_of(blk_of(d) * C, C), C), at_l]
                ids = ref[d, start : start + C, :]
                parts = ref[d, start + C : start + C + 8, :]
                big = [x + jnp.where(ids == e, values, 0.0) for x, e in zip(big, owned)]
                little = [x + jnp.where(spot == e, parts, 0.0) for x, e in zip(little, owned)]
                return big, little

            totals, small = lax.fori_loop(0, n_blk, add, (totals, small), unroll=min(4, n_blk))
    factor = 1.0 / (2.0 * C * L / 2) ** 0.5
    for r in range(2):
        patch_grad[0, r] = (jnp.sum(totals[r]) + jnp.sum(small[r])) * factor
    for copy in copies:
        copy.wait()


def ring(x, axis, by):
    count = lax.axis_size(axis)
    return lax.ppermute(x, axis, [(i, (i + by) % count) for i in range(count)])


def across(x):
    n_wall = lax.axis_size("wall")
    pairs = [(l * n_wall + w, (1 - l) * n_wall + (w + 1) % n_wall) for l in range(2) for w in range(n_wall)]
    return lax.ppermute(x, ("len", "wall"), pairs)


def call(kernel, ins, outs, scratch, name, work=0):
    places = {"vmem": pltpu.VMEM, "smem": pltpu.SMEM, "any": pl.ANY}

    def specs(kinds):
        return [pl.BlockSpec(memory_space=places[kind]) for kind in kinds]

    cost = pl.CostEstimate(flops=work, bytes_accessed=work, transcendentals=0) if work else None
    return pl.pallas_call(
        kernel,
        out_shape=[jax.ShapeDtypeStruct(shape, F32) for shape, _ in outs],
        in_specs=specs(ins),
        out_specs=specs(kind for _, kind in outs),
        scratch_shapes=[pltpu.VMEM(shape, F32) if isinstance(shape, tuple) else shape for shape in scratch],
        compiler_params=pltpu.CompilerParams(vmem_limit_bytes=48 * 2**20),
        cost_estimate=cost,
        name=name,
    )


def body(adj_next, ion_slope, misfit, tissue_mask, patch_ids, owner_map):
    W, C, L = adj_next.shape
    n_blk, n_len, n_wall = lax.axis_size("blk"), lax.axis_size("len"), lax.axis_size("wall")
    electrodes = owner_map.shape[0]
    assert L == LANES and H * W == LANES and n_wall == 2 and electrodes == 2 * n_blk * n_len * n_wall
    N = W + 2 * H
    n_dir = 1 if n_len == 2 else 2
    cells = W * C
    vmem = "vmem"
    field, own = (N * C, L), (cells, L)
    raw = [x.reshape(cells, L) for x in (adj_next, ion_slope, tissue_mask, misfit)]

    *fields, wall_out = (faces := call(
        functools.partial(pack_faces, n_len),
        ["any"] * 4,
        [(own, vmem)] * 4
        + [((sum(FACES), C, L), vmem)]
        + [((4, C, L), vmem)] * n_dir
        + [((C, L), vmem)] * n_dir,
        [pltpu.VMEM(own, jnp.int32), pltpu.SemaphoreType.DMA((4, 2))],
        "faces",
    )(*raw))[:5]
    strip_out, corner_out = faces[5 : 5 + n_dir], faces[5 + n_dir :]
    wall_in = ring(wall_out, "wall", 1)
    if n_dir == 1:
        strips = [ring(strip_out[0], "len", 1)]
        corners = [across(corner_out[0])]
    else:
        strips = [ring(strip_out[1], "len", -1), ring(strip_out[0], "len", 1)]
        corners = [ring(ring(corner_out[1], "wall", 1), "len", -1), ring(ring(corner_out[0], "wall", 1), "len", 1)]

    near = (5 * N + 16, L)
    *fields, to_next, to_prev, own_rows = call(
        functools.partial(boundary, n_len, C),
        [vmem] * (5 + 2 * n_dir),
        [(field, vmem)] * 8 + [(near, vmem)] * 2 + [((2, 6, N, L), vmem)],
        [],
        "boundary",
    )(*fields, wall_in, *strips, *corners)
    from_next = ring(to_prev, "blk", -1)
    from_prev = ring(to_next, "blk", 1)
    qm, bm, be, coarse, surface = call(
        functools.partial(sector, n_len, n_wall, C),
        [vmem] * 8,
        [(field, vmem)] * 3 + [((cells // 8, L), vmem), ((C, L), vmem)],
        [field, (cells // 2, L)],
        "sector",
        work=16 * 10**6,
    )(*fields)

    rows = (8, N, L)
    wide = LANES * ((electrodes + LANES - 1) // LANES)
    message = (cells // 8 + C + 8, L)
    rows_n, rows_p, mine = call(
        functools.partial(correct, electrodes, n_len, n_wall),
        [vmem] * 6,
        [(rows, vmem), (rows, vmem), (message, vmem)],
        [(1, N, L), (wide, L)],
        "correct",
    )(own_rows, from_next, from_prev, coarse, surface, patch_ids)

    relative = n_blk <= 4
    if relative:
        sector_blocks = jnp.stack([mine] + [ring(mine, "blk", d) for d in range(1, n_blk)])
    else:
        sector_blocks = lax.all_gather(mine, "blk")
    if n_len == 2:
        here = [sector_blocks, ring(sector_blocks, "len", 1)]
    else:
        gathered = lax.all_gather(sector_blocks, "len")
        here = [gathered[j] for j in range(n_len)]
    blocks = here + [ring(x, "wall", 1) for x in here]

    base_adj, base_pot, patches = call(
        functools.partial(source_part, n_blk, n_len, n_wall, C, electrodes),
        [vmem] * 7,
        [(own, vmem), (own, vmem), ((8, L), vmem)],
        [field] * 4 + [(2, N, L)],
        "source_part",
        work=12 * 10**6,
    )(bm, be, rows_n, rows_p, qm, fields[2], owner_map.reshape(1, electrodes))

    NC1, NL1 = n_blk * C // 2, n_len * L // 2
    planes = n_wall * W // 2
    grids = [(planes // k + 2, NC1, NL1) for k in (1, 1, 2, 2, 4, 4)]
    Q = W // 2 + 2
    tall = (Q * (C + 8), L)
    taller = ((W + 2) * (C + 8), L)
    scratch = grids + [(Q * C, NL1), (2 * Q * C, L), tall, tall, taller, taller, own, own]
    scratch += [(2, n_blk * C, n_len * L), pltpu.SemaphoreType.DMA((2, 2))]
    adj_prev, potential, patch_grad = call(
        functools.partial(solve, (n_blk, n_len, n_wall), relative, C, W),
        [vmem] * (n_len * n_wall + 4),
        [(own, "any"), (own, "any"), ((1, 2), "smem")],
        scratch,
        "solve",
    )(*blocks, base_adj, base_pot, fields[2], patches)
    return adj_prev.reshape(W, C, L), potential.reshape(W, C, L), patch_grad


def solution(mesh):
    field = P(("groups", "wall"), "blk", "len")
    return jax.shard_map(
        body,
        mesh=mesh,
        in_specs=(field, field, field, field, field, P("groups")),
        out_specs=(field, field, P(("groups", "blk", "len", "wall"), None)),
        check_vma=False,
    )
```

time: 51.5 us -> 49.6 us (0.963)
  waiting for transfers between devices: 19.2 us -> 14.4 us
  Pallas kernels: 15.7 us -> 19 us
  starting transfers between devices: 11.3 us -> 10.7 us
    ppermute x10, waiting for transfers between devices: 16.1 us -> 11.4 us  [ring(): return lax.ppermute(x, axis, [(i, (i + by) % count) for i in range(count)])]
    pallas_call x4 -> x6, Pallas kernels: 15.7 us -> 19 us  [the longest x1 6.55 us: body(): call(functools.partial(solve, (n_blk, n_len, n_wall), relative, C, W), [v...]
    ppermute x10, starting transfers between devices: 11.2 us -> 10.6 us  [ring(): return lax.ppermute(x, axis, [(i, (i + by) % count) for i in range(count)])]
    unnamed x14 -> x12, local copies, waits for them, and re-layouts: 4.45 us -> 4.45 us
  transfers between devices with their start and end apart: 11 -> 11, of which waited for: 8 -> 6; matrix products, arithmetic and copies ran while one was open for 0% -> 0% of each run, Pallas kernels for 0% -> 17%
where the time goes in v2:
time: 49.6 us; the launch traced here: 49.3 us
  Pallas kernels  19 us (38%)
  waiting for transfers between devices  14.4 us (29%)
  starting transfers between devices  10.7 us (22%)
  local copies, waits for them, and re-layouts  4.45 us (9%)
  between operations  0.71 us (1%)
    ppermute x10, waiting for transfers between devices, ring(): return lax.ppermute(x, axis, [(i, (i + by) % count) for i in range(count)])  11.4 us
    ppermute x10, starting transfers between devices, ring(): return lax.ppermute(x, axis, [(i, (i + by) % count) for i in range(count)])  10.6 us
    pallas_call x1, Pallas kernels, body(): call(functools.partial(solve, (n_blk, n_len, n_wall), relative, C, W), [v...  6.55 us
    pallas_call x1, Pallas kernels, body(): call(functools.partial(sector, n_len, n_wall, C), [vmem] * 8, [(field, vm...  5.13 us
    unnamed x12, local copies, waits for them, and re-layouts  4.45 us
    pallas_call x1, Pallas kernels, body(): call(functools.partial(source_part, n_blk, n_len, n_wall, C, electrodes),...  3.44 us
    ppermute x1, waiting for transfers between devices, across(): return lax.ppermute(x, ('len', 'wall'), pairs)  3.01 us
    pallas_call x1, Pallas kernels, body(): call(functools.partial(pack_faces, n_len), ['any'] * 4, [(own, vmem)] * 4...  1.97 us
  transfers between devices with their start and end apart: 11, of which 6 were waited for; matrix products, arithmetic and copies ran while one was open for 0% of the time, Pallas kernels for 17%

profile of v2, /device:TPU:0, one launch (start us, length us, event | category | flops | bytes accessed | tf_op | source)
XLA Modules:
  0.0 49.3 jit_solution(10423714199654713988)
XLA Ops:
  0.6 0.0 copy-start
  0.6 0.9 %copy-done = f32[32,16,128]{2,1,0:T(8,128)S(1)} copy-done((f32[32,16,128]{2,1,0:T(8,128)S(1)}, f32[32,16,128]{2,1,0:T(8,128)}, u32[]{:S(2)}) %copy-start) | copy-done | bytes 262168
  1.6 0.0 copy-start.1
  1.6 0.9 %copy-done.1 = f32[32,16,128]{2,1,0:T(8,128)S(1)} copy-done((f32[32,16,128]{2,1,0:T(8,128)S(1)}, f32[32,16,128]{2,1,0:T(8,128)}, u32[]{:S(2)}) %copy-start.1) | copy-done | bytes 262168
  2.5 0.0 copy-start.2
  2.5 0.9 %copy-done.2 = s32[32,16,128]{2,1,0:T(8,128)S(1)} copy-done((s32[32,16,128]{2,1,0:T(8,128)S(1)}, s32[32,16,128]{2,1,0:T(8,128)}, u32[]{:S(2)}) %copy-start.2) | copy-done | bytes 262168
  3.5 0.0 copy-start.3
  3.5 0.9 %copy-done.3 = f32[32,16,128]{2,1,0:T(8,128)S(1)} copy-done((f32[32,16,128]{2,1,0:T(8,128)S(1)}, f32[32,16,128]{2,1,0:T(8,128)}, u32[]{:S(2)}) %copy-start.3) | copy-done | bytes 262168
  4.4 2.0 %faces.1 = (f32[512,128]{1,0:T(8,128)S(1)}, f32[512,128]{1,0:T(8,128)S(1)}, f32[512,128]{1,0:T(8,128)S(1)}, f32[512,128]{1,0:T(8,128)S(1)}, f32[12,16,128]{2,1,0...) custom-call(f32[512,128]{1,0:T(8,128)S(1)} %bitcast.11, f32[512,128]{1,0:T(8,128)S(1)} %bitcast.12, ...), custom_call_target="tpu_custom_call" | custom-call | tf_op jit(solution)/shard_map/faces/pallas_call | solution.py:802
  6.4 0.5 %collective-permute-start = (f32[12,16,128]{2,1,0:T(8,128)S(1)}, f32[12,16,128]{2,1,0:T(8,128)S(1)}, u32[]{:S(2)}, u32[]{:S(2)}) collective-permute-start(f32[12,16,128]{2,1,0:T(8,128)S(1)} %get-tuple-element.39), channel_id=1, source_target_pairs={{0,1},{1,0},{2,3},{3,2},{4,5},{5,4},{6,7},{7,6},{8,9},{9,8},{10,11... | collective-permute-start | bytes 294920 | tf_op jit(solution)/shard_map/ppermute | solution.py:762
  6.9 2.6 %collective-permute-start.1 = (f32[4,16,128]{2,1,0:T(8,128)S(1)}, f32[4,16,128]{2,1,0:T(8,128)S(1)}, u32[]{:S(2)}, u32[]{:S(2)}) collective-permute-start(f32[4,16,128]{2,1,0:T(8,128)S(1)} %get-tuple-element.40), channel_id=1, source_target_pairs={{0,2},{2,0},{1,3},{3,1},{4,6},{6,4},{5,7},{7,5},{8,10},{10,8},{9,1... | collective-permute-start | bytes 98312 | tf_op jit(solution)/shard_map/ppermute | solution.py:762
  9.5 0.1 collective-permute-start.2
  9.6 3.0 %collective-permute-done.2.rest_1_ = f32[16,128]{1,0:T(8,128)S(1)} collective-permute-done((f32[16,128]{1,0:T(8,128)S(1)}, f32[16,128]{1,0:T(8,128)S(1)}, u32[]{:S(2)}, u32[]{:S(2)}) %collective-permute-start.2) | collective-permute-done | bytes 8224 | tf_op jit(solution)/shard_map/ppermute | solution.py:768
  12.6 0.0 collective-permute-done.1.rest_0_
  12.6 0.0 collective-permute-done.wall_in
  12.6 0.9 %boundary.1 = (f32[640,128]{1,0:T(8,128)S(1)}, f32[640,128]{1,0:T(8,128)S(1)}, f32[640,128]{1,0:T(8,128)S(1)}, f32[640,128]{1,0:T(8,128)S(1)}, f32[640,128]{1,0:...) custom-call(f32[512,128]{1,0:T(8,128)S(1)} %get-tuple-element.35.xm0, ...), custom_call_target="tpu_custom_call" | custom-call | tf_op jit(solution)/shard_map/boundary/pallas_call | solution.py:822
  13.5 3.6 %collective-permute-start.3 = (f32[216,128]{1,0:T(8,128)S(1)}, f32[216,128]{1,0:T(8,128)S(1)}, u32[]{:S(2)}, u32[]{:S(2)}) collective-permute-start(f32[216,128]{1,0:T(8,128)S(1)} %get-tuple-element.43), channel_id=1, source_target_pairs={{0,12},{4,0},{8,4},{12,8},{1,13},{5,1},{9,5},{13,9},{2,14},{6,2},{... | collective-permute-start | bytes 331784 | tf_op jit(solution)/shard_map/ppermute | solution.py:762
  17.1 0.0 collective-permute-start.4
  17.1 0.0 copy-start.4
  17.1 5.1 %sector.1 = (f32[640,128]{1,0:T(8,128)S(1)}, f32[640,128]{1,0:T(8,128)S(1)}, f32[640,128]{1,0:T(8,128)S(1)}, f32[64,128]{1,0:T(8,128)S(1)}, f32[16,128]{1,0:T(8,128)S(1)}) custom-call(f32[640,128]{1,0:T(8,128)S(1)} %get-tuple-element.45.xm0, f32[640,128]{1,0:T(8,128)S(1)} %get-tuple-element.46.xm1, f32[640,128]{1,0:T(8,128)S(1)} %get-tuple-element.47.xm2.mask.refs_6_, ...), custom_call_target="tpu_custom_call" | custom-call | flops 16000000 | bytes 16000000 | tf_op jit(solution)/shard_map/sector/pallas_call | solution.py:831
  22.3 0.0 collective-permute-done.3.from_next
  22.3 1.5 %collective-permute-done.4.from_prev = f32[216,128]{1,0:T(8,128)S(1)} collective-permute-done((f32[216,128]{1,0:T(8,128)S(1)}, f32[216,128]{1,0:T(8,128)S(1)}, u32[]{:S(2)}, u32[]{:S(2)}) %collective-permute-start.4) | collective-permute-done | bytes 110624 | tf_op jit(solution)/shard_map/ppermute | solution.py:762
  23.8 0.0 copy-done.4
  23.8 1.0 %correct.1 = (f32[8,40,128]{2,1,0:T(8,128)S(1)}, f32[8,40,128]{2,1,0:T(8,128)S(1)}, f32[88,128]{1,0:T(8,128)S(1)}) custom-call(f32[2,6,40,128]{3,2,1,0:T(8,128)S(1)} %get-tuple-element.42.own_rows, f32[216,128]{1,0:T(8,128)S(1)} %collective-permute-done.3.from_next, f32[216,128]{1,0:T(8,128)S(1)} %collective-permute-done.4.from_prev, ...), custom_call_target="tpu_custom_call" | custom-call | tf_op jit(solution)/shard_map/correct/pallas_call | solution.py:843
  24.8 2.4 %collective-permute-start.7 = (f32[88,128]{1,0:T(8,128)S(1)}, f32[88,128]{1,0:T(8,128)S(1)}, u32[]{:S(2)}, u32[]{:S(2)}) collective-permute-start(f32[88,128]{1,0:T(8,128)S(1)} %get-tuple-element.55), channel_id=1, source_target_pairs={{0,12},{4,0},{8,4},{12,8},{1,13},{5,1},{9,5},{13,9},{2,14},{6,2},{... | collective-permute-start | bytes 135176 | tf_op jit(solution)/shard_map/ppermute | solution.py:762
  27.1 0.0 collective-permute-start.6
  27.2 0.6 %collective-permute-start.5 = (f32[88,128]{1,0:T(8,128)S(1)}, f32[88,128]{1,0:T(8,128)S(1)}, u32[]{:S(2)}, u32[]{:S(2)}) collective-permute-start(f32[88,128]{1,0:T(8,128)S(1)} %get-tuple-element.55), channel_id=1, source_target_pairs={{0,4},{4,8},{8,12},{12,0},{1,5},{5,9},{9,13},{13,1},{2,6},{6,10},{... | collective-permute-start | bytes 135176 | tf_op jit(solution)/shard_map/ppermute | solution.py:762
  27.7 1.1 %collective-permute-done.7 = f32[88,128]{1,0:T(8,128)S(1)} collective-permute-done((f32[88,128]{1,0:T(8,128)S(1)}, f32[88,128]{1,0:T(8,128)S(1)}, u32[]{:S(2)}, u32[]{:S(2)}) %collective-permute-start.7) | collective-permute-done | bytes 45088 | tf_op jit(solution)/shard_map/ppermute | solution.py:762
  28.9 3.3 %collective-permute-done.6 = f32[88,128]{1,0:T(8,128)S(1)} collective-permute-done((f32[88,128]{1,0:T(8,128)S(1)}, f32[88,128]{1,0:T(8,128)S(1)}, u32[]{:S(2)}, u32[]{:S(2)}) %collective-permute-start.6) | collective-permute-done | bytes 45088 | tf_op jit(solution)/shard_map/ppermute | solution.py:762
  32.2 0.8 %collective-permute-done.5 = f32[88,128]{1,0:T(8,128)S(1)} collective-permute-done((f32[88,128]{1,0:T(8,128)S(1)}, f32[88,128]{1,0:T(8,128)S(1)}, u32[]{:S(2)}, u32[]{:S(2)}) %collective-permute-start.5) | collective-permute-done | bytes 45088 | tf_op jit(solution)/shard_map/ppermute | solution.py:762
  33.0 0.9 %collective-permute-start.8 = (f32[4,88,128]{2,1,0:T(8,128)S(1)}, f32[4,88,128]{2,1,0:T(8,128)S(1)}, u32[]{:S(2)}, u32[]{:S(2)}) collective-permute-start(f32[4,88,128]{2,1,0:T(8,128)S(1)} %pad_maximum_fusion.refs_0_), channel_id=1, source_target_pairs={{0,2},{2,0},{1,3},{3,1},{4,6},{6,4},{5,7},{7,5},{8,10},{10,8},{9,1... | collective-permute-start | bytes 540680 | tf_op jit(solution)/shard_map/ppermute | solution.py:762
  34.0 0.0 collective-permute-start.9
  34.0 4.6 %collective-permute-done.8.refs_1_ = f32[4,88,128]{2,1,0:T(8,128)S(1)} collective-permute-done((f32[4,88,128]{2,1,0:T(8,128)S(1)}, f32[4,88,128]{2,1,0:T(8,128)S(1)}, u32[]{:S(2)}, u32[]{:S(2)}) %collective-permute-start.8) | collective-permute-done | bytes 180256 | tf_op jit(solution)/shard_map/ppermute | solution.py:762
  38.6 0.0 collective-permute-start.10
  38.6 0.0 copy-start.5
  38.6 0.7 %copy-done.5 = s32[32]{0:T(128)S(1)} copy-done((s32[32]{0:T(128)S(1)}, s32[32]{0:T(128)}, u32[]{:S(2)}) %copy-start.5) | copy-done | bytes 152
  39.2 3.4 %source_part.1 = (f32[512,128]{1,0:T(8,128)S(1)}, f32[512,128]{1,0:T(8,128)S(1)}, f32[8,128]{1,0:T(8,128)S(1)}) custom-call(f32[640,128]{1,0:T(8,128)S(1)} %get-tuple-element.56.bm, f32[640,128]{1,0:T(8,128)S(1)} %get-tuple-element.57.be, f32[8,40,128]{2,1,0:T(8,128)S(1)} %get-tuple-element.58.rows_n, f32[8,40,128]{2,1,0:T(8,128)S(1)} %get-tuple-element.59.rows_p, ...), custom_call_target="tpu_custom_call" | custom-call | flops 12000000 | bytes 12000000 | tf_op jit(solution)/shard_map/source_part/pallas_call | solution.py:863
  42.7 0.0 collective-permute-done.9.refs_2_
  42.7 0.0 collective-permute-done.10.refs_3_
  42.7 6.5 %solve.1 = (f32[512,128]{1,0:T(8,128)}, f32[512,128]{1,0:T(8,128)}, f32[1,2]{1,0:T(1,128)}) custom-call(f32[4,88,128]{2,1,0:T(8,128)S(1)} %pad_maximum_fusion.refs_0_, f32[4,88,128]{2,1,0:T(8,128)S(1)} %collective-permute-done.8.refs_1_, f32[4,88,128]{2,1,0:T(8,128)S(1)} %collective-permute-done.9.refs_2_, ...), custom_call_target="tpu_custom_call" | custom-call | tf_op jit(solution)/shard_map/solve/pallas_call | solution.py:880
  (1 shorter events, 0.0 us)
Async XLA Ops:
  0.6 1.0 %copy-start = (f32[32,16,128]{2,1,0:T(8,128)S(1)}, f32[32,16,128]{2,1,0:T(8,128)}, u32[]{:S(2)}) copy-start(f32[32,16,128]{2,1,0:T(8,128)} %param.6) | copy-start | bytes 786436
  1.6 0.9 %copy-start.1 = (f32[32,16,128]{2,1,0:T(8,128)S(1)}, f32[32,16,128]{2,1,0:T(8,128)}, u32[]{:S(2)}) copy-start(f32[32,16,128]{2,1,0:T(8,128)} %param.7) | copy-start | bytes 786436
  2.5 0.9 %copy-start.2 = (s32[32,16,128]{2,1,0:T(8,128)S(1)}, s32[32,16,128]{2,1,0:T(8,128)}, u32[]{:S(2)}) copy-start(s32[32,16,128]{2,1,0:T(8,128)} %param.9) | copy-start | bytes 786436
  3.5 0.9 %copy-start.3 = (f32[32,16,128]{2,1,0:T(8,128)S(1)}, f32[32,16,128]{2,1,0:T(8,128)}, u32[]{:S(2)}) copy-start(f32[32,16,128]{2,1,0:T(8,128)} %param.8) | copy-start | bytes 786436
  6.4 6.2 %collective-permute-start = (f32[12,16,128]{2,1,0:T(8,128)S(1)}, f32[12,16,128]{2,1,0:T(8,128)S(1)}, u32[]{:S(2)}, u32[]{:S(2)}) collective-permute-start(f32[12,16,128]{2,1,0:T(8,128)S(1)} %get-tuple-element.39), channel_id=1, source_target_pairs={{0,1},{1,0},{2,3},{3,2},{4,5},{5,4},{6,7},{7,6},{8,9},{9,8},{10,11... | collective-permute-start | bytes 294920 | tf_op jit(solution)/shard_map/ppermute | solution.py:762
  6.9 5.6 %collective-permute-start.1 = (f32[4,16,128]{2,1,0:T(8,128)S(1)}, f32[4,16,128]{2,1,0:T(8,128)S(1)}, u32[]{:S(2)}, u32[]{:S(2)}) collective-permute-start(f32[4,16,128]{2,1,0:T(8,128)S(1)} %get-tuple-element.40), channel_id=1, source_target_pairs={{0,2},{2,0},{1,3},{3,1},{4,6},{6,4},{5,7},{7,5},{8,10},{10,8},{9,1... | collective-permute-start | bytes 98312 | tf_op jit(solution)/shard_map/ppermute | solution.py:762
  9.5 3.1 %collective-permute-start.2 = (f32[16,128]{1,0:T(8,128)S(1)}, f32[16,128]{1,0:T(8,128)S(1)}, u32[]{:S(2)}, u32[]{:S(2)}) collective-permute-start(f32[16,128]{1,0:T(8,128)S(1)} %get-tuple-element.41), channel_id=1, source_target_pairs={{0,3},{1,2},{2,1},{3,0},{4,7},{5,6},{6,5},{7,4},{8,11},{9,10},{10,... | collective-permute-start | bytes 24584 | tf_op jit(solution)/shard_map/ppermute | solution.py:768
  13.5 8.8 %collective-permute-start.3 = (f32[216,128]{1,0:T(8,128)S(1)}, f32[216,128]{1,0:T(8,128)S(1)}, u32[]{:S(2)}, u32[]{:S(2)}) collective-permute-start(f32[216,128]{1,0:T(8,128)S(1)} %get-tuple-element.43), channel_id=1, source_target_pairs={{0,12},{4,0},{8,4},{12,8},{1,13},{5,1},{9,5},{13,9},{2,14},{6,2},{... | collective-permute-start | bytes 331784 | tf_op jit(solution)/shard_map/ppermute | solution.py:762
  17.1 6.6 %collective-permute-start.4 = (f32[216,128]{1,0:T(8,128)S(1)}, f32[216,128]{1,0:T(8,128)S(1)}, u32[]{:S(2)}, u32[]{:S(2)}) collective-permute-start(f32[216,128]{1,0:T(8,128)S(1)} %get-tuple-element.44), channel_id=1, source_target_pairs={{0,4},{4,8},{8,12},{12,0},{1,5},{5,9},{9,13},{13,1},{2,6},{6,10},{... | collective-permute-start | bytes 331784 | tf_op jit(solution)/shard_map/ppermute | solution.py:762
  17.1 6.6 %copy-start.4 = (s32[1,16,128]{2,1,0:T(8,128)S(1)}, s32[1,16,128]{2,1,0:T(8,128)}, u32[]{:S(2)}) copy-start(s32[1,16,128]{2,1,0:T(8,128)} %ids.1) | copy-start | bytes 24580
  24.8 4.1 %collective-permute-start.7 = (f32[88,128]{1,0:T(8,128)S(1)}, f32[88,128]{1,0:T(8,128)S(1)}, u32[]{:S(2)}, u32[]{:S(2)}) collective-permute-start(f32[88,128]{1,0:T(8,128)S(1)} %get-tuple-element.55), channel_id=1, source_target_pairs={{0,12},{4,0},{8,4},{12,8},{1,13},{5,1},{9,5},{13,9},{2,14},{6,2},{... | collective-permute-start | bytes 135176 | tf_op jit(solution)/shard_map/ppermute | solution.py:762
  27.1 5.0 %collective-permute-start.6 = (f32[88,128]{1,0:T(8,128)S(1)}, f32[88,128]{1,0:T(8,128)S(1)}, u32[]{:S(2)}, u32[]{:S(2)}) collective-permute-start(f32[88,128]{1,0:T(8,128)S(1)} %get-tuple-element.55), channel_id=1, source_target_pairs={{0,8},{4,12},{8,0},{12,4},{1,9},{5,13},{9,1},{13,5},{2,10},{6,14},... | collective-permute-start | bytes 135176 | tf_op jit(solution)/shard_map/ppermute | solution.py:762
  27.2 5.8 %collective-permute-start.5 = (f32[88,128]{1,0:T(8,128)S(1)}, f32[88,128]{1,0:T(8,128)S(1)}, u32[]{:S(2)}, u32[]{:S(2)}) collective-permute-start(f32[88,128]{1,0:T(8,128)S(1)} %get-tuple-element.55), channel_id=1, source_target_pairs={{0,4},{4,8},{8,12},{12,0},{1,5},{5,9},{9,13},{13,1},{2,6},{6,10},{... | collective-permute-start | bytes 135176 | tf_op jit(solution)/shard_map/ppermute | solution.py:762
  33.0 5.6 %collective-permute-start.8 = (f32[4,88,128]{2,1,0:T(8,128)S(1)}, f32[4,88,128]{2,1,0:T(8,128)S(1)}, u32[]{:S(2)}, u32[]{:S(2)}) collective-permute-start(f32[4,88,128]{2,1,0:T(8,128)S(1)} %pad_maximum_fusion.refs_0_), channel_id=1, source_target_pairs={{0,2},{2,0},{1,3},{3,1},{4,6},{6,4},{5,7},{7,5},{8,10},{10,8},{9,1... | collective-permute-start | bytes 540680 | tf_op jit(solution)/shard_map/ppermute | solution.py:762
  34.0 8.7 %collective-permute-start.9 = (f32[4,88,128]{2,1,0:T(8,128)S(1)}, f32[4,88,128]{2,1,0:T(8,128)S(1)}, u32[]{:S(2)}, u32[]{:S(2)}) collective-permute-start(f32[4,88,128]{2,1,0:T(8,128)S(1)} %pad_maximum_fusion.refs_0_), channel_id=1, source_target_pairs={{0,1},{1,0},{2,3},{3,2},{4,5},{5,4},{6,7},{7,6},{8,9},{9,8},{10,11... | collective-permute-start | bytes 540680 | tf_op jit(solution)/shard_map/ppermute | solution.py:762
  38.6 4.1 %collective-permute-start.10 = (f32[4,88,128]{2,1,0:T(8,128)S(1)}, f32[4,88,128]{2,1,0:T(8,128)S(1)}, u32[]{:S(2)}, u32[]{:S(2)}) collective-permute-start(f32[4,88,128]{2,1,0:T(8,128)S(1)} %collective-permute-done.8.refs_1_), channel_id=1, source_target_pairs={{0,1},{1,0},{2,3},{3,2},{4,5},{5,4},{6,7},{7,6},{8,9},{9,8},{10,11... | collective-permute-start | bytes 540680 | tf_op jit(solution)/shard_map/ppermute | solution.py:762
  38.6 0.7 %copy-start.5 = (s32[32]{0:T(128)S(1)}, s32[32]{0:T(128)}, u32[]{:S(2)}) copy-start(s32[32]{0:T(128)} %param.11) | copy-start | bytes 388

commit v3 on v2

--- a/solution.py
+++ b/solution.py
@@ -162,6 +162,19 @@
     return out
 
 
+def near_rows(n_dir, W):
+    start, places = 8 * n_dir, []
+    for reach in (0, 1, 2, 2, 3):
+        places.append((start, H - reach, W + 2 * reach))
+        start += W + 2 * reach
+    assert start % 8 == 0
+    return places
+
+
+def rim_tiles(values):
+    return [value[s : s + 8] for value in values for s in range(0, value.shape[0], 8)]
+
+
 def boundary(n_len, C, xm0, xm1, xm2, xm3, wall_in, *rest):
     n_dir = 1 if n_len == 2 else 2
     strips, corners, rest = rest[:n_dir], rest[n_dir : 2 * n_dir], rest[2 * n_dir :]
@@ -201,8 +214,6 @@
             set_plane(xm[a], here + p, C, wall_in[first + p])
             set_plane(xe[a], here + p, C, rim(packed, H * (first + p)))
 
-    pos_of = lane_of((8, LANES)) // 8
-    tiles = N // 8
     for side, (out, order) in enumerate(((to_next, (C - 1, C - 2, C - 3, C - 4)), (to_prev, (0, 1, 2, 3)))):
         adj = [dense_pair(xm[0], xe[0], r, N, C) for r in order]
         mask = [dense_pair(xm[2], xe[2], r, N, C) for r in order[:3]]
@@ -215,17 +226,17 @@
         mis = dense_pair(xm[3], xe[3], order[0], N, C)
         near = [near[j] + mis[j] for j in range(2)]
         second = dense_apply(q[1], q[2], q[0], SI)[0] + dense(xm[3], order[1], N, C)
-        mains = (adj[0][0], mask[0][0], q[0][0], near[0], second)
-        for k, value in enumerate(mains):
-            out[k * N : (k + 1) * N, :] = value
-        packs = [jnp.zeros((8, LANES), F32), jnp.zeros((8, LANES), F32)]
-        for k, value in enumerate((adj[0][1], mask[0][1], q[0][1], near[1])):
-            for s in range(tiles):
-                t = k * tiles + s
-                turned = pltpu.roll(value[8 * s : 8 * s + 8], (H + 8 * (t % 16)) % LANES, 1)
-                packs[t // 16] = jnp.where(pos_of == t % 16, turned, packs[t // 16])
-        out[5 * N : 5 * N + 8, :] = packs[0]
-        out[5 * N + 8 : 5 * N + 16, :] = packs[1]
+        for value, (start, first, count) in zip((second, near[0], q[0][0], mask[0][0], adj[0][0]), near_rows(n_dir, W)):
+            out[start : start + count, :] = value[first : first + count]
+        group = lane_of((8, LANES)) // (H * n_dir)
+        shift = jnp.where(length == 0, 0, H) if n_dir == 1 else H
+        packs = [jnp.zeros((8, LANES), F32) for _ in range(n_dir)]
+        for t, tile in enumerate(rim_tiles((near[1], q[0][1], mask[0][1], adj[0][1]))):
+            k, at = divmod(t, LANES // (H * n_dir))
+            turned = pltpu.roll(tile, lax.rem(shift + H * n_dir * at, LANES), 1)
+            packs[k] = jnp.where(group == at, turned, packs[k])
+        for k in range(n_dir):
+            out[8 * k : 8 * k + 8, :] = packs[k]
         for k, pair in enumerate((adj[0], mask[0], q[0])):
             own_rows[side, 2 * k] = pair[0]
             own_rows[side, 2 * k + 1] = pair[1]
@@ -327,21 +338,26 @@
     coarse[...] = precise(z[:half], low) + precise(z[half:], high)
 
 
-def unpacked(ref, N):
-    lane = lane_of((8, LANES))
-    rim = jnp.logical_or(lane < H, lane >= LANES - H)
-    tiles = N // 8
-    mains = [ref[q * N : (q + 1) * N, :] for q in range(5)]
-    packs = [ref[5 * N : 5 * N + 8, :], ref[5 * N + 8 : 5 * N + 16, :]]
+def unpacked(ref, n_len, length, N):
+    n_dir = 1 if n_len == 2 else 2
+    mains = []
+    for start, first, count in near_rows(n_dir, N - 2 * H):
+        begin = min(start - first, ref.shape[0] - N)
+        value = ref[begin : begin + N, :]
+        behind = start - first - begin
+        mains.append(pltpu.roll(value, N - behind, 0) if behind else value)
+    rim = rim_lanes(lane_of((8, LANES)), length, n_len)
+    shift = jnp.where(length == 0, 0, H) if n_dir == 1 else H
     rims = []
-    for q in range(4):
+    for k in range(4):
         parts = []
-        for s in range(tiles):
-            t = q * tiles + s
-            turned = pltpu.roll(packs[t // 16], (2 * LANES - H - 8 * (t % 16)) % LANES, 1)
-            parts.append(jnp.where(rim, turned, 0.0))
+        for s in range(N // 8):
+            pack, at = divmod(k * (N // 8) + s, LANES // (H * n_dir))
+            back = lax.rem(2 * LANES - shift - H * n_dir * at, LANES)
+            parts.append(jnp.where(rim, pltpu.roll(ref[8 * pack : 8 * pack + 8, :], back, 1), 0.0))
         rims.append(jnp.concatenate(parts, 0))
-    return [(mains[q], rims[q]) for q in range(4)] + [mains[4]]
+    second, near, q, mask, adj = mains
+    return (adj, rims[3]), (mask, rims[2]), (q, rims[1]), (near, rims[0]), second
 
 
 def lateral(pair):
@@ -381,7 +397,7 @@
         ((from_next, rows_n, (C - 1, C - 2, C - 3)), (from_prev, rows_p, (0, 1, 2)))
     ):
         own = [(own_rows[side, 2 * k], own_rows[side, 2 * k + 1]) for k in range(3)]
-        near, second, halo, halo_second, delta = source_rows(own, unpacked(other, N))
+        near, second, halo, halo_second, delta = source_rows(own, unpacked(other, n_len, length, N))
         near = [jnp.where(ok_m, near[0], 0.0), jnp.where(ok_e, near[1], 0.0)]
         second = [jnp.where(ok_m, second[0], 0.0), jnp.where(ok_e, second[1], 0.0)]
         out[0] = halo_m = jnp.where(ok_m, halo[0], 0.0)
@@ -768,8 +784,8 @@
     return lax.ppermute(x, ("len", "wall"), pairs)
 
 
-def call(kernel, ins, outs, scratch, name, work=0):
-    places = {"vmem": pltpu.VMEM, "smem": pltpu.SMEM, "any": pl.ANY}
+def call(kernel, ins, outs, scratch, name, work=0, room=48):
+    places = {"vmem": pltpu.VMEM, "smem": pltpu.SMEM, "any": pl.ANY, "hbm": pltpu.HBM}
 
     def specs(kinds):
         return [pl.BlockSpec(memory_space=places[kind]) for kind in kinds]
@@ -781,7 +797,7 @@
         in_specs=specs(ins),
         out_specs=specs(kind for _, kind in outs),
         scratch_shapes=[pltpu.VMEM(shape, F32) if isinstance(shape, tuple) else shape for shape in scratch],
-        compiler_params=pltpu.CompilerParams(vmem_limit_bytes=48 * 2**20),
+        compiler_params=pltpu.CompilerParams(vmem_limit_bytes=int(room * 2**20)),
         cost_estimate=cost,
         name=name,
     )
@@ -801,13 +817,14 @@
 
     *fields, wall_out = (faces := call(
         functools.partial(pack_faces, n_len),
-        ["any"] * 4,
+        ["hbm"] * 4,
         [(own, vmem)] * 4
         + [((sum(FACES), C, L), vmem)]
         + [((4, C, L), vmem)] * n_dir
         + [((C, L), vmem)] * n_dir,
         [pltpu.VMEM(own, jnp.int32), pltpu.SemaphoreType.DMA((4, 2))],
         "faces",
+        room=52.75,
     )(*raw))[:5]
     strip_out, corner_out = faces[5 : 5 + n_dir], faces[5 + n_dir :]
     wall_in = ring(wall_out, "wall", 1)
@@ -818,7 +835,7 @@
         strips = [ring(strip_out[1], "len", -1), ring(strip_out[0], "len", 1)]
         corners = [ring(ring(corner_out[1], "wall", 1), "len", -1), ring(ring(corner_out[0], "wall", 1), "len", 1)]
 
-    near = (5 * N + 16, L)
+    near = (sum(near_rows(n_dir, W)[-1][::2]), L)
     *fields, to_next, to_prev, own_rows = call(
         functools.partial(boundary, n_len, C),
         [vmem] * (5 + 2 * n_dir),
@@ -849,17 +866,7 @@
     )(own_rows, from_next, from_prev, coarse, surface, patch_ids)
 
     relative = n_blk <= 4
-    if relative:
-        sector_blocks = jnp.stack([mine] + [ring(mine, "blk", d) for d in range(1, n_blk)])
-    else:
-        sector_blocks = lax.all_gather(mine, "blk")
-    if n_len == 2:
-        here = [sector_blocks, ring(sector_blocks, "len", 1)]
-    else:
-        gathered = lax.all_gather(sector_blocks, "len")
-        here = [gathered[j] for j in range(n_len)]
-    blocks = here + [ring(x, "wall", 1) for x in here]
-
+    moved = [ring(mine, "blk", d) for d in range(1, n_blk)] if relative else [lax.all_gather(mine, "blk")]
     base_adj, base_pot, patches = call(
         functools.partial(source_part, n_blk, n_len, n_wall, C, electrodes),
         [vmem] * 7,
@@ -868,6 +875,14 @@
         "source_part",
         work=12 * 10**6,
     )(bm, be, rows_n, rows_p, qm, fields[2], owner_map.reshape(1, electrodes))
+    moved, base_adj = lax.optimization_barrier((moved, base_adj))
+    sector_blocks = jnp.stack([mine] + moved) if relative else moved[0]
+    if n_len == 2:
+        here = [sector_blocks, ring(sector_blocks, "len", 1)]
+    else:
+        gathered = lax.all_gather(sector_blocks, "len")
+        here = [gathered[j] for j in range(n_len)]
+    blocks = here + [ring(x, "wall", 1) for x in here]
 
     NC1, NL1 = n_blk * C // 2, n_len * L // 2
     planes = n_wall * W // 2

time: 49.6 us -> 42.6 us (0.86)
  local copies, waits for them, and re-layouts: 4.45 us -> 0.66 us
  waiting for transfers between devices: 14.4 us -> 11.4 us
    unnamed x12 -> x4, local copies, waits for them, and re-layouts: 4.45 us -> 0.66 us
    ppermute x10, waiting for transfers between devices: 11.4 us -> 8.42 us  [ring(): return lax.ppermute(x, axis, [(i, (i + by) % count) for i in range(count)])]
  transfers between devices with their start and end apart: 11 -> 11, of which waited for: 6 -> 6; matrix products, arithmetic and copies ran while one was open for 0% -> 0% of each run, Pallas kernels for 17% -> 20%
where the time goes in v3:
time: 42.6 us; the launch traced here: 42.4 us
  Pallas kernels  18.7 us (44%)
  waiting for transfers between devices  11.4 us (27%)
  starting transfers between devices  11 us (26%)
  between operations  0.69 us (2%)
  local copies, waits for them, and re-layouts  0.66 us (2%)
    ppermute x10, starting transfers between devices, ring(): return lax.ppermute(x, axis, [(i, (i + by) % count) for i in range(count)])  10.9 us
    ppermute x10, waiting for transfers between devices, ring(): return lax.ppermute(x, axis, [(i, (i + by) % count) for i in range(count)])  8.42 us
    pallas_call x1, Pallas kernels, body(): call(functools.partial(solve, (n_blk, n_len, n_wall), relative, C, W), [v...  6.52 us
    pallas_call x1, Pallas kernels, body(): call(functools.partial(sector, n_len, n_wall, C), [vmem] * 8, [(field, vm...  5.13 us
    pallas_call x1, Pallas kernels, body(): call(functools.partial(source_part, n_blk, n_len, n_wall, C, electrodes),...  3.44 us
    ppermute x1, waiting for transfers between devices, across(): return lax.ppermute(x, ('len', 'wall'), pairs)  3.01 us
    pallas_call x1, Pallas kernels, body(): call(functools.partial(pack_faces, n_len), ['hbm'] * 4, [(own, vmem)] * 4...  1.65 us
    pallas_call x1, Pallas kernels, body(): call(functools.partial(correct, electrodes, n_len, n_wall), [vmem] * 6, [...  1.01 us
  transfers between devices with their start and end apart: 11, of which 6 were waited for; matrix products, arithmetic and copies ran while one was open for 0% of the time, Pallas kernels for 20%

profile of v3, /device:TPU:0, one launch (start us, length us, event | category | flops | bytes accessed | tf_op | source)
XLA Modules:
  0.0 42.4 jit_solution(8453055930134684211)
XLA Ops:
  0.6 1.6 %faces.1 = (f32[512,128]{1,0:T(8,128)S(1)}, f32[512,128]{1,0:T(8,128)S(1)}, f32[512,128]{1,0:T(8,128)S(1)}, f32[512,128]{1,0:T(8,128)S(1)}, f32[12,16,128]{2,1,0...) custom-call(f32[512,128]{1,0:T(8,128)} %bitcast.13, f32[512,128]{1,0:T(8,128)} %bitcast.14, ...), custom_call_target="tpu_custom_call" | custom-call | tf_op jit(solution)/shard_map/faces/pallas_call | solution.py:818
  2.3 0.5 %collective-permute-start = (f32[12,16,128]{2,1,0:T(8,128)S(1)}, f32[12,16,128]{2,1,0:T(8,128)S(1)}, u32[]{:S(2)}, u32[]{:S(2)}) collective-permute-start(f32[12,16,128]{2,1,0:T(8,128)S(1)} %get-tuple-element.43), channel_id=1, source_target_pairs={{0,1},{1,0},{2,3},{3,2},{4,5},{5,4},{6,7},{7,6},{8,9},{9,8},{10,11... | collective-permute-start | bytes 294920 | tf_op jit(solution)/shard_map/ppermute | solution.py:778
  2.8 2.6 %collective-permute-start.1 = (f32[4,16,128]{2,1,0:T(8,128)S(1)}, f32[4,16,128]{2,1,0:T(8,128)S(1)}, u32[]{:S(2)}, u32[]{:S(2)}) collective-permute-start(f32[4,16,128]{2,1,0:T(8,128)S(1)} %get-tuple-element.44), channel_id=1, source_target_pairs={{0,2},{2,0},{1,3},{3,1},{4,6},{6,4},{5,7},{7,5},{8,10},{10,8},{9,1... | collective-permute-start | bytes 98312 | tf_op jit(solution)/shard_map/ppermute | solution.py:778
  5.4 0.1 collective-permute-start.2
  5.4 3.0 %collective-permute-done.2.rest_1_ = f32[16,128]{1,0:T(8,128)S(1)} collective-permute-done((f32[16,128]{1,0:T(8,128)S(1)}, f32[16,128]{1,0:T(8,128)S(1)}, u32[]{:S(2)}, u32[]{:S(2)}) %collective-permute-start.2) | collective-permute-done | bytes 8224 | tf_op jit(solution)/shard_map/ppermute | solution.py:784
  8.4 0.0 collective-permute-done.1.rest_0_
  8.4 0.0 collective-permute-done.wall_in
  8.5 0.9 %boundary.1 = (f32[640,128]{1,0:T(8,128)S(1)}, f32[640,128]{1,0:T(8,128)S(1)}, f32[640,128]{1,0:T(8,128)S(1)}, f32[640,128]{1,0:T(8,128)S(1)}, f32[640,128]{1,0:...) custom-call(f32[512,128]{1,0:T(8,128)S(1)} %get-tuple-element.39.xm0, ...), custom_call_target="tpu_custom_call" | custom-call | tf_op jit(solution)/shard_map/boundary/pallas_call | solution.py:839
  9.4 3.7 %collective-permute-start.3 = (f32[184,128]{1,0:T(8,128)S(1)}, f32[184,128]{1,0:T(8,128)S(1)}, u32[]{:S(2)}, u32[]{:S(2)}) collective-permute-start(f32[184,128]{1,0:T(8,128)S(1)} %get-tuple-element.47), channel_id=1, source_target_pairs={{0,12},{4,0},{8,4},{12,8},{1,13},{5,1},{9,5},{13,9},{2,14},{6,2},{... | collective-permute-start | bytes 282632 | tf_op jit(solution)/shard_map/ppermute | solution.py:778
  13.0 0.0 collective-permute-start.4
  13.0 0.0 copy-start
  13.0 5.1 %sector.1 = (f32[640,128]{1,0:T(8,128)S(1)}, f32[640,128]{1,0:T(8,128)S(1)}, f32[640,128]{1,0:T(8,128)S(1)}, f32[64,128]{1,0:T(8,128)S(1)}, f32[16,128]{1,0:T(8,128)S(1)}) custom-call(f32[640,128]{1,0:T(8,128)S(1)} %get-tuple-element.49.xm0, f32[640,128]{1,0:T(8,128)S(1)} %get-tuple-element.50.xm1, f32[640,128]{1,0:T(8,128)S(1)} %get-tuple-element.51.xm2.mask.refs_6_, ...), custom_call_target="tpu_custom_call" | custom-call | flops 16000000 | bytes 16000000 | tf_op jit(solution)/shard_map/sector/pallas_call | solution.py:848
  18.2 0.0 collective-permute-done.3.from_next
  18.2 1.2 %collective-permute-done.4.from_prev = f32[184,128]{1,0:T(8,128)S(1)} collective-permute-done((f32[184,128]{1,0:T(8,128)S(1)}, f32[184,128]{1,0:T(8,128)S(1)}, u32[]{:S(2)}, u32[]{:S(2)}) %collective-permute-start.4) | collective-permute-done | bytes 94240 | tf_op jit(solution)/shard_map/ppermute | solution.py:778
  19.4 0.0 copy-done
  19.4 1.0 %correct.1 = (f32[8,40,128]{2,1,0:T(8,128)S(1)}, f32[8,40,128]{2,1,0:T(8,128)S(1)}, f32[88,128]{1,0:T(8,128)S(1)}) custom-call(f32[2,6,40,128]{3,2,1,0:T(8,128)S(1)} %get-tuple-element.46.own_rows, f32[184,128]{1,0:T(8,128)S(1)} %collective-permute-done.3.from_next, f32[184,128]{1,0:T(8,128)S(1)} %collective-permute-done.4.from_prev, ...), custom_call_target="tpu_custom_call" | custom-call | tf_op jit(solution)/shard_map/correct/pallas_call | solution.py:860
  20.4 2.7 %collective-permute-start.7 = (f32[88,128]{1,0:T(8,128)S(1)}, f32[88,128]{1,0:T(8,128)S(1)}, u32[]{:S(2)}, u32[]{:S(2)}) collective-permute-start(f32[88,128]{1,0:T(8,128)S(1)} %get-tuple-element.59), channel_id=1, source_target_pairs={{0,12},{4,0},{8,4},{12,8},{1,13},{5,1},{9,5},{13,9},{2,14},{6,2},{... | collective-permute-start | bytes 135176 | tf_op jit(solution)/shard_map/ppermute | solution.py:778
  23.1 0.0 collective-permute-start.6
  23.1 0.6 %collective-permute-start.5 = (f32[88,128]{1,0:T(8,128)S(1)}, f32[88,128]{1,0:T(8,128)S(1)}, u32[]{:S(2)}, u32[]{:S(2)}) collective-permute-start(f32[88,128]{1,0:T(8,128)S(1)} %get-tuple-element.59), channel_id=1, source_target_pairs={{0,4},{4,8},{8,12},{12,0},{1,5},{5,9},{9,13},{13,1},{2,6},{6,10},{... | collective-permute-start | bytes 135176 | tf_op jit(solution)/shard_map/ppermute | solution.py:778
  23.6 0.0 copy-start.1
  23.6 0.7 %copy-done.1 = s32[32]{0:T(128)S(1)} copy-done((s32[32]{0:T(128)S(1)}, s32[32]{0:T(128)}, u32[]{:S(2)}) %copy-start.1) | copy-done | bytes 152
  24.3 3.4 %source_part.1 = (f32[512,128]{1,0:T(8,128)S(1)}, f32[512,128]{1,0:T(8,128)S(1)}, f32[8,128]{1,0:T(8,128)S(1)}) custom-call(f32[640,128]{1,0:T(8,128)S(1)} %get-tuple-element.60.bm, f32[640,128]{1,0:T(8,128)S(1)} %get-tuple-element.61.be, f32[8,40,128]{2,1,0:T(8,128)S(1)} %get-tuple-element.62.rows_n, f32[8,40,128]{2,1,0:T(8,128)S(1)} %get-tuple-element.63.rows_p, ...), custom_call_target="tpu_custom_call" | custom-call | flops 12000000 | bytes 12000000 | tf_op jit(solution)/shard_map/source_part/pallas_call | solution.py:870
  27.7 0.0 collective-permute-done.7
  27.7 0.3 collective-permute-done.6
  28.0 0.9 %collective-permute-done.5 = f32[88,128]{1,0:T(8,128)S(1)} collective-permute-done((f32[88,128]{1,0:T(8,128)S(1)}, f32[88,128]{1,0:T(8,128)S(1)}, u32[]{:S(2)}, u32[]{:S(2)}) %collective-permute-start.5) | collective-permute-done | bytes 45088 | tf_op jit(solution)/shard_map/ppermute | solution.py:778
  28.9 0.9 %collective-permute-start.8 = (f32[4,88,128]{2,1,0:T(8,128)S(1)}, f32[4,88,128]{2,1,0:T(8,128)S(1)}, u32[]{:S(2)}, u32[]{:S(2)}) collective-permute-start(f32[4,88,128]{2,1,0:T(8,128)S(1)} %pad_maximum_fusion.refs_0_), channel_id=1, source_target_pairs={{0,2},{2,0},{1,3},{3,1},{4,6},{6,4},{5,7},{7,5},{8,10},{10,8},{9,1... | collective-permute-start | bytes 540680 | tf_op jit(solution)/shard_map/ppermute | solution.py:778
  29.9 0.0 collective-permute-start.9
  29.9 4.6 %collective-permute-done.8.refs_1_ = f32[4,88,128]{2,1,0:T(8,128)S(1)} collective-permute-done((f32[4,88,128]{2,1,0:T(8,128)S(1)}, f32[4,88,128]{2,1,0:T(8,128)S(1)}, u32[]{:S(2)}, u32[]{:S(2)}) %collective-permute-start.8) | collective-permute-done | bytes 180256 | tf_op jit(solution)/shard_map/ppermute | solution.py:778
  34.5 0.0 collective-permute-start.10
  34.5 0.0 collective-permute-done.9.refs_2_
  34.5 1.4 %collective-permute-done.10.refs_3_ = f32[4,88,128]{2,1,0:T(8,128)S(1)} collective-permute-done((f32[4,88,128]{2,1,0:T(8,128)S(1)}, f32[4,88,128]{2,1,0:T(8,128)S(1)}, u32[]{:S(2)}, u32[]{:S(2)}) %collective-permute-start.10) | collective-permute-done | bytes 180256 | tf_op jit(solution)/shard_map/ppermute | solution.py:778
  35.9 6.5 %solve.1 = (f32[512,128]{1,0:T(8,128)}, f32[512,128]{1,0:T(8,128)}, f32[1,2]{1,0:T(1,128)}) custom-call(f32[4,88,128]{2,1,0:T(8,128)S(1)} %pad_maximum_fusion.refs_0_, f32[4,88,128]{2,1,0:T(8,128)S(1)} %collective-permute-done.8.refs_1_, f32[4,88,128]{2,1,0:T(8,128)S(1)} %collective-permute-done.9.refs_2_, ...), custom_call_target="tpu_custom_call" | custom-call | tf_op jit(solution)/shard_map/solve/pallas_call | solution.py:895
  (1 shorter events, 0.0 us)
Async XLA Ops:
  2.3 6.2 %collective-permute-start = (f32[12,16,128]{2,1,0:T(8,128)S(1)}, f32[12,16,128]{2,1,0:T(8,128)S(1)}, u32[]{:S(2)}, u32[]{:S(2)}) collective-permute-start(f32[12,16,128]{2,1,0:T(8,128)S(1)} %get-tuple-element.43), channel_id=1, source_target_pairs={{0,1},{1,0},{2,3},{3,2},{4,5},{5,4},{6,7},{7,6},{8,9},{9,8},{10,11... | collective-permute-start | bytes 294920 | tf_op jit(solution)/shard_map/ppermute | solution.py:778
  2.8 5.6 %collective-permute-start.1 = (f32[4,16,128]{2,1,0:T(8,128)S(1)}, f32[4,16,128]{2,1,0:T(8,128)S(1)}, u32[]{:S(2)}, u32[]{:S(2)}) collective-permute-start(f32[4,16,128]{2,1,0:T(8,128)S(1)} %get-tuple-element.44), channel_id=1, source_target_pairs={{0,2},{2,0},{1,3},{3,1},{4,6},{6,4},{5,7},{7,5},{8,10},{10,8},{9,1... | collective-permute-start | bytes 98312 | tf_op jit(solution)/shard_map/ppermute | solution.py:778
  5.4 3.1 %collective-permute-start.2 = (f32[16,128]{1,0:T(8,128)S(1)}, f32[16,128]{1,0:T(8,128)S(1)}, u32[]{:S(2)}, u32[]{:S(2)}) collective-permute-start(f32[16,128]{1,0:T(8,128)S(1)} %get-tuple-element.45), channel_id=1, source_target_pairs={{0,3},{1,2},{2,1},{3,0},{4,7},{5,6},{6,5},{7,4},{8,11},{9,10},{10,... | collective-permute-start | bytes 24584 | tf_op jit(solution)/shard_map/ppermute | solution.py:784
  9.4 8.8 %collective-permute-start.3 = (f32[184,128]{1,0:T(8,128)S(1)}, f32[184,128]{1,0:T(8,128)S(1)}, u32[]{:S(2)}, u32[]{:S(2)}) collective-permute-start(f32[184,128]{1,0:T(8,128)S(1)} %get-tuple-element.47), channel_id=1, source_target_pairs={{0,12},{4,0},{8,4},{12,8},{1,13},{5,1},{9,5},{13,9},{2,14},{6,2},{... | collective-permute-start | bytes 282632 | tf_op jit(solution)/shard_map/ppermute | solution.py:778
  13.0 6.4 %collective-permute-start.4 = (f32[184,128]{1,0:T(8,128)S(1)}, f32[184,128]{1,0:T(8,128)S(1)}, u32[]{:S(2)}, u32[]{:S(2)}) collective-permute-start(f32[184,128]{1,0:T(8,128)S(1)} %get-tuple-element.48), channel_id=1, source_target_pairs={{0,4},{4,8},{8,12},{12,0},{1,5},{5,9},{9,13},{13,1},{2,6},{6,10},{... | collective-permute-start | bytes 282632 | tf_op jit(solution)/shard_map/ppermute | solution.py:778
  13.0 6.4 %copy-start = (s32[1,16,128]{2,1,0:T(8,128)S(1)}, s32[1,16,128]{2,1,0:T(8,128)}, u32[]{:S(2)}) copy-start(s32[1,16,128]{2,1,0:T(8,128)} %ids.1) | copy-start | bytes 24580
  20.4 7.3 %collective-permute-start.7 = (f32[88,128]{1,0:T(8,128)S(1)}, f32[88,128]{1,0:T(8,128)S(1)}, u32[]{:S(2)}, u32[]{:S(2)}) collective-permute-start(f32[88,128]{1,0:T(8,128)S(1)} %get-tuple-element.59), channel_id=1, source_target_pairs={{0,12},{4,0},{8,4},{12,8},{1,13},{5,1},{9,5},{13,9},{2,14},{6,2},{... | collective-permute-start | bytes 135176 | tf_op jit(solution)/shard_map/ppermute | solution.py:778
  23.1 4.9 %collective-permute-start.6 = (f32[88,128]{1,0:T(8,128)S(1)}, f32[88,128]{1,0:T(8,128)S(1)}, u32[]{:S(2)}, u32[]{:S(2)}) collective-permute-start(f32[88,128]{1,0:T(8,128)S(1)} %get-tuple-element.59), channel_id=1, source_target_pairs={{0,8},{4,12},{8,0},{12,4},{1,9},{5,13},{9,1},{13,5},{2,10},{6,14},... | collective-permute-start | bytes 135176 | tf_op jit(solution)/shard_map/ppermute | solution.py:778
  23.1 5.8 %collective-permute-start.5 = (f32[88,128]{1,0:T(8,128)S(1)}, f32[88,128]{1,0:T(8,128)S(1)}, u32[]{:S(2)}, u32[]{:S(2)}) collective-permute-start(f32[88,128]{1,0:T(8,128)S(1)} %get-tuple-element.59), channel_id=1, source_target_pairs={{0,4},{4,8},{8,12},{12,0},{1,5},{5,9},{9,13},{13,1},{2,6},{6,10},{... | collective-permute-start | bytes 135176 | tf_op jit(solution)/shard_map/ppermute | solution.py:778
  23.6 0.7 %copy-start.1 = (s32[32]{0:T(128)S(1)}, s32[32]{0:T(128)}, u32[]{:S(2)}) copy-start(s32[32]{0:T(128)} %param.11) | copy-start | bytes 388
  28.9 5.6 %collective-permute-start.8 = (f32[4,88,128]{2,1,0:T(8,128)S(1)}, f32[4,88,128]{2,1,0:T(8,128)S(1)}, u32[]{:S(2)}, u32[]{:S(2)}) collective-permute-start(f32[4,88,128]{2,1,0:T(8,128)S(1)} %pad_maximum_fusion.refs_0_), channel_id=1, source_target_pairs={{0,2},{2,0},{1,3},{3,1},{4,6},{6,4},{5,7},{7,5},{8,10},{10,8},{9,1... | collective-permute-start | bytes 540680 | tf_op jit(solution)/shard_map/ppermute | solution.py:778
  29.9 4.6 %collective-permute-start.9 = (f32[4,88,128]{2,1,0:T(8,128)S(1)}, f32[4,88,128]{2,1,0:T(8,128)S(1)}, u32[]{:S(2)}, u32[]{:S(2)}) collective-permute-start(f32[4,88,128]{2,1,0:T(8,128)S(1)} %pad_maximum_fusion.refs_0_), channel_id=1, source_target_pairs={{0,1},{1,0},{2,3},{3,2},{4,5},{5,4},{6,7},{7,6},{8,9},{9,8},{10,11... | collective-permute-start | bytes 540680 | tf_op jit(solution)/shard_map/ppermute | solution.py:778
  34.5 1.4 %collective-permute-start.10 = (f32[4,88,128]{2,1,0:T(8,128)S(1)}, f32[4,88,128]{2,1,0:T(8,128)S(1)}, u32[]{:S(2)}, u32[]{:S(2)}) collective-permute-start(f32[4,88,128]{2,1,0:T(8,128)S(1)} %collective-permute-done.8.refs_1_), channel_id=1, source_target_pairs={{0,1},{1,0},{2,3},{3,2},{4,5},{5,4},{6,7},{7,6},{8,9},{9,8},{10,11... | collective-permute-start | bytes 540680 | tf_op jit(solution)/shard_map/ppermute | solution.py:778

commit v4 on v3

--- a/solution.py
+++ b/solution.py
@@ -266,12 +266,19 @@
     return jnp.logical_and(w >= 0, w < n_wall * W)
 
 
-def halving():
-    src = lax.broadcasted_iota(jnp.int32, (LANES, LANES), 0) // 2
-    dst = lax.broadcasted_iota(jnp.int32, (LANES, LANES), 1)
-    low = jnp.where(src == dst, 0.125, 0.0).astype(F32)
-    high = jnp.where(src == dst - LANES // 2, 0.125, 0.0).astype(F32)
-    return low, high
+def lanes_at(x, index):
+    return jnp.take_along_axis(x, index, axis=1, mode="promise_in_bounds")
+
+
+def rows_at(x, index):
+    return jnp.take_along_axis(x, index, axis=0, mode="promise_in_bounds")
+
+
+def halved(low, high):
+    lane = lane_of(low.shape)
+    even = 2 * lane % LANES
+    pairs = [lanes_at(x, even) + lanes_at(x, even + 1) for x in (low, high)]
+    return 0.125 * jnp.where(lane < LANES // 2, pairs[0], pairs[1])
 
 
 def precise(a, b):
@@ -334,8 +341,7 @@
 
     half = W * C // 8
     z = pairs[pl.ds(0, 2 * half, stride=2), :] + pairs[pl.ds(1, 2 * half, stride=2), :]
-    low, high = halving()
-    coarse[...] = precise(z[:half], low) + precise(z[half:], high)
+    coarse[...] = halved(z[:half], z[half:])
 
 
 def unpacked(ref, n_len, length, N):
@@ -424,8 +430,7 @@
             both = lines[0, pl.ds(H, W1, stride=2), :] + lines[0, pl.ds(H + 1, W1, stride=2), :]
             lows.append(both[: W1 // 2])
             highs.append(both[W1 // 2 :])
-    low, high = halving()
-    add = precise(jnp.concatenate(lows, 0), low) + precise(jnp.concatenate(highs, 0), high)
+    add = halved(jnp.concatenate(lows, 0), jnp.concatenate(highs, 0))
     half = W * C // 8
     message[0:half, :] = coarse[...]
     for k, c1 in enumerate((C1 - 1, C1 - 2, 0, 1)):
@@ -529,12 +534,14 @@
     return x + jnp.where((lane & by) == 0, pltpu.roll(x, lanes - by, 1), pltpu.roll(x, by, 1))
 
 
-def solve(sizes, relative, C, W, *refs):
+def solve(sizes, relative, quad, C, W, *refs):
     n_blk, n_len, n_wall = sizes
-    count = n_len * n_wall
+    count = 1 if quad else n_len * n_wall
     blocks, refs = refs[:count], refs[count:]
+    if quad:
+        blocks = [blocks[0].at[j * n_wall + v] for v in range(n_wall) for j in range(n_len)]
     base_adj, base_pot, mask, patches, adj_prev, potential, patch_grad = refs[:7]
-    b1, x1, b2, x2, b3, x3, near, wide, pm, pe, tm, te, adj_out, pot_out, sheet, sems = refs[7:]
+    b1, x1, b2, x2, b3, x3, near, pm, pe, tm, te, adj_out, pot_out, sheet, sems = refs[7:]
     L = LANES
     W1, C1 = W // 2, C // 2
     planes, NC1, NL1 = b1.shape
@@ -549,7 +556,10 @@
         return lax.rem(blk - d + n_blk, n_blk) if relative else d
 
     def length_of(j):
-        return (length + j) % n_len if n_len == 2 else j
+        return (length + j) % n_len if n_len == 2 and not quad else j
+
+    def wall_of(v):
+        return v if quad else (wall + v) % n_wall
 
     zero1 = jnp.zeros((NC1, NL1), F32)
     for ref in (b1, x1, b2, x2, b3, x3):
@@ -557,7 +567,7 @@
         ref[ref.shape[0] - 1] = zero1
 
     for v in range(n_wall):
-        wall_s = (wall + v) % n_wall
+        wall_s = wall_of(v)
         mine = blocks[v * n_len : (v + 1) * n_len]
 
         def unpack(d):
@@ -566,7 +576,7 @@
                 one, two = mine[2 * t], mine[2 * t + 1]
                 for i in range(half):
                     a, b = one[d, i * C1 : (i + 1) * C1, :], two[d, i * C1 : (i + 1) * C1, :]
-                    if n_len == 2:
+                    if n_len == 2 and not quad:
                         a, b = jnp.where(length == 0, a, b), jnp.where(length == 0, b, a)
                     spot = 1 + wall_s * W1 + i
                     lanes = slice(t * LANES, (t + 1) * LANES)
@@ -640,7 +650,6 @@
     sectors = (blk, lax.rem(blk + 1, n_blk), lax.rem(blk + n_blk - 1, n_blk))
     spots3 = [pl.ds(pl.multiple_of(s * C1, C1), C1) for s in sectors]
     row8 = lax.broadcasted_iota(jnp.int32, (C1, NL1), 0)
-    NR = 2 * C1
 
     def three(ref, i):
         return jnp.concatenate([ref[i, s, :] for s in spots3], 0)
@@ -656,26 +665,40 @@
 
     loop(0, Q, finish1, min(often, 6))
 
-    lane = lane_of((NL1, LANES))
-    source = lax.broadcasted_iota(jnp.int32, (NL1, LANES), 0)
     first = length * middle
-    take_m = jnp.where(source == first + lane // 2, 1.0, 0.0).astype(F32)
-    at_e = jnp.where(lane < H, middle + lane // 2, jnp.where(lane >= LANES - H, lane // 2 - middle, 4 * NL1))
-    take_e = jnp.where(source == first + at_e, 1.0, 0.0).astype(F32)
     R = C + 8
     row8 = lax.broadcasted_iota(jnp.int32, (8, LANES), 0)
-    for out, sel in ((pm, take_m), (pe, take_e)):
-        value = precise(near[...], sel)
-        wide[pl.ds(0, Q * NR, stride=2), :] = value
-        wide[pl.ds(1, Q * NR, stride=2), :] = value
-        for q in range(Q):
-            base = 2 * NR * q
-            out[R * q : R * q + C, :] = wide[base : base + C, :]
-            out[R * q + C : R * (q + 1), :] = jnp.where(
-                row8 < H, wide[base + C : base + C + 8, :], wide[base + 2 * NR - 8 : base + 2 * NR, :]
-            )
+    tile_lane = lane_of((8, LANES))
+    at_e = jnp.where(tile_lane < H, middle + tile_lane // 2, tile_lane // 2 - middle)
+    rim8 = rim_lanes(tile_lane, length, n_len)
+    if NL1 == LANES:
+        index_m, index_e = first + tile_lane // 2, jnp.clip(first + at_e, 0, LANES - 1)
+
+        def spread(tile):
+            return lanes_at(tile, index_m), jnp.where(rim8, lanes_at(tile, index_e), 0.0)
+
+    else:
+        source = lax.broadcasted_iota(jnp.int32, (NL1, LANES), 0)
+        lane = lane_of((NL1, LANES))
+        at_all = jnp.where(lane < H, middle + lane // 2, jnp.where(lane >= LANES - H, lane // 2 - middle, 4 * NL1))
+        take_m = jnp.where(source == first + lane // 2, 1.0, 0.0).astype(F32)
+        take_e = jnp.where(source == first + at_all, 1.0, 0.0).astype(F32)
+
+        def spread(tile):
+            return precise(tile, take_m), precise(tile, take_e)
+
+    picks = (row8 // 2, H + row8 // 2, jnp.where(row8 < H, row8 // 2, H + row8 // 2))
+
+    def fine_rows(q):
+        own = spread(plane(near, 2 * q, C1))
+        beside = spread(plane(near, 2 * q + 1, C1))
+        for out, a, b in ((pm, own[0], beside[0]), (pe, own[1], beside[1])):
+            parts = (rows_at(a, picks[0]), rows_at(a, picks[1]), rows_at(b, picks[2]))
+            set_plane(out, q, R, jnp.concatenate(parts, 0))
+
+    loop(0, Q, fine_rows, min(often, 6))
     coef, k0 = level_coef(0), level_step(0)
-    rim = rim_lanes(lane_of((R, LANES)), length, n_len)
+    rim = rim_lanes(lane_of((C, LANES)), length, n_len)
 
     def rows_beside(x):
         return pltpu.roll(x, 1, 0) + pltpu.roll(x, x.shape[0] - 1, 0)
@@ -685,30 +708,26 @@
         lm, le = beside_lanes(m, e)
         gm = (1.0 - OMEGA) * m + k0 * (coef[0] * m + coef[1] * rows_beside(m) + coef[2] * lm)
         ge = (1.0 - OMEGA) * e + k0 * (coef[0] * e + coef[1] * rows_beside(e) + coef[2] * le)
-        return gm, ge
+        return gm, ge[:C]
 
     ks = k0 * coef[0]
 
-    def put(t, gm, ge, other, ok):
-        m = gm + ks * plane(pm, other, R)
-        e = jnp.where(rim, ge + ks * plane(pe, other, R), 0.0)
-        if ok is not None:
-            m, e = jnp.where(ok, m, 0.0), jnp.where(ok, e, 0.0)
-        set_plane(tm, t, R, m)
-        set_plane(te, t, R, e)
-
-    put(0, *coarse_terms(0), 1, wall > 0)
-    put(W + 1, *coarse_terms(Q - 1), Q - 2, wall < n_wall - 1)
+    def put_end(t, q, other, ok):
+        set_plane(tm, t, R, jnp.where(ok, coarse_terms(q)[0] + ks * plane(pm, other, R), 0.0))
+
+    put_end(0, 0, 1, wall > 0)
+    put_end(W + 1, Q - 1, Q - 2, wall < n_wall - 1)
 
     def level0(q):
         gm, ge = coarse_terms(q)
-        put(2 * q - 1, gm, ge, q - 1, None)
-        put(2 * q, gm, ge, q + 1, None)
-        for w in (2 * q - 2, 2 * q - 1):
-            set_plane(pot_out, w, C, plane(base_pot, w, C) + plane(tm, w + 1, R)[:C])
+        for t, other in ((2 * q - 1, q - 1), (2 * q, q + 1)):
+            m = gm + ks * plane(pm, other, R)
+            set_plane(tm, t, R, m)
+            set_plane(te, t - 1, C, jnp.where(rim, ge + ks * plane(pe, other, R)[:C], 0.0))
+            set_plane(pot_out, t - 1, C, plane(base_pot, t - 1, C) + m[:C])
 
     def finish0(w):
-        m, e = plane(tm, w + 1, R), plane(te, w + 1, R)[:C]
+        m, e = plane(tm, w + 1, R), plane(te, w, C)
         cm = rows_beside(m)[:C]
         m = m[:C]
         wm = plane(tm, w, R)[:C] + plane(tm, w + 2, R)[:C]
@@ -733,14 +752,23 @@
         send(adj_out, adj_prev, k, sems.at[1, k])
 
     NC, NL = sheet.shape[1:]
-    twice_c = jnp.where(
-        lax.broadcasted_iota(jnp.int32, (NC, NC1), 0) // 2 == lax.broadcasted_iota(jnp.int32, (NC, NC1), 1), 1.0, 0.0
-    ).astype(F32)
-    twice_l = jnp.where(
-        lax.broadcasted_iota(jnp.int32, (NL1, NL), 1) // 2 == lax.broadcasted_iota(jnp.int32, (NL1, NL), 0), 1.0, 0.0
-    ).astype(F32)
+
+    def whole_fine(x):
+        if NL1 == LANES:
+            parts = []
+            for t in range(0, NC1, 8):
+                wide8 = [lanes_at(x[t : t + 8], tile_lane // 2 + k * middle) for k in range(2)]
+                for pick in picks[:2]:
+                    parts.append(jnp.concatenate([rows_at(v, pick) for v in wide8], 1))
+            return jnp.concatenate(parts, 0)
+        along_c = lax.broadcasted_iota(jnp.int32, (NC, NC1), 0) // 2
+        along_l = lax.broadcasted_iota(jnp.int32, (NL1, NL), 1) // 2
+        twice_c = jnp.where(along_c == lax.broadcasted_iota(jnp.int32, (NC, NC1), 1), 1.0, 0.0).astype(F32)
+        twice_l = jnp.where(along_l == lax.broadcasted_iota(jnp.int32, (NL1, NL), 0), 1.0, 0.0).astype(F32)
+        return precise(precise(twice_c, x), twice_l)
+
     for s, i in enumerate((1, planes)):
-        p = precise(precise(twice_c, sweep(x1, b1, i, 1)), twice_l)
+        p = whole_fine(sweep(x1, b1, i, 1))
         c, l = around(p, 1)
         sheet[s] = (1.0 - OMEGA) * p + k0 * (coef[0] * p + coef[1] * c + coef[2] * l)
 
@@ -751,7 +779,7 @@
     totals = [jnp.zeros((C, LANES), F32) for _ in owned]
     small = [jnp.zeros((8, LANES), F32) for _ in owned]
     for v in range(n_wall):
-        wall_s = (wall + v) % n_wall
+        wall_s = wall_of(v)
         for j in range(n_len):
             ref = blocks[v * n_len + j]
             at_l = pl.ds(pl.multiple_of(length_of(j) * L, L), L)
@@ -877,12 +905,8 @@
     )(bm, be, rows_n, rows_p, qm, fields[2], owner_map.reshape(1, electrodes))
     moved, base_adj = lax.optimization_barrier((moved, base_adj))
     sector_blocks = jnp.stack([mine] + moved) if relative else moved[0]
-    if n_len == 2:
-        here = [sector_blocks, ring(sector_blocks, "len", 1)]
-    else:
-        gathered = lax.all_gather(sector_blocks, "len")
-        here = [gathered[j] for j in range(n_len)]
-    blocks = here + [ring(x, "wall", 1) for x in here]
+    quad = True
+    blocks = [lax.all_gather(sector_blocks, ("len", "wall"))]
 
     NC1, NL1 = n_blk * C // 2, n_len * L // 2
     planes = n_wall * W // 2
@@ -890,14 +914,15 @@
     Q = W // 2 + 2
     tall = (Q * (C + 8), L)
     taller = ((W + 2) * (C + 8), L)
-    scratch = grids + [(Q * C, NL1), (2 * Q * C, L), tall, tall, taller, taller, own, own]
+    scratch = grids + [(Q * C, NL1), tall, tall, taller, own, own, own]
     scratch += [(2, n_blk * C, n_len * L), pltpu.SemaphoreType.DMA((2, 2))]
     adj_prev, potential, patch_grad = call(
-        functools.partial(solve, (n_blk, n_len, n_wall), relative, C, W),
-        [vmem] * (n_len * n_wall + 4),
+        functools.partial(solve, (n_blk, n_len, n_wall), relative, quad, C, W),
+        [vmem] * (len(blocks) + 4),
         [(own, "any"), (own, "any"), ((1, 2), "smem")],
         scratch,
         "solve",
+        room=48 if NC1 * NL1 <= 4096 else 58,
     )(*blocks, base_adj, base_pot, fields[2], patches)
     return adj_prev.reshape(W, C, L), potential.reshape(W, C, L), patch_grad
 

time: 42.6 us -> 42.3 us (level)
  blocking collectives: 0 us -> 7.63 us
  waiting for transfers between devices: 11.4 us -> 5.52 us
  starting transfers between devices: 11 us -> 9.91 us
  Pallas kernels: 18.7 us -> 17.7 us
    all_gather x0 -> x1, blocking collectives: none -> 7.63 us  [body(): blocks = [lax.all_gather(sector_blocks, ('len', 'wall'))]]
    ppermute x10 -> x7, waiting for transfers between devices: 8.42 us -> 2.52 us  [ring(): return lax.ppermute(x, axis, [(i, (i + by) % count) for i in range(count)])]
    ppermute x10 -> x7, starting transfers between devices: 10.9 us -> 9.84 us  [ring(): return lax.ppermute(x, axis, [(i, (i + by) % count) for i in range(count)])]
    pallas_call x1, Pallas kernels: 6.52 us -> 5.95 us  [body(): call(functools.partial(solve, (n_blk, n_len, n_wall), relative, quad, C,...]
  transfers between devices with their start and end apart: 11 -> 8, of which waited for: 6 -> 4; matrix products, arithmetic and copies ran while one was open for 0% -> 0% of each run, Pallas kernels for 20% -> 20%
where the time goes in v4:
time: 42.3 us; the launch traced here: 42.1 us
  Pallas kernels  17.7 us (42%)
  starting transfers between devices  9.91 us (23%)
  blocking collectives  7.63 us (18%)
  waiting for transfers between devices  5.52 us (13%)
  between operations  0.69 us (2%)
  local copies, waits for them, and re-layouts  0.66 us (2%)
    ppermute x7, starting transfers between devices, ring(): return lax.ppermute(x, axis, [(i, (i + by) % count) for i in range(count)])  9.84 us
    all_gather x1, blocking collectives, body(): blocks = [lax.all_gather(sector_blocks, ('len', 'wall'))]  7.63 us
    pallas_call x1, Pallas kernels, body(): call(functools.partial(solve, (n_blk, n_len, n_wall), relative, quad, C,...  5.95 us
    pallas_call x1, Pallas kernels, body(): call(functools.partial(sector, n_len, n_wall, C), [vmem] * 8, [(field, vm...  5.01 us
    pallas_call x1, Pallas kernels, body(): call(functools.partial(source_part, n_blk, n_len, n_wall, C, electrodes),...  3.44 us
    ppermute x1, waiting for transfers between devices, across(): return lax.ppermute(x, ('len', 'wall'), pairs)  3.01 us
    ppermute x7, waiting for transfers between devices, ring(): return lax.ppermute(x, axis, [(i, (i + by) % count) for i in range(count)])  2.52 us
    pallas_call x1, Pallas kernels, body(): call(functools.partial(pack_faces, n_len), ['hbm'] * 4, [(own, vmem)] * 4...  1.65 us
  transfers between devices with their start and end apart: 8, of which 4 were waited for; matrix products, arithmetic and copies ran while one was open for 0% of the time, Pallas kernels for 20%

profile of v4, /device:TPU:0, one launch (start us, length us, event | category | flops | bytes accessed | tf_op | source)
XLA Modules:
  0.0 42.1 jit_solution(16365002057579629206)
XLA Ops:
  0.6 1.6 %faces.1 = (f32[512,128]{1,0:T(8,128)S(1)}, f32[512,128]{1,0:T(8,128)S(1)}, f32[512,128]{1,0:T(8,128)S(1)}, f32[512,128]{1,0:T(8,128)S(1)}, f32[12,16,128]{2,1,0...) custom-call(f32[512,128]{1,0:T(8,128)} %bitcast.15, f32[512,128]{1,0:T(8,128)} %bitcast.16, ...), custom_call_target="tpu_custom_call" | custom-call | tf_op jit(solution)/shard_map/faces/pallas_call | solution.py:846
  2.3 0.5 %collective-permute-start = (f32[12,16,128]{2,1,0:T(8,128)S(1)}, f32[12,16,128]{2,1,0:T(8,128)S(1)}, u32[]{:S(2)}, u32[]{:S(2)}) collective-permute-start(f32[12,16,128]{2,1,0:T(8,128)S(1)} %get-tuple-element.43), channel_id=1, source_target_pairs={{0,1},{1,0},{2,3},{3,2},{4,5},{5,4},{6,7},{7,6},{8,9},{9,8},{10,11... | collective-permute-start | bytes 294920 | tf_op jit(solution)/shard_map/ppermute | solution.py:806
  2.8 2.6 %collective-permute-start.1 = (f32[4,16,128]{2,1,0:T(8,128)S(1)}, f32[4,16,128]{2,1,0:T(8,128)S(1)}, u32[]{:S(2)}, u32[]{:S(2)}) collective-permute-start(f32[4,16,128]{2,1,0:T(8,128)S(1)} %get-tuple-element.44), channel_id=1, source_target_pairs={{0,2},{2,0},{1,3},{3,1},{4,6},{6,4},{5,7},{7,5},{8,10},{10,8},{9,1... | collective-permute-start | bytes 98312 | tf_op jit(solution)/shard_map/ppermute | solution.py:806
  5.4 0.1 collective-permute-start.2
  5.4 3.0 %collective-permute-done.2.rest_1_ = f32[16,128]{1,0:T(8,128)S(1)} collective-permute-done((f32[16,128]{1,0:T(8,128)S(1)}, f32[16,128]{1,0:T(8,128)S(1)}, u32[]{:S(2)}, u32[]{:S(2)}) %collective-permute-start.2) | collective-permute-done | bytes 8224 | tf_op jit(solution)/shard_map/ppermute | solution.py:812
  8.4 0.0 collective-permute-done.1.rest_0_
  8.4 0.0 collective-permute-done.wall_in
  8.5 0.9 %boundary.1 = (f32[640,128]{1,0:T(8,128)S(1)}, f32[640,128]{1,0:T(8,128)S(1)}, f32[640,128]{1,0:T(8,128)S(1)}, f32[640,128]{1,0:T(8,128)S(1)}, f32[640,128]{1,0:...) custom-call(f32[512,128]{1,0:T(8,128)S(1)} %get-tuple-element.39.xm0, ...), custom_call_target="tpu_custom_call" | custom-call | tf_op jit(solution)/shard_map/boundary/pallas_call | solution.py:867
  9.4 3.7 %collective-permute-start.3 = (f32[184,128]{1,0:T(8,128)S(1)}, f32[184,128]{1,0:T(8,128)S(1)}, u32[]{:S(2)}, u32[]{:S(2)}) collective-permute-start(f32[184,128]{1,0:T(8,128)S(1)} %get-tuple-element.47), channel_id=1, source_target_pairs={{0,12},{4,0},{8,4},{12,8},{1,13},{5,1},{9,5},{13,9},{2,14},{6,2},{... | collective-permute-start | bytes 282632 | tf_op jit(solution)/shard_map/ppermute | solution.py:806
  13.0 0.0 collective-permute-start.4
  13.0 0.0 copy-start
  13.0 5.0 %sector.1 = (f32[640,128]{1,0:T(8,128)S(1)}, f32[640,128]{1,0:T(8,128)S(1)}, f32[640,128]{1,0:T(8,128)S(1)}, f32[64,128]{1,0:T(8,128)S(1)}, f32[16,128]{1,0:T(8,128)S(1)}) custom-call(f32[640,128]{1,0:T(8,128)S(1)} %get-tuple-element.49.xm0, f32[640,128]{1,0:T(8,128)S(1)} %get-tuple-element.50.xm1, f32[640,128]{1,0:T(8,128)S(1)} %get-tuple-element.51.xm2.mask.refs_3_, ...), custom_call_target="tpu_custom_call" | custom-call | flops 16000000 | bytes 16000000 | tf_op jit(solution)/shard_map/sector/pallas_call | solution.py:876
  18.0 0.0 collective-permute-done.3.from_next
  18.1 1.3 %collective-permute-done.4.from_prev = f32[184,128]{1,0:T(8,128)S(1)} collective-permute-done((f32[184,128]{1,0:T(8,128)S(1)}, f32[184,128]{1,0:T(8,128)S(1)}, u32[]{:S(2)}, u32[]{:S(2)}) %collective-permute-start.4) | collective-permute-done | bytes 94240 | tf_op jit(solution)/shard_map/ppermute | solution.py:806
  19.4 0.0 copy-done
  19.4 0.7 %correct.1 = (f32[8,40,128]{2,1,0:T(8,128)S(1)}, f32[8,40,128]{2,1,0:T(8,128)S(1)}, f32[88,128]{1,0:T(8,128)S(1)}) custom-call(f32[2,6,40,128]{3,2,1,0:T(8,128)S(1)} %get-tuple-element.46.own_rows, f32[184,128]{1,0:T(8,128)S(1)} %collective-permute-done.3.from_next, f32[184,128]{1,0:T(8,128)S(1)} %collective-permute-done.4.from_prev, ...), custom_call_target="tpu_custom_call" | custom-call | tf_op jit(solution)/shard_map/correct/pallas_call | solution.py:888
  20.1 2.5 %collective-permute-start.7 = (f32[88,128]{1,0:T(8,128)S(1)}, f32[88,128]{1,0:T(8,128)S(1)}, u32[]{:S(2)}, u32[]{:S(2)}) collective-permute-start(f32[88,128]{1,0:T(8,128)S(1)} %get-tuple-element.59), channel_id=1, source_target_pairs={{0,12},{4,0},{8,4},{12,8},{1,13},{5,1},{9,5},{13,9},{2,14},{6,2},{... | collective-permute-start | bytes 135176 | tf_op jit(solution)/shard_map/ppermute | solution.py:806
  22.7 0.0 collective-permute-start.6
  22.7 0.6 %collective-permute-start.5 = (f32[88,128]{1,0:T(8,128)S(1)}, f32[88,128]{1,0:T(8,128)S(1)}, u32[]{:S(2)}, u32[]{:S(2)}) collective-permute-start(f32[88,128]{1,0:T(8,128)S(1)} %get-tuple-element.59), channel_id=1, source_target_pairs={{0,4},{4,8},{8,12},{12,0},{1,5},{5,9},{9,13},{13,1},{2,6},{6,10},{... | collective-permute-start | bytes 135176 | tf_op jit(solution)/shard_map/ppermute | solution.py:806
  23.2 0.0 copy-start.1
  23.2 0.7 %copy-done.1 = s32[32]{0:T(128)S(1)} copy-done((s32[32]{0:T(128)S(1)}, s32[32]{0:T(128)}, u32[]{:S(2)}) %copy-start.1) | copy-done | bytes 152
  23.9 3.4 %source_part.1 = (f32[512,128]{1,0:T(8,128)S(1)}, f32[512,128]{1,0:T(8,128)S(1)}, f32[8,128]{1,0:T(8,128)S(1)}) custom-call(f32[640,128]{1,0:T(8,128)S(1)} %get-tuple-element.60.bm, f32[640,128]{1,0:T(8,128)S(1)} %get-tuple-element.61.be, f32[8,40,128]{2,1,0:T(8,128)S(1)} %get-tuple-element.62.rows_n, f32[8,40,128]{2,1,0:T(8,128)S(1)} %get-tuple-element.63.rows_p, ...), custom_call_target="tpu_custom_call" | custom-call | flops 12000000 | bytes 12000000 | tf_op jit(solution)/shard_map/source_part/pallas_call | solution.py:898
  27.3 0.0 collective-permute-done.7
  27.3 0.3 collective-permute-done.6
  27.6 0.9 %collective-permute-done.5 = f32[88,128]{1,0:T(8,128)S(1)} collective-permute-done((f32[88,128]{1,0:T(8,128)S(1)}, f32[88,128]{1,0:T(8,128)S(1)}, u32[]{:S(2)}, u32[]{:S(2)}) %collective-permute-start.5) | collective-permute-done | bytes 45088 | tf_op jit(solution)/shard_map/ppermute | solution.py:806
  28.5 7.6 %all-gather = f32[16,88,128]{2,1,0:T(8,128)S(1)} all-gather(f32[4,88,128]{2,1,0:T(8,128)S(1)} %pad_maximum_fusion), channel_id=2, replica_groups=mesh['groups'=2,'blk'=4,'len'=2,'wall'=2] {'len','wall'}, dimensions={0}, use_global_device_ids=true | all-gather | bytes 901120 | tf_op jit(solution)/shard_map/all_gather | solution.py:909
  36.2 5.9 %solve.1 = (f32[512,128]{1,0:T(8,128)}, f32[512,128]{1,0:T(8,128)}, f32[1,2]{1,0:T(1,128)}) custom-call(f32[4,4,88,128]{3,2,1,0:T(8,128)S(1)} %bitcast.12, f32[512,128]{1,0:T(8,128)S(1)} %get-tuple-element.69.refs_1_, f32[512,128]{1,0:T(8,128)S(1)} %get-tuple-element.70.refs_2_, f32[640,128]{1,0:T(8,128)S(1)} %get-tuple-element.51.xm2.mask.refs_3_, ...), custom_call_target="tpu_custom_call" | custom-call | tf_op jit(solution)/shard_map/solve/pallas_call | solution.py:919
  (1 shorter events, 0.0 us)
Async XLA Ops:
  2.3 6.2 %collective-permute-start = (f32[12,16,128]{2,1,0:T(8,128)S(1)}, f32[12,16,128]{2,1,0:T(8,128)S(1)}, u32[]{:S(2)}, u32[]{:S(2)}) collective-permute-start(f32[12,16,128]{2,1,0:T(8,128)S(1)} %get-tuple-element.43), channel_id=1, source_target_pairs={{0,1},{1,0},{2,3},{3,2},{4,5},{5,4},{6,7},{7,6},{8,9},{9,8},{10,11... | collective-permute-start | bytes 294920 | tf_op jit(solution)/shard_map/ppermute | solution.py:806
  2.8 5.6 %collective-permute-start.1 = (f32[4,16,128]{2,1,0:T(8,128)S(1)}, f32[4,16,128]{2,1,0:T(8,128)S(1)}, u32[]{:S(2)}, u32[]{:S(2)}) collective-permute-start(f32[4,16,128]{2,1,0:T(8,128)S(1)} %get-tuple-element.44), channel_id=1, source_target_pairs={{0,2},{2,0},{1,3},{3,1},{4,6},{6,4},{5,7},{7,5},{8,10},{10,8},{9,1... | collective-permute-start | bytes 98312 | tf_op jit(solution)/shard_map/ppermute | solution.py:806
  5.4 3.1 %collective-permute-start.2 = (f32[16,128]{1,0:T(8,128)S(1)}, f32[16,128]{1,0:T(8,128)S(1)}, u32[]{:S(2)}, u32[]{:S(2)}) collective-permute-start(f32[16,128]{1,0:T(8,128)S(1)} %get-tuple-element.45), channel_id=1, source_target_pairs={{0,3},{1,2},{2,1},{3,0},{4,7},{5,6},{6,5},{7,4},{8,11},{9,10},{10,... | collective-permute-start | bytes 24584 | tf_op jit(solution)/shard_map/ppermute | solution.py:812
  9.4 8.7 %collective-permute-start.3 = (f32[184,128]{1,0:T(8,128)S(1)}, f32[184,128]{1,0:T(8,128)S(1)}, u32[]{:S(2)}, u32[]{:S(2)}) collective-permute-start(f32[184,128]{1,0:T(8,128)S(1)} %get-tuple-element.47), channel_id=1, source_target_pairs={{0,12},{4,0},{8,4},{12,8},{1,13},{5,1},{9,5},{13,9},{2,14},{6,2},{... | collective-permute-start | bytes 282632 | tf_op jit(solution)/shard_map/ppermute | solution.py:806
  13.0 6.4 %collective-permute-start.4 = (f32[184,128]{1,0:T(8,128)S(1)}, f32[184,128]{1,0:T(8,128)S(1)}, u32[]{:S(2)}, u32[]{:S(2)}) collective-permute-start(f32[184,128]{1,0:T(8,128)S(1)} %get-tuple-element.48), channel_id=1, source_target_pairs={{0,4},{4,8},{8,12},{12,0},{1,5},{5,9},{9,13},{13,1},{2,6},{6,10},{... | collective-permute-start | bytes 282632 | tf_op jit(solution)/shard_map/ppermute | solution.py:806
  13.0 6.4 %copy-start = (s32[1,16,128]{2,1,0:T(8,128)S(1)}, s32[1,16,128]{2,1,0:T(8,128)}, u32[]{:S(2)}) copy-start(s32[1,16,128]{2,1,0:T(8,128)} %ids.1) | copy-start | bytes 24580
  20.1 7.2 %collective-permute-start.7 = (f32[88,128]{1,0:T(8,128)S(1)}, f32[88,128]{1,0:T(8,128)S(1)}, u32[]{:S(2)}, u32[]{:S(2)}) collective-permute-start(f32[88,128]{1,0:T(8,128)S(1)} %get-tuple-element.59), channel_id=1, source_target_pairs={{0,12},{4,0},{8,4},{12,8},{1,13},{5,1},{9,5},{13,9},{2,14},{6,2},{... | collective-permute-start | bytes 135176 | tf_op jit(solution)/shard_map/ppermute | solution.py:806
  22.7 4.9 %collective-permute-start.6 = (f32[88,128]{1,0:T(8,128)S(1)}, f32[88,128]{1,0:T(8,128)S(1)}, u32[]{:S(2)}, u32[]{:S(2)}) collective-permute-start(f32[88,128]{1,0:T(8,128)S(1)} %get-tuple-element.59), channel_id=1, source_target_pairs={{0,8},{4,12},{8,0},{12,4},{1,9},{5,13},{9,1},{13,5},{2,10},{6,14},... | collective-permute-start | bytes 135176 | tf_op jit(solution)/shard_map/ppermute | solution.py:806
  22.7 5.8 %collective-permute-start.5 = (f32[88,128]{1,0:T(8,128)S(1)}, f32[88,128]{1,0:T(8,128)S(1)}, u32[]{:S(2)}, u32[]{:S(2)}) collective-permute-start(f32[88,128]{1,0:T(8,128)S(1)} %get-tuple-element.59), channel_id=1, source_target_pairs={{0,4},{4,8},{8,12},{12,0},{1,5},{5,9},{9,13},{13,1},{2,6},{6,10},{... | collective-permute-start | bytes 135176 | tf_op jit(solution)/shard_map/ppermute | solution.py:806
  23.2 0.7 %copy-start.1 = (s32[32]{0:T(128)S(1)}, s32[32]{0:T(128)}, u32[]{:S(2)}) copy-start(s32[32]{0:T(128)} %param.11) | copy-start | bytes 388

commit v5 on v4

--- a/solution.py
+++ b/solution.py
@@ -7,7 +7,6 @@
 from jax.experimental.pallas import tpu as pltpu
 from jax.sharding import PartitionSpec as P
 
-SWEEPS = 2
 SI = (0.6, 1.0, 3.0)
 SE = (0.8, 1.2, 2.0)
 SHIFT = 0.002
@@ -55,8 +54,9 @@
 
 def beside_lanes_main(m, e):
     lane = lane_of(m.shape)
-    left = jnp.where(lane == 0, pltpu.roll(e, 1, 1), pltpu.roll(m, 1, 1))
-    right = jnp.where(lane == LANES - 1, pltpu.roll(e, LANES - 1, 1), pltpu.roll(m, LANES - 1, 1))
+    ends = lanes_at(e, LANES - 1 - lane)
+    left = jnp.where(lane == 0, ends, pltpu.roll(m, 1, 1))
+    right = jnp.where(lane == LANES - 1, ends, pltpu.roll(m, LANES - 1, 1))
     return left + right
 
 
@@ -175,65 +175,71 @@
     return [value[s : s + 8] for value in values for s in range(0, value.shape[0], 8)]
 
 
-def boundary(n_len, C, xm0, xm1, xm2, xm3, wall_in, *rest):
+def rim_places(n_len, length):
+    if n_len == 2:
+        return [(jnp.where(length == 0, 0, LANES - H), True)]
+    return [(0, length < n_len - 1), (LANES - H, length > 0)]
+
+
+def boundary(n_len, C, *refs):
     n_dir = 1 if n_len == 2 else 2
-    strips, corners, rest = rest[:n_dir], rest[n_dir : 2 * n_dir], rest[2 * n_dir :]
-    xm, xe, to_next, to_prev, own_rows = rest[:4], rest[4:8], rest[8], rest[9], rest[10]
-    N = xm[0].shape[0] // C
-    W = N - 2 * H
+    raw, wall_in, refs = refs[:4], refs[4], refs[5:]
+    strips, corners, refs = refs[:n_dir], refs[n_dir : 2 * n_dir], refs[2 * n_dir :]
+    to_next, to_prev, own_rows, build = refs
+    W = raw[0].shape[0] // C
+    N = W + 2 * H
     wall, length = lax.axis_index("wall"), lax.axis_index("len")
-    lane = lane_of((C, LANES))
-    if n_dir == 1:
-        offs, valid = [jnp.where(length == 0, 0, LANES - H)], [True]
-    else:
-        offs, valid = [0, LANES - H], [length < n_len - 1, length > 0]
-    seen = [jnp.logical_and(lax.rem(lane - off + LANES, LANES) < H, ok) for off, ok in zip(offs, valid)]
-
-    def rim(packed, base):
-        out = jnp.zeros((C, LANES), F32)
-        for d in range(n_dir):
-            out = jnp.where(seen[d], pltpu.roll(packed[d], lax.rem(offs[d] - base + LANES, LANES), 1), out)
+    places = rim_places(n_len, length)
+
+    def strip_rows(packed, first, count):
+        lane, k = lane_of((count, LANES)), lax.broadcasted_iota(jnp.int32, (count, LANES), 0)
+        out = jnp.zeros((count, LANES), F32)
+        for row, (off, ok) in zip(packed, places):
+            j = lax.rem(lane - off + LANES, LANES)
+            index = jnp.clip(H * (first + k) + j, 0, LANES - 1)
+            taken = lanes_at(jnp.broadcast_to(row, (count, LANES)), index)
+            out = jnp.where(jnp.logical_and(j < H, ok), taken, out)
         return out
 
-    zero = jnp.zeros((C, LANES), F32)
-    last = N - H
-    for a, own in enumerate((xm0, xm1, xm2, xm3)):
-        packed = [strip[a] for strip in strips]
-        for w in range(W):
-            set_plane(xm[a], w + H, C, plane(own, w, C))
-            set_plane(xe[a], w + H, C, rim(packed, H * w))
-        packed = [corner[...] for corner in corners]
-        for i in range(H):
-            set_plane(xm[a], i, C, zero)
-            set_plane(xe[a], i, C, zero)
-            set_plane(xm[a], last + i, C, zero)
-            set_plane(xe[a], last + i, C, zero)
+    slots = iter(range(build.shape[0]))
+
+    def assembled(own, halo, count):
+        ref = build.at[next(slots)]
+        ref[0:8, :] = jnp.zeros((8, LANES), F32)
+        ref[N - 8 : N, :] = jnp.zeros((8, LANES), F32)
+        ref[H : H + W, :] = own
+        ref[H - count : H, :] = jnp.where(wall == 0, 0.0, halo)
+        ref[H + W : H + W + count, :] = jnp.where(wall == 0, halo, 0.0)
+        return ref[...]
+
+    def row_of(a, r):
         count, first = face_planes(a)
-        here = jnp.where(wall == 0, last, H - count)
-        for p in range(count):
-            set_plane(xm[a], here + p, C, wall_in[first + p])
-            set_plane(xe[a], here + p, C, rim(packed, H * (first + p)))
-
+        halo = jnp.concatenate([wall_in[first + p, r : r + 1, :] for p in range(count)], 0)
+        m = assembled(raw[a][pl.ds(r, W, stride=C), :], halo, count)
+        own = strip_rows([strip[a, r : r + 1, :] for strip in strips], 0, W)
+        halo = strip_rows([corner[r : r + 1, :] for corner in corners], first, 8)[:count]
+        return m, assembled(own, halo, count)
+
+    length_shift = jnp.where(length == 0, 0, H) if n_dir == 1 else H
+    group = lane_of((8, LANES)) // (H * n_dir)
     for side, (out, order) in enumerate(((to_next, (C - 1, C - 2, C - 3, C - 4)), (to_prev, (0, 1, 2, 3)))):
-        adj = [dense_pair(xm[0], xe[0], r, N, C) for r in order]
-        mask = [dense_pair(xm[2], xe[2], r, N, C) for r in order[:3]]
+        adj = [row_of(0, r) for r in order]
+        mask = [row_of(2, r) for r in order[:3]]
         q = []
         for k in range(3):
-            ion = dense_pair(xm[1], xe[1], order[k], N, C)
+            ion = row_of(1, order[k])
             moved = dense_apply(adj[k], adj[k + 1], adj[k - 1] if k else None, SI)
             q.append([adj[k][j] - DT * mask[k][j] * (moved[j] + ion[j] * adj[k][j]) for j in range(2)])
         near = dense_apply(q[0], q[1], None, SI)
-        mis = dense_pair(xm[3], xe[3], order[0], N, C)
+        mis = row_of(3, order[0])
         near = [near[j] + mis[j] for j in range(2)]
-        second = dense_apply(q[1], q[2], q[0], SI)[0] + dense(xm[3], order[1], N, C)
+        second = dense_apply(q[1], q[2], q[0], SI)[0] + row_of(3, order[1])[0]
         for value, (start, first, count) in zip((second, near[0], q[0][0], mask[0][0], adj[0][0]), near_rows(n_dir, W)):
             out[start : start + count, :] = value[first : first + count]
-        group = lane_of((8, LANES)) // (H * n_dir)
-        shift = jnp.where(length == 0, 0, H) if n_dir == 1 else H
         packs = [jnp.zeros((8, LANES), F32) for _ in range(n_dir)]
         for t, tile in enumerate(rim_tiles((near[1], q[0][1], mask[0][1], adj[0][1]))):
             k, at = divmod(t, LANES // (H * n_dir))
-            turned = pltpu.roll(tile, lax.rem(shift + H * n_dir * at, LANES), 1)
+            turned = pltpu.roll(tile, lax.rem(length_shift + H * n_dir * at, LANES), 1)
             packs[k] = jnp.where(group == at, turned, packs[k])
         for k in range(n_dir):
             out[8 * k : 8 * k + 8, :] = packs[k]
@@ -285,8 +291,46 @@
     return jnp.dot(a, b, precision=HIGHEST, preferred_element_type=F32)
 
 
-def sector(n_len, n_wall, C, xm0, xm1, xm2, xm3, xe0, xe1, xe2, xe3, qm, bm, be, coarse, surface, qe, pairs):
-    xm, xe = (xm0, xm1, xm2, xm3), (xe0, xe1, xe2, xe3)
+def assemble(n_len, C, raw, wall_in, strips, corners, xm, xe):
+    W = raw[0].shape[0] // C
+    N = W + 2 * H
+    wall, length = lax.axis_index("wall"), lax.axis_index("len")
+    lane = lane_of((C, LANES))
+    places = rim_places(n_len, length)
+    seen = [jnp.logical_and(lax.rem(lane - off + LANES, LANES) < H, ok) for off, ok in places]
+
+    def rim(packed, base):
+        out = jnp.zeros((C, LANES), F32)
+        for row, ok, (off, _) in zip(packed, seen, places):
+            out = jnp.where(ok, pltpu.roll(row, lax.rem(off - base + LANES, LANES), 1), out)
+        return out
+
+    zero = jnp.zeros((C, LANES), F32)
+    last = N - H
+    for a, own in enumerate(raw):
+        packed = [strip[a] for strip in strips]
+        for w in range(W):
+            set_plane(xm[a], w + H, C, plane(own, w, C))
+            set_plane(xe[a], w + H, C, rim(packed, H * w))
+        packed = [corner[...] for corner in corners]
+        for i in range(H):
+            for at in (i, last + i):
+                set_plane(xm[a], at, C, zero)
+                set_plane(xe[a], at, C, zero)
+        count, first = face_planes(a)
+        here = jnp.where(wall == 0, last, H - count)
+        for p in range(count):
+            set_plane(xm[a], here + p, C, wall_in[first + p])
+            set_plane(xe[a], here + p, C, rim(packed, H * (first + p)))
+
+
+def sector(n_len, n_wall, C, *refs):
+    n_dir = 1 if n_len == 2 else 2
+    raw, wall_in, refs = refs[:4], refs[4], refs[5:]
+    strips, corners, refs = refs[:n_dir], refs[n_dir : 2 * n_dir], refs[2 * n_dir :]
+    qm, bm, be, coarse, surface, qe, pairs = refs[:7]
+    xm, xe = refs[7:11], refs[11:15]
+    assemble(n_len, C, raw, wall_in, strips, corners, xm, xe)
     N = qm.shape[0] // C
     W = N - 2 * H
     wall, length = lax.axis_index("wall"), lax.axis_index("len")
@@ -503,7 +547,7 @@
         lam = plane(qm, i, C)
         lam = lam + jnp.where(row == C - 1, rows_n[3, at, :], 0.0) + jnp.where(row == 0, rows_p[3, at, :], 0.0)
         moved = 2.0 * sum(SI) * m - SI[0] * wm - SI[1] * cm - SI[2] * lm
-        set_plane(base_adj, w, C, lam - DT * plane(mask, i, C) * moved)
+        set_plane(base_adj, w, C, lam - DT * plane(mask, w, C) * moved)
         set_plane(base_pot, w, C, m)
 
     loop(0, W, finish, 2)
@@ -528,18 +572,20 @@
 
 def twins(x, by):
     rows, lanes = x.shape
+    if lanes == LANES:
+        index = lax.broadcasted_iota(jnp.int32, (8, LANES), 0) ^ by
+        x = x + jnp.concatenate([rows_at(x[t : t + 8], index) for t in range(0, rows, 8)], 0)
+        return x + lanes_at(x, lane_of(x.shape) ^ by)
     row = lax.broadcasted_iota(jnp.int32, x.shape, 0)
     lane = lane_of(x.shape)
     x = x + jnp.where((row & by) == 0, pltpu.roll(x, rows - by, 0), pltpu.roll(x, by, 0))
     return x + jnp.where((lane & by) == 0, pltpu.roll(x, lanes - by, 1), pltpu.roll(x, by, 1))
 
 
-def solve(sizes, relative, quad, C, W, *refs):
+def solve(sizes, relative, C, W, *refs):
     n_blk, n_len, n_wall = sizes
-    count = 1 if quad else n_len * n_wall
+    count = n_len * n_wall
     blocks, refs = refs[:count], refs[count:]
-    if quad:
-        blocks = [blocks[0].at[j * n_wall + v] for v in range(n_wall) for j in range(n_len)]
     base_adj, base_pot, mask, patches, adj_prev, potential, patch_grad = refs[:7]
     b1, x1, b2, x2, b3, x3, near, pm, pe, tm, te, adj_out, pot_out, sheet, sems = refs[7:]
     L = LANES
@@ -556,10 +602,10 @@
         return lax.rem(blk - d + n_blk, n_blk) if relative else d
 
     def length_of(j):
-        return (length + j) % n_len if n_len == 2 and not quad else j
+        return (length + j) % n_len if n_len == 2 else j
 
     def wall_of(v):
-        return v if quad else (wall + v) % n_wall
+        return (wall + v) % n_wall
 
     zero1 = jnp.zeros((NC1, NL1), F32)
     for ref in (b1, x1, b2, x2, b3, x3):
@@ -576,7 +622,7 @@
                 one, two = mine[2 * t], mine[2 * t + 1]
                 for i in range(half):
                     a, b = one[d, i * C1 : (i + 1) * C1, :], two[d, i * C1 : (i + 1) * C1, :]
-                    if n_len == 2 and not quad:
+                    if n_len == 2:
                         a, b = jnp.where(length == 0, a, b), jnp.where(length == 0, b, a)
                     spot = 1 + wall_s * W1 + i
                     lanes = slice(t * LANES, (t + 1) * LANES)
@@ -590,9 +636,9 @@
         c, l = around(x, by)
         return level_step(level) * (coef[0] * wsum + coef[1] * c + coef[2] * l)
 
-    def left(ref, i, level):
-        b = ref[i]
-        return (1.0 - OMEGA) * b + total_of(b, ref[i - 1] + ref[i + 1], level, 2 ** (level - 1))
+    def left_pair(ref, i, level):
+        both = ref[i] + ref[i + 1]
+        return (1.0 - OMEGA) * both + total_of(both, ref[i - 1] + both + ref[i + 2], level, 2 ** (level - 1))
 
     def sweep(x_ref, b_ref, i, level):
         x = x_ref[i]
@@ -600,34 +646,30 @@
         return (1.0 - OMEGA) * x + level_step(level) * b_ref[i] + total
 
     def down1(q):
-        b2[1 + q] = 0.125 * twins(left(b1, 2 * q + 1, 1) + left(b1, 2 * q + 2, 1), 1)
+        b2[1 + q] = 0.125 * twins(left_pair(b1, 2 * q + 1, 1), 1)
 
     loop(0, planes // 2, down1, often)
 
     def down2(q):
-        b3[1 + q] = 0.125 * twins(left(b2, 2 * q + 1, 2) + left(b2, 2 * q + 2, 2), 2)
+        b3[1 + q] = 0.125 * twins(left_pair(b2, 2 * q + 1, 2), 2)
 
     loop(0, planes // 4, down2, often)
 
     deep = planes // 4
     k3 = level_step(3)
 
+    x2[1 + deep] = zero1
+
     def start3(q):
-        x3[1 + q] = k3 * b3[1 + q]
+        b = b3[1 + q]
+        x2[1 + q] = k3 * ((2.0 - OMEGA) * b + total_of(b, b3[q] + b3[2 + q], 3, 4))
 
     loop(0, deep, start3, often)
-    for k in range(SWEEPS):
-        from_ref, to_ref = (x3, x2) if k % 2 == 0 else (x2, x3)
-
-        if k == 1:
-            x2[1 + deep] = zero1
-
-        def sweep3(q):
-            to_ref[1 + q] = sweep(from_ref, b3, 1 + q, 3)
-
-        loop(0, deep, sweep3, often)
-    deepest = x3 if SWEEPS % 2 == 0 else x2
-    assert deepest is x3
+
+    def sweep3(q):
+        x3[1 + q] = sweep(x2, b3, 1 + q, 3)
+
+    loop(0, deep, sweep3, often)
     k2 = level_step(2)
 
     def up2(q):
@@ -733,7 +775,7 @@
         wm = plane(tm, w, R)[:C] + plane(tm, w + 2, R)[:C]
         lm = beside_lanes_main(m, e)
         moved = 2.0 * sum(SI) * m - SI[0] * wm - SI[1] * cm - SI[2] * lm
-        set_plane(adj_out, w, C, plane(base_adj, w, C) - DT * plane(mask, w + H, C) * moved)
+        set_plane(adj_out, w, C, plane(base_adj, w, C) - DT * plane(mask, w, C) * moved)
 
     parts = 2
     size = W // parts
@@ -864,23 +906,24 @@
         corners = [ring(ring(corner_out[1], "wall", 1), "len", -1), ring(ring(corner_out[0], "wall", 1), "len", 1)]
 
     near = (sum(near_rows(n_dir, W)[-1][::2]), L)
-    *fields, to_next, to_prev, own_rows = call(
+    halos = [wall_in, *strips, *corners]
+    to_next, to_prev, own_rows = call(
         functools.partial(boundary, n_len, C),
         [vmem] * (5 + 2 * n_dir),
-        [(field, vmem)] * 8 + [(near, vmem)] * 2 + [((2, 6, N, L), vmem)],
-        [],
+        [(near, vmem)] * 2 + [((2, 6, N, L), vmem)],
+        [(48, N, L)],
         "boundary",
-    )(*fields, wall_in, *strips, *corners)
+    )(*fields, *halos)
     from_next = ring(to_prev, "blk", -1)
     from_prev = ring(to_next, "blk", 1)
     qm, bm, be, coarse, surface = call(
         functools.partial(sector, n_len, n_wall, C),
-        [vmem] * 8,
+        [vmem] * (5 + 2 * n_dir),
         [(field, vmem)] * 3 + [((cells // 8, L), vmem), ((C, L), vmem)],
-        [field, (cells // 2, L)],
+        [field, (cells // 2, L)] + [field] * 8,
         "sector",
         work=16 * 10**6,
-    )(*fields)
+    )(*fields, *halos)
 
     rows = (8, N, L)
     wide = LANES * ((electrodes + LANES - 1) // LANES)
@@ -905,8 +948,12 @@
     )(bm, be, rows_n, rows_p, qm, fields[2], owner_map.reshape(1, electrodes))
     moved, base_adj = lax.optimization_barrier((moved, base_adj))
     sector_blocks = jnp.stack([mine] + moved) if relative else moved[0]
-    quad = True
-    blocks = [lax.all_gather(sector_blocks, ("len", "wall"))]
+    if n_len == 2:
+        here = [sector_blocks, ring(sector_blocks, "len", 1)]
+    else:
+        gathered = lax.all_gather(sector_blocks, "len")
+        here = [gathered[j] for j in range(n_len)]
+    blocks = here + [ring(x, "wall", 1) for x in here]
 
     NC1, NL1 = n_blk * C // 2, n_len * L // 2
     planes = n_wall * W // 2
@@ -917,7 +964,7 @@
     scratch = grids + [(Q * C, NL1), tall, tall, taller, own, own, own]
     scratch += [(2, n_blk * C, n_len * L), pltpu.SemaphoreType.DMA((2, 2))]
     adj_prev, potential, patch_grad = call(
-        functools.partial(solve, (n_blk, n_len, n_wall), relative, quad, C, W),
+        functools.partial(solve, (n_blk, n_len, n_wall), relative, C, W),
         [vmem] * (len(blocks) + 4),
         [(own, "any"), (own, "any"), ((1, 2), "smem")],
         scratch,

time: 42.3 us -> 40.9 us (0.967)
  blocking collectives: 7.63 us -> 0 us
  waiting for transfers between devices: 5.52 us -> 11.3 us
  starting transfers between devices: 9.91 us -> 11.2 us
  Pallas kernels: 17.7 us -> 16.9 us
    all_gather x1 -> x0, blocking collectives: 7.63 us -> none  [body(): blocks = [lax.all_gather(sector_blocks, ('len', 'wall'))]]
    ppermute x7 -> x10, waiting for transfers between devices: 2.52 us -> 8.25 us  [ring(): return lax.ppermute(x, axis, [(i, (i + by) % count) for i in range(count)])]
    ppermute x7 -> x10, starting transfers between devices: 9.84 us -> 11.2 us  [ring(): return lax.ppermute(x, axis, [(i, (i + by) % count) for i in range(count)])]
    pallas_call x3, Pallas kernels: 11.9 us -> 11.2 us  [the longest x1 5.37 us: body(): call(functools.partial(sector, n_len, n_wall, C), [vmem] * (5 + 2 * n_dir...]
  transfers between devices with their start and end apart: 8 -> 11, of which waited for: 4 -> 6; matrix products, arithmetic and copies ran while one was open for 0% -> 0% of each run, Pallas kernels for 20% -> 21%
where the time goes in v5:
time: 40.9 us; the launch traced here: 40.8 us
  Pallas kernels  16.9 us (41%)
  waiting for transfers between devices  11.3 us (28%)
  starting transfers between devices  11.2 us (27%)
  between operations  0.69 us (2%)
  local copies, waits for them, and re-layouts  0.66 us (2%)
    ppermute x10, starting transfers between devices, ring(): return lax.ppermute(x, axis, [(i, (i + by) % count) for i in range(count)])  11.2 us
    ppermute x10, waiting for transfers between devices, ring(): return lax.ppermute(x, axis, [(i, (i + by) % count) for i in range(count)])  8.25 us
    pallas_call x1, Pallas kernels, body(): call(functools.partial(sector, n_len, n_wall, C), [vmem] * (5 + 2 * n_dir...  5.37 us
    pallas_call x1, Pallas kernels, body(): call(functools.partial(solve, (n_blk, n_len, n_wall), relative, C, W), [v...  5.02 us
    pallas_call x1, Pallas kernels, body(): call(functools.partial(source_part, n_blk, n_len, n_wall, C, electrodes),...  3.36 us
    ppermute x1, waiting for transfers between devices, across(): return lax.ppermute(x, ('len', 'wall'), pairs)  3.01 us
    pallas_call x1, Pallas kernels, body(): call(functools.partial(pack_faces, n_len), ['hbm'] * 4, [(own, vmem)] * 4...  1.65 us
  transfers between devices with their start and end apart: 11, of which 6 were waited for; matrix products, arithmetic and copies ran while one was open for 0% of the time, Pallas kernels for 21%

profile of v5, /device:TPU:0, one launch (start us, length us, event | category | flops | bytes accessed | tf_op | source)
XLA Modules:
  0.0 40.8 jit_solution(1077447796432471578)
XLA Ops:
  0.6 1.6 %faces.1 = (f32[512,128]{1,0:T(8,128)S(1)}, f32[512,128]{1,0:T(8,128)S(1)}, f32[512,128]{1,0:T(8,128)S(1)}, f32[512,128]{1,0:T(8,128)S(1)}, f32[12,16,128]{2,1,0...) custom-call(f32[512,128]{1,0:T(8,128)} %bitcast.13, f32[512,128]{1,0:T(8,128)} %bitcast.14, ...), custom_call_target="tpu_custom_call" | custom-call | tf_op jit(solution)/shard_map/faces/pallas_call | solution.py:888
  2.3 0.5 %collective-permute-start = (f32[12,16,128]{2,1,0:T(8,128)S(1)}, f32[12,16,128]{2,1,0:T(8,128)S(1)}, u32[]{:S(2)}, u32[]{:S(2)}) collective-permute-start(f32[12,16,128]{2,1,0:T(8,128)S(1)} %get-tuple-element.35), channel_id=1, source_target_pairs={{0,1},{1,0},{2,3},{3,2},{4,5},{5,4},{6,7},{7,6},{8,9},{9,8},{10,11... | collective-permute-start | bytes 294920 | tf_op jit(solution)/shard_map/ppermute | solution.py:848
  2.8 2.6 %collective-permute-start.1 = (f32[4,16,128]{2,1,0:T(8,128)S(1)}, f32[4,16,128]{2,1,0:T(8,128)S(1)}, u32[]{:S(2)}, u32[]{:S(2)}) collective-permute-start(f32[4,16,128]{2,1,0:T(8,128)S(1)} %get-tuple-element.36), channel_id=1, source_target_pairs={{0,2},{2,0},{1,3},{3,1},{4,6},{6,4},{5,7},{7,5},{8,10},{10,8},{9,1... | collective-permute-start | bytes 98312 | tf_op jit(solution)/shard_map/ppermute | solution.py:848
  5.4 0.1 collective-permute-start.2
  5.4 3.0 %collective-permute-done.2.refs_6_ = f32[16,128]{1,0:T(8,128)S(1)} collective-permute-done((f32[16,128]{1,0:T(8,128)S(1)}, f32[16,128]{1,0:T(8,128)S(1)}, u32[]{:S(2)}, u32[]{:S(2)}) %collective-permute-start.2) | collective-permute-done | bytes 8224 | tf_op jit(solution)/shard_map/ppermute | solution.py:854
  8.4 0.0 collective-permute-done.1.refs_5_
  8.4 0.0 collective-permute-done.refs_4_
  8.5 0.8 %boundary.1 = (f32[184,128]{1,0:T(8,128)S(1)}, f32[184,128]{1,0:T(8,128)S(1)}, f32[2,6,40,128]{3,2,1,0:T(8,128)S(1)}) custom-call(f32[512,128]{1,0:T(8,128)S(1)} %get-tuple-element.31.refs_0_, f32[512,128]{1,0:T(8,128)S(1)} %get-tuple-element.32.refs_1_, f32[512,128]{1,0:T(8,128)S(1)} %get-tuple-element.33.refs_2_.mask.refs_6_, ...), custom_call_target="tpu_custom_call" | custom-call | tf_op jit(solution)/shard_map/boundary/pallas_call | solution.py:910
  9.3 3.7 %collective-permute-start.3 = (f32[184,128]{1,0:T(8,128)S(1)}, f32[184,128]{1,0:T(8,128)S(1)}, u32[]{:S(2)}, u32[]{:S(2)}) collective-permute-start(f32[184,128]{1,0:T(8,128)S(1)} %get-tuple-element.39), channel_id=1, source_target_pairs={{0,12},{4,0},{8,4},{12,8},{1,13},{5,1},{9,5},{13,9},{2,14},{6,2},{... | collective-permute-start | bytes 282632 | tf_op jit(solution)/shard_map/ppermute | solution.py:848
  12.9 0.0 collective-permute-start.4
  12.9 0.0 copy-start
  12.9 5.4 %sector.1 = (f32[640,128]{1,0:T(8,128)S(1)}, f32[640,128]{1,0:T(8,128)S(1)}, f32[640,128]{1,0:T(8,128)S(1)}, f32[64,128]{1,0:T(8,128)S(1)}, f32[16,128]{1,0:T(8,128)S(1)}) custom-call(f32[512,128]{1,0:T(8,128)S(1)} %get-tuple-element.31.refs_0_, f32[512,128]{1,0:T(8,128)S(1)} %get-tuple-element.32.refs_1_, ...), custom_call_target="tpu_custom_call" | custom-call | flops 16000000 | bytes 16000000 | tf_op jit(solution)/shard_map/sector/pallas_call | solution.py:919
  18.3 0.0 collective-permute-done.3.from_next
  18.3 1.0 %collective-permute-done.4.from_prev = f32[184,128]{1,0:T(8,128)S(1)} collective-permute-done((f32[184,128]{1,0:T(8,128)S(1)}, f32[184,128]{1,0:T(8,128)S(1)}, u32[]{:S(2)}, u32[]{:S(2)}) %collective-permute-start.4) | collective-permute-done | bytes 94240 | tf_op jit(solution)/shard_map/ppermute | solution.py:848
  19.3 0.0 copy-done
  19.3 0.7 %correct.1 = (f32[8,40,128]{2,1,0:T(8,128)S(1)}, f32[8,40,128]{2,1,0:T(8,128)S(1)}, f32[88,128]{1,0:T(8,128)S(1)}) custom-call(f32[2,6,40,128]{3,2,1,0:T(8,128)S(1)} %get-tuple-element.38.own_rows, f32[184,128]{1,0:T(8,128)S(1)} %collective-permute-done.3.from_next, f32[184,128]{1,0:T(8,128)S(1)} %collective-permute-done.4.from_prev, ...), custom_call_target="tpu_custom_call" | custom-call | tf_op jit(solution)/shard_map/correct/pallas_call | solution.py:931
  20.0 2.9 %collective-permute-start.7 = (f32[88,128]{1,0:T(8,128)S(1)}, f32[88,128]{1,0:T(8,128)S(1)}, u32[]{:S(2)}, u32[]{:S(2)}) collective-permute-start(f32[88,128]{1,0:T(8,128)S(1)} %get-tuple-element.43), channel_id=1, source_target_pairs={{0,12},{4,0},{8,4},{12,8},{1,13},{5,1},{9,5},{13,9},{2,14},{6,2},{... | collective-permute-start | bytes 135176 | tf_op jit(solution)/shard_map/ppermute | solution.py:848
  22.9 0.0 collective-permute-start.6
  22.9 0.6 %collective-permute-start.5 = (f32[88,128]{1,0:T(8,128)S(1)}, f32[88,128]{1,0:T(8,128)S(1)}, u32[]{:S(2)}, u32[]{:S(2)}) collective-permute-start(f32[88,128]{1,0:T(8,128)S(1)} %get-tuple-element.43), channel_id=1, source_target_pairs={{0,4},{4,8},{8,12},{12,0},{1,5},{5,9},{9,13},{13,1},{2,6},{6,10},{... | collective-permute-start | bytes 135176 | tf_op jit(solution)/shard_map/ppermute | solution.py:848
  23.5 0.0 copy-start.1
  23.5 0.7 %copy-done.1 = s32[32]{0:T(128)S(1)} copy-done((s32[32]{0:T(128)S(1)}, s32[32]{0:T(128)}, u32[]{:S(2)}) %copy-start.1) | copy-done | bytes 152
  24.1 3.4 %source_part.1 = (f32[512,128]{1,0:T(8,128)S(1)}, f32[512,128]{1,0:T(8,128)S(1)}, f32[8,128]{1,0:T(8,128)S(1)}) custom-call(f32[640,128]{1,0:T(8,128)S(1)} %get-tuple-element.44.bm, f32[640,128]{1,0:T(8,128)S(1)} %get-tuple-element.45.be, f32[8,40,128]{2,1,0:T(8,128)S(1)} %get-tuple-element.46.rows_n, f32[8,40,128]{2,1,0:T(8,128)S(1)} %get-tuple-element.47.rows_p, ...), custom_call_target="tpu_custom_call" | custom-call | flops 12000000 | bytes 12000000 | tf_op jit(solution)/shard_map/source_part/pallas_call | solution.py:941
  27.5 0.0 collective-permute-done.7
  27.5 0.3 collective-permute-done.6
  27.9 0.9 %collective-permute-done.5 = f32[88,128]{1,0:T(8,128)S(1)} collective-permute-done((f32[88,128]{1,0:T(8,128)S(1)}, f32[88,128]{1,0:T(8,128)S(1)}, u32[]{:S(2)}, u32[]{:S(2)}) %collective-permute-start.5) | collective-permute-done | bytes 45088 | tf_op jit(solution)/shard_map/ppermute | solution.py:848
  28.8 0.9 %collective-permute-start.8 = (f32[4,88,128]{2,1,0:T(8,128)S(1)}, f32[4,88,128]{2,1,0:T(8,128)S(1)}, u32[]{:S(2)}, u32[]{:S(2)}) collective-permute-start(f32[4,88,128]{2,1,0:T(8,128)S(1)} %pad_maximum_fusion.refs_0_), channel_id=1, source_target_pairs={{0,2},{2,0},{1,3},{3,1},{4,6},{6,4},{5,7},{7,5},{8,10},{10,8},{9,1... | collective-permute-start | bytes 540680 | tf_op jit(solution)/shard_map/ppermute | solution.py:848
  29.7 0.0 collective-permute-start.9
  29.7 4.6 %collective-permute-done.8.refs_1_ = f32[4,88,128]{2,1,0:T(8,128)S(1)} collective-permute-done((f32[4,88,128]{2,1,0:T(8,128)S(1)}, f32[4,88,128]{2,1,0:T(8,128)S(1)}, u32[]{:S(2)}, u32[]{:S(2)}) %collective-permute-start.8) | collective-permute-done | bytes 180256 | tf_op jit(solution)/shard_map/ppermute | solution.py:848
  34.3 0.0 collective-permute-start.10
  34.4 0.0 collective-permute-done.9.refs_2_
  34.4 1.4 %collective-permute-done.10.refs_3_ = f32[4,88,128]{2,1,0:T(8,128)S(1)} collective-permute-done((f32[4,88,128]{2,1,0:T(8,128)S(1)}, f32[4,88,128]{2,1,0:T(8,128)S(1)}, u32[]{:S(2)}, u32[]{:S(2)}) %collective-permute-start.10) | collective-permute-done | bytes 180256 | tf_op jit(solution)/shard_map/ppermute | solution.py:848
  35.8 5.0 %solve.1 = (f32[512,128]{1,0:T(8,128)}, f32[512,128]{1,0:T(8,128)}, f32[1,2]{1,0:T(1,128)}) custom-call(f32[4,88,128]{2,1,0:T(8,128)S(1)} %pad_maximum_fusion.refs_0_, f32[4,88,128]{2,1,0:T(8,128)S(1)} %collective-permute-done.8.refs_1_, f32[4,88,128]{2,1,0:T(8,128)S(1)} %collective-permute-done.9.refs_2_, ...), custom_call_target="tpu_custom_call" | custom-call | tf_op jit(solution)/shard_map/solve/pallas_call | solution.py:966
  (1 shorter events, 0.0 us)
Async XLA Ops:
  2.3 6.2 %collective-permute-start = (f32[12,16,128]{2,1,0:T(8,128)S(1)}, f32[12,16,128]{2,1,0:T(8,128)S(1)}, u32[]{:S(2)}, u32[]{:S(2)}) collective-permute-start(f32[12,16,128]{2,1,0:T(8,128)S(1)} %get-tuple-element.35), channel_id=1, source_target_pairs={{0,1},{1,0},{2,3},{3,2},{4,5},{5,4},{6,7},{7,6},{8,9},{9,8},{10,11... | collective-permute-start | bytes 294920 | tf_op jit(solution)/shard_map/ppermute | solution.py:848
  2.8 5.6 %collective-permute-start.1 = (f32[4,16,128]{2,1,0:T(8,128)S(1)}, f32[4,16,128]{2,1,0:T(8,128)S(1)}, u32[]{:S(2)}, u32[]{:S(2)}) collective-permute-start(f32[4,16,128]{2,1,0:T(8,128)S(1)} %get-tuple-element.36), channel_id=1, source_target_pairs={{0,2},{2,0},{1,3},{3,1},{4,6},{6,4},{5,7},{7,5},{8,10},{10,8},{9,1... | collective-permute-start | bytes 98312 | tf_op jit(solution)/shard_map/ppermute | solution.py:848
  5.4 3.1 %collective-permute-start.2 = (f32[16,128]{1,0:T(8,128)S(1)}, f32[16,128]{1,0:T(8,128)S(1)}, u32[]{:S(2)}, u32[]{:S(2)}) collective-permute-start(f32[16,128]{1,0:T(8,128)S(1)} %get-tuple-element.37), channel_id=1, source_target_pairs={{0,3},{1,2},{2,1},{3,0},{4,7},{5,6},{6,5},{7,4},{8,11},{9,10},{10,... | collective-permute-start | bytes 24584 | tf_op jit(solution)/shard_map/ppermute | solution.py:854
  9.3 9.0 %collective-permute-start.3 = (f32[184,128]{1,0:T(8,128)S(1)}, f32[184,128]{1,0:T(8,128)S(1)}, u32[]{:S(2)}, u32[]{:S(2)}) collective-permute-start(f32[184,128]{1,0:T(8,128)S(1)} %get-tuple-element.39), channel_id=1, source_target_pairs={{0,12},{4,0},{8,4},{12,8},{1,13},{5,1},{9,5},{13,9},{2,14},{6,2},{... | collective-permute-start | bytes 282632 | tf_op jit(solution)/shard_map/ppermute | solution.py:848
  12.9 6.4 %collective-permute-start.4 = (f32[184,128]{1,0:T(8,128)S(1)}, f32[184,128]{1,0:T(8,128)S(1)}, u32[]{:S(2)}, u32[]{:S(2)}) collective-permute-start(f32[184,128]{1,0:T(8,128)S(1)} %get-tuple-element.40), channel_id=1, source_target_pairs={{0,4},{4,8},{8,12},{12,0},{1,5},{5,9},{9,13},{13,1},{2,6},{6,10},{... | collective-permute-start | bytes 282632 | tf_op jit(solution)/shard_map/ppermute | solution.py:848
  12.9 6.4 %copy-start = (s32[1,16,128]{2,1,0:T(8,128)S(1)}, s32[1,16,128]{2,1,0:T(8,128)}, u32[]{:S(2)}) copy-start(s32[1,16,128]{2,1,0:T(8,128)} %ids.1) | copy-start | bytes 24580
  20.0 7.5 %collective-permute-start.7 = (f32[88,128]{1,0:T(8,128)S(1)}, f32[88,128]{1,0:T(8,128)S(1)}, u32[]{:S(2)}, u32[]{:S(2)}) collective-permute-start(f32[88,128]{1,0:T(8,128)S(1)} %get-tuple-element.43), channel_id=1, source_target_pairs={{0,12},{4,0},{8,4},{12,8},{1,13},{5,1},{9,5},{13,9},{2,14},{6,2},{... | collective-permute-start | bytes 135176 | tf_op jit(solution)/shard_map/ppermute | solution.py:848
  22.9 4.9 %collective-permute-start.6 = (f32[88,128]{1,0:T(8,128)S(1)}, f32[88,128]{1,0:T(8,128)S(1)}, u32[]{:S(2)}, u32[]{:S(2)}) collective-permute-start(f32[88,128]{1,0:T(8,128)S(1)} %get-tuple-element.43), channel_id=1, source_target_pairs={{0,8},{4,12},{8,0},{12,4},{1,9},{5,13},{9,1},{13,5},{2,10},{6,14},... | collective-permute-start | bytes 135176 | tf_op jit(solution)/shard_map/ppermute | solution.py:848
  22.9 5.8 %collective-permute-start.5 = (f32[88,128]{1,0:T(8,128)S(1)}, f32[88,128]{1,0:T(8,128)S(1)}, u32[]{:S(2)}, u32[]{:S(2)}) collective-permute-start(f32[88,128]{1,0:T(8,128)S(1)} %get-tuple-element.43), channel_id=1, source_target_pairs={{0,4},{4,8},{8,12},{12,0},{1,5},{5,9},{9,13},{13,1},{2,6},{6,10},{... | collective-permute-start | bytes 135176 | tf_op jit(solution)/shard_map/ppermute | solution.py:848
  23.5 0.7 %copy-start.1 = (s32[32]{0:T(128)S(1)}, s32[32]{0:T(128)}, u32[]{:S(2)}) copy-start(s32[32]{0:T(128)} %param.11) | copy-start | bytes 388
  28.8 5.6 %collective-permute-start.8 = (f32[4,88,128]{2,1,0:T(8,128)S(1)}, f32[4,88,128]{2,1,0:T(8,128)S(1)}, u32[]{:S(2)}, u32[]{:S(2)}) collective-permute-start(f32[4,88,128]{2,1,0:T(8,128)S(1)} %pad_maximum_fusion.refs_0_), channel_id=1, source_target_pairs={{0,2},{2,0},{1,3},{3,1},{4,6},{6,4},{5,7},{7,5},{8,10},{10,8},{9,1... | collective-permute-start | bytes 540680 | tf_op jit(solution)/shard_map/ppermute | solution.py:848
  29.7 4.6 %collective-permute-start.9 = (f32[4,88,128]{2,1,0:T(8,128)S(1)}, f32[4,88,128]{2,1,0:T(8,128)S(1)}, u32[]{:S(2)}, u32[]{:S(2)}) collective-permute-start(f32[4,88,128]{2,1,0:T(8,128)S(1)} %pad_maximum_fusion.refs_0_), channel_id=1, source_target_pairs={{0,1},{1,0},{2,3},{3,2},{4,5},{5,4},{6,7},{7,6},{8,9},{9,8},{10,11... | collective-permute-start | bytes 540680 | tf_op jit(solution)/shard_map/ppermute | solution.py:848
  34.3 1.4 %collective-permute-start.10 = (f32[4,88,128]{2,1,0:T(8,128)S(1)}, f32[4,88,128]{2,1,0:T(8,128)S(1)}, u32[]{:S(2)}, u32[]{:S(2)}) collective-permute-start(f32[4,88,128]{2,1,0:T(8,128)S(1)} %collective-permute-done.8.refs_1_), channel_id=1, source_target_pairs={{0,1},{1,0},{2,3},{3,2},{4,5},{5,4},{6,7},{7,6},{8,9},{9,8},{10,11... | collective-permute-start | bytes 540680 | tf_op jit(solution)/shard_map/ppermute | solution.py:848

commit v6 on v5

--- a/solution.py
+++ b/solution.py
@@ -936,7 +936,7 @@
         "correct",
     )(own_rows, from_next, from_prev, coarse, surface, patch_ids)
 
-    relative = n_blk <= 4
+    relative = False
     moved = [ring(mine, "blk", d) for d in range(1, n_blk)] if relative else [lax.all_gather(mine, "blk")]
     base_adj, base_pot, patches = call(
         functools.partial(source_part, n_blk, n_len, n_wall, C, electrodes),
@@ -946,10 +946,10 @@
         "source_part",
         work=12 * 10**6,
     )(bm, be, rows_n, rows_p, qm, fields[2], owner_map.reshape(1, electrodes))
-    moved, base_adj = lax.optimization_barrier((moved, base_adj))
     sector_blocks = jnp.stack([mine] + moved) if relative else moved[0]
     if n_len == 2:
         here = [sector_blocks, ring(sector_blocks, "len", 1)]
+        here[1], base_adj = lax.optimization_barrier((here[1], base_adj))
     else:
         gathered = lax.all_gather(sector_blocks, "len")
         here = [gathered[j] for j in range(n_len)]

time: 40.9 us -> 45.7 us (1.12)
  blocking collectives: 0 us -> 13.6 us
  waiting for transfers between devices: 11.3 us -> 6.03 us
  starting transfers between devices: 11.2 us -> 7.65 us
    all_gather x0 -> x1, blocking collectives: none -> 13.6 us  [body(): lax.all_gather(mine, 'blk')]
    ppermute x10 -> x7, waiting for transfers between devices: 8.25 us -> 3.02 us  [ring(): return lax.ppermute(x, axis, [(i, (i + by) % count) for i in range(count)])]
    ppermute x10 -> x7, starting transfers between devices: 11.2 us -> 7.58 us  [ring(): return lax.ppermute(x, axis, [(i, (i + by) % count) for i in range(count)])]
  transfers between devices with their start and end apart: 11 -> 8, of which waited for: 6 -> 4; matrix products, arithmetic and copies ran while one was open for 0% -> 0% of each run, Pallas kernels for 21% -> 19%
where the time goes in v6:
time: 45.7 us; the launch traced here: 45.5 us
  Pallas kernels  16.9 us (37%)
  blocking collectives  13.6 us (30%)
  starting transfers between devices  7.65 us (17%)
  waiting for transfers between devices  6.03 us (13%)
  between operations  0.68 us (1%)
  local copies, waits for them, and re-layouts  0.66 us (1%)
    all_gather x1, blocking collectives, body(): lax.all_gather(mine, 'blk')  13.6 us
    ppermute x7, starting transfers between devices, ring(): return lax.ppermute(x, axis, [(i, (i + by) % count) for i in range(count)])  7.58 us
    pallas_call x1, Pallas kernels, body(): call(functools.partial(sector, n_len, n_wall, C), [vmem] * (5 + 2 * n_dir...  5.37 us
    pallas_call x1, Pallas kernels, body(): call(functools.partial(solve, (n_blk, n_len, n_wall), relative, C, W), [v...  5.01 us
    pallas_call x1, Pallas kernels, body(): call(functools.partial(source_part, n_blk, n_len, n_wall, C, electrodes),...  3.36 us
    ppermute x7, waiting for transfers between devices, ring(): return lax.ppermute(x, axis, [(i, (i + by) % count) for i in range(count)])  3.02 us
    ppermute x1, waiting for transfers between devices, across(): return lax.ppermute(x, ('len', 'wall'), pairs)  3.01 us
    pallas_call x1, Pallas kernels, body(): call(functools.partial(pack_faces, n_len), ['hbm'] * 4, [(own, vmem)] * 4...  1.65 us
  transfers between devices with their start and end apart: 8, of which 4 were waited for; matrix products, arithmetic and copies ran while one was open for 0% of the time, Pallas kernels for 19%

profile of v6, /device:TPU:0, one launch (start us, length us, event | category | flops | bytes accessed | tf_op | source)
XLA Modules:
  0.0 45.5 jit_solution(13603620059718180974)
XLA Ops:
  0.6 1.6 %faces.1 = (f32[512,128]{1,0:T(8,128)S(1)}, f32[512,128]{1,0:T(8,128)S(1)}, f32[512,128]{1,0:T(8,128)S(1)}, f32[512,128]{1,0:T(8,128)S(1)}, f32[12,16,128]{2,1,0...) custom-call(f32[512,128]{1,0:T(8,128)} %bitcast.12, f32[512,128]{1,0:T(8,128)} %bitcast.13, ...), custom_call_target="tpu_custom_call" | custom-call | tf_op jit(solution)/shard_map/faces/pallas_call | solution.py:888
  2.3 0.5 %collective-permute-start = (f32[12,16,128]{2,1,0:T(8,128)S(1)}, f32[12,16,128]{2,1,0:T(8,128)S(1)}, u32[]{:S(2)}, u32[]{:S(2)}) collective-permute-start(f32[12,16,128]{2,1,0:T(8,128)S(1)} %get-tuple-element.33), channel_id=1, source_target_pairs={{0,1},{1,0},{2,3},{3,2},{4,5},{5,4},{6,7},{7,6},{8,9},{9,8},{10,11... | collective-permute-start | bytes 294920 | tf_op jit(solution)/shard_map/ppermute | solution.py:848
  2.8 2.6 %collective-permute-start.1 = (f32[4,16,128]{2,1,0:T(8,128)S(1)}, f32[4,16,128]{2,1,0:T(8,128)S(1)}, u32[]{:S(2)}, u32[]{:S(2)}) collective-permute-start(f32[4,16,128]{2,1,0:T(8,128)S(1)} %get-tuple-element.34), channel_id=1, source_target_pairs={{0,2},{2,0},{1,3},{3,1},{4,6},{6,4},{5,7},{7,5},{8,10},{10,8},{9,1... | collective-permute-start | bytes 98312 | tf_op jit(solution)/shard_map/ppermute | solution.py:848
  5.4 0.1 collective-permute-start.2
  5.4 3.0 %collective-permute-done.2.refs_6_ = f32[16,128]{1,0:T(8,128)S(1)} collective-permute-done((f32[16,128]{1,0:T(8,128)S(1)}, f32[16,128]{1,0:T(8,128)S(1)}, u32[]{:S(2)}, u32[]{:S(2)}) %collective-permute-start.2) | collective-permute-done | bytes 8224 | tf_op jit(solution)/shard_map/ppermute | solution.py:854
  8.4 0.0 collective-permute-done.1.refs_5_
  8.4 0.0 collective-permute-done.refs_4_
  8.5 0.8 %boundary.1 = (f32[184,128]{1,0:T(8,128)S(1)}, f32[184,128]{1,0:T(8,128)S(1)}, f32[2,6,40,128]{3,2,1,0:T(8,128)S(1)}) custom-call(f32[512,128]{1,0:T(8,128)S(1)} %get-tuple-element.29.refs_0_, f32[512,128]{1,0:T(8,128)S(1)} %get-tuple-element.30.refs_1_, f32[512,128]{1,0:T(8,128)S(1)} %get-tuple-element.31.refs_2_.mask.refs_6_, ...), custom_call_target="tpu_custom_call" | custom-call | tf_op jit(solution)/shard_map/boundary/pallas_call | solution.py:910
  9.3 3.7 %collective-permute-start.3 = (f32[184,128]{1,0:T(8,128)S(1)}, f32[184,128]{1,0:T(8,128)S(1)}, u32[]{:S(2)}, u32[]{:S(2)}) collective-permute-start(f32[184,128]{1,0:T(8,128)S(1)} %get-tuple-element.37), channel_id=1, source_target_pairs={{0,12},{4,0},{8,4},{12,8},{1,13},{5,1},{9,5},{13,9},{2,14},{6,2},{... | collective-permute-start | bytes 282632 | tf_op jit(solution)/shard_map/ppermute | solution.py:848
  12.9 0.0 collective-permute-start.4
  12.9 0.0 copy-start
  12.9 5.4 %sector.1 = (f32[640,128]{1,0:T(8,128)S(1)}, f32[640,128]{1,0:T(8,128)S(1)}, f32[640,128]{1,0:T(8,128)S(1)}, f32[64,128]{1,0:T(8,128)S(1)}, f32[16,128]{1,0:T(8,128)S(1)}) custom-call(f32[512,128]{1,0:T(8,128)S(1)} %get-tuple-element.29.refs_0_, f32[512,128]{1,0:T(8,128)S(1)} %get-tuple-element.30.refs_1_, ...), custom_call_target="tpu_custom_call" | custom-call | flops 16000000 | bytes 16000000 | tf_op jit(solution)/shard_map/sector/pallas_call | solution.py:919
  18.3 0.0 collective-permute-done.3.from_next
  18.3 1.0 %collective-permute-done.4.from_prev = f32[184,128]{1,0:T(8,128)S(1)} collective-permute-done((f32[184,128]{1,0:T(8,128)S(1)}, f32[184,128]{1,0:T(8,128)S(1)}, u32[]{:S(2)}, u32[]{:S(2)}) %collective-permute-start.4) | collective-permute-done | bytes 94240 | tf_op jit(solution)/shard_map/ppermute | solution.py:848
  19.3 0.0 copy-done
  19.3 0.7 %correct.1 = (f32[8,40,128]{2,1,0:T(8,128)S(1)}, f32[8,40,128]{2,1,0:T(8,128)S(1)}, f32[88,128]{1,0:T(8,128)S(1)}) custom-call(f32[2,6,40,128]{3,2,1,0:T(8,128)S(1)} %get-tuple-element.36.own_rows, f32[184,128]{1,0:T(8,128)S(1)} %collective-permute-done.3.from_next, f32[184,128]{1,0:T(8,128)S(1)} %collective-permute-done.4.from_prev, ...), custom_call_target="tpu_custom_call" | custom-call | tf_op jit(solution)/shard_map/correct/pallas_call | solution.py:931
  20.0 13.6 %all-gather = f32[352,128]{1,0:T(8,128)S(1)} all-gather(f32[88,128]{1,0:T(8,128)S(1)} %get-tuple-element.41), channel_id=2, replica_groups=mesh['groups'=2,'blk'=4,'len'=2,'wall'=2] {'blk'}, dimensions={0}, use_global_device_ids=true | all-gather | bytes 225280 | tf_op jit(solution)/shard_map/all_gather | solution.py:940
  33.6 0.8 %collective-permute-start.5 = (f32[4,88,128]{2,1,0:T(8,128)S(1)}, f32[4,88,128]{2,1,0:T(8,128)S(1)}, u32[]{:S(2)}, u32[]{:S(2)}) collective-permute-start(f32[4,88,128]{2,1,0:T(8,128)S(1)} %bitcast.8), channel_id=1, source_target_pairs={{0,2},{2,0},{1,3},{3,1},{4,6},{6,4},{5,7},{7,5},{8,10},{10,8},{9,1... | collective-permute-start | bytes 540680 | tf_op jit(solution)/shard_map/ppermute | solution.py:848
  34.4 0.0 collective-permute-start.6
  34.4 0.0 copy-start.1
  34.4 0.7 %copy-done.1 = s32[32]{0:T(128)S(1)} copy-done((s32[32]{0:T(128)S(1)}, s32[32]{0:T(128)}, u32[]{:S(2)}) %copy-start.1) | copy-done | bytes 152
  35.1 3.4 %source_part.1 = (f32[512,128]{1,0:T(8,128)S(1)}, f32[512,128]{1,0:T(8,128)S(1)}, f32[8,128]{1,0:T(8,128)S(1)}) custom-call(f32[640,128]{1,0:T(8,128)S(1)} %get-tuple-element.42.bm, f32[640,128]{1,0:T(8,128)S(1)} %get-tuple-element.43.be, f32[8,40,128]{2,1,0:T(8,128)S(1)} %get-tuple-element.44.rows_n, f32[8,40,128]{2,1,0:T(8,128)S(1)} %get-tuple-element.45.rows_p, ...), custom_call_target="tpu_custom_call" | custom-call | flops 12000000 | bytes 12000000 | tf_op jit(solution)/shard_map/source_part/pallas_call | solution.py:941
  38.5 0.6 %collective-permute-done.5.refs_1_ = f32[4,88,128]{2,1,0:T(8,128)S(1)} collective-permute-done((f32[4,88,128]{2,1,0:T(8,128)S(1)}, f32[4,88,128]{2,1,0:T(8,128)S(1)}, u32[]{:S(2)}, u32[]{:S(2)}) %collective-permute-start.5) | collective-permute-done | bytes 180256 | tf_op jit(solution)/shard_map/ppermute | solution.py:848
  39.1 0.0 collective-permute-start.7
  39.1 0.0 collective-permute-done.6.refs_2_
  39.1 1.4 %collective-permute-done.7.refs_3_ = f32[4,88,128]{2,1,0:T(8,128)S(1)} collective-permute-done((f32[4,88,128]{2,1,0:T(8,128)S(1)}, f32[4,88,128]{2,1,0:T(8,128)S(1)}, u32[]{:S(2)}, u32[]{:S(2)}) %collective-permute-start.7) | collective-permute-done | bytes 180256 | tf_op jit(solution)/shard_map/ppermute | solution.py:848
  40.5 5.0 %solve.1 = (f32[512,128]{1,0:T(8,128)}, f32[512,128]{1,0:T(8,128)}, f32[1,2]{1,0:T(1,128)}) custom-call(f32[4,88,128]{2,1,0:T(8,128)S(1)} %bitcast.10, f32[4,88,128]{2,1,0:T(8,128)S(1)} %collective-permute-done.5.refs_1_, f32[4,88,128]{2,1,0:T(8,128)S(1)} %collective-permute-done.6.refs_2_, f32[4,88,128]{2,1,0:T(8,128)S(1)} %collective-permute-done.7.refs_3_, ...), custom_call_target="tpu_custom_call" | custom-call | tf_op jit(solution)/shard_map/solve/pallas_call | solution.py:966
Async XLA Ops:
  2.3 6.2 %collective-permute-start = (f32[12,16,128]{2,1,0:T(8,128)S(1)}, f32[12,16,128]{2,1,0:T(8,128)S(1)}, u32[]{:S(2)}, u32[]{:S(2)}) collective-permute-start(f32[12,16,128]{2,1,0:T(8,128)S(1)} %get-tuple-element.33), channel_id=1, source_target_pairs={{0,1},{1,0},{2,3},{3,2},{4,5},{5,4},{6,7},{7,6},{8,9},{9,8},{10,11... | collective-permute-start | bytes 294920 | tf_op jit(solution)/shard_map/ppermute | solution.py:848
  2.8 5.6 %collective-permute-start.1 = (f32[4,16,128]{2,1,0:T(8,128)S(1)}, f32[4,16,128]{2,1,0:T(8,128)S(1)}, u32[]{:S(2)}, u32[]{:S(2)}) collective-permute-start(f32[4,16,128]{2,1,0:T(8,128)S(1)} %get-tuple-element.34), channel_id=1, source_target_pairs={{0,2},{2,0},{1,3},{3,1},{4,6},{6,4},{5,7},{7,5},{8,10},{10,8},{9,1... | collective-permute-start | bytes 98312 | tf_op jit(solution)/shard_map/ppermute | solution.py:848
  5.4 3.1 %collective-permute-start.2 = (f32[16,128]{1,0:T(8,128)S(1)}, f32[16,128]{1,0:T(8,128)S(1)}, u32[]{:S(2)}, u32[]{:S(2)}) collective-permute-start(f32[16,128]{1,0:T(8,128)S(1)} %get-tuple-element.35), channel_id=1, source_target_pairs={{0,3},{1,2},{2,1},{3,0},{4,7},{5,6},{6,5},{7,4},{8,11},{9,10},{10,... | collective-permute-start | bytes 24584 | tf_op jit(solution)/shard_map/ppermute | solution.py:854
  9.3 9.0 %collective-permute-start.3 = (f32[184,128]{1,0:T(8,128)S(1)}, f32[184,128]{1,0:T(8,128)S(1)}, u32[]{:S(2)}, u32[]{:S(2)}) collective-permute-start(f32[184,128]{1,0:T(8,128)S(1)} %get-tuple-element.37), channel_id=1, source_target_pairs={{0,12},{4,0},{8,4},{12,8},{1,13},{5,1},{9,5},{13,9},{2,14},{6,2},{... | collective-permute-start | bytes 282632 | tf_op jit(solution)/shard_map/ppermute | solution.py:848
  12.9 6.4 %collective-permute-start.4 = (f32[184,128]{1,0:T(8,128)S(1)}, f32[184,128]{1,0:T(8,128)S(1)}, u32[]{:S(2)}, u32[]{:S(2)}) collective-permute-start(f32[184,128]{1,0:T(8,128)S(1)} %get-tuple-element.38), channel_id=1, source_target_pairs={{0,4},{4,8},{8,12},{12,0},{1,5},{5,9},{9,13},{13,1},{2,6},{6,10},{... | collective-permute-start | bytes 282632 | tf_op jit(solution)/shard_map/ppermute | solution.py:848
  12.9 6.4 %copy-start = (s32[1,16,128]{2,1,0:T(8,128)S(1)}, s32[1,16,128]{2,1,0:T(8,128)}, u32[]{:S(2)}) copy-start(s32[1,16,128]{2,1,0:T(8,128)} %ids.1) | copy-start | bytes 24580
  33.6 5.5 %collective-permute-start.5 = (f32[4,88,128]{2,1,0:T(8,128)S(1)}, f32[4,88,128]{2,1,0:T(8,128)S(1)}, u32[]{:S(2)}, u32[]{:S(2)}) collective-permute-start(f32[4,88,128]{2,1,0:T(8,128)S(1)} %bitcast.8), channel_id=1, source_target_pairs={{0,2},{2,0},{1,3},{3,1},{4,6},{6,4},{5,7},{7,5},{8,10},{10,8},{9,1... | collective-permute-start | bytes 540680 | tf_op jit(solution)/shard_map/ppermute | solution.py:848
  34.4 4.7 %collective-permute-start.6 = (f32[4,88,128]{2,1,0:T(8,128)S(1)}, f32[4,88,128]{2,1,0:T(8,128)S(1)}, u32[]{:S(2)}, u32[]{:S(2)}) collective-permute-start(f32[4,88,128]{2,1,0:T(8,128)S(1)} %bitcast.9), channel_id=1, source_target_pairs={{0,1},{1,0},{2,3},{3,2},{4,5},{5,4},{6,7},{7,6},{8,9},{9,8},{10,11... | collective-permute-start | bytes 540680 | tf_op jit(solution)/shard_map/ppermute | solution.py:848
  34.4 0.7 %copy-start.1 = (s32[32]{0:T(128)S(1)}, s32[32]{0:T(128)}, u32[]{:S(2)}) copy-start(s32[32]{0:T(128)} %param.11) | copy-start | bytes 388
  39.1 1.4 %collective-permute-start.7 = (f32[4,88,128]{2,1,0:T(8,128)S(1)}, f32[4,88,128]{2,1,0:T(8,128)S(1)}, u32[]{:S(2)}, u32[]{:S(2)}) collective-permute-start(f32[4,88,128]{2,1,0:T(8,128)S(1)} %collective-permute-done.5.refs_1_), channel_id=1, source_target_pairs={{0,1},{1,0},{2,3},{3,2},{4,5},{5,4},{6,7},{7,6},{8,9},{9,8},{10,11... | collective-permute-start | bytes 540680 | tf_op jit(solution)/shard_map/ppermute | solution.py:848

commit v7 on v5

--- a/solution.py
+++ b/solution.py
@@ -560,6 +560,61 @@
     patches[2:8, :] = jnp.zeros((6, LANES), F32)
 
 
+def halves(shape):
+    lane = lane_of(shape)
+    return lane, lane % (LANES // 2)
+
+
+def compact(C, W, blocks, out, sheet1, coarse2):
+    n_blk = blocks.shape[0]
+    W1, C1 = W // 2, C // 2
+    half, start, middle = W1 // 2, W1 // 2 * C1, LANES // 2
+    blk, length, wall = lax.axis_index("blk"), lax.axis_index("len"), lax.axis_index("wall")
+    sums = jnp.zeros((8, LANES), F32)
+    for d in range(n_blk):
+        b = lax.rem(blk - d + n_blk, n_blk)
+        for i in range(half):
+            sheet1[i, pl.ds(pl.multiple_of(C1 * b, C1), C1), :] = blocks[d, i * C1 : (i + 1) * C1, :]
+        out[pl.ds(pl.multiple_of(96 + C * b, C), C), :] = blocks[d, start : start + C, :]
+        sums = sums + blocks[d, start + C : start + C + 8, :]
+    out[160:168, :] = sums
+    NC1 = sheet1.shape[1]
+    lane, at = halves((NC1, LANES))
+    low = lane < middle
+    coef, k1 = level_coef(1), level_step(1)
+    ends = pltpu.roll(sheet1[half - 1], middle, 1), pltpu.roll(sheet1[0], middle, 1)
+    for q in range(half // 2):
+        both = sheet1[2 * q] + sheet1[2 * q + 1]
+        prev = sheet1[2 * q - 1] if q else jnp.where(low, 0.0, ends[0])
+        after_it = sheet1[2 * q + 2] if 2 * q + 2 < half else jnp.where(low, ends[1], 0.0)
+        c = pltpu.roll(both, 1, 0) + pltpu.roll(both, NC1 - 1, 0)
+        l = jnp.where(at == 0, 0.0, pltpu.roll(both, 1, 1)) + jnp.where(
+            at == middle - 1, 0.0, pltpu.roll(both, LANES - 1, 1)
+        )
+        left = (1.0 - OMEGA) * both + k1 * (coef[0] * (prev + both + after_it) + coef[1] * c + coef[2] * l)
+        coarse2[q] = 0.125 * twins(left, 1)
+    coarse2[half // 2] = 0.125 * twins(jnp.where(wall == 0, sheet1[half - 1], sheet1[0]), 1)
+    rows2 = NC1 // 2
+    lane2, at2 = halves((rows2, LANES))
+    pick = lane2 - at2 + 2 * (at2 % (middle // 2))
+    for p in range(half // 4):
+        pair = [lanes_at(coarse2[2 * p + k, pl.ds(0, rows2, stride=2), :], pick) for k in range(2)]
+        out[rows2 * p : rows2 * (p + 1), :] = jnp.where(at2 < middle // 2, pair[0], pair[1])
+    beside = jnp.zeros((NC1, LANES), F32)
+    base = jnp.where(length == 0, middle - H, 0)
+    for i in range(half):
+        turned = pltpu.roll(sheet1[i], lax.rem(H * i - base + LANES, LANES), 1)
+        beside = jnp.where(at // H == i, turned, beside)
+    out[32 : 32 + NC1, :] = beside
+    face = coarse2[half // 2, pl.ds(0, rows2, stride=2), :]
+    face = lanes_at(face, jnp.where(wall == 0, middle, 0) + 2 * (at2 % (middle // 2)))
+    inner = jnp.logical_and(lane2 >= middle // 2, lane2 < middle)
+    out[32 : 32 + rows2, :] = jnp.where(inner, face, beside[:rows2])
+    inner_surface = jnp.where(low, sheet1[0], pltpu.roll(sheet1[1], middle, 1))
+    outer_surface = jnp.where(low, pltpu.roll(sheet1[half - 2], middle, 1), sheet1[half - 1])
+    out[64 : 64 + NC1, :] = jnp.where(wall == 0, inner_surface, outer_surface)
+
+
 def around(x, by):
     rows, lanes = x.shape
     lane = lane_of(x.shape)
@@ -582,12 +637,12 @@
     return x + jnp.where((lane & by) == 0, pltpu.roll(x, lanes - by, 1), pltpu.roll(x, by, 1))
 
 
-def solve(sizes, relative, C, W, *refs):
+def solve(sizes, relative, compacted, C, W, *refs):
     n_blk, n_len, n_wall = sizes
     count = n_len * n_wall
     blocks, refs = refs[:count], refs[count:]
     base_adj, base_pot, mask, patches, adj_prev, potential, patch_grad = refs[:7]
-    b1, x1, b2, x2, b3, x3, near, pm, pe, tm, te, adj_out, pot_out, sheet, sems = refs[7:]
+    b1, x1, b2, x2, b3, x3, near, pm, pe, tm, te, adj_out, pot_out, sheet, both_walls, sems = refs[7:]
     L = LANES
     W1, C1 = W // 2, C // 2
     planes, NC1, NL1 = b1.shape
@@ -612,24 +667,67 @@
         ref[0] = zero1
         ref[ref.shape[0] - 1] = zero1
 
-    for v in range(n_wall):
-        wall_s = wall_of(v)
-        mine = blocks[v * n_len : (v + 1) * n_len]
-
-        def unpack(d):
-            at = pl.ds(pl.multiple_of(C1 * blk_of(d), C1), C1)
-            for t in range(n_len // 2):
-                one, two = mine[2 * t], mine[2 * t + 1]
+    if not compacted:
+        for v in range(n_wall):
+            wall_s = wall_of(v)
+            mine = blocks[v * n_len : (v + 1) * n_len]
+
+            def unpack(d):
+                at = pl.ds(pl.multiple_of(C1 * blk_of(d), C1), C1)
+                for t in range(n_len // 2):
+                    one, two = mine[2 * t], mine[2 * t + 1]
+                    for i in range(half):
+                        a, b = one[d, i * C1 : (i + 1) * C1, :], two[d, i * C1 : (i + 1) * C1, :]
+                        if n_len == 2:
+                            a, b = jnp.where(length == 0, a, b), jnp.where(length == 0, b, a)
+                        spot = 1 + wall_s * W1 + i
+                        lanes = slice(t * LANES, (t + 1) * LANES)
+                        b1[spot, at, lanes] = jnp.where(lane8 < middle, a, pltpu.roll(b, middle, 1))
+                        b1[spot + half, at, lanes] = jnp.where(lane8 < middle, pltpu.roll(a, middle, 1), b)
+
+            loop(0, n_blk, unpack, 4)
+    if compacted:
+        lane8 = lane_of((C1, LANES))
+        here8 = lane8 // middle == length
+        face_lane = jnp.where(length == 0, middle, middle - H)
+        near8 = jnp.logical_and(lane8 >= face_lane, lane8 < face_lane + H)
+        for v in range(n_wall):
+            wall_s = wall_of(v)
+            own, other = blocks[2 * v], blocks[2 * v + 1]
+            for d in range(n_blk):
+                row = pl.multiple_of(C1 * blk_of(d), C1)
+                at = pl.ds(row, C1)
+                beside = other[pl.ds(32 + row, C1), :]
                 for i in range(half):
-                    a, b = one[d, i * C1 : (i + 1) * C1, :], two[d, i * C1 : (i + 1) * C1, :]
-                    if n_len == 2:
-                        a, b = jnp.where(length == 0, a, b), jnp.where(length == 0, b, a)
-                    spot = 1 + wall_s * W1 + i
-                    lanes = slice(t * LANES, (t + 1) * LANES)
-                    b1[spot, at, lanes] = jnp.where(lane8 < middle, a, pltpu.roll(b, middle, 1))
-                    b1[spot + half, at, lanes] = jnp.where(lane8 < middle, pltpu.roll(a, middle, 1), b)
-
-        loop(0, n_blk, unpack, 4)
+                    a = own[d, i * C1 : (i + 1) * C1, :]
+                    b = pltpu.roll(a, middle, 1)
+                    for k, value in enumerate((jnp.where(length == 0, a, b), jnp.where(length == 0, b, a))):
+                        turn = lax.rem(face_lane - H * i - middle * k + 2 * LANES, LANES)
+                        rest = jnp.where(near8, pltpu.roll(beside, turn, 1), 0.0)
+                        b1[1 + wall_s * W1 + i + half * k, at, :] = jnp.where(here8, value, rest)
+            surface = other[64 : 64 + NC1, :]
+            turned = pltpu.roll(surface, middle, 1)
+            spot = jnp.where(wall_s == 0, 1, planes - 1)
+            here = lane_of((NC1, LANES)) // middle == length
+            b1[spot] = jnp.where(here, b1[spot], jnp.where(length == 0, turned, surface))
+            b1[spot + 1] = jnp.where(here, b1[spot + 1], jnp.where(length == 0, surface, turned))
+        for k in range(2):
+            both_walls[k] = jnp.where(wall == k, blocks[1][0:48, :], blocks[3][0:48, :])
+        tile_lane8 = lane_of((8, LANES)) % middle // 2
+        row_of_8 = lax.broadcasted_iota(jnp.int32, (8, LANES), 0) // 2
+
+        def widened(w, first, t, lane):
+            tile = both_walls[w, first + 8 * (t // 2) : first + 8 * (t // 2) + 8, :]
+            return lanes_at(rows_at(tile, 4 * (t % 2) + row_of_8), lane + tile_lane8)
+
+        for w2 in range(planes // 2):
+            w, q = divmod(w2, half)
+            high, q = divmod(q, half // 2)
+            for t in range(NC1 // 8):
+                value = widened(w, NC1 // 2 * (q // 2), t, middle // 2 * (q % 2) + middle * high)
+                if w2 in (half - 1, half):
+                    value = value + level_step(1) * level_coef(1)[0] * widened(1 - w, 32, t, middle // 2)
+                b2[1 + w2, 8 * t : 8 * t + 8, :] = value
 
     def total_of(x, wsum, level, by):
         coef = level_coef(level)
@@ -645,8 +743,12 @@
         total = total_of(x, x_ref[i - 1] + x_ref[i + 1], level, 2 ** (level - 1))
         return (1.0 - OMEGA) * x + level_step(level) * b_ref[i] + total
 
+    lane1 = lane_of((NC1, NL1))
+    exact = jnp.logical_or(lane1 // middle == length, lane1 // 2 == jnp.where(length == 0, middle // 2, middle // 2 - 1))
+
     def down1(q):
-        b2[1 + q] = 0.125 * twins(left_pair(b1, 2 * q + 1, 1), 1)
+        value = 0.125 * twins(left_pair(b1, 2 * q + 1, 1), 1)
+        b2[1 + q] = jnp.where(exact, value, b2[1 + q]) if compacted else value
 
     loop(0, planes // 2, down1, often)
 
@@ -825,6 +927,13 @@
         for j in range(n_len):
             ref = blocks[v * n_len + j]
             at_l = pl.ds(pl.multiple_of(length_of(j) * L, L), L)
+            if compacted and j == 1:
+                for b in range(n_blk):
+                    values = sheet[wall_s, b * C : (b + 1) * C, at_l]
+                    ids = ref[96 + b * C : 96 + (b + 1) * C, :]
+                    totals = [x + jnp.where(ids == e, values, 0.0) for x, e in zip(totals, owned)]
+                small = [x + jnp.where(spot == e, ref[160:168, :], 0.0) for x, e in zip(small, owned)]
+                continue
 
             def add(d, carry):
                 big, little = carry
@@ -948,7 +1057,17 @@
     )(bm, be, rows_n, rows_p, qm, fields[2], owner_map.reshape(1, electrodes))
     moved, base_adj = lax.optimization_barrier((moved, base_adj))
     sector_blocks = jnp.stack([mine] + moved) if relative else moved[0]
-    if n_len == 2:
+    compacted = (n_blk, n_len, C, W) == (4, 2, 16, 32)
+    if compacted:
+        (brief,) = call(
+            functools.partial(compact, C, W),
+            [vmem],
+            [((168, L), vmem)],
+            [(W // 4, n_blk * C // 2, L), (W // 8 + 1, n_blk * C // 2, L)],
+            "compact",
+        )(sector_blocks)
+        here = [sector_blocks, ring(brief, "len", 1)]
+    elif n_len == 2:
         here = [sector_blocks, ring(sector_blocks, "len", 1)]
     else:
         gathered = lax.all_gather(sector_blocks, "len")
@@ -962,9 +1081,9 @@
     tall = (Q * (C + 8), L)
     taller = ((W + 2) * (C + 8), L)
     scratch = grids + [(Q * C, NL1), tall, tall, taller, own, own, own]
-    scratch += [(2, n_blk * C, n_len * L), pltpu.SemaphoreType.DMA((2, 2))]
+    scratch += [(2, n_blk * C, n_len * L), (2, 48, L), pltpu.SemaphoreType.DMA((2, 2))]
     adj_prev, potential, patch_grad = call(
-        functools.partial(solve, (n_blk, n_len, n_wall), relative, C, W),
+        functools.partial(solve, (n_blk, n_len, n_wall), relative, compacted, C, W),
         [vmem] * (len(blocks) + 4),
         [(own, "any"), (own, "any"), ((1, 2), "smem")],
         scratch,

time: 40.9 us -> 40.8 us (level)
  waiting for transfers between devices: 11.3 us -> 10.6 us
  Pallas kernels: 16.9 us -> 17.4 us
    ppermute x10, waiting for transfers between devices: 8.25 us -> 7.55 us  [ring(): return lax.ppermute(x, axis, [(i, (i + by) % count) for i in range(count)])]
    pallas_call x1 -> x2, Pallas kernels: 5.02 us -> 5.52 us  [the longest x1 5.24 us: body(): call(functools.partial(solve, (n_blk, n_len, n_wall), relative, compacted...]
  transfers between devices with their start and end apart: 11 -> 11, of which waited for: 6 -> 6; matrix products, arithmetic and copies ran while one was open for 0% -> 0% of each run, Pallas kernels for 21% -> 22%
where the time goes in v7:
time: 40.8 us; the launch traced here: 40.7 us
  Pallas kernels  17.4 us (43%)
  starting transfers between devices  11.3 us (28%)
  waiting for transfers between devices  10.6 us (26%)
  between operations  0.71 us (2%)
  local copies, waits for them, and re-layouts  0.66 us (2%)
    ppermute x10, starting transfers between devices, ring(): return lax.ppermute(x, axis, [(i, (i + by) % count) for i in range(count)])  11.2 us
    ppermute x10, waiting for transfers between devices, ring(): return lax.ppermute(x, axis, [(i, (i + by) % count) for i in range(count)])  7.55 us
    pallas_call x1, Pallas kernels, body(): call(functools.partial(sector, n_len, n_wall, C), [vmem] * (5 + 2 * n_dir...  5.37 us
    pallas_call x1, Pallas kernels, body(): call(functools.partial(solve, (n_blk, n_len, n_wall), relative, compacted...  5.24 us
    pallas_call x1, Pallas kernels, body(): call(functools.partial(source_part, n_blk, n_len, n_wall, C, electrodes),...  3.36 us
    ppermute x1, waiting for transfers between devices, across(): return lax.ppermute(x, ('len', 'wall'), pairs)  3.01 us
    pallas_call x1, Pallas kernels, body(): call(functools.partial(pack_faces, n_len), ['hbm'] * 4, [(own, vmem)] * 4...  1.65 us
  transfers between devices with their start and end apart: 11, of which 6 were waited for; matrix products, arithmetic and copies ran while one was open for 0% of the time, Pallas kernels for 22%

profile of v7, /device:TPU:0, one launch (start us, length us, event | category | flops | bytes accessed | tf_op | source)
XLA Modules:
  0.0 40.7 jit_solution(18146614555510655555)
XLA Ops:
  0.6 1.6 %faces.1 = (f32[512,128]{1,0:T(8,128)S(1)}, f32[512,128]{1,0:T(8,128)S(1)}, f32[512,128]{1,0:T(8,128)S(1)}, f32[512,128]{1,0:T(8,128)S(1)}, f32[12,16,128]{2,1,0...) custom-call(f32[512,128]{1,0:T(8,128)} %bitcast.13, f32[512,128]{1,0:T(8,128)} %bitcast.14, ...), custom_call_target="tpu_custom_call" | custom-call | tf_op jit(solution)/shard_map/faces/pallas_call | solution.py:997
  2.3 0.5 %collective-permute-start = (f32[12,16,128]{2,1,0:T(8,128)S(1)}, f32[12,16,128]{2,1,0:T(8,128)S(1)}, u32[]{:S(2)}, u32[]{:S(2)}) collective-permute-start(f32[12,16,128]{2,1,0:T(8,128)S(1)} %get-tuple-element.35), channel_id=1, source_target_pairs={{0,1},{1,0},{2,3},{3,2},{4,5},{5,4},{6,7},{7,6},{8,9},{9,8},{10,11... | collective-permute-start | bytes 294920 | tf_op jit(solution)/shard_map/ppermute | solution.py:957
  2.8 2.6 %collective-permute-start.1 = (f32[4,16,128]{2,1,0:T(8,128)S(1)}, f32[4,16,128]{2,1,0:T(8,128)S(1)}, u32[]{:S(2)}, u32[]{:S(2)}) collective-permute-start(f32[4,16,128]{2,1,0:T(8,128)S(1)} %get-tuple-element.36), channel_id=1, source_target_pairs={{0,2},{2,0},{1,3},{3,1},{4,6},{6,4},{5,7},{7,5},{8,10},{10,8},{9,1... | collective-permute-start | bytes 98312 | tf_op jit(solution)/shard_map/ppermute | solution.py:957
  5.4 0.1 collective-permute-start.2
  5.4 3.0 %collective-permute-done.2.refs_6_ = f32[16,128]{1,0:T(8,128)S(1)} collective-permute-done((f32[16,128]{1,0:T(8,128)S(1)}, f32[16,128]{1,0:T(8,128)S(1)}, u32[]{:S(2)}, u32[]{:S(2)}) %collective-permute-start.2) | collective-permute-done | bytes 8224 | tf_op jit(solution)/shard_map/ppermute | solution.py:963
  8.4 0.0 collective-permute-done.1.refs_5_
  8.4 0.0 collective-permute-done.refs_4_
  8.5 0.8 %boundary.1 = (f32[184,128]{1,0:T(8,128)S(1)}, f32[184,128]{1,0:T(8,128)S(1)}, f32[2,6,40,128]{3,2,1,0:T(8,128)S(1)}) custom-call(f32[512,128]{1,0:T(8,128)S(1)} %get-tuple-element.31.refs_0_, f32[512,128]{1,0:T(8,128)S(1)} %get-tuple-element.32.refs_1_, f32[512,128]{1,0:T(8,128)S(1)} %get-tuple-element.33.refs_2_.mask.refs_6_, ...), custom_call_target="tpu_custom_call" | custom-call | tf_op jit(solution)/shard_map/boundary/pallas_call | solution.py:1019
  9.3 3.7 %collective-permute-start.3 = (f32[184,128]{1,0:T(8,128)S(1)}, f32[184,128]{1,0:T(8,128)S(1)}, u32[]{:S(2)}, u32[]{:S(2)}) collective-permute-start(f32[184,128]{1,0:T(8,128)S(1)} %get-tuple-element.39), channel_id=1, source_target_pairs={{0,12},{4,0},{8,4},{12,8},{1,13},{5,1},{9,5},{13,9},{2,14},{6,2},{... | collective-permute-start | bytes 282632 | tf_op jit(solution)/shard_map/ppermute | solution.py:957
  12.9 0.0 collective-permute-start.4
  12.9 0.0 copy-start
  12.9 5.4 %sector.1 = (f32[640,128]{1,0:T(8,128)S(1)}, f32[640,128]{1,0:T(8,128)S(1)}, f32[640,128]{1,0:T(8,128)S(1)}, f32[64,128]{1,0:T(8,128)S(1)}, f32[16,128]{1,0:T(8,128)S(1)}) custom-call(f32[512,128]{1,0:T(8,128)S(1)} %get-tuple-element.31.refs_0_, f32[512,128]{1,0:T(8,128)S(1)} %get-tuple-element.32.refs_1_, ...), custom_call_target="tpu_custom_call" | custom-call | flops 16000000 | bytes 16000000 | tf_op jit(solution)/shard_map/sector/pallas_call | solution.py:1028
  18.3 0.0 collective-permute-done.3.from_next
  18.3 1.0 %collective-permute-done.4.from_prev = f32[184,128]{1,0:T(8,128)S(1)} collective-permute-done((f32[184,128]{1,0:T(8,128)S(1)}, f32[184,128]{1,0:T(8,128)S(1)}, u32[]{:S(2)}, u32[]{:S(2)}) %collective-permute-start.4) | collective-permute-done | bytes 94240 | tf_op jit(solution)/shard_map/ppermute | solution.py:957
  19.3 0.0 copy-done
  19.3 0.7 %correct.1 = (f32[8,40,128]{2,1,0:T(8,128)S(1)}, f32[8,40,128]{2,1,0:T(8,128)S(1)}, f32[88,128]{1,0:T(8,128)S(1)}) custom-call(f32[2,6,40,128]{3,2,1,0:T(8,128)S(1)} %get-tuple-element.38.own_rows, f32[184,128]{1,0:T(8,128)S(1)} %collective-permute-done.3.from_next, f32[184,128]{1,0:T(8,128)S(1)} %collective-permute-done.4.from_prev, ...), custom_call_target="tpu_custom_call" | custom-call | tf_op jit(solution)/shard_map/correct/pallas_call | solution.py:1040
  20.0 2.9 %collective-permute-start.7 = (f32[88,128]{1,0:T(8,128)S(1)}, f32[88,128]{1,0:T(8,128)S(1)}, u32[]{:S(2)}, u32[]{:S(2)}) collective-permute-start(f32[88,128]{1,0:T(8,128)S(1)} %get-tuple-element.43), channel_id=1, source_target_pairs={{0,12},{4,0},{8,4},{12,8},{1,13},{5,1},{9,5},{13,9},{2,14},{6,2},{... | collective-permute-start | bytes 135176 | tf_op jit(solution)/shard_map/ppermute | solution.py:957
  22.9 0.0 collective-permute-start.6
  22.9 0.6 %collective-permute-start.5 = (f32[88,128]{1,0:T(8,128)S(1)}, f32[88,128]{1,0:T(8,128)S(1)}, u32[]{:S(2)}, u32[]{:S(2)}) collective-permute-start(f32[88,128]{1,0:T(8,128)S(1)} %get-tuple-element.43), channel_id=1, source_target_pairs={{0,4},{4,8},{8,12},{12,0},{1,5},{5,9},{9,13},{13,1},{2,6},{6,10},{... | collective-permute-start | bytes 135176 | tf_op jit(solution)/shard_map/ppermute | solution.py:957
  23.5 0.0 copy-start.1
  23.5 0.7 %copy-done.1 = s32[32]{0:T(128)S(1)} copy-done((s32[32]{0:T(128)S(1)}, s32[32]{0:T(128)}, u32[]{:S(2)}) %copy-start.1) | copy-done | bytes 152
  24.1 3.4 %source_part.1 = (f32[512,128]{1,0:T(8,128)S(1)}, f32[512,128]{1,0:T(8,128)S(1)}, f32[8,128]{1,0:T(8,128)S(1)}) custom-call(f32[640,128]{1,0:T(8,128)S(1)} %get-tuple-element.44.bm, f32[640,128]{1,0:T(8,128)S(1)} %get-tuple-element.45.be, f32[8,40,128]{2,1,0:T(8,128)S(1)} %get-tuple-element.46.rows_n, f32[8,40,128]{2,1,0:T(8,128)S(1)} %get-tuple-element.47.rows_p, ...), custom_call_target="tpu_custom_call" | custom-call | flops 12000000 | bytes 12000000 | tf_op jit(solution)/shard_map/source_part/pallas_call | solution.py:1050
  27.5 0.0 collective-permute-done.7
  27.5 0.3 collective-permute-done.6
  27.9 0.9 %collective-permute-done.5 = f32[88,128]{1,0:T(8,128)S(1)} collective-permute-done((f32[88,128]{1,0:T(8,128)S(1)}, f32[88,128]{1,0:T(8,128)S(1)}, u32[]{:S(2)}, u32[]{:S(2)}) %collective-permute-start.5) | collective-permute-done | bytes 45088 | tf_op jit(solution)/shard_map/ppermute | solution.py:957
  28.8 0.1 collective-permute-start.9
  28.9 0.3 compact.1
  29.2 0.9 %collective-permute-start.8 = (f32[168,128]{1,0:T(8,128)S(1)}, f32[168,128]{1,0:T(8,128)S(1)}, u32[]{:S(2)}, u32[]{:S(2)}) collective-permute-start(f32[168,128]{1,0:T(8,128)S(1)} %compact.1), channel_id=1, source_target_pairs={{0,2},{2,0},{1,3},{3,1},{4,6},{6,4},{5,7},{7,5},{8,10},{10,8},{9,1... | collective-permute-start | bytes 258056 | tf_op jit(solution)/shard_map/ppermute | solution.py:957
  30.1 4.0 %collective-permute-done.8.refs_1_ = f32[168,128]{1,0:T(8,128)S(1)} collective-permute-done((f32[168,128]{1,0:T(8,128)S(1)}, f32[168,128]{1,0:T(8,128)S(1)}, u32[]{:S(2)}, u32[]{:S(2)}) %collective-permute-start.8) | collective-permute-done | bytes 86048 | tf_op jit(solution)/shard_map/ppermute | solution.py:957
  34.2 0.0 collective-permute-start.10
  34.2 1.3 %collective-permute-done.10.refs_3_ = f32[168,128]{1,0:T(8,128)S(1)} collective-permute-done((f32[168,128]{1,0:T(8,128)S(1)}, f32[168,128]{1,0:T(8,128)S(1)}, u32[]{:S(2)}, u32[]{:S(2)}) %collective-permute-start.10) | collective-permute-done | bytes 86048 | tf_op jit(solution)/shard_map/ppermute | solution.py:957
  35.4 0.0 collective-permute-done.9.refs_2_
  35.4 5.2 %solve.1 = (f32[512,128]{1,0:T(8,128)}, f32[512,128]{1,0:T(8,128)}, f32[1,2]{1,0:T(1,128)}) custom-call(f32[4,88,128]{2,1,0:T(8,128)S(1)} %pad_maximum_fusion.blocks.refs_0_, f32[168,128]{1,0:T(8,128)S(1)} %collective-permute-done.8.refs_1_, f32[4,88,128]{2,1,0:T(8,128)S(1)} %collective-permute-done.9.refs_2_, ...), custom_call_target="tpu_custom_call" | custom-call | tf_op jit(solution)/shard_map/solve/pallas_call | solution.py:1085
  (1 shorter events, 0.0 us)
Async XLA Ops:
  2.3 6.2 %collective-permute-start = (f32[12,16,128]{2,1,0:T(8,128)S(1)}, f32[12,16,128]{2,1,0:T(8,128)S(1)}, u32[]{:S(2)}, u32[]{:S(2)}) collective-permute-start(f32[12,16,128]{2,1,0:T(8,128)S(1)} %get-tuple-element.35), channel_id=1, source_target_pairs={{0,1},{1,0},{2,3},{3,2},{4,5},{5,4},{6,7},{7,6},{8,9},{9,8},{10,11... | collective-permute-start | bytes 294920 | tf_op jit(solution)/shard_map/ppermute | solution.py:957
  2.8 5.6 %collective-permute-start.1 = (f32[4,16,128]{2,1,0:T(8,128)S(1)}, f32[4,16,128]{2,1,0:T(8,128)S(1)}, u32[]{:S(2)}, u32[]{:S(2)}) collective-permute-start(f32[4,16,128]{2,1,0:T(8,128)S(1)} %get-tuple-element.36), channel_id=1, source_target_pairs={{0,2},{2,0},{1,3},{3,1},{4,6},{6,4},{5,7},{7,5},{8,10},{10,8},{9,1... | collective-permute-start | bytes 98312 | tf_op jit(solution)/shard_map/ppermute | solution.py:957
  5.4 3.1 %collective-permute-start.2 = (f32[16,128]{1,0:T(8,128)S(1)}, f32[16,128]{1,0:T(8,128)S(1)}, u32[]{:S(2)}, u32[]{:S(2)}) collective-permute-start(f32[16,128]{1,0:T(8,128)S(1)} %get-tuple-element.37), channel_id=1, source_target_pairs={{0,3},{1,2},{2,1},{3,0},{4,7},{5,6},{6,5},{7,4},{8,11},{9,10},{10,... | collective-permute-start | bytes 24584 | tf_op jit(solution)/shard_map/ppermute | solution.py:963
  9.3 9.0 %collective-permute-start.3 = (f32[184,128]{1,0:T(8,128)S(1)}, f32[184,128]{1,0:T(8,128)S(1)}, u32[]{:S(2)}, u32[]{:S(2)}) collective-permute-start(f32[184,128]{1,0:T(8,128)S(1)} %get-tuple-element.39), channel_id=1, source_target_pairs={{0,12},{4,0},{8,4},{12,8},{1,13},{5,1},{9,5},{13,9},{2,14},{6,2},{... | collective-permute-start | bytes 282632 | tf_op jit(solution)/shard_map/ppermute | solution.py:957
  12.9 6.4 %collective-permute-start.4 = (f32[184,128]{1,0:T(8,128)S(1)}, f32[184,128]{1,0:T(8,128)S(1)}, u32[]{:S(2)}, u32[]{:S(2)}) collective-permute-start(f32[184,128]{1,0:T(8,128)S(1)} %get-tuple-element.40), channel_id=1, source_target_pairs={{0,4},{4,8},{8,12},{12,0},{1,5},{5,9},{9,13},{13,1},{2,6},{6,10},{... | collective-permute-start | bytes 282632 | tf_op jit(solution)/shard_map/ppermute | solution.py:957
  12.9 6.4 %copy-start = (s32[1,16,128]{2,1,0:T(8,128)S(1)}, s32[1,16,128]{2,1,0:T(8,128)}, u32[]{:S(2)}) copy-start(s32[1,16,128]{2,1,0:T(8,128)} %ids.1) | copy-start | bytes 24580
  20.0 7.5 %collective-permute-start.7 = (f32[88,128]{1,0:T(8,128)S(1)}, f32[88,128]{1,0:T(8,128)S(1)}, u32[]{:S(2)}, u32[]{:S(2)}) collective-permute-start(f32[88,128]{1,0:T(8,128)S(1)} %get-tuple-element.43), channel_id=1, source_target_pairs={{0,12},{4,0},{8,4},{12,8},{1,13},{5,1},{9,5},{13,9},{2,14},{6,2},{... | collective-permute-start | bytes 135176 | tf_op jit(solution)/shard_map/ppermute | solution.py:957
  22.9 4.9 %collective-permute-start.6 = (f32[88,128]{1,0:T(8,128)S(1)}, f32[88,128]{1,0:T(8,128)S(1)}, u32[]{:S(2)}, u32[]{:S(2)}) collective-permute-start(f32[88,128]{1,0:T(8,128)S(1)} %get-tuple-element.43), channel_id=1, source_target_pairs={{0,8},{4,12},{8,0},{12,4},{1,9},{5,13},{9,1},{13,5},{2,10},{6,14},... | collective-permute-start | bytes 135176 | tf_op jit(solution)/shard_map/ppermute | solution.py:957
  22.9 5.8 %collective-permute-start.5 = (f32[88,128]{1,0:T(8,128)S(1)}, f32[88,128]{1,0:T(8,128)S(1)}, u32[]{:S(2)}, u32[]{:S(2)}) collective-permute-start(f32[88,128]{1,0:T(8,128)S(1)} %get-tuple-element.43), channel_id=1, source_target_pairs={{0,4},{4,8},{8,12},{12,0},{1,5},{5,9},{9,13},{13,1},{2,6},{6,10},{... | collective-permute-start | bytes 135176 | tf_op jit(solution)/shard_map/ppermute | solution.py:957
  23.5 0.7 %copy-start.1 = (s32[32]{0:T(128)S(1)}, s32[32]{0:T(128)}, u32[]{:S(2)}) copy-start(s32[32]{0:T(128)} %param.11) | copy-start | bytes 388
  28.8 6.7 %collective-permute-start.9 = (f32[4,88,128]{2,1,0:T(8,128)S(1)}, f32[4,88,128]{2,1,0:T(8,128)S(1)}, u32[]{:S(2)}, u32[]{:S(2)}) collective-permute-start(f32[4,88,128]{2,1,0:T(8,128)S(1)} %pad_maximum_fusion.blocks.refs_0_), channel_id=1, source_target_pairs={{0,1},{1,0},{2,3},{3,2},{4,5},{5,4},{6,7},{7,6},{8,9},{9,8},{10,11... | collective-permute-start | bytes 540680 | tf_op jit(solution)/shard_map/ppermute | solution.py:957
  29.2 5.0 %collective-permute-start.8 = (f32[168,128]{1,0:T(8,128)S(1)}, f32[168,128]{1,0:T(8,128)S(1)}, u32[]{:S(2)}, u32[]{:S(2)}) collective-permute-start(f32[168,128]{1,0:T(8,128)S(1)} %compact.1), channel_id=1, source_target_pairs={{0,2},{2,0},{1,3},{3,1},{4,6},{6,4},{5,7},{7,5},{8,10},{10,8},{9,1... | collective-permute-start | bytes 258056 | tf_op jit(solution)/shard_map/ppermute | solution.py:957
  34.2 1.3 %collective-permute-start.10 = (f32[168,128]{1,0:T(8,128)S(1)}, f32[168,128]{1,0:T(8,128)S(1)}, u32[]{:S(2)}, u32[]{:S(2)}) collective-permute-start(f32[168,128]{1,0:T(8,128)S(1)} %collective-permute-done.8.refs_1_), channel_id=1, source_target_pairs={{0,1},{1,0},{2,3},{3,2},{4,5},{5,4},{6,7},{7,6},{8,9},{9,8},{10,11... | collective-permute-start | bytes 258056 | tf_op jit(solution)/shard_map/ppermute | solution.py:957

commit v8 on v7

--- a/solution.py
+++ b/solution.py
@@ -107,8 +107,8 @@
     targets = (fields[0], fields[1], whole_mask, fields[3])
     copies = []
     for a, (src, dst) in enumerate(zip((adj, ion, mask, mis), targets)):
-        part = cells // 2
-        for k in range(2):
+        part = cells // 4
+        for k in range(4):
             spot = pl.ds(k * part, part)
             copies.append(pltpu.make_async_copy(src.at[spot], dst.at[spot], sems.at[a, k]))
             copies[-1].start()
@@ -118,8 +118,8 @@
     turns = [jnp.where(length == 0, H, 0)] if n_dir == 1 else [H, 0]
     corner = [jnp.zeros((C, LANES), F32) for _ in range(n_dir)]
     for a in (0, 1, 3, 2):
-        copies[2 * a].wait()
-        copies[2 * a + 1].wait()
+        for k in range(4):
+            copies[4 * a + k].wait()
         if a == 2:
             fields[2][...] = whole_mask[...].astype(F32)
         ref = fields[a]
@@ -324,12 +324,12 @@
             set_plane(xe[a], here + p, C, rim(packed, H * (first + p)))
 
 
-def sector(n_len, n_wall, C, *refs):
+def sector(n_len, n_wall, C, electrodes, *refs):
     n_dir = 1 if n_len == 2 else 2
     raw, wall_in, refs = refs[:4], refs[4], refs[5:]
     strips, corners, refs = refs[:n_dir], refs[n_dir : 2 * n_dir], refs[2 * n_dir :]
-    qm, bm, be, coarse, surface, qe, pairs = refs[:7]
-    xm, xe = refs[7:11], refs[11:15]
+    owner, qm, bm, be, coarse, surface, patches, qe, pairs = refs[:9]
+    xm, xe = refs[9:13], refs[13:17]
     assemble(n_len, C, raw, wall_in, strips, corners, xm, xe)
     N = qm.shape[0] // C
     W = N - 2 * H
@@ -386,6 +386,14 @@
     half = W * C // 8
     z = pairs[pl.ds(0, 2 * half, stride=2), :] + pairs[pl.ds(1, 2 * half, stride=2), :]
     coarse[...] = halved(z[:half], z[half:])
+
+    blk = lax.axis_index("blk")
+    me = (blk * n_len + length) * n_wall + wall
+    which = lax.broadcasted_iota(jnp.int32, (1, electrodes), 1).astype(F32)
+    mine = owner[...] == me
+    patches[0:1, :] = jnp.full((1, LANES), jnp.min(jnp.where(mine, which, float(electrodes))))
+    patches[1:2, :] = jnp.full((1, LANES), jnp.max(jnp.where(mine, which, -1.0)))
+    patches[2:8, :] = jnp.zeros((6, LANES), F32)
 
 
 def unpacked(ref, n_len, length, N):
@@ -498,11 +506,10 @@
         message[half + C + t : half + C + t + 1, :] = totals[0:1, t * LANES : (t + 1) * LANES]
 
 
-def source_part(n_blk, n_len, n_wall, C, electrodes, bm, be, rows_n, rows_p, qm, mask, owner, base_adj, base_pot, *rest):
-    patches, fm, fe, tm, te, hp = rest
+def source_part(n_len, n_wall, C, bm, be, rows_n, rows_p, qm, mask, base_adj, base_pot, fm, fe, tm, te, hp):
     N = bm.shape[0] // C
     W = N - 2 * H
-    blk, length, wall = lax.axis_index("blk"), lax.axis_index("len"), lax.axis_index("wall")
+    length, wall = lax.axis_index("len"), lax.axis_index("wall")
     fm[...] = bm[...]
     fe[...] = be[...]
     for rows, near, second in ((rows_n, C - 1, C - 2), (rows_p, 0, 1)):
@@ -551,13 +558,6 @@
         set_plane(base_pot, w, C, m)
 
     loop(0, W, finish, 2)
-
-    me = (blk * n_len + length) * n_wall + wall
-    which = lax.broadcasted_iota(jnp.int32, (1, electrodes), 1).astype(F32)
-    mine = owner[...] == me
-    patches[0:1, :] = jnp.full((1, LANES), jnp.min(jnp.where(mine, which, float(electrodes))))
-    patches[1:2, :] = jnp.full((1, LANES), jnp.max(jnp.where(mine, which, -1.0)))
-    patches[2:8, :] = jnp.zeros((6, LANES), F32)
 
 
 def halves(shape):
@@ -831,69 +831,74 @@
         def spread(tile):
             return precise(tile, take_m), precise(tile, take_e)
 
-    picks = (row8 // 2, H + row8 // 2, jnp.where(row8 < H, row8 // 2, H + row8 // 2))
+    picks = (row8 // 2, H + row8 // 2)
+    ends = jnp.where(row8 < H, 6 + row8 // 2, row8 // 2 - 2)
 
     def fine_rows(q):
         own = spread(plane(near, 2 * q, C1))
         beside = spread(plane(near, 2 * q + 1, C1))
         for out, a, b in ((pm, own[0], beside[0]), (pe, own[1], beside[1])):
-            parts = (rows_at(a, picks[0]), rows_at(a, picks[1]), rows_at(b, picks[2]))
-            set_plane(out, q, R, jnp.concatenate(parts, 0))
+            parts = (jnp.where(row8 < 6, a, b), a, jnp.where(row8 < 2, b, a))
+            index = (ends, 2 + row8 // 2, ends)
+            for k in range(3):
+                out[pl.ds(pl.multiple_of(8 + R * q + 8 * k, 8), 8), :] = rows_at(parts[k], index[k])
 
     loop(0, Q, fine_rows, min(often, 6))
+    for ref in (pm, pe):
+        ref[0:8, :] = jnp.zeros((8, LANES), F32)
+        ref[8 + R * Q : 16 + R * Q, :] = jnp.zeros((8, LANES), F32)
     coef, k0 = level_coef(0), level_step(0)
-    rim = rim_lanes(lane_of((C, LANES)), length, n_len)
-
-    def rows_beside(x):
-        return pltpu.roll(x, 1, 0) + pltpu.roll(x, x.shape[0] - 1, 0)
+    def fine(ref, t, by=0, count=R):
+        return ref[pl.ds(8 + R * t + by, count), :]
 
     def coarse_terms(q):
-        m, e = plane(pm, q, R), plane(pe, q, R)
-        lm, le = beside_lanes(m, e)
-        gm = (1.0 - OMEGA) * m + k0 * (coef[0] * m + coef[1] * rows_beside(m) + coef[2] * lm)
-        ge = (1.0 - OMEGA) * e + k0 * (coef[0] * e + coef[1] * rows_beside(e) + coef[2] * le)
-        return gm, ge[:C]
+        out = []
+        sides = beside_lanes(fine(pm, q), fine(pe, q))
+        for ref, l in zip((pm, pe), sides):
+            x = fine(ref, q)
+            c = fine(ref, q, -1) + fine(ref, q, 1)
+            out.append((1.0 - OMEGA) * x + k0 * (coef[0] * x + coef[1] * c + coef[2] * l))
+        return out
 
     ks = k0 * coef[0]
 
+    def set_fine(ref, t, value):
+        ref[pl.ds(pl.multiple_of(8 + R * t, 8), R), :] = value
+
     def put_end(t, q, other, ok):
-        set_plane(tm, t, R, jnp.where(ok, coarse_terms(q)[0] + ks * plane(pm, other, R), 0.0))
+        set_fine(tm, t, jnp.where(ok, coarse_terms(q)[0] + ks * fine(pm, other), 0.0))
 
     put_end(0, 0, 1, wall > 0)
     put_end(W + 1, Q - 1, Q - 2, wall < n_wall - 1)
+    rim = rim_lanes(lane_of((R, LANES)), length, n_len)
 
     def level0(q):
         gm, ge = coarse_terms(q)
         for t, other in ((2 * q - 1, q - 1), (2 * q, q + 1)):
-            m = gm + ks * plane(pm, other, R)
-            set_plane(tm, t, R, m)
-            set_plane(te, t - 1, C, jnp.where(rim, ge + ks * plane(pe, other, R)[:C], 0.0))
-            set_plane(pot_out, t - 1, C, plane(base_pot, t - 1, C) + m[:C])
+            set_fine(tm, t, gm + ks * fine(pm, other))
+            set_fine(te, t, jnp.where(rim, ge + ks * fine(pe, other), 0.0))
+
+    loop(1, 1 + W1, level0, 4)
 
     def finish0(w):
-        m, e = plane(tm, w + 1, R), plane(te, w, C)
-        cm = rows_beside(m)[:C]
-        m = m[:C]
-        wm = plane(tm, w, R)[:C] + plane(tm, w + 2, R)[:C]
+        t = w + 1
+        m, e = fine(tm, t, H, C), fine(te, t, H, C)
+        cm = fine(tm, t, H - 1, C) + fine(tm, t, H + 1, C)
+        wm = fine(tm, t - 1, H, C) + fine(tm, t + 1, H, C)
         lm = beside_lanes_main(m, e)
         moved = 2.0 * sum(SI) * m - SI[0] * wm - SI[1] * cm - SI[2] * lm
         set_plane(adj_out, w, C, plane(base_adj, w, C) - DT * plane(mask, w, C) * moved)
+        set_plane(pot_out, w, C, plane(base_pot, w, C) + m)
 
     parts = 2
     size = W // parts
     copies = []
-
-    def send(src, dst, k, sem):
-        spot = pl.ds(k * size * C, size * C)
-        copies.append(pltpu.make_async_copy(src.at[spot], dst.at[spot], sem))
-        copies[-1].start()
-
-    for k in range(parts):
-        loop(1 + k * W1 // parts, 1 + (k + 1) * W1 // parts, level0, 4)
-        send(pot_out, potential, k, sems.at[0, k])
     for k in range(parts):
         loop(k * size, (k + 1) * size, finish0, 4)
-        send(adj_out, adj_prev, k, sems.at[1, k])
+        spot = pl.ds(k * size * C, size * C)
+        for n, (src, dst) in enumerate(((adj_out, adj_prev), (pot_out, potential))):
+            copies.append(pltpu.make_async_copy(src.at[spot], dst.at[spot], sems.at[n, k]))
+            copies[-1].start()
 
     NC, NL = sheet.shape[1:]
 
@@ -1001,7 +1006,7 @@
         + [((sum(FACES), C, L), vmem)]
         + [((4, C, L), vmem)] * n_dir
         + [((C, L), vmem)] * n_dir,
-        [pltpu.VMEM(own, jnp.int32), pltpu.SemaphoreType.DMA((4, 2))],
+        [pltpu.VMEM(own, jnp.int32), pltpu.SemaphoreType.DMA((4, 4))],
         "faces",
         room=52.75,
     )(*raw))[:5]
@@ -1025,14 +1030,14 @@
     )(*fields, *halos)
     from_next = ring(to_prev, "blk", -1)
     from_prev = ring(to_next, "blk", 1)
-    qm, bm, be, coarse, surface = call(
-        functools.partial(sector, n_len, n_wall, C),
-        [vmem] * (5 + 2 * n_dir),
-        [(field, vmem)] * 3 + [((cells // 8, L), vmem), ((C, L), vmem)],
+    qm, bm, be, coarse, surface, patches = call(
+        functools.partial(sector, n_len, n_wall, C, electrodes),
+        [vmem] * (6 + 2 * n_dir),
+        [(field, vmem)] * 3 + [((cells // 8, L), vmem), ((C, L), vmem), ((8, L), vmem)],
         [field, (cells // 2, L)] + [field] * 8,
         "sector",
         work=16 * 10**6,
-    )(*fields, *halos)
+    )(*fields, *halos, owner_map.reshape(1, electrodes))
 
     rows = (8, N, L)
     wide = LANES * ((electrodes + LANES - 1) // LANES)
@@ -1047,14 +1052,14 @@
 
     relative = n_blk <= 4
     moved = [ring(mine, "blk", d) for d in range(1, n_blk)] if relative else [lax.all_gather(mine, "blk")]
-    base_adj, base_pot, patches = call(
-        functools.partial(source_part, n_blk, n_len, n_wall, C, electrodes),
-        [vmem] * 7,
-        [(own, vmem), (own, vmem), ((8, L), vmem)],
+    base_adj, base_pot = call(
+        functools.partial(source_part, n_len, n_wall, C),
+        [vmem] * 6,
+        [(own, vmem), (own, vmem)],
         [field] * 4 + [(2, N, L)],
         "source_part",
         work=12 * 10**6,
-    )(bm, be, rows_n, rows_p, qm, fields[2], owner_map.reshape(1, electrodes))
+    )(bm, be, rows_n, rows_p, qm, fields[2])
     moved, base_adj = lax.optimization_barrier((moved, base_adj))
     sector_blocks = jnp.stack([mine] + moved) if relative else moved[0]
     compacted = (n_blk, n_len, C, W) == (4, 2, 16, 32)
@@ -1066,6 +1071,7 @@
             [(W // 4, n_blk * C // 2, L), (W // 8 + 1, n_blk * C // 2, L)],
             "compact",
         )(sector_blocks)
+        brief, sector_blocks = lax.optimization_barrier((brief, sector_blocks))
         here = [sector_blocks, ring(brief, "len", 1)]
     elif n_len == 2:
         here = [sector_blocks, ring(sector_blocks, "len", 1)]
@@ -1078,9 +1084,9 @@
     planes = n_wall * W // 2
     grids = [(planes // k + 2, NC1, NL1) for k in (1, 1, 2, 2, 4, 4)]
     Q = W // 2 + 2
-    tall = (Q * (C + 8), L)
-    taller = ((W + 2) * (C + 8), L)
-    scratch = grids + [(Q * C, NL1), tall, tall, taller, own, own, own]
+    tall = (Q * (C + 8) + 16, L)
+    taller = ((W + 2) * (C + 8) + 16, L)
+    scratch = grids + [(Q * C, NL1), tall, tall, taller, taller, own, own]
     scratch += [(2, n_blk * C, n_len * L), (2, 48, L), pltpu.SemaphoreType.DMA((2, 2))]
     adj_prev, potential, patch_grad = call(
         functools.partial(solve, (n_blk, n_len, n_wall), relative, compacted, C, W),

time: 40.8 us -> 40.9 us (level)
  transfers between devices with their start and end apart: 11 -> 11, of which waited for: 6 -> 6; matrix products, arithmetic and copies ran while one was open for 0% -> 0% of each run, Pallas kernels for 22% -> 21%
where the time goes in v8:
time: 40.9 us; the launch traced here: 40.7 us
  Pallas kernels  17.4 us (43%)
  starting transfers between devices  11.3 us (28%)
  waiting for transfers between devices  10.6 us (26%)
  between operations  0.7 us (2%)
  local copies, waits for them, and re-layouts  0.66 us (2%)
    ppermute x10, starting transfers between devices, ring(): return lax.ppermute(x, axis, [(i, (i + by) % count) for i in range(count)])  11.3 us
    ppermute x10, waiting for transfers between devices, ring(): return lax.ppermute(x, axis, [(i, (i + by) % count) for i in range(count)])  7.6 us
    pallas_call x1, Pallas kernels, body(): call(functools.partial(sector, n_len, n_wall, C, electrodes), [vmem] * (6...  5.41 us
    pallas_call x1, Pallas kernels, body(): call(functools.partial(solve, (n_blk, n_len, n_wall), relative, compacted...  5.28 us
    pallas_call x1, Pallas kernels, body(): call(functools.partial(source_part, n_len, n_wall, C), [vmem] * 6, [(own,...  3.24 us
    ppermute x1, waiting for transfers between devices, across(): return lax.ppermute(x, ('len', 'wall'), pairs)  3.01 us
    pallas_call x1, Pallas kernels, body(): call(functools.partial(pack_faces, n_len), ['hbm'] * 4, [(own, vmem)] * 4...  1.67 us
  transfers between devices with their start and end apart: 11, of which 6 were waited for; matrix products, arithmetic and copies ran while one was open for 0% of the time, Pallas kernels for 21%

profile of v8, /device:TPU:0, one launch (start us, length us, event | category | flops | bytes accessed | tf_op | source)
XLA Modules:
  0.0 40.7 jit_solution(153839697036432963)
XLA Ops:
  0.6 1.7 %faces.1 = (f32[512,128]{1,0:T(8,128)S(1)}, f32[512,128]{1,0:T(8,128)S(1)}, f32[512,128]{1,0:T(8,128)S(1)}, f32[512,128]{1,0:T(8,128)S(1)}, f32[12,16,128]{2,1,0...) custom-call(f32[512,128]{1,0:T(8,128)} %bitcast.13, f32[512,128]{1,0:T(8,128)} %bitcast.14, ...), custom_call_target="tpu_custom_call" | custom-call | tf_op jit(solution)/shard_map/faces/pallas_call | solution.py:1002
  2.3 0.5 %collective-permute-start = (f32[12,16,128]{2,1,0:T(8,128)S(1)}, f32[12,16,128]{2,1,0:T(8,128)S(1)}, u32[]{:S(2)}, u32[]{:S(2)}) collective-permute-start(f32[12,16,128]{2,1,0:T(8,128)S(1)} %get-tuple-element.37), channel_id=1, source_target_pairs={{0,1},{1,0},{2,3},{3,2},{4,5},{5,4},{6,7},{7,6},{8,9},{9,8},{10,11... | collective-permute-start | bytes 294920 | tf_op jit(solution)/shard_map/ppermute | solution.py:962
  2.8 2.6 %collective-permute-start.1 = (f32[4,16,128]{2,1,0:T(8,128)S(1)}, f32[4,16,128]{2,1,0:T(8,128)S(1)}, u32[]{:S(2)}, u32[]{:S(2)}) collective-permute-start(f32[4,16,128]{2,1,0:T(8,128)S(1)} %get-tuple-element.38), channel_id=1, source_target_pairs={{0,2},{2,0},{1,3},{3,1},{4,6},{6,4},{5,7},{7,5},{8,10},{10,8},{9,1... | collective-permute-start | bytes 98312 | tf_op jit(solution)/shard_map/ppermute | solution.py:962
  5.4 0.1 collective-permute-start.2
  5.5 3.0 %collective-permute-done.2.refs_6_ = f32[16,128]{1,0:T(8,128)S(1)} collective-permute-done((f32[16,128]{1,0:T(8,128)S(1)}, f32[16,128]{1,0:T(8,128)S(1)}, u32[]{:S(2)}, u32[]{:S(2)}) %collective-permute-start.2) | collective-permute-done | bytes 8224 | tf_op jit(solution)/shard_map/ppermute | solution.py:968
  8.5 0.0 collective-permute-done.1.refs_5_
  8.5 0.0 collective-permute-done.refs_4_
  8.5 0.8 %boundary.1 = (f32[184,128]{1,0:T(8,128)S(1)}, f32[184,128]{1,0:T(8,128)S(1)}, f32[2,6,40,128]{3,2,1,0:T(8,128)S(1)}) custom-call(f32[512,128]{1,0:T(8,128)S(1)} %get-tuple-element.33.refs_0_, f32[512,128]{1,0:T(8,128)S(1)} %get-tuple-element.34.refs_1_, f32[512,128]{1,0:T(8,128)S(1)} %get-tuple-element.35.refs_2_.mask.refs_6_, ...), custom_call_target="tpu_custom_call" | custom-call | tf_op jit(solution)/shard_map/boundary/pallas_call | solution.py:1024
  9.3 3.7 %collective-permute-start.3 = (f32[184,128]{1,0:T(8,128)S(1)}, f32[184,128]{1,0:T(8,128)S(1)}, u32[]{:S(2)}, u32[]{:S(2)}) collective-permute-start(f32[184,128]{1,0:T(8,128)S(1)} %get-tuple-element.41), channel_id=1, source_target_pairs={{0,12},{4,0},{8,4},{12,8},{1,13},{5,1},{9,5},{13,9},{2,14},{6,2},{... | collective-permute-start | bytes 282632 | tf_op jit(solution)/shard_map/ppermute | solution.py:962
  12.9 0.0 copy-start.1
  12.9 0.0 collective-permute-start.4
  12.9 0.7 %copy-done.1 = s32[32]{0:T(128)S(1)} copy-done((s32[32]{0:T(128)S(1)}, s32[32]{0:T(128)}, u32[]{:S(2)}) %copy-start.1) | copy-done | bytes 152
  13.6 0.0 copy-start
  13.6 5.4 %sector.1 = (f32[640,128]{1,0:T(8,128)S(1)}, f32[640,128]{1,0:T(8,128)S(1)}, f32[640,128]{1,0:T(8,128)S(1)}, f32[64,128]{1,0:T(8,128)S(1)}, f32[16,128]{1,0:T(8,128)S(1)}, /*index=5*/f32[8,128]{1,0:T(8,128)S(1)}) custom-call(f32[512,128]{1,0:T(8,128)S(1)} %get-tuple-element.33.refs_0_, f32[512,128]{1,0:T(8,128)S(1)} %get-tuple-element.34.refs_1_, ...), custom_call_target="tpu_custom_call" | custom-call | flops 16000000 | bytes 16000000 | tf_op jit(solution)/shard_map/sector/pallas_call | solution.py:1033
  19.0 0.0 collective-permute-done.3.from_next
  19.0 0.3 collective-permute-done.4.from_prev
  19.3 0.0 copy-done
  19.3 0.7 %correct.1 = (f32[8,40,128]{2,1,0:T(8,128)S(1)}, f32[8,40,128]{2,1,0:T(8,128)S(1)}, f32[88,128]{1,0:T(8,128)S(1)}) custom-call(f32[2,6,40,128]{3,2,1,0:T(8,128)S(1)} %get-tuple-element.40.own_rows, f32[184,128]{1,0:T(8,128)S(1)} %collective-permute-done.3.from_next, f32[184,128]{1,0:T(8,128)S(1)} %collective-permute-done.4.from_prev, ...), custom_call_target="tpu_custom_call" | custom-call | tf_op jit(solution)/shard_map/correct/pallas_call | solution.py:1045
  20.1 2.9 %collective-permute-start.7 = (f32[88,128]{1,0:T(8,128)S(1)}, f32[88,128]{1,0:T(8,128)S(1)}, u32[]{:S(2)}, u32[]{:S(2)}) collective-permute-start(f32[88,128]{1,0:T(8,128)S(1)} %get-tuple-element.45), channel_id=1, source_target_pairs={{0,12},{4,0},{8,4},{12,8},{1,13},{5,1},{9,5},{13,9},{2,14},{6,2},{... | collective-permute-start | bytes 135176 | tf_op jit(solution)/shard_map/ppermute | solution.py:962
  23.0 0.0 collective-permute-start.6
  23.0 0.6 %collective-permute-start.5 = (f32[88,128]{1,0:T(8,128)S(1)}, f32[88,128]{1,0:T(8,128)S(1)}, u32[]{:S(2)}, u32[]{:S(2)}) collective-permute-start(f32[88,128]{1,0:T(8,128)S(1)} %get-tuple-element.45), channel_id=1, source_target_pairs={{0,4},{4,8},{8,12},{12,0},{1,5},{5,9},{9,13},{13,1},{2,6},{6,10},{... | collective-permute-start | bytes 135176 | tf_op jit(solution)/shard_map/ppermute | solution.py:962
  23.6 3.2 %source_part.1 = (f32[512,128]{1,0:T(8,128)S(1)}, f32[512,128]{1,0:T(8,128)S(1)}) custom-call(f32[640,128]{1,0:T(8,128)S(1)} %get-tuple-element.46.bm, f32[640,128]{1,0:T(8,128)S(1)} %get-tuple-element.47.be, f32[8,40,128]{2,1,0:T(8,128)S(1)} %get-tuple-element.48.rows_n, f32[8,40,128]{2,1,0:T(8,128)S(1)} %get-tuple-element.49.rows_p, ...), custom_call_target="tpu_custom_call" | custom-call | flops 12000000 | bytes 12000000 | tf_op jit(solution)/shard_map/source_part/pallas_call | solution.py:1055
  26.8 0.0 collective-permute-done.7
  26.8 1.1 %collective-permute-done.6 = f32[88,128]{1,0:T(8,128)S(1)} collective-permute-done((f32[88,128]{1,0:T(8,128)S(1)}, f32[88,128]{1,0:T(8,128)S(1)}, u32[]{:S(2)}, u32[]{:S(2)}) %collective-permute-start.6) | collective-permute-done | bytes 45088 | tf_op jit(solution)/shard_map/ppermute | solution.py:962
  27.9 0.9 %collective-permute-done.5 = f32[88,128]{1,0:T(8,128)S(1)} collective-permute-done((f32[88,128]{1,0:T(8,128)S(1)}, f32[88,128]{1,0:T(8,128)S(1)}, u32[]{:S(2)}, u32[]{:S(2)}) %collective-permute-start.5) | collective-permute-done | bytes 45088 | tf_op jit(solution)/shard_map/ppermute | solution.py:962
  28.9 0.3 compact.1
  29.2 0.1 collective-permute-start.9
  29.2 0.9 %collective-permute-start.8 = (f32[168,128]{1,0:T(8,128)S(1)}, f32[168,128]{1,0:T(8,128)S(1)}, u32[]{:S(2)}, u32[]{:S(2)}) collective-permute-start(f32[168,128]{1,0:T(8,128)S(1)} %compact.1), channel_id=1, source_target_pairs={{0,2},{2,0},{1,3},{3,1},{4,6},{6,4},{5,7},{7,5},{8,10},{10,8},{9,1... | collective-permute-start | bytes 258056 | tf_op jit(solution)/shard_map/ppermute | solution.py:962
  30.2 4.0 %collective-permute-done.8.refs_1_ = f32[168,128]{1,0:T(8,128)S(1)} collective-permute-done((f32[168,128]{1,0:T(8,128)S(1)}, f32[168,128]{1,0:T(8,128)S(1)}, u32[]{:S(2)}, u32[]{:S(2)}) %collective-permute-start.8) | collective-permute-done | bytes 86048 | tf_op jit(solution)/shard_map/ppermute | solution.py:962
  34.2 0.0 collective-permute-start.10
  34.2 1.3 %collective-permute-done.10.refs_3_ = f32[168,128]{1,0:T(8,128)S(1)} collective-permute-done((f32[168,128]{1,0:T(8,128)S(1)}, f32[168,128]{1,0:T(8,128)S(1)}, u32[]{:S(2)}, u32[]{:S(2)}) %collective-permute-start.10) | collective-permute-done | bytes 86048 | tf_op jit(solution)/shard_map/ppermute | solution.py:962
  35.5 0.0 collective-permute-done.9.refs_2_
  35.5 5.3 %solve.1 = (f32[512,128]{1,0:T(8,128)}, f32[512,128]{1,0:T(8,128)}, f32[1,2]{1,0:T(1,128)}) custom-call(f32[4,88,128]{2,1,0:T(8,128)S(1)} %pad_maximum_fusion.blocks.refs_0_, f32[168,128]{1,0:T(8,128)S(1)} %collective-permute-done.8.refs_1_, f32[4,88,128]{2,1,0:T(8,128)S(1)} %collective-permute-done.9.refs_2_, ...), custom_call_target="tpu_custom_call" | custom-call | tf_op jit(solution)/shard_map/solve/pallas_call | solution.py:1091
  (1 shorter events, 0.0 us)
Async XLA Ops:
  2.3 6.2 %collective-permute-start = (f32[12,16,128]{2,1,0:T(8,128)S(1)}, f32[12,16,128]{2,1,0:T(8,128)S(1)}, u32[]{:S(2)}, u32[]{:S(2)}) collective-permute-start(f32[12,16,128]{2,1,0:T(8,128)S(1)} %get-tuple-element.37), channel_id=1, source_target_pairs={{0,1},{1,0},{2,3},{3,2},{4,5},{5,4},{6,7},{7,6},{8,9},{9,8},{10,11... | collective-permute-start | bytes 294920 | tf_op jit(solution)/shard_map/ppermute | solution.py:962
  2.8 5.6 %collective-permute-start.1 = (f32[4,16,128]{2,1,0:T(8,128)S(1)}, f32[4,16,128]{2,1,0:T(8,128)S(1)}, u32[]{:S(2)}, u32[]{:S(2)}) collective-permute-start(f32[4,16,128]{2,1,0:T(8,128)S(1)} %get-tuple-element.38), channel_id=1, source_target_pairs={{0,2},{2,0},{1,3},{3,1},{4,6},{6,4},{5,7},{7,5},{8,10},{10,8},{9,1... | collective-permute-start | bytes 98312 | tf_op jit(solution)/shard_map/ppermute | solution.py:962
  5.4 3.1 %collective-permute-start.2 = (f32[16,128]{1,0:T(8,128)S(1)}, f32[16,128]{1,0:T(8,128)S(1)}, u32[]{:S(2)}, u32[]{:S(2)}) collective-permute-start(f32[16,128]{1,0:T(8,128)S(1)} %get-tuple-element.39), channel_id=1, source_target_pairs={{0,3},{1,2},{2,1},{3,0},{4,7},{5,6},{6,5},{7,4},{8,11},{9,10},{10,... | collective-permute-start | bytes 24584 | tf_op jit(solution)/shard_map/ppermute | solution.py:968
  9.3 9.7 %collective-permute-start.3 = (f32[184,128]{1,0:T(8,128)S(1)}, f32[184,128]{1,0:T(8,128)S(1)}, u32[]{:S(2)}, u32[]{:S(2)}) collective-permute-start(f32[184,128]{1,0:T(8,128)S(1)} %get-tuple-element.41), channel_id=1, source_target_pairs={{0,12},{4,0},{8,4},{12,8},{1,13},{5,1},{9,5},{13,9},{2,14},{6,2},{... | collective-permute-start | bytes 282632 | tf_op jit(solution)/shard_map/ppermute | solution.py:962
  12.9 0.7 %copy-start.1 = (s32[32]{0:T(128)S(1)}, s32[32]{0:T(128)}, u32[]{:S(2)}) copy-start(s32[32]{0:T(128)} %param.11) | copy-start | bytes 388
  12.9 6.4 %collective-permute-start.4 = (f32[184,128]{1,0:T(8,128)S(1)}, f32[184,128]{1,0:T(8,128)S(1)}, u32[]{:S(2)}, u32[]{:S(2)}) collective-permute-start(f32[184,128]{1,0:T(8,128)S(1)} %get-tuple-element.42), channel_id=1, source_target_pairs={{0,4},{4,8},{8,12},{12,0},{1,5},{5,9},{9,13},{13,1},{2,6},{6,10},{... | collective-permute-start | bytes 282632 | tf_op jit(solution)/shard_map/ppermute | solution.py:962
  13.6 5.7 %copy-start = (s32[1,16,128]{2,1,0:T(8,128)S(1)}, s32[1,16,128]{2,1,0:T(8,128)}, u32[]{:S(2)}) copy-start(s32[1,16,128]{2,1,0:T(8,128)} %ids.1) | copy-start | bytes 24580
  20.1 6.8 %collective-permute-start.7 = (f32[88,128]{1,0:T(8,128)S(1)}, f32[88,128]{1,0:T(8,128)S(1)}, u32[]{:S(2)}, u32[]{:S(2)}) collective-permute-start(f32[88,128]{1,0:T(8,128)S(1)} %get-tuple-element.45), channel_id=1, source_target_pairs={{0,12},{4,0},{8,4},{12,8},{1,13},{5,1},{9,5},{13,9},{2,14},{6,2},{... | collective-permute-start | bytes 135176 | tf_op jit(solution)/shard_map/ppermute | solution.py:962
  23.0 4.9 %collective-permute-start.6 = (f32[88,128]{1,0:T(8,128)S(1)}, f32[88,128]{1,0:T(8,128)S(1)}, u32[]{:S(2)}, u32[]{:S(2)}) collective-permute-start(f32[88,128]{1,0:T(8,128)S(1)} %get-tuple-element.45), channel_id=1, source_target_pairs={{0,8},{4,12},{8,0},{12,4},{1,9},{5,13},{9,1},{13,5},{2,10},{6,14},... | collective-permute-start | bytes 135176 | tf_op jit(solution)/shard_map/ppermute | solution.py:962
  23.0 5.8 %collective-permute-start.5 = (f32[88,128]{1,0:T(8,128)S(1)}, f32[88,128]{1,0:T(8,128)S(1)}, u32[]{:S(2)}, u32[]{:S(2)}) collective-permute-start(f32[88,128]{1,0:T(8,128)S(1)} %get-tuple-element.45), channel_id=1, source_target_pairs={{0,4},{4,8},{8,12},{12,0},{1,5},{5,9},{9,13},{13,1},{2,6},{6,10},{... | collective-permute-start | bytes 135176 | tf_op jit(solution)/shard_map/ppermute | solution.py:962
  29.2 6.3 %collective-permute-start.9 = (f32[4,88,128]{2,1,0:T(8,128)S(1)}, f32[4,88,128]{2,1,0:T(8,128)S(1)}, u32[]{:S(2)}, u32[]{:S(2)}) collective-permute-start(f32[4,88,128]{2,1,0:T(8,128)S(1)} %pad_maximum_fusion.blocks.refs_0_), channel_id=1, source_target_pairs={{0,1},{1,0},{2,3},{3,2},{4,5},{5,4},{6,7},{7,6},{8,9},{9,8},{10,11... | collective-permute-start | bytes 540680 | tf_op jit(solution)/shard_map/ppermute | solution.py:962
  29.2 4.9 %collective-permute-start.8 = (f32[168,128]{1,0:T(8,128)S(1)}, f32[168,128]{1,0:T(8,128)S(1)}, u32[]{:S(2)}, u32[]{:S(2)}) collective-permute-start(f32[168,128]{1,0:T(8,128)S(1)} %compact.1), channel_id=1, source_target_pairs={{0,2},{2,0},{1,3},{3,1},{4,6},{6,4},{5,7},{7,5},{8,10},{10,8},{9,1... | collective-permute-start | bytes 258056 | tf_op jit(solution)/shard_map/ppermute | solution.py:962
  34.2 1.3 %collective-permute-start.10 = (f32[168,128]{1,0:T(8,128)S(1)}, f32[168,128]{1,0:T(8,128)S(1)}, u32[]{:S(2)}, u32[]{:S(2)}) collective-permute-start(f32[168,128]{1,0:T(8,128)S(1)} %collective-permute-done.8.refs_1_), channel_id=1, source_target_pairs={{0,1},{1,0},{2,3},{3,2},{4,5},{5,4},{6,7},{7,6},{8,9},{9,8},{10,11... | collective-permute-start | bytes 258056 | tf_op jit(solution)/shard_map/ppermute | solution.py:962

commit v9 on v8

--- a/solution.py
+++ b/solution.py
@@ -565,7 +565,7 @@
     return lane, lane % (LANES // 2)
 
 
-def compact(C, W, blocks, out, sheet1, coarse2):
+def compact(C, W, blocks, out, wall_out, sheet1, coarse2):
     n_blk = blocks.shape[0]
     W1, C1 = W // 2, C // 2
     half, start, middle = W1 // 2, W1 // 2 * C1, LANES // 2
@@ -605,6 +605,13 @@
     for i in range(half):
         turned = pltpu.roll(sheet1[i], lax.rem(H * i - base + LANES, LANES), 1)
         beside = jnp.where(at // H == i, turned, beside)
+    index = lax.broadcasted_iota(jnp.int32, (8, LANES), 0) ^ 1
+    line = beside + jnp.concatenate([rows_at(beside[t : t + 8], index) for t in range(0, NC1, 8)], 0)
+    line = 0.125 * (line + pltpu.roll(line, LANES - H, 1))
+    m = lane - 96
+    spot = jnp.where(m < H, 8 * m, middle + 8 * (m - H)) + jnp.where(length == 0, H - 1, 0)
+    line = lanes_at(line, jnp.clip(spot, 0, LANES - 1))
+    beside = jnp.where(jnp.logical_and(m >= 0, m < 8), line, beside)
     out[32 : 32 + NC1, :] = beside
     face = coarse2[half // 2, pl.ds(0, rows2, stride=2), :]
     face = lanes_at(face, jnp.where(wall == 0, middle, 0) + 2 * (at2 % (middle // 2)))
@@ -613,6 +620,9 @@
     inner_surface = jnp.where(low, sheet1[0], pltpu.roll(sheet1[1], middle, 1))
     outer_surface = jnp.where(low, pltpu.roll(sheet1[half - 2], middle, 1), sheet1[half - 1])
     out[64 : 64 + NC1, :] = jnp.where(wall == 0, inner_surface, outer_surface)
+    wall_out[0:168, :] = out[...]
+    last = jnp.where(low, pltpu.roll(sheet1[half - 1], middle, 1), sheet1[half - 2])
+    wall_out[168 : 168 + NC1, :] = jnp.where(wall == 0, last, inner_surface)
 
 
 def around(x, by):
@@ -639,10 +649,10 @@
 
 def solve(sizes, relative, compacted, C, W, *refs):
     n_blk, n_len, n_wall = sizes
-    count = n_len * n_wall
+    count = n_len * n_wall + compacted
     blocks, refs = refs[:count], refs[count:]
     base_adj, base_pot, mask, patches, adj_prev, potential, patch_grad = refs[:7]
-    b1, x1, b2, x2, b3, x3, near, pm, pe, tm, te, adj_out, pot_out, sheet, both_walls, sems = refs[7:]
+    b1, x1, b2, x2, b3, x3, near, pm, pe, tm, te, adj_out, pot_out, sheet, briefs, sems = refs[7:]
     L = LANES
     W1, C1 = W // 2, C // 2
     planes, NC1, NL1 = b1.shape
@@ -687,47 +697,71 @@
 
             loop(0, n_blk, unpack, 4)
     if compacted:
+        stack, len_brief, wall_brief, both_brief, own_brief = blocks
         lane8 = lane_of((C1, LANES))
         here8 = lane8 // middle == length
+        here = lane_of((NC1, LANES)) // middle == length
         face_lane = jnp.where(length == 0, middle, middle - H)
         near8 = jnp.logical_and(lane8 >= face_lane, lane8 < face_lane + H)
-        for v in range(n_wall):
-            wall_s = wall_of(v)
-            own, other = blocks[2 * v], blocks[2 * v + 1]
-            for d in range(n_blk):
-                row = pl.multiple_of(C1 * blk_of(d), C1)
-                at = pl.ds(row, C1)
-                beside = other[pl.ds(32 + row, C1), :]
-                for i in range(half):
-                    a = own[d, i * C1 : (i + 1) * C1, :]
-                    b = pltpu.roll(a, middle, 1)
-                    for k, value in enumerate((jnp.where(length == 0, a, b), jnp.where(length == 0, b, a))):
-                        turn = lax.rem(face_lane - H * i - middle * k + 2 * LANES, LANES)
-                        rest = jnp.where(near8, pltpu.roll(beside, turn, 1), 0.0)
-                        b1[1 + wall_s * W1 + i + half * k, at, :] = jnp.where(here8, value, rest)
-            surface = other[64 : 64 + NC1, :]
-            turned = pltpu.roll(surface, middle, 1)
-            spot = jnp.where(wall_s == 0, 1, planes - 1)
-            here = lane_of((NC1, LANES)) // middle == length
-            b1[spot] = jnp.where(here, b1[spot], jnp.where(length == 0, turned, surface))
-            b1[spot + 1] = jnp.where(here, b1[spot + 1], jnp.where(length == 0, surface, turned))
+        at_face = jnp.logical_and(lane_of((NC1, LANES)) >= face_lane, lane_of((NC1, LANES)) < face_lane + H)
+        for d in range(n_blk):
+            row = pl.multiple_of(C1 * blk_of(d), C1)
+            beside = len_brief[pl.ds(32 + row, C1), :]
+            for i in range(half):
+                a = stack[d, i * C1 : (i + 1) * C1, :]
+                b = pltpu.roll(a, middle, 1)
+                for k, value in enumerate((jnp.where(length == 0, a, b), jnp.where(length == 0, b, a))):
+                    turn = lax.rem(face_lane - H * i - middle * k + 2 * LANES, LANES)
+                    rest = jnp.where(near8, pltpu.roll(beside, turn, 1), 0.0)
+                    b1[1 + wall * W1 + i + half * k, pl.ds(row, C1), :] = jnp.where(here8, value, rest)
+
+        def two_planes(tile):
+            turned = pltpu.roll(tile, middle, 1)
+            return jnp.where(length == 0, tile, turned), jnp.where(length == 0, turned, tile)
+
+        beyond = two_planes(wall_brief[168 : 168 + NC1, :])
+        beside = both_brief[32 : 32 + NC1, :]
         for k in range(2):
-            both_walls[k] = jnp.where(wall == k, blocks[1][0:48, :], blocks[3][0:48, :])
+            off = jnp.where(wall == 0, H * k, middle + H * (half - 1 - k))
+            rest = jnp.where(at_face, pltpu.roll(beside, lax.rem(face_lane - off + 2 * LANES, LANES), 1), 0.0)
+            b1[jnp.where(wall == 0, 1 + W1 + k, W1 - k)] = jnp.where(here, beyond[k], rest)
+        for k in range(2):
+            theirs = two_planes(len_brief[64 : 64 + NC1, :])[1 - k]
+            spot = jnp.where(wall == 0, 1, planes - 1) + k
+            b1[spot] = jnp.where(here, b1[spot], theirs)
+            ours = two_planes(wall_brief[64 : 64 + NC1, :])[k]
+            theirs = two_planes(both_brief[64 : 64 + NC1, :])[1 - k]
+            b1[jnp.where(wall == 0, planes - 1, 1) + k] = jnp.where(here, ours, theirs)
+        for k in range(2):
+            briefs[0, k] = jnp.where(wall == k, own_brief[0:64, :], wall_brief[0:64, :])
+            briefs[1, k] = jnp.where(wall == k, len_brief[0:64, :], both_brief[0:64, :])
         tile_lane8 = lane_of((8, LANES)) % middle // 2
         row_of_8 = lax.broadcasted_iota(jnp.int32, (8, LANES), 0) // 2
-
-        def widened(w, first, t, lane):
-            tile = both_walls[w, first + 8 * (t // 2) : first + 8 * (t // 2) + 8, :]
-            return lanes_at(rows_at(tile, 4 * (t % 2) + row_of_8), lane + tile_lane8)
-
-        for w2 in range(planes // 2):
-            w, q = divmod(w2, half)
-            high, q = divmod(q, half // 2)
+        here_8 = lane_of((8, LANES)) // middle == length
+        mine8 = lane_of((8, LANES)) // 2 == jnp.where(length == 0, middle // 2 - 1, middle // 2)
+        other8 = lane_of((8, LANES)) // 2 == jnp.where(length == 0, middle // 2, middle // 2 - 1)
+        coef1 = [level_step(1) * x for x in level_coef(1)]
+        tiles2 = {}
+
+        def widened(w, first, t, start):
+            key = (w, first, t)
+            if key not in tiles2:
+                at = first + 8 * (t // 2)
+                tiles2[key] = [rows_at(briefs[h, w, at : at + 8, :], 4 * (t % 2) + row_of_8) for h in range(2)]
+            return jnp.where(here_8, *[lanes_at(x, start + tile_lane8) for x in tiles2[key]])
+
+        for w in range(n_wall):
             for t in range(NC1 // 8):
-                value = widened(w, NC1 // 2 * (q // 2), t, middle // 2 * (q % 2) + middle * high)
-                if w2 in (half - 1, half):
-                    value = value + level_step(1) * level_coef(1)[0] * widened(1 - w, 32, t, middle // 2)
-                b2[1 + w2, 8 * t : 8 * t + 8, :] = value
+                lines = [briefs[h, w, 32 + 8 * t : 40 + 8 * t, :] for h in range(2)]
+                lines = jnp.where(lane_of((8, LANES)) < 104, lines[0], pltpu.roll(lines[1], 8, 1))
+                for k in range(half):
+                    high, q = divmod(k, half // 2)
+                    value = widened(w, NC1 // 2 * (q // 2), t, middle // 2 * (q % 2) + middle * high)
+                    index = jnp.where(mine8, 104 + k, jnp.where(other8, 96 + k, LANES - 1))
+                    value = value + coef1[2] * lanes_at(lines, index)
+                    if k == (half - 1 if w == 0 else 0):
+                        value = value + coef1[0] * widened(1 - w, 32, t, middle // 2)
+                    b2[1 + w * half + k, 8 * t : 8 * t + 8, :] = value
 
     def total_of(x, wsum, level, by):
         coef = level_coef(level)
@@ -743,14 +777,11 @@
         total = total_of(x, x_ref[i - 1] + x_ref[i + 1], level, 2 ** (level - 1))
         return (1.0 - OMEGA) * x + level_step(level) * b_ref[i] + total
 
-    lane1 = lane_of((NC1, NL1))
-    exact = jnp.logical_or(lane1 // middle == length, lane1 // 2 == jnp.where(length == 0, middle // 2, middle // 2 - 1))
-
     def down1(q):
-        value = 0.125 * twins(left_pair(b1, 2 * q + 1, 1), 1)
-        b2[1 + q] = jnp.where(exact, value, b2[1 + q]) if compacted else value
-
-    loop(0, planes // 2, down1, often)
+        b2[1 + q] = 0.125 * twins(left_pair(b1, 2 * q + 1, 1), 1)
+
+    if not compacted:
+        loop(0, planes // 2, down1, often)
 
     def down2(q):
         b3[1 + q] = 0.125 * twins(left_pair(b2, 2 * q + 1, 2), 2)
@@ -788,7 +819,12 @@
         x1[1 + 2 * q] = k1 * b1[1 + 2 * q] + fine
         x1[2 + 2 * q] = k1 * b1[2 + 2 * q] + fine
 
-    loop(0, planes // 2, up1, often)
+    if compacted:
+        loop(0, half, lambda q: up1(half * wall + q), often)
+        up1(half - wall)
+        up1((planes // 2 - 1) * (1 - wall))
+    else:
+        loop(0, planes // 2, up1, often)
 
     Q = W1 + 2
     sectors = (blk, lax.rem(blk + 1, n_blk), lax.rem(blk + n_blk - 1, n_blk))
@@ -932,7 +968,7 @@
         for j in range(n_len):
             ref = blocks[v * n_len + j]
             at_l = pl.ds(pl.multiple_of(length_of(j) * L, L), L)
-            if compacted and j == 1:
+            if compacted and v + j:
                 for b in range(n_blk):
                     values = sheet[wall_s, b * C : (b + 1) * C, at_l]
                     ids = ref[96 + b * C : 96 + (b + 1) * C, :]
@@ -1064,21 +1100,22 @@
     sector_blocks = jnp.stack([mine] + moved) if relative else moved[0]
     compacted = (n_blk, n_len, C, W) == (4, 2, 16, 32)
     if compacted:
-        (brief,) = call(
+        brief, across_wall = call(
             functools.partial(compact, C, W),
             [vmem],
-            [((168, L), vmem)],
+            [((168, L), vmem), ((200, L), vmem)],
             [(W // 4, n_blk * C // 2, L), (W // 8 + 1, n_blk * C // 2, L)],
             "compact",
         )(sector_blocks)
-        brief, sector_blocks = lax.optimization_barrier((brief, sector_blocks))
-        here = [sector_blocks, ring(brief, "len", 1)]
+        len_brief = ring(brief, "len", 1)
+        blocks = [sector_blocks, len_brief, ring(across_wall, "wall", 1), ring(len_brief, "wall", 1), brief]
     elif n_len == 2:
         here = [sector_blocks, ring(sector_blocks, "len", 1)]
     else:
         gathered = lax.all_gather(sector_blocks, "len")
         here = [gathered[j] for j in range(n_len)]
-    blocks = here + [ring(x, "wall", 1) for x in here]
+    if not compacted:
+        blocks = here + [ring(x, "wall", 1) for x in here]
 
     NC1, NL1 = n_blk * C // 2, n_len * L // 2
     planes = n_wall * W // 2
@@ -1087,7 +1124,7 @@
     tall = (Q * (C + 8) + 16, L)
     taller = ((W + 2) * (C + 8) + 16, L)
     scratch = grids + [(Q * C, NL1), tall, tall, taller, taller, own, own]
-    scratch += [(2, n_blk * C, n_len * L), (2, 48, L), pltpu.SemaphoreType.DMA((2, 2))]
+    scratch += [(2, n_blk * C, n_len * L), (2, 2, 64, L), pltpu.SemaphoreType.DMA((2, 2))]
     adj_prev, potential, patch_grad = call(
         functools.partial(solve, (n_blk, n_len, n_wall), relative, compacted, C, W),
         [vmem] * (len(blocks) + 4),

time: 40.9 us -> 41.1 us (level)
  Pallas kernels: 17.4 us -> 18.1 us
    pallas_call x1, Pallas kernels: 5.28 us -> 5.86 us  [body(): call(functools.partial(solve, (n_blk, n_len, n_wall), relative, compacted...]
where the time goes in v9:
time: 41.1 us; the launch traced here: 40.9 us
  Pallas kernels  18.1 us (44%)
  starting transfers between devices  11.3 us (27%)
  waiting for transfers between devices  10.2 us (25%)
  between operations  0.7 us (2%)
  local copies, waits for them, and re-layouts  0.66 us (2%)
    ppermute x10, starting transfers between devices, ring(): return lax.ppermute(x, axis, [(i, (i + by) % count) for i in range(count)])  11.2 us
    ppermute x10, waiting for transfers between devices, ring(): return lax.ppermute(x, axis, [(i, (i + by) % count) for i in range(count)])  7.19 us
    pallas_call x1, Pallas kernels, body(): call(functools.partial(solve, (n_blk, n_len, n_wall), relative, compacted...  5.86 us
    pallas_call x1, Pallas kernels, body(): call(functools.partial(sector, n_len, n_wall, C, electrodes), [vmem] * (6...  5.41 us
    pallas_call x1, Pallas kernels, body(): call(functools.partial(source_part, n_len, n_wall, C), [vmem] * 6, [(own,...  3.25 us
    ppermute x1, waiting for transfers between devices, across(): return lax.ppermute(x, ('len', 'wall'), pairs)  3.01 us
    pallas_call x1, Pallas kernels, body(): call(functools.partial(pack_faces, n_len), ['hbm'] * 4, [(own, vmem)] * 4...  1.67 us
  transfers between devices with their start and end apart: 11, of which 6 were waited for; matrix products, arithmetic and copies ran while one was open for 0% of the time, Pallas kernels for 21%

profile of v9, /device:TPU:0, one launch (start us, length us, event | category | flops | bytes accessed | tf_op | source)
XLA Modules:
  0.0 40.9 jit_solution(3292323790113955295)
XLA Ops:
  0.6 1.7 %faces.1 = (f32[512,128]{1,0:T(8,128)S(1)}, f32[512,128]{1,0:T(8,128)S(1)}, f32[512,128]{1,0:T(8,128)S(1)}, f32[512,128]{1,0:T(8,128)S(1)}, f32[12,16,128]{2,1,0...) custom-call(f32[512,128]{1,0:T(8,128)} %bitcast.13, f32[512,128]{1,0:T(8,128)} %bitcast.14, ...), custom_call_target="tpu_custom_call" | custom-call | tf_op jit(solution)/shard_map/faces/pallas_call | solution.py:1038
  2.3 0.5 %collective-permute-start = (f32[12,16,128]{2,1,0:T(8,128)S(1)}, f32[12,16,128]{2,1,0:T(8,128)S(1)}, u32[]{:S(2)}, u32[]{:S(2)}) collective-permute-start(f32[12,16,128]{2,1,0:T(8,128)S(1)} %get-tuple-element.37), channel_id=1, source_target_pairs={{0,1},{1,0},{2,3},{3,2},{4,5},{5,4},{6,7},{7,6},{8,9},{9,8},{10,11... | collective-permute-start | bytes 294920 | tf_op jit(solution)/shard_map/ppermute | solution.py:998
  2.8 2.6 %collective-permute-start.1 = (f32[4,16,128]{2,1,0:T(8,128)S(1)}, f32[4,16,128]{2,1,0:T(8,128)S(1)}, u32[]{:S(2)}, u32[]{:S(2)}) collective-permute-start(f32[4,16,128]{2,1,0:T(8,128)S(1)} %get-tuple-element.38), channel_id=1, source_target_pairs={{0,2},{2,0},{1,3},{3,1},{4,6},{6,4},{5,7},{7,5},{8,10},{10,8},{9,1... | collective-permute-start | bytes 98312 | tf_op jit(solution)/shard_map/ppermute | solution.py:998
  5.4 0.1 collective-permute-start.2
  5.5 3.0 %collective-permute-done.2.refs_6_ = f32[16,128]{1,0:T(8,128)S(1)} collective-permute-done((f32[16,128]{1,0:T(8,128)S(1)}, f32[16,128]{1,0:T(8,128)S(1)}, u32[]{:S(2)}, u32[]{:S(2)}) %collective-permute-start.2) | collective-permute-done | bytes 8224 | tf_op jit(solution)/shard_map/ppermute | solution.py:1004
  8.5 0.0 collective-permute-done.1.refs_5_
  8.5 0.0 collective-permute-done.refs_4_
  8.5 0.8 %boundary.1 = (f32[184,128]{1,0:T(8,128)S(1)}, f32[184,128]{1,0:T(8,128)S(1)}, f32[2,6,40,128]{3,2,1,0:T(8,128)S(1)}) custom-call(f32[512,128]{1,0:T(8,128)S(1)} %get-tuple-element.33.refs_0_, f32[512,128]{1,0:T(8,128)S(1)} %get-tuple-element.34.refs_1_, f32[512,128]{1,0:T(8,128)S(1)} %get-tuple-element.35.refs_2_.mask.refs_7_, ...), custom_call_target="tpu_custom_call" | custom-call | tf_op jit(solution)/shard_map/boundary/pallas_call | solution.py:1060
  9.3 3.7 %collective-permute-start.3 = (f32[184,128]{1,0:T(8,128)S(1)}, f32[184,128]{1,0:T(8,128)S(1)}, u32[]{:S(2)}, u32[]{:S(2)}) collective-permute-start(f32[184,128]{1,0:T(8,128)S(1)} %get-tuple-element.41), channel_id=1, source_target_pairs={{0,12},{4,0},{8,4},{12,8},{1,13},{5,1},{9,5},{13,9},{2,14},{6,2},{... | collective-permute-start | bytes 282632 | tf_op jit(solution)/shard_map/ppermute | solution.py:998
  12.9 0.0 copy-start.1
  12.9 0.0 collective-permute-start.4
  12.9 0.7 %copy-done.1 = s32[32]{0:T(128)S(1)} copy-done((s32[32]{0:T(128)S(1)}, s32[32]{0:T(128)}, u32[]{:S(2)}) %copy-start.1) | copy-done | bytes 152
  13.6 0.0 copy-start
  13.6 5.4 %sector.1 = (f32[640,128]{1,0:T(8,128)S(1)}, f32[640,128]{1,0:T(8,128)S(1)}, f32[640,128]{1,0:T(8,128)S(1)}, f32[64,128]{1,0:T(8,128)S(1)}, f32[16,128]{1,0:T(8,128)S(1)}, /*index=5*/f32[8,128]{1,0:T(8,128)S(1)}) custom-call(f32[512,128]{1,0:T(8,128)S(1)} %get-tuple-element.33.refs_0_, f32[512,128]{1,0:T(8,128)S(1)} %get-tuple-element.34.refs_1_, ...), custom_call_target="tpu_custom_call" | custom-call | flops 16000000 | bytes 16000000 | tf_op jit(solution)/shard_map/sector/pallas_call | solution.py:1069
  19.0 0.0 collective-permute-done.3.from_next
  19.0 0.3 collective-permute-done.4.from_prev
  19.3 0.0 copy-done
  19.3 0.7 %correct.1 = (f32[8,40,128]{2,1,0:T(8,128)S(1)}, f32[8,40,128]{2,1,0:T(8,128)S(1)}, f32[88,128]{1,0:T(8,128)S(1)}) custom-call(f32[2,6,40,128]{3,2,1,0:T(8,128)S(1)} %get-tuple-element.40.own_rows, f32[184,128]{1,0:T(8,128)S(1)} %collective-permute-done.3.from_next, f32[184,128]{1,0:T(8,128)S(1)} %collective-permute-done.4.from_prev, ...), custom_call_target="tpu_custom_call" | custom-call | tf_op jit(solution)/shard_map/correct/pallas_call | solution.py:1081
  20.1 2.9 %collective-permute-start.7 = (f32[88,128]{1,0:T(8,128)S(1)}, f32[88,128]{1,0:T(8,128)S(1)}, u32[]{:S(2)}, u32[]{:S(2)}) collective-permute-start(f32[88,128]{1,0:T(8,128)S(1)} %get-tuple-element.45), channel_id=1, source_target_pairs={{0,12},{4,0},{8,4},{12,8},{1,13},{5,1},{9,5},{13,9},{2,14},{6,2},{... | collective-permute-start | bytes 135176 | tf_op jit(solution)/shard_map/ppermute | solution.py:998
  23.0 0.0 collective-permute-start.6
  23.0 0.6 %collective-permute-start.5 = (f32[88,128]{1,0:T(8,128)S(1)}, f32[88,128]{1,0:T(8,128)S(1)}, u32[]{:S(2)}, u32[]{:S(2)}) collective-permute-start(f32[88,128]{1,0:T(8,128)S(1)} %get-tuple-element.45), channel_id=1, source_target_pairs={{0,4},{4,8},{8,12},{12,0},{1,5},{5,9},{9,13},{13,1},{2,6},{6,10},{... | collective-permute-start | bytes 135176 | tf_op jit(solution)/shard_map/ppermute | solution.py:998
  23.6 3.2 %source_part.1 = (f32[512,128]{1,0:T(8,128)S(1)}, f32[512,128]{1,0:T(8,128)S(1)}) custom-call(f32[640,128]{1,0:T(8,128)S(1)} %get-tuple-element.46.bm, f32[640,128]{1,0:T(8,128)S(1)} %get-tuple-element.47.be, f32[8,40,128]{2,1,0:T(8,128)S(1)} %get-tuple-element.48.rows_n, f32[8,40,128]{2,1,0:T(8,128)S(1)} %get-tuple-element.49.rows_p, ...), custom_call_target="tpu_custom_call" | custom-call | flops 12000000 | bytes 12000000 | tf_op jit(solution)/shard_map/source_part/pallas_call | solution.py:1091
  26.8 0.0 collective-permute-done.7
  26.8 1.1 %collective-permute-done.6 = f32[88,128]{1,0:T(8,128)S(1)} collective-permute-done((f32[88,128]{1,0:T(8,128)S(1)}, f32[88,128]{1,0:T(8,128)S(1)}, u32[]{:S(2)}, u32[]{:S(2)}) %collective-permute-start.6) | collective-permute-done | bytes 45088 | tf_op jit(solution)/shard_map/ppermute | solution.py:998
  27.9 0.9 %collective-permute-done.5 = f32[88,128]{1,0:T(8,128)S(1)} collective-permute-done((f32[88,128]{1,0:T(8,128)S(1)}, f32[88,128]{1,0:T(8,128)S(1)}, u32[]{:S(2)}, u32[]{:S(2)}) %collective-permute-start.5) | collective-permute-done | bytes 45088 | tf_op jit(solution)/shard_map/ppermute | solution.py:998
  28.9 0.3 compact.1
  29.2 0.9 %collective-permute-start.8 = (f32[168,128]{1,0:T(8,128)S(1)}, f32[168,128]{1,0:T(8,128)S(1)}, u32[]{:S(2)}, u32[]{:S(2)}) collective-permute-start(f32[168,128]{1,0:T(8,128)S(1)} %get-tuple-element.55.refs_4_), channel_id=1, source_target_pairs={{0,2},{2,0},{1,3},{3,1},{4,6},{6,4},{5,7},{7,5},{8,10},{10,8},{9,1... | collective-permute-start | bytes 258056 | tf_op jit(solution)/shard_map/ppermute | solution.py:998
  30.1 0.0 collective-permute-start.9
  30.1 3.6 %collective-permute-done.8.refs_1_ = f32[168,128]{1,0:T(8,128)S(1)} collective-permute-done((f32[168,128]{1,0:T(8,128)S(1)}, f32[168,128]{1,0:T(8,128)S(1)}, u32[]{:S(2)}, u32[]{:S(2)}) %collective-permute-start.8) | collective-permute-done | bytes 86048 | tf_op jit(solution)/shard_map/ppermute | solution.py:998
  33.7 0.0 collective-permute-start.10
  33.7 0.0 collective-permute-done.9.refs_2_
  33.7 1.3 %collective-permute-done.10.refs_3_ = f32[168,128]{1,0:T(8,128)S(1)} collective-permute-done((f32[168,128]{1,0:T(8,128)S(1)}, f32[168,128]{1,0:T(8,128)S(1)}, u32[]{:S(2)}, u32[]{:S(2)}) %collective-permute-start.10) | collective-permute-done | bytes 86048 | tf_op jit(solution)/shard_map/ppermute | solution.py:998
  35.0 5.9 %solve.1 = (f32[512,128]{1,0:T(8,128)}, f32[512,128]{1,0:T(8,128)}, f32[1,2]{1,0:T(1,128)}) custom-call(f32[4,88,128]{2,1,0:T(8,128)S(1)} %pad_maximum_fusion.blocks.refs_0_, f32[168,128]{1,0:T(8,128)S(1)} %collective-permute-done.8.refs_1_, f32[200,128]{1,0:T(8,128)S(1)} %collective-permute-done.9.refs_2_, f32[168,128]{1,0:T(8,128)S(1)} %collective-permute-done.10.refs_3_, ...), custom_call_target="tpu_custom_call" | custom-call | tf_op jit(solution)/shard_map/solve/pallas_call | solution.py:1128
  (1 shorter events, 0.0 us)
Async XLA Ops:
  2.3 6.2 %collective-permute-start = (f32[12,16,128]{2,1,0:T(8,128)S(1)}, f32[12,16,128]{2,1,0:T(8,128)S(1)}, u32[]{:S(2)}, u32[]{:S(2)}) collective-permute-start(f32[12,16,128]{2,1,0:T(8,128)S(1)} %get-tuple-element.37), channel_id=1, source_target_pairs={{0,1},{1,0},{2,3},{3,2},{4,5},{5,4},{6,7},{7,6},{8,9},{9,8},{10,11... | collective-permute-start | bytes 294920 | tf_op jit(solution)/shard_map/ppermute | solution.py:998
  2.8 5.6 %collective-permute-start.1 = (f32[4,16,128]{2,1,0:T(8,128)S(1)}, f32[4,16,128]{2,1,0:T(8,128)S(1)}, u32[]{:S(2)}, u32[]{:S(2)}) collective-permute-start(f32[4,16,128]{2,1,0:T(8,128)S(1)} %get-tuple-element.38), channel_id=1, source_target_pairs={{0,2},{2,0},{1,3},{3,1},{4,6},{6,4},{5,7},{7,5},{8,10},{10,8},{9,1... | collective-permute-start | bytes 98312 | tf_op jit(solution)/shard_map/ppermute | solution.py:998
  5.4 3.1 %collective-permute-start.2 = (f32[16,128]{1,0:T(8,128)S(1)}, f32[16,128]{1,0:T(8,128)S(1)}, u32[]{:S(2)}, u32[]{:S(2)}) collective-permute-start(f32[16,128]{1,0:T(8,128)S(1)} %get-tuple-element.39), channel_id=1, source_target_pairs={{0,3},{1,2},{2,1},{3,0},{4,7},{5,6},{6,5},{7,4},{8,11},{9,10},{10,... | collective-permute-start | bytes 24584 | tf_op jit(solution)/shard_map/ppermute | solution.py:1004
  9.3 9.7 %collective-permute-start.3 = (f32[184,128]{1,0:T(8,128)S(1)}, f32[184,128]{1,0:T(8,128)S(1)}, u32[]{:S(2)}, u32[]{:S(2)}) collective-permute-start(f32[184,128]{1,0:T(8,128)S(1)} %get-tuple-element.41), channel_id=1, source_target_pairs={{0,12},{4,0},{8,4},{12,8},{1,13},{5,1},{9,5},{13,9},{2,14},{6,2},{... | collective-permute-start | bytes 282632 | tf_op jit(solution)/shard_map/ppermute | solution.py:998
  12.9 0.7 %copy-start.1 = (s32[32]{0:T(128)S(1)}, s32[32]{0:T(128)}, u32[]{:S(2)}) copy-start(s32[32]{0:T(128)} %param.11) | copy-start | bytes 388
  12.9 6.4 %collective-permute-start.4 = (f32[184,128]{1,0:T(8,128)S(1)}, f32[184,128]{1,0:T(8,128)S(1)}, u32[]{:S(2)}, u32[]{:S(2)}) collective-permute-start(f32[184,128]{1,0:T(8,128)S(1)} %get-tuple-element.42), channel_id=1, source_target_pairs={{0,4},{4,8},{8,12},{12,0},{1,5},{5,9},{9,13},{13,1},{2,6},{6,10},{... | collective-permute-start | bytes 282632 | tf_op jit(solution)/shard_map/ppermute | solution.py:998
  13.6 5.7 %copy-start = (s32[1,16,128]{2,1,0:T(8,128)S(1)}, s32[1,16,128]{2,1,0:T(8,128)}, u32[]{:S(2)}) copy-start(s32[1,16,128]{2,1,0:T(8,128)} %ids.1) | copy-start | bytes 24580
  20.1 6.8 %collective-permute-start.7 = (f32[88,128]{1,0:T(8,128)S(1)}, f32[88,128]{1,0:T(8,128)S(1)}, u32[]{:S(2)}, u32[]{:S(2)}) collective-permute-start(f32[88,128]{1,0:T(8,128)S(1)} %get-tuple-element.45), channel_id=1, source_target_pairs={{0,12},{4,0},{8,4},{12,8},{1,13},{5,1},{9,5},{13,9},{2,14},{6,2},{... | collective-permute-start | bytes 135176 | tf_op jit(solution)/shard_map/ppermute | solution.py:998
  23.0 4.9 %collective-permute-start.6 = (f32[88,128]{1,0:T(8,128)S(1)}, f32[88,128]{1,0:T(8,128)S(1)}, u32[]{:S(2)}, u32[]{:S(2)}) collective-permute-start(f32[88,128]{1,0:T(8,128)S(1)} %get-tuple-element.45), channel_id=1, source_target_pairs={{0,8},{4,12},{8,0},{12,4},{1,9},{5,13},{9,1},{13,5},{2,10},{6,14},... | collective-permute-start | bytes 135176 | tf_op jit(solution)/shard_map/ppermute | solution.py:998
  23.0 5.8 %collective-permute-start.5 = (f32[88,128]{1,0:T(8,128)S(1)}, f32[88,128]{1,0:T(8,128)S(1)}, u32[]{:S(2)}, u32[]{:S(2)}) collective-permute-start(f32[88,128]{1,0:T(8,128)S(1)} %get-tuple-element.45), channel_id=1, source_target_pairs={{0,4},{4,8},{8,12},{12,0},{1,5},{5,9},{9,13},{13,1},{2,6},{6,10},{... | collective-permute-start | bytes 135176 | tf_op jit(solution)/shard_map/ppermute | solution.py:998
  29.2 4.6 %collective-permute-start.8 = (f32[168,128]{1,0:T(8,128)S(1)}, f32[168,128]{1,0:T(8,128)S(1)}, u32[]{:S(2)}, u32[]{:S(2)}) collective-permute-start(f32[168,128]{1,0:T(8,128)S(1)} %get-tuple-element.55.refs_4_), channel_id=1, source_target_pairs={{0,2},{2,0},{1,3},{3,1},{4,6},{6,4},{5,7},{7,5},{8,10},{10,8},{9,1... | collective-permute-start | bytes 258056 | tf_op jit(solution)/shard_map/ppermute | solution.py:998
  30.1 3.6 %collective-permute-start.9 = (f32[200,128]{1,0:T(8,128)S(1)}, f32[200,128]{1,0:T(8,128)S(1)}, u32[]{:S(2)}, u32[]{:S(2)}) collective-permute-start(f32[200,128]{1,0:T(8,128)S(1)} %get-tuple-element.56), channel_id=1, source_target_pairs={{0,1},{1,0},{2,3},{3,2},{4,5},{5,4},{6,7},{7,6},{8,9},{9,8},{10,11... | collective-permute-start | bytes 307208 | tf_op jit(solution)/shard_map/ppermute | solution.py:998
  33.7 1.3 %collective-permute-start.10 = (f32[168,128]{1,0:T(8,128)S(1)}, f32[168,128]{1,0:T(8,128)S(1)}, u32[]{:S(2)}, u32[]{:S(2)}) collective-permute-start(f32[168,128]{1,0:T(8,128)S(1)} %collective-permute-done.8.refs_1_), channel_id=1, source_target_pairs={{0,1},{1,0},{2,3},{3,2},{4,5},{5,4},{6,7},{7,6},{8,9},{9,8},{10,11... | collective-permute-start | bytes 258056 | tf_op jit(solution)/shard_map/ppermute | solution.py:998

commit v10 on v9

--- a/solution.py
+++ b/solution.py
@@ -732,36 +732,43 @@
             ours = two_planes(wall_brief[64 : 64 + NC1, :])[k]
             theirs = two_planes(both_brief[64 : 64 + NC1, :])[1 - k]
             b1[jnp.where(wall == 0, planes - 1, 1) + k] = jnp.where(here, ours, theirs)
+        first_half = length == 0
         for k in range(2):
-            briefs[0, k] = jnp.where(wall == k, own_brief[0:64, :], wall_brief[0:64, :])
-            briefs[1, k] = jnp.where(wall == k, len_brief[0:64, :], both_brief[0:64, :])
-        tile_lane8 = lane_of((8, LANES)) % middle // 2
-        row_of_8 = lax.broadcasted_iota(jnp.int32, (8, LANES), 0) // 2
-        here_8 = lane_of((8, LANES)) // middle == length
-        mine8 = lane_of((8, LANES)) // 2 == jnp.where(length == 0, middle // 2 - 1, middle // 2)
-        other8 = lane_of((8, LANES)) // 2 == jnp.where(length == 0, middle // 2, middle // 2 - 1)
+            ours = jnp.where(wall == k, own_brief[0:64, :], wall_brief[0:64, :])
+            theirs = jnp.where(wall == k, len_brief[0:64, :], both_brief[0:64, :])
+            briefs[0, k] = jnp.where(first_half, ours, theirs)
+            briefs[1, k] = jnp.where(first_half, theirs, ours)
+        lane_8 = lane_of((8, LANES))
+        quarter = middle // 2
+        left_quarter = lane_8 % middle < quarter
+        pairs_index = [lane_8 // 2, middle + lane_8 // 2]
+        facing = jnp.logical_and(lane_8 >= middle - 2, lane_8 < middle + 2)
         coef1 = [level_step(1) * x for x in level_coef(1)]
-        tiles2 = {}
-
-        def widened(w, first, t, start):
-            key = (w, first, t)
-            if key not in tiles2:
-                at = first + 8 * (t // 2)
-                tiles2[key] = [rows_at(briefs[h, w, at : at + 8, :], 4 * (t % 2) + row_of_8) for h in range(2)]
-            return jnp.where(here_8, *[lanes_at(x, start + tile_lane8) for x in tiles2[key]])
+        rows2 = NC1 // 2
+
+        def merged(w, start):
+            one, two = briefs[0, w, start : start + 8, :], briefs[1, w, start : start + 8, :]
+            even = jnp.where(left_quarter, one, pltpu.roll(two, quarter, 1))
+            odd = jnp.where(left_quarter, pltpu.roll(one, LANES - quarter, 1), two)
+            return even, odd
 
         for w in range(n_wall):
-            for t in range(NC1 // 8):
-                lines = [briefs[h, w, 32 + 8 * t : 40 + 8 * t, :] for h in range(2)]
-                lines = jnp.where(lane_of((8, LANES)) < 104, lines[0], pltpu.roll(lines[1], 8, 1))
-                for k in range(half):
-                    high, q = divmod(k, half // 2)
-                    value = widened(w, NC1 // 2 * (q // 2), t, middle // 2 * (q % 2) + middle * high)
-                    index = jnp.where(mine8, 104 + k, jnp.where(other8, 96 + k, LANES - 1))
-                    value = value + coef1[2] * lanes_at(lines, index)
-                    if k == (half - 1 if w == 0 else 0):
-                        value = value + coef1[0] * widened(1 - w, 32, t, middle // 2)
-                    b2[1 + w * half + k, 8 * t : 8 * t + 8, :] = value
+            for t in range(rows2 // 8):
+                lines = [briefs[h, w, pl.ds(32 + 16 * t, 8, stride=2), :] for h in range(2)]
+                lines = [lanes_at(x, jnp.minimum(96 + lane_8 // 4, LANES - 1)) for x in lines]
+                lines = coef1[2] * jnp.where(lane_8 % 4 < 2, lines[1], lines[0])
+                for p in range(half // 4):
+                    tiles = merged(w, rows2 * p + 8 * t)
+                    for odd in range(2):
+                        for high in range(2):
+                            k = 2 * p + odd + half // 2 * high
+                            value = lanes_at(tiles[odd], pairs_index[high])
+                            line = pltpu.roll(lines, middle - 2 - 4 * k, 1)
+                            value = value + jnp.where(facing, line, 0.0)
+                            if k == (half - 1 if w == 0 else 0):
+                                value = value + coef1[0] * lanes_at(merged(1 - w, 32 + 8 * t)[1], pairs_index[0])
+                            for r in range(2):
+                                b2[1 + w * half + k, pl.ds(16 * t + r, 8, stride=2), :] = value
 
     def total_of(x, wsum, level, by):
         coef = level_coef(level)

time: 41.1 us -> 40.8 us (level)
  no operation moved by 1% of the time
where the time goes in v10:
time: 40.8 us; the launch traced here: 40.6 us
  Pallas kernels  17.8 us (44%)
  starting transfers between devices  11.3 us (28%)
  waiting for transfers between devices  10.2 us (25%)
  between operations  0.7 us (2%)
  local copies, waits for them, and re-layouts  0.66 us (2%)
    ppermute x10, starting transfers between devices, ring(): return lax.ppermute(x, axis, [(i, (i + by) % count) for i in range(count)])  11.2 us
    ppermute x10, waiting for transfers between devices, ring(): return lax.ppermute(x, axis, [(i, (i + by) % count) for i in range(count)])  7.19 us
    pallas_call x1, Pallas kernels, body(): call(functools.partial(solve, (n_blk, n_len, n_wall), relative, compacted...  5.62 us
    pallas_call x1, Pallas kernels, body(): call(functools.partial(sector, n_len, n_wall, C, electrodes), [vmem] * (6...  5.41 us
    pallas_call x1, Pallas kernels, body(): call(functools.partial(source_part, n_len, n_wall, C), [vmem] * 6, [(own,...  3.25 us
    ppermute x1, waiting for transfers between devices, across(): return lax.ppermute(x, ('len', 'wall'), pairs)  3.01 us
    pallas_call x1, Pallas kernels, body(): call(functools.partial(pack_faces, n_len), ['hbm'] * 4, [(own, vmem)] * 4...  1.67 us
  transfers between devices with their start and end apart: 11, of which 6 were waited for; matrix products, arithmetic and copies ran while one was open for 0% of the time, Pallas kernels for 21%

profile of v10, /device:TPU:0, one launch (start us, length us, event | category | flops | bytes accessed | tf_op | source)
XLA Modules:
  0.0 40.6 jit_solution(4794733035462374768)
XLA Ops:
  0.6 1.7 %faces.1 = (f32[512,128]{1,0:T(8,128)S(1)}, f32[512,128]{1,0:T(8,128)S(1)}, f32[512,128]{1,0:T(8,128)S(1)}, f32[512,128]{1,0:T(8,128)S(1)}, f32[12,16,128]{2,1,0...) custom-call(f32[512,128]{1,0:T(8,128)} %bitcast.13, f32[512,128]{1,0:T(8,128)} %bitcast.14, ...), custom_call_target="tpu_custom_call" | custom-call | tf_op jit(solution)/shard_map/faces/pallas_call | solution.py:1045
  2.3 0.5 %collective-permute-start = (f32[12,16,128]{2,1,0:T(8,128)S(1)}, f32[12,16,128]{2,1,0:T(8,128)S(1)}, u32[]{:S(2)}, u32[]{:S(2)}) collective-permute-start(f32[12,16,128]{2,1,0:T(8,128)S(1)} %get-tuple-element.37), channel_id=1, source_target_pairs={{0,1},{1,0},{2,3},{3,2},{4,5},{5,4},{6,7},{7,6},{8,9},{9,8},{10,11... | collective-permute-start | bytes 294920 | tf_op jit(solution)/shard_map/ppermute | solution.py:1005
  2.8 2.6 %collective-permute-start.1 = (f32[4,16,128]{2,1,0:T(8,128)S(1)}, f32[4,16,128]{2,1,0:T(8,128)S(1)}, u32[]{:S(2)}, u32[]{:S(2)}) collective-permute-start(f32[4,16,128]{2,1,0:T(8,128)S(1)} %get-tuple-element.38), channel_id=1, source_target_pairs={{0,2},{2,0},{1,3},{3,1},{4,6},{6,4},{5,7},{7,5},{8,10},{10,8},{9,1... | collective-permute-start | bytes 98312 | tf_op jit(solution)/shard_map/ppermute | solution.py:1005
  5.4 0.1 collective-permute-start.2
  5.5 3.0 %collective-permute-done.2.refs_6_ = f32[16,128]{1,0:T(8,128)S(1)} collective-permute-done((f32[16,128]{1,0:T(8,128)S(1)}, f32[16,128]{1,0:T(8,128)S(1)}, u32[]{:S(2)}, u32[]{:S(2)}) %collective-permute-start.2) | collective-permute-done | bytes 8224 | tf_op jit(solution)/shard_map/ppermute | solution.py:1011
  8.5 0.0 collective-permute-done.1.refs_5_
  8.5 0.0 collective-permute-done.refs_4_
  8.5 0.8 %boundary.1 = (f32[184,128]{1,0:T(8,128)S(1)}, f32[184,128]{1,0:T(8,128)S(1)}, f32[2,6,40,128]{3,2,1,0:T(8,128)S(1)}) custom-call(f32[512,128]{1,0:T(8,128)S(1)} %get-tuple-element.33.refs_0_, f32[512,128]{1,0:T(8,128)S(1)} %get-tuple-element.34.refs_1_, f32[512,128]{1,0:T(8,128)S(1)} %get-tuple-element.35.refs_2_.mask.refs_7_, ...), custom_call_target="tpu_custom_call" | custom-call | tf_op jit(solution)/shard_map/boundary/pallas_call | solution.py:1067
  9.3 3.7 %collective-permute-start.3 = (f32[184,128]{1,0:T(8,128)S(1)}, f32[184,128]{1,0:T(8,128)S(1)}, u32[]{:S(2)}, u32[]{:S(2)}) collective-permute-start(f32[184,128]{1,0:T(8,128)S(1)} %get-tuple-element.41), channel_id=1, source_target_pairs={{0,12},{4,0},{8,4},{12,8},{1,13},{5,1},{9,5},{13,9},{2,14},{6,2},{... | collective-permute-start | bytes 282632 | tf_op jit(solution)/shard_map/ppermute | solution.py:1005
  12.9 0.0 copy-start.1
  12.9 0.0 collective-permute-start.4
  12.9 0.7 %copy-done.1 = s32[32]{0:T(128)S(1)} copy-done((s32[32]{0:T(128)S(1)}, s32[32]{0:T(128)}, u32[]{:S(2)}) %copy-start.1) | copy-done | bytes 152
  13.6 0.0 copy-start
  13.6 5.4 %sector.1 = (f32[640,128]{1,0:T(8,128)S(1)}, f32[640,128]{1,0:T(8,128)S(1)}, f32[640,128]{1,0:T(8,128)S(1)}, f32[64,128]{1,0:T(8,128)S(1)}, f32[16,128]{1,0:T(8,128)S(1)}, /*index=5*/f32[8,128]{1,0:T(8,128)S(1)}) custom-call(f32[512,128]{1,0:T(8,128)S(1)} %get-tuple-element.33.refs_0_, f32[512,128]{1,0:T(8,128)S(1)} %get-tuple-element.34.refs_1_, ...), custom_call_target="tpu_custom_call" | custom-call | flops 16000000 | bytes 16000000 | tf_op jit(solution)/shard_map/sector/pallas_call | solution.py:1076
  19.0 0.0 collective-permute-done.3.from_next
  19.0 0.3 collective-permute-done.4.from_prev
  19.3 0.0 copy-done
  19.3 0.7 %correct.1 = (f32[8,40,128]{2,1,0:T(8,128)S(1)}, f32[8,40,128]{2,1,0:T(8,128)S(1)}, f32[88,128]{1,0:T(8,128)S(1)}) custom-call(f32[2,6,40,128]{3,2,1,0:T(8,128)S(1)} %get-tuple-element.40.own_rows, f32[184,128]{1,0:T(8,128)S(1)} %collective-permute-done.3.from_next, f32[184,128]{1,0:T(8,128)S(1)} %collective-permute-done.4.from_prev, ...), custom_call_target="tpu_custom_call" | custom-call | tf_op jit(solution)/shard_map/correct/pallas_call | solution.py:1088
  20.1 2.9 %collective-permute-start.7 = (f32[88,128]{1,0:T(8,128)S(1)}, f32[88,128]{1,0:T(8,128)S(1)}, u32[]{:S(2)}, u32[]{:S(2)}) collective-permute-start(f32[88,128]{1,0:T(8,128)S(1)} %get-tuple-element.45), channel_id=1, source_target_pairs={{0,12},{4,0},{8,4},{12,8},{1,13},{5,1},{9,5},{13,9},{2,14},{6,2},{... | collective-permute-start | bytes 135176 | tf_op jit(solution)/shard_map/ppermute | solution.py:1005
  23.0 0.0 collective-permute-start.6
  23.0 0.6 %collective-permute-start.5 = (f32[88,128]{1,0:T(8,128)S(1)}, f32[88,128]{1,0:T(8,128)S(1)}, u32[]{:S(2)}, u32[]{:S(2)}) collective-permute-start(f32[88,128]{1,0:T(8,128)S(1)} %get-tuple-element.45), channel_id=1, source_target_pairs={{0,4},{4,8},{8,12},{12,0},{1,5},{5,9},{9,13},{13,1},{2,6},{6,10},{... | collective-permute-start | bytes 135176 | tf_op jit(solution)/shard_map/ppermute | solution.py:1005
  23.6 3.2 %source_part.1 = (f32[512,128]{1,0:T(8,128)S(1)}, f32[512,128]{1,0:T(8,128)S(1)}) custom-call(f32[640,128]{1,0:T(8,128)S(1)} %get-tuple-element.46.bm, f32[640,128]{1,0:T(8,128)S(1)} %get-tuple-element.47.be, f32[8,40,128]{2,1,0:T(8,128)S(1)} %get-tuple-element.48.rows_n, f32[8,40,128]{2,1,0:T(8,128)S(1)} %get-tuple-element.49.rows_p, ...), custom_call_target="tpu_custom_call" | custom-call | flops 12000000 | bytes 12000000 | tf_op jit(solution)/shard_map/source_part/pallas_call | solution.py:1098
  26.8 0.0 collective-permute-done.7
  26.8 1.1 %collective-permute-done.6 = f32[88,128]{1,0:T(8,128)S(1)} collective-permute-done((f32[88,128]{1,0:T(8,128)S(1)}, f32[88,128]{1,0:T(8,128)S(1)}, u32[]{:S(2)}, u32[]{:S(2)}) %collective-permute-start.6) | collective-permute-done | bytes 45088 | tf_op jit(solution)/shard_map/ppermute | solution.py:1005
  27.9 0.9 %collective-permute-done.5 = f32[88,128]{1,0:T(8,128)S(1)} collective-permute-done((f32[88,128]{1,0:T(8,128)S(1)}, f32[88,128]{1,0:T(8,128)S(1)}, u32[]{:S(2)}, u32[]{:S(2)}) %collective-permute-start.5) | collective-permute-done | bytes 45088 | tf_op jit(solution)/shard_map/ppermute | solution.py:1005
  28.9 0.3 compact.1
  29.2 0.9 %collective-permute-start.8 = (f32[168,128]{1,0:T(8,128)S(1)}, f32[168,128]{1,0:T(8,128)S(1)}, u32[]{:S(2)}, u32[]{:S(2)}) collective-permute-start(f32[168,128]{1,0:T(8,128)S(1)} %get-tuple-element.55.refs_4_), channel_id=1, source_target_pairs={{0,2},{2,0},{1,3},{3,1},{4,6},{6,4},{5,7},{7,5},{8,10},{10,8},{9,1... | collective-permute-start | bytes 258056 | tf_op jit(solution)/shard_map/ppermute | solution.py:1005
  30.1 0.0 collective-permute-start.9
  30.1 3.6 %collective-permute-done.8.refs_1_ = f32[168,128]{1,0:T(8,128)S(1)} collective-permute-done((f32[168,128]{1,0:T(8,128)S(1)}, f32[168,128]{1,0:T(8,128)S(1)}, u32[]{:S(2)}, u32[]{:S(2)}) %collective-permute-start.8) | collective-permute-done | bytes 86048 | tf_op jit(solution)/shard_map/ppermute | solution.py:1005
  33.7 0.0 collective-permute-start.10
  33.7 0.0 collective-permute-done.9.refs_2_
  33.7 1.3 %collective-permute-done.10.refs_3_ = f32[168,128]{1,0:T(8,128)S(1)} collective-permute-done((f32[168,128]{1,0:T(8,128)S(1)}, f32[168,128]{1,0:T(8,128)S(1)}, u32[]{:S(2)}, u32[]{:S(2)}) %collective-permute-start.10) | collective-permute-done | bytes 86048 | tf_op jit(solution)/shard_map/ppermute | solution.py:1005
  35.0 5.6 %solve.1 = (f32[512,128]{1,0:T(8,128)}, f32[512,128]{1,0:T(8,128)}, f32[1,2]{1,0:T(1,128)}) custom-call(f32[4,88,128]{2,1,0:T(8,128)S(1)} %pad_maximum_fusion.blocks.refs_0_, f32[168,128]{1,0:T(8,128)S(1)} %collective-permute-done.8.refs_1_, f32[200,128]{1,0:T(8,128)S(1)} %collective-permute-done.9.refs_2_, f32[168,128]{1,0:T(8,128)S(1)} %collective-permute-done.10.refs_3_, ...), custom_call_target="tpu_custom_call" | custom-call | tf_op jit(solution)/shard_map/solve/pallas_call | solution.py:1135
  (1 shorter events, 0.0 us)
Async XLA Ops:
  2.3 6.2 %collective-permute-start = (f32[12,16,128]{2,1,0:T(8,128)S(1)}, f32[12,16,128]{2,1,0:T(8,128)S(1)}, u32[]{:S(2)}, u32[]{:S(2)}) collective-permute-start(f32[12,16,128]{2,1,0:T(8,128)S(1)} %get-tuple-element.37), channel_id=1, source_target_pairs={{0,1},{1,0},{2,3},{3,2},{4,5},{5,4},{6,7},{7,6},{8,9},{9,8},{10,11... | collective-permute-start | bytes 294920 | tf_op jit(solution)/shard_map/ppermute | solution.py:1005
  2.8 5.6 %collective-permute-start.1 = (f32[4,16,128]{2,1,0:T(8,128)S(1)}, f32[4,16,128]{2,1,0:T(8,128)S(1)}, u32[]{:S(2)}, u32[]{:S(2)}) collective-permute-start(f32[4,16,128]{2,1,0:T(8,128)S(1)} %get-tuple-element.38), channel_id=1, source_target_pairs={{0,2},{2,0},{1,3},{3,1},{4,6},{6,4},{5,7},{7,5},{8,10},{10,8},{9,1... | collective-permute-start | bytes 98312 | tf_op jit(solution)/shard_map/ppermute | solution.py:1005
  5.4 3.1 %collective-permute-start.2 = (f32[16,128]{1,0:T(8,128)S(1)}, f32[16,128]{1,0:T(8,128)S(1)}, u32[]{:S(2)}, u32[]{:S(2)}) collective-permute-start(f32[16,128]{1,0:T(8,128)S(1)} %get-tuple-element.39), channel_id=1, source_target_pairs={{0,3},{1,2},{2,1},{3,0},{4,7},{5,6},{6,5},{7,4},{8,11},{9,10},{10,... | collective-permute-start | bytes 24584 | tf_op jit(solution)/shard_map/ppermute | solution.py:1011
  9.3 9.7 %collective-permute-start.3 = (f32[184,128]{1,0:T(8,128)S(1)}, f32[184,128]{1,0:T(8,128)S(1)}, u32[]{:S(2)}, u32[]{:S(2)}) collective-permute-start(f32[184,128]{1,0:T(8,128)S(1)} %get-tuple-element.41), channel_id=1, source_target_pairs={{0,12},{4,0},{8,4},{12,8},{1,13},{5,1},{9,5},{13,9},{2,14},{6,2},{... | collective-permute-start | bytes 282632 | tf_op jit(solution)/shard_map/ppermute | solution.py:1005
  12.9 0.7 %copy-start.1 = (s32[32]{0:T(128)S(1)}, s32[32]{0:T(128)}, u32[]{:S(2)}) copy-start(s32[32]{0:T(128)} %param.11) | copy-start | bytes 388
  12.9 6.4 %collective-permute-start.4 = (f32[184,128]{1,0:T(8,128)S(1)}, f32[184,128]{1,0:T(8,128)S(1)}, u32[]{:S(2)}, u32[]{:S(2)}) collective-permute-start(f32[184,128]{1,0:T(8,128)S(1)} %get-tuple-element.42), channel_id=1, source_target_pairs={{0,4},{4,8},{8,12},{12,0},{1,5},{5,9},{9,13},{13,1},{2,6},{6,10},{... | collective-permute-start | bytes 282632 | tf_op jit(solution)/shard_map/ppermute | solution.py:1005
  13.6 5.7 %copy-start = (s32[1,16,128]{2,1,0:T(8,128)S(1)}, s32[1,16,128]{2,1,0:T(8,128)}, u32[]{:S(2)}) copy-start(s32[1,16,128]{2,1,0:T(8,128)} %ids.1) | copy-start | bytes 24580
  20.1 6.8 %collective-permute-start.7 = (f32[88,128]{1,0:T(8,128)S(1)}, f32[88,128]{1,0:T(8,128)S(1)}, u32[]{:S(2)}, u32[]{:S(2)}) collective-permute-start(f32[88,128]{1,0:T(8,128)S(1)} %get-tuple-element.45), channel_id=1, source_target_pairs={{0,12},{4,0},{8,4},{12,8},{1,13},{5,1},{9,5},{13,9},{2,14},{6,2},{... | collective-permute-start | bytes 135176 | tf_op jit(solution)/shard_map/ppermute | solution.py:1005
  23.0 4.9 %collective-permute-start.6 = (f32[88,128]{1,0:T(8,128)S(1)}, f32[88,128]{1,0:T(8,128)S(1)}, u32[]{:S(2)}, u32[]{:S(2)}) collective-permute-start(f32[88,128]{1,0:T(8,128)S(1)} %get-tuple-element.45), channel_id=1, source_target_pairs={{0,8},{4,12},{8,0},{12,4},{1,9},{5,13},{9,1},{13,5},{2,10},{6,14},... | collective-permute-start | bytes 135176 | tf_op jit(solution)/shard_map/ppermute | solution.py:1005
  23.0 5.8 %collective-permute-start.5 = (f32[88,128]{1,0:T(8,128)S(1)}, f32[88,128]{1,0:T(8,128)S(1)}, u32[]{:S(2)}, u32[]{:S(2)}) collective-permute-start(f32[88,128]{1,0:T(8,128)S(1)} %get-tuple-element.45), channel_id=1, source_target_pairs={{0,4},{4,8},{8,12},{12,0},{1,5},{5,9},{9,13},{13,1},{2,6},{6,10},{... | collective-permute-start | bytes 135176 | tf_op jit(solution)/shard_map/ppermute | solution.py:1005
  29.2 4.6 %collective-permute-start.8 = (f32[168,128]{1,0:T(8,128)S(1)}, f32[168,128]{1,0:T(8,128)S(1)}, u32[]{:S(2)}, u32[]{:S(2)}) collective-permute-start(f32[168,128]{1,0:T(8,128)S(1)} %get-tuple-element.55.refs_4_), channel_id=1, source_target_pairs={{0,2},{2,0},{1,3},{3,1},{4,6},{6,4},{5,7},{7,5},{8,10},{10,8},{9,1... | collective-permute-start | bytes 258056 | tf_op jit(solution)/shard_map/ppermute | solution.py:1005
  30.1 3.6 %collective-permute-start.9 = (f32[200,128]{1,0:T(8,128)S(1)}, f32[200,128]{1,0:T(8,128)S(1)}, u32[]{:S(2)}, u32[]{:S(2)}) collective-permute-start(f32[200,128]{1,0:T(8,128)S(1)} %get-tuple-element.56), channel_id=1, source_target_pairs={{0,1},{1,0},{2,3},{3,2},{4,5},{5,4},{6,7},{7,6},{8,9},{9,8},{10,11... | collective-permute-start | bytes 307208 | tf_op jit(solution)/shard_map/ppermute | solution.py:1005
  33.7 1.3 %collective-permute-start.10 = (f32[168,128]{1,0:T(8,128)S(1)}, f32[168,128]{1,0:T(8,128)S(1)}, u32[]{:S(2)}, u32[]{:S(2)}) collective-permute-start(f32[168,128]{1,0:T(8,128)S(1)} %collective-permute-done.8.refs_1_), channel_id=1, source_target_pairs={{0,1},{1,0},{2,3},{3,2},{4,5},{5,4},{6,7},{7,6},{8,9},{9,8},{10,11... | collective-permute-start | bytes 258056 | tf_op jit(solution)/shard_map/ppermute | solution.py:1005

commit v11 on v10

--- a/solution.py
+++ b/solution.py
@@ -661,7 +661,7 @@
     half = W1 // 2
     middle = LANES // 2
     lane8 = lane_of((C1, LANES))
-    often = 8 if NC1 * NL1 <= 4096 else 1
+    often = 4 if NC1 * NL1 <= 4096 else 1
 
     def blk_of(d):
         return lax.rem(blk - d + n_blk, n_blk) if relative else d
@@ -704,7 +704,7 @@
         face_lane = jnp.where(length == 0, middle, middle - H)
         near8 = jnp.logical_and(lane8 >= face_lane, lane8 < face_lane + H)
         at_face = jnp.logical_and(lane_of((NC1, LANES)) >= face_lane, lane_of((NC1, LANES)) < face_lane + H)
-        for d in range(n_blk):
+        def unpack_mine(d):
             row = pl.multiple_of(C1 * blk_of(d), C1)
             beside = len_brief[pl.ds(32 + row, C1), :]
             for i in range(half):
@@ -714,6 +714,8 @@
                     turn = lax.rem(face_lane - H * i - middle * k + 2 * LANES, LANES)
                     rest = jnp.where(near8, pltpu.roll(beside, turn, 1), 0.0)
                     b1[1 + wall * W1 + i + half * k, pl.ds(row, C1), :] = jnp.where(here8, value, rest)
+
+        loop(0, n_blk, unpack_mine, 1)
 
         def two_planes(tile):
             turned = pltpu.roll(tile, middle, 1)
@@ -747,28 +749,33 @@
         rows2 = NC1 // 2
 
         def merged(w, start):
-            one, two = briefs[0, w, start : start + 8, :], briefs[1, w, start : start + 8, :]
+            at = pl.ds(pl.multiple_of(start, 8), 8)
+            one, two = briefs[0, w, at, :], briefs[1, w, at, :]
             even = jnp.where(left_quarter, one, pltpu.roll(two, quarter, 1))
             odd = jnp.where(left_quarter, pltpu.roll(one, LANES - quarter, 1), two)
             return even, odd
 
-        for w in range(n_wall):
-            for t in range(rows2 // 8):
-                lines = [briefs[h, w, pl.ds(32 + 16 * t, 8, stride=2), :] for h in range(2)]
-                lines = [lanes_at(x, jnp.minimum(96 + lane_8 // 4, LANES - 1)) for x in lines]
-                lines = coef1[2] * jnp.where(lane_8 % 4 < 2, lines[1], lines[0])
-                for p in range(half // 4):
-                    tiles = merged(w, rows2 * p + 8 * t)
-                    for odd in range(2):
-                        for high in range(2):
-                            k = 2 * p + odd + half // 2 * high
-                            value = lanes_at(tiles[odd], pairs_index[high])
-                            line = pltpu.roll(lines, middle - 2 - 4 * k, 1)
-                            value = value + jnp.where(facing, line, 0.0)
-                            if k == (half - 1 if w == 0 else 0):
-                                value = value + coef1[0] * lanes_at(merged(1 - w, 32 + 8 * t)[1], pairs_index[0])
-                            for r in range(2):
-                                b2[1 + w * half + k, pl.ds(16 * t + r, 8, stride=2), :] = value
+        def fill(n):
+            w, t = n // 2, n % 2
+            lines = [briefs[h, w, pl.ds(32 + 16 * t, 8, stride=2), :] for h in range(2)]
+            lines = [lanes_at(x, jnp.minimum(96 + lane_8 // 4, LANES - 1)) for x in lines]
+            lines = coef1[2] * jnp.where(lane_8 % 4 < 2, lines[1], lines[0])
+            for p in range(half // 4):
+                tiles = merged(w, rows2 * p + 8 * t)
+                for odd in range(2):
+                    for high in range(2):
+                        k = 2 * p + odd + half // 2 * high
+                        value = lanes_at(tiles[odd], pairs_index[high])
+                        value = value + jnp.where(facing, pltpu.roll(lines, middle - 2 - 4 * k, 1), 0.0)
+                        for r in range(2):
+                            b2[1 + w * half + k, pl.ds(16 * t + r, 8, stride=2), :] = value
+            value = coef1[0] * lanes_at(merged(1 - w, 32 + 8 * t)[1], pairs_index[0])
+            for r in range(2):
+                at = pl.ds(16 * t + r, 8, stride=2)
+                b2[half + w, at, :] = b2[half + w, at, :] + value
+
+        assert rows2 == 16 and n_wall == 2
+        loop(0, 4, fill, 1)
 
     def total_of(x, wsum, level, by):
         coef = level_coef(level)

time: 40.8 us -> 41.6 us (1.020)
  Pallas kernels: 17.8 us -> 18.6 us
    pallas_call x1, Pallas kernels: 5.62 us -> 6.36 us  [body(): call(functools.partial(solve, (n_blk, n_len, n_wall), relative, compacted...]
where the time goes in v11:
time: 41.6 us; the launch traced here: 41.4 us
  Pallas kernels  18.6 us (45%)
  starting transfers between devices  11.3 us (27%)
  waiting for transfers between devices  10.2 us (25%)
  between operations  0.7 us (2%)
  local copies, waits for them, and re-layouts  0.66 us (2%)
    ppermute x10, starting transfers between devices, ring(): return lax.ppermute(x, axis, [(i, (i + by) % count) for i in range(count)])  11.2 us
    ppermute x10, waiting for transfers between devices, ring(): return lax.ppermute(x, axis, [(i, (i + by) % count) for i in range(count)])  7.19 us
    pallas_call x1, Pallas kernels, body(): call(functools.partial(solve, (n_blk, n_len, n_wall), relative, compacted...  6.36 us
    pallas_call x1, Pallas kernels, body(): call(functools.partial(sector, n_len, n_wall, C, electrodes), [vmem] * (6...  5.41 us
    pallas_call x1, Pallas kernels, body(): call(functools.partial(source_part, n_len, n_wall, C), [vmem] * 6, [(own,...  3.25 us
    ppermute x1, waiting for transfers between devices, across(): return lax.ppermute(x, ('len', 'wall'), pairs)  3.01 us
    pallas_call x1, Pallas kernels, body(): call(functools.partial(pack_faces, n_len), ['hbm'] * 4, [(own, vmem)] * 4...  1.67 us
  transfers between devices with their start and end apart: 11, of which 6 were waited for; matrix products, arithmetic and copies ran while one was open for 0% of the time, Pallas kernels for 21%

profile of v11, /device:TPU:0, one launch (start us, length us, event | category | flops | bytes accessed | tf_op | source)
XLA Modules:
  0.0 41.4 jit_solution(6823380839755098138)
XLA Ops:
  0.6 1.7 %faces.1 = (f32[512,128]{1,0:T(8,128)S(1)}, f32[512,128]{1,0:T(8,128)S(1)}, f32[512,128]{1,0:T(8,128)S(1)}, f32[512,128]{1,0:T(8,128)S(1)}, f32[12,16,128]{2,1,0...) custom-call(f32[512,128]{1,0:T(8,128)} %bitcast.13, f32[512,128]{1,0:T(8,128)} %bitcast.14, ...), custom_call_target="tpu_custom_call" | custom-call | tf_op jit(solution)/shard_map/faces/pallas_call | solution.py:1052
  2.3 0.5 %collective-permute-start = (f32[12,16,128]{2,1,0:T(8,128)S(1)}, f32[12,16,128]{2,1,0:T(8,128)S(1)}, u32[]{:S(2)}, u32[]{:S(2)}) collective-permute-start(f32[12,16,128]{2,1,0:T(8,128)S(1)} %get-tuple-element.37), channel_id=1, source_target_pairs={{0,1},{1,0},{2,3},{3,2},{4,5},{5,4},{6,7},{7,6},{8,9},{9,8},{10,11... | collective-permute-start | bytes 294920 | tf_op jit(solution)/shard_map/ppermute | solution.py:1012
  2.8 2.6 %collective-permute-start.1 = (f32[4,16,128]{2,1,0:T(8,128)S(1)}, f32[4,16,128]{2,1,0:T(8,128)S(1)}, u32[]{:S(2)}, u32[]{:S(2)}) collective-permute-start(f32[4,16,128]{2,1,0:T(8,128)S(1)} %get-tuple-element.38), channel_id=1, source_target_pairs={{0,2},{2,0},{1,3},{3,1},{4,6},{6,4},{5,7},{7,5},{8,10},{10,8},{9,1... | collective-permute-start | bytes 98312 | tf_op jit(solution)/shard_map/ppermute | solution.py:1012
  5.4 0.1 collective-permute-start.2
  5.5 3.0 %collective-permute-done.2.refs_6_ = f32[16,128]{1,0:T(8,128)S(1)} collective-permute-done((f32[16,128]{1,0:T(8,128)S(1)}, f32[16,128]{1,0:T(8,128)S(1)}, u32[]{:S(2)}, u32[]{:S(2)}) %collective-permute-start.2) | collective-permute-done | bytes 8224 | tf_op jit(solution)/shard_map/ppermute | solution.py:1018
  8.5 0.0 collective-permute-done.1.refs_5_
  8.5 0.0 collective-permute-done.refs_4_
  8.5 0.8 %boundary.1 = (f32[184,128]{1,0:T(8,128)S(1)}, f32[184,128]{1,0:T(8,128)S(1)}, f32[2,6,40,128]{3,2,1,0:T(8,128)S(1)}) custom-call(f32[512,128]{1,0:T(8,128)S(1)} %get-tuple-element.33.refs_0_, f32[512,128]{1,0:T(8,128)S(1)} %get-tuple-element.34.refs_1_, f32[512,128]{1,0:T(8,128)S(1)} %get-tuple-element.35.refs_2_.mask.refs_7_, ...), custom_call_target="tpu_custom_call" | custom-call | tf_op jit(solution)/shard_map/boundary/pallas_call | solution.py:1074
  9.3 3.7 %collective-permute-start.3 = (f32[184,128]{1,0:T(8,128)S(1)}, f32[184,128]{1,0:T(8,128)S(1)}, u32[]{:S(2)}, u32[]{:S(2)}) collective-permute-start(f32[184,128]{1,0:T(8,128)S(1)} %get-tuple-element.41), channel_id=1, source_target_pairs={{0,12},{4,0},{8,4},{12,8},{1,13},{5,1},{9,5},{13,9},{2,14},{6,2},{... | collective-permute-start | bytes 282632 | tf_op jit(solution)/shard_map/ppermute | solution.py:1012
  12.9 0.0 copy-start.1
  12.9 0.0 collective-permute-start.4
  12.9 0.7 %copy-done.1 = s32[32]{0:T(128)S(1)} copy-done((s32[32]{0:T(128)S(1)}, s32[32]{0:T(128)}, u32[]{:S(2)}) %copy-start.1) | copy-done | bytes 152
  13.6 0.0 copy-start
  13.6 5.4 %sector.1 = (f32[640,128]{1,0:T(8,128)S(1)}, f32[640,128]{1,0:T(8,128)S(1)}, f32[640,128]{1,0:T(8,128)S(1)}, f32[64,128]{1,0:T(8,128)S(1)}, f32[16,128]{1,0:T(8,128)S(1)}, /*index=5*/f32[8,128]{1,0:T(8,128)S(1)}) custom-call(f32[512,128]{1,0:T(8,128)S(1)} %get-tuple-element.33.refs_0_, f32[512,128]{1,0:T(8,128)S(1)} %get-tuple-element.34.refs_1_, ...), custom_call_target="tpu_custom_call" | custom-call | flops 16000000 | bytes 16000000 | tf_op jit(solution)/shard_map/sector/pallas_call | solution.py:1083
  19.0 0.0 collective-permute-done.3.from_next
  19.0 0.3 collective-permute-done.4.from_prev
  19.3 0.0 copy-done
  19.3 0.7 %correct.1 = (f32[8,40,128]{2,1,0:T(8,128)S(1)}, f32[8,40,128]{2,1,0:T(8,128)S(1)}, f32[88,128]{1,0:T(8,128)S(1)}) custom-call(f32[2,6,40,128]{3,2,1,0:T(8,128)S(1)} %get-tuple-element.40.own_rows, f32[184,128]{1,0:T(8,128)S(1)} %collective-permute-done.3.from_next, f32[184,128]{1,0:T(8,128)S(1)} %collective-permute-done.4.from_prev, ...), custom_call_target="tpu_custom_call" | custom-call | tf_op jit(solution)/shard_map/correct/pallas_call | solution.py:1095
  20.1 2.9 %collective-permute-start.7 = (f32[88,128]{1,0:T(8,128)S(1)}, f32[88,128]{1,0:T(8,128)S(1)}, u32[]{:S(2)}, u32[]{:S(2)}) collective-permute-start(f32[88,128]{1,0:T(8,128)S(1)} %get-tuple-element.45), channel_id=1, source_target_pairs={{0,12},{4,0},{8,4},{12,8},{1,13},{5,1},{9,5},{13,9},{2,14},{6,2},{... | collective-permute-start | bytes 135176 | tf_op jit(solution)/shard_map/ppermute | solution.py:1012
  23.0 0.0 collective-permute-start.6
  23.0 0.6 %collective-permute-start.5 = (f32[88,128]{1,0:T(8,128)S(1)}, f32[88,128]{1,0:T(8,128)S(1)}, u32[]{:S(2)}, u32[]{:S(2)}) collective-permute-start(f32[88,128]{1,0:T(8,128)S(1)} %get-tuple-element.45), channel_id=1, source_target_pairs={{0,4},{4,8},{8,12},{12,0},{1,5},{5,9},{9,13},{13,1},{2,6},{6,10},{... | collective-permute-start | bytes 135176 | tf_op jit(solution)/shard_map/ppermute | solution.py:1012
  23.6 3.2 %source_part.1 = (f32[512,128]{1,0:T(8,128)S(1)}, f32[512,128]{1,0:T(8,128)S(1)}) custom-call(f32[640,128]{1,0:T(8,128)S(1)} %get-tuple-element.46.bm, f32[640,128]{1,0:T(8,128)S(1)} %get-tuple-element.47.be, f32[8,40,128]{2,1,0:T(8,128)S(1)} %get-tuple-element.48.rows_n, f32[8,40,128]{2,1,0:T(8,128)S(1)} %get-tuple-element.49.rows_p, ...), custom_call_target="tpu_custom_call" | custom-call | flops 12000000 | bytes 12000000 | tf_op jit(solution)/shard_map/source_part/pallas_call | solution.py:1105
  26.8 0.0 collective-permute-done.7
  26.8 1.1 %collective-permute-done.6 = f32[88,128]{1,0:T(8,128)S(1)} collective-permute-done((f32[88,128]{1,0:T(8,128)S(1)}, f32[88,128]{1,0:T(8,128)S(1)}, u32[]{:S(2)}, u32[]{:S(2)}) %collective-permute-start.6) | collective-permute-done | bytes 45088 | tf_op jit(solution)/shard_map/ppermute | solution.py:1012
  27.9 0.9 %collective-permute-done.5 = f32[88,128]{1,0:T(8,128)S(1)} collective-permute-done((f32[88,128]{1,0:T(8,128)S(1)}, f32[88,128]{1,0:T(8,128)S(1)}, u32[]{:S(2)}, u32[]{:S(2)}) %collective-permute-start.5) | collective-permute-done | bytes 45088 | tf_op jit(solution)/shard_map/ppermute | solution.py:1012
  28.9 0.3 compact.1
  29.2 0.9 %collective-permute-start.8 = (f32[168,128]{1,0:T(8,128)S(1)}, f32[168,128]{1,0:T(8,128)S(1)}, u32[]{:S(2)}, u32[]{:S(2)}) collective-permute-start(f32[168,128]{1,0:T(8,128)S(1)} %get-tuple-element.55.refs_4_), channel_id=1, source_target_pairs={{0,2},{2,0},{1,3},{3,1},{4,6},{6,4},{5,7},{7,5},{8,10},{10,8},{9,1... | collective-permute-start | bytes 258056 | tf_op jit(solution)/shard_map/ppermute | solution.py:1012
  30.1 0.0 collective-permute-start.9
  30.1 3.6 %collective-permute-done.8.refs_1_ = f32[168,128]{1,0:T(8,128)S(1)} collective-permute-done((f32[168,128]{1,0:T(8,128)S(1)}, f32[168,128]{1,0:T(8,128)S(1)}, u32[]{:S(2)}, u32[]{:S(2)}) %collective-permute-start.8) | collective-permute-done | bytes 86048 | tf_op jit(solution)/shard_map/ppermute | solution.py:1012
  33.7 0.0 collective-permute-start.10
  33.7 0.0 collective-permute-done.9.refs_2_
  33.7 1.3 %collective-permute-done.10.refs_3_ = f32[168,128]{1,0:T(8,128)S(1)} collective-permute-done((f32[168,128]{1,0:T(8,128)S(1)}, f32[168,128]{1,0:T(8,128)S(1)}, u32[]{:S(2)}, u32[]{:S(2)}) %collective-permute-start.10) | collective-permute-done | bytes 86048 | tf_op jit(solution)/shard_map/ppermute | solution.py:1012
  35.0 6.4 %solve.1 = (f32[512,128]{1,0:T(8,128)}, f32[512,128]{1,0:T(8,128)}, f32[1,2]{1,0:T(1,128)}) custom-call(f32[4,88,128]{2,1,0:T(8,128)S(1)} %pad_maximum_fusion.blocks.refs_0_, f32[168,128]{1,0:T(8,128)S(1)} %collective-permute-done.8.refs_1_, f32[200,128]{1,0:T(8,128)S(1)} %collective-permute-done.9.refs_2_, f32[168,128]{1,0:T(8,128)S(1)} %collective-permute-done.10.refs_3_, ...), custom_call_target="tpu_custom_call" | custom-call | tf_op jit(solution)/shard_map/solve/pallas_call | solution.py:1142
  (1 shorter events, 0.0 us)
Async XLA Ops:
  2.3 6.2 %collective-permute-start = (f32[12,16,128]{2,1,0:T(8,128)S(1)}, f32[12,16,128]{2,1,0:T(8,128)S(1)}, u32[]{:S(2)}, u32[]{:S(2)}) collective-permute-start(f32[12,16,128]{2,1,0:T(8,128)S(1)} %get-tuple-element.37), channel_id=1, source_target_pairs={{0,1},{1,0},{2,3},{3,2},{4,5},{5,4},{6,7},{7,6},{8,9},{9,8},{10,11... | collective-permute-start | bytes 294920 | tf_op jit(solution)/shard_map/ppermute | solution.py:1012
  2.8 5.6 %collective-permute-start.1 = (f32[4,16,128]{2,1,0:T(8,128)S(1)}, f32[4,16,128]{2,1,0:T(8,128)S(1)}, u32[]{:S(2)}, u32[]{:S(2)}) collective-permute-start(f32[4,16,128]{2,1,0:T(8,128)S(1)} %get-tuple-element.38), channel_id=1, source_target_pairs={{0,2},{2,0},{1,3},{3,1},{4,6},{6,4},{5,7},{7,5},{8,10},{10,8},{9,1... | collective-permute-start | bytes 98312 | tf_op jit(solution)/shard_map/ppermute | solution.py:1012
  5.4 3.1 %collective-permute-start.2 = (f32[16,128]{1,0:T(8,128)S(1)}, f32[16,128]{1,0:T(8,128)S(1)}, u32[]{:S(2)}, u32[]{:S(2)}) collective-permute-start(f32[16,128]{1,0:T(8,128)S(1)} %get-tuple-element.39), channel_id=1, source_target_pairs={{0,3},{1,2},{2,1},{3,0},{4,7},{5,6},{6,5},{7,4},{8,11},{9,10},{10,... | collective-permute-start | bytes 24584 | tf_op jit(solution)/shard_map/ppermute | solution.py:1018
  9.3 9.7 %collective-permute-start.3 = (f32[184,128]{1,0:T(8,128)S(1)}, f32[184,128]{1,0:T(8,128)S(1)}, u32[]{:S(2)}, u32[]{:S(2)}) collective-permute-start(f32[184,128]{1,0:T(8,128)S(1)} %get-tuple-element.41), channel_id=1, source_target_pairs={{0,12},{4,0},{8,4},{12,8},{1,13},{5,1},{9,5},{13,9},{2,14},{6,2},{... | collective-permute-start | bytes 282632 | tf_op jit(solution)/shard_map/ppermute | solution.py:1012
  12.9 0.7 %copy-start.1 = (s32[32]{0:T(128)S(1)}, s32[32]{0:T(128)}, u32[]{:S(2)}) copy-start(s32[32]{0:T(128)} %param.11) | copy-start | bytes 388
  12.9 6.4 %collective-permute-start.4 = (f32[184,128]{1,0:T(8,128)S(1)}, f32[184,128]{1,0:T(8,128)S(1)}, u32[]{:S(2)}, u32[]{:S(2)}) collective-permute-start(f32[184,128]{1,0:T(8,128)S(1)} %get-tuple-element.42), channel_id=1, source_target_pairs={{0,4},{4,8},{8,12},{12,0},{1,5},{5,9},{9,13},{13,1},{2,6},{6,10},{... | collective-permute-start | bytes 282632 | tf_op jit(solution)/shard_map/ppermute | solution.py:1012
  13.6 5.7 %copy-start = (s32[1,16,128]{2,1,0:T(8,128)S(1)}, s32[1,16,128]{2,1,0:T(8,128)}, u32[]{:S(2)}) copy-start(s32[1,16,128]{2,1,0:T(8,128)} %ids.1) | copy-start | bytes 24580
  20.1 6.8 %collective-permute-start.7 = (f32[88,128]{1,0:T(8,128)S(1)}, f32[88,128]{1,0:T(8,128)S(1)}, u32[]{:S(2)}, u32[]{:S(2)}) collective-permute-start(f32[88,128]{1,0:T(8,128)S(1)} %get-tuple-element.45), channel_id=1, source_target_pairs={{0,12},{4,0},{8,4},{12,8},{1,13},{5,1},{9,5},{13,9},{2,14},{6,2},{... | collective-permute-start | bytes 135176 | tf_op jit(solution)/shard_map/ppermute | solution.py:1012
  23.0 4.9 %collective-permute-start.6 = (f32[88,128]{1,0:T(8,128)S(1)}, f32[88,128]{1,0:T(8,128)S(1)}, u32[]{:S(2)}, u32[]{:S(2)}) collective-permute-start(f32[88,128]{1,0:T(8,128)S(1)} %get-tuple-element.45), channel_id=1, source_target_pairs={{0,8},{4,12},{8,0},{12,4},{1,9},{5,13},{9,1},{13,5},{2,10},{6,14},... | collective-permute-start | bytes 135176 | tf_op jit(solution)/shard_map/ppermute | solution.py:1012
  23.0 5.8 %collective-permute-start.5 = (f32[88,128]{1,0:T(8,128)S(1)}, f32[88,128]{1,0:T(8,128)S(1)}, u32[]{:S(2)}, u32[]{:S(2)}) collective-permute-start(f32[88,128]{1,0:T(8,128)S(1)} %get-tuple-element.45), channel_id=1, source_target_pairs={{0,4},{4,8},{8,12},{12,0},{1,5},{5,9},{9,13},{13,1},{2,6},{6,10},{... | collective-permute-start | bytes 135176 | tf_op jit(solution)/shard_map/ppermute | solution.py:1012
  29.2 4.6 %collective-permute-start.8 = (f32[168,128]{1,0:T(8,128)S(1)}, f32[168,128]{1,0:T(8,128)S(1)}, u32[]{:S(2)}, u32[]{:S(2)}) collective-permute-start(f32[168,128]{1,0:T(8,128)S(1)} %get-tuple-element.55.refs_4_), channel_id=1, source_target_pairs={{0,2},{2,0},{1,3},{3,1},{4,6},{6,4},{5,7},{7,5},{8,10},{10,8},{9,1... | collective-permute-start | bytes 258056 | tf_op jit(solution)/shard_map/ppermute | solution.py:1012
  30.1 3.6 %collective-permute-start.9 = (f32[200,128]{1,0:T(8,128)S(1)}, f32[200,128]{1,0:T(8,128)S(1)}, u32[]{:S(2)}, u32[]{:S(2)}) collective-permute-start(f32[200,128]{1,0:T(8,128)S(1)} %get-tuple-element.56), channel_id=1, source_target_pairs={{0,1},{1,0},{2,3},{3,2},{4,5},{5,4},{6,7},{7,6},{8,9},{9,8},{10,11... | collective-permute-start | bytes 307208 | tf_op jit(solution)/shard_map/ppermute | solution.py:1012
  33.7 1.3 %collective-permute-start.10 = (f32[168,128]{1,0:T(8,128)S(1)}, f32[168,128]{1,0:T(8,128)S(1)}, u32[]{:S(2)}, u32[]{:S(2)}) collective-permute-start(f32[168,128]{1,0:T(8,128)S(1)} %collective-permute-done.8.refs_1_), channel_id=1, source_target_pairs={{0,1},{1,0},{2,3},{3,2},{4,5},{5,4},{6,7},{7,6},{8,9},{9,8},{10,11... | collective-permute-start | bytes 258056 | tf_op jit(solution)/shard_map/ppermute | solution.py:1012

commit v12 on v10

--- a/solution.py
+++ b/solution.py
@@ -85,7 +85,11 @@
         step(i)
         return carry
 
-    lax.fori_loop(low, high, wrapped, 0, unroll=min(unroll, high - low))
+    if unroll >= high - low:
+        for i in range(low, high):
+            step(i)
+        return
+    lax.fori_loop(low, high, wrapped, 0, unroll=unroll)
 
 
 FACES = (H, H - 1, H - 1, H - 2)
@@ -661,7 +665,7 @@
     half = W1 // 2
     middle = LANES // 2
     lane8 = lane_of((C1, LANES))
-    often = 8 if NC1 * NL1 <= 4096 else 1
+    often = 40 if NC1 * NL1 <= 4096 else 1
 
     def blk_of(d):
         return lax.rem(blk - d + n_blk, n_blk) if relative else d
@@ -850,7 +854,7 @@
         set_plane(near, 2 * q, C1, value[:C1])
         set_plane(near, 2 * q + 1, C1, jnp.where(row8 < 2, value[C1 : 2 * C1], value[2 * C1 :]))
 
-    loop(0, Q, finish1, min(often, 6))
+    loop(0, Q, finish1, often)
 
     first = length * middle
     R = C + 8
@@ -886,7 +890,7 @@
             for k in range(3):
                 out[pl.ds(pl.multiple_of(8 + R * q + 8 * k, 8), 8), :] = rows_at(parts[k], index[k])
 
-    loop(0, Q, fine_rows, min(often, 6))
+    loop(0, Q, fine_rows, often)
     for ref in (pm, pe):
         ref[0:8, :] = jnp.zeros((8, LANES), F32)
         ref[8 + R * Q : 16 + R * Q, :] = jnp.zeros((8, LANES), F32)
@@ -921,7 +925,7 @@
             set_fine(tm, t, gm + ks * fine(pm, other))
             set_fine(te, t, jnp.where(rim, ge + ks * fine(pe, other), 0.0))
 
-    loop(1, 1 + W1, level0, 4)
+    loop(1, 1 + W1, level0, often)
 
     def finish0(w):
         t = w + 1
@@ -937,7 +941,7 @@
     size = W // parts
     copies = []
     for k in range(parts):
-        loop(k * size, (k + 1) * size, finish0, 4)
+        loop(k * size, (k + 1) * size, finish0, often)
         spot = pl.ds(k * size * C, size * C)
         for n, (src, dst) in enumerate(((adj_out, adj_prev), (pot_out, potential))):
             copies.append(pltpu.make_async_copy(src.at[spot], dst.at[spot], sems.at[n, k]))

time: 40.8 us -> 39.7 us (0.973)
  Pallas kernels: 17.8 us -> 16.7 us
    pallas_call x1, Pallas kernels: 5.62 us -> 4.5 us  [body(): call(functools.partial(solve, (n_blk, n_len, n_wall), relative, compacted...]
  transfers between devices with their start and end apart: 11 -> 11, of which waited for: 6 -> 6; matrix products, arithmetic and copies ran while one was open for 0% -> 0% of each run, Pallas kernels for 21% -> 22%
where the time goes in v12:
time: 39.7 us; the launch traced here: 39.5 us
  Pallas kernels  16.7 us (42%)
  starting transfers between devices  11.3 us (28%)
  waiting for transfers between devices  10.2 us (26%)
  between operations  0.7 us (2%)
  local copies, waits for them, and re-layouts  0.66 us (2%)
    ppermute x10, starting transfers between devices, ring(): return lax.ppermute(x, axis, [(i, (i + by) % count) for i in range(count)])  11.2 us
    ppermute x10, waiting for transfers between devices, ring(): return lax.ppermute(x, axis, [(i, (i + by) % count) for i in range(count)])  7.19 us
    pallas_call x1, Pallas kernels, body(): call(functools.partial(sector, n_len, n_wall, C, electrodes), [vmem] * (6...  5.41 us
    pallas_call x1, Pallas kernels, body(): call(functools.partial(solve, (n_blk, n_len, n_wall), relative, compacted...  4.5 us
    pallas_call x1, Pallas kernels, body(): call(functools.partial(source_part, n_len, n_wall, C), [vmem] * 6, [(own,...  3.25 us
    ppermute x1, waiting for transfers between devices, across(): return lax.ppermute(x, ('len', 'wall'), pairs)  3.01 us
    pallas_call x1, Pallas kernels, body(): call(functools.partial(pack_faces, n_len), ['hbm'] * 4, [(own, vmem)] * 4...  1.67 us
    pallas_call x1, Pallas kernels, body(): call(functools.partial(boundary, n_len, C), [vmem] * (5 + 2 * n_dir), [(n...  0.8 us
  transfers between devices with their start and end apart: 11, of which 6 were waited for; matrix products, arithmetic and copies ran while one was open for 0% of the time, Pallas kernels for 22%

profile of v12, /device:TPU:0, one launch (start us, length us, event | category | flops | bytes accessed | tf_op | source)
XLA Modules:
  0.0 39.5 jit_solution(9820258866868829679)
XLA Ops:
  0.6 1.7 %faces.1 = (f32[512,128]{1,0:T(8,128)S(1)}, f32[512,128]{1,0:T(8,128)S(1)}, f32[512,128]{1,0:T(8,128)S(1)}, f32[512,128]{1,0:T(8,128)S(1)}, f32[12,16,128]{2,1,0...) custom-call(f32[512,128]{1,0:T(8,128)} %bitcast.13, f32[512,128]{1,0:T(8,128)} %bitcast.14, ...), custom_call_target="tpu_custom_call" | custom-call | tf_op jit(solution)/shard_map/faces/pallas_call | solution.py:1049
  2.3 0.5 %collective-permute-start = (f32[12,16,128]{2,1,0:T(8,128)S(1)}, f32[12,16,128]{2,1,0:T(8,128)S(1)}, u32[]{:S(2)}, u32[]{:S(2)}) collective-permute-start(f32[12,16,128]{2,1,0:T(8,128)S(1)} %get-tuple-element.37), channel_id=1, source_target_pairs={{0,1},{1,0},{2,3},{3,2},{4,5},{5,4},{6,7},{7,6},{8,9},{9,8},{10,11... | collective-permute-start | bytes 294920 | tf_op jit(solution)/shard_map/ppermute | solution.py:1009
  2.8 2.6 %collective-permute-start.1 = (f32[4,16,128]{2,1,0:T(8,128)S(1)}, f32[4,16,128]{2,1,0:T(8,128)S(1)}, u32[]{:S(2)}, u32[]{:S(2)}) collective-permute-start(f32[4,16,128]{2,1,0:T(8,128)S(1)} %get-tuple-element.38), channel_id=1, source_target_pairs={{0,2},{2,0},{1,3},{3,1},{4,6},{6,4},{5,7},{7,5},{8,10},{10,8},{9,1... | collective-permute-start | bytes 98312 | tf_op jit(solution)/shard_map/ppermute | solution.py:1009
  5.4 0.1 collective-permute-start.2
  5.5 3.0 %collective-permute-done.2.refs_6_ = f32[16,128]{1,0:T(8,128)S(1)} collective-permute-done((f32[16,128]{1,0:T(8,128)S(1)}, f32[16,128]{1,0:T(8,128)S(1)}, u32[]{:S(2)}, u32[]{:S(2)}) %collective-permute-start.2) | collective-permute-done | bytes 8224 | tf_op jit(solution)/shard_map/ppermute | solution.py:1015
  8.5 0.0 collective-permute-done.1.refs_5_
  8.5 0.0 collective-permute-done.refs_4_
  8.5 0.8 %boundary.1 = (f32[184,128]{1,0:T(8,128)S(1)}, f32[184,128]{1,0:T(8,128)S(1)}, f32[2,6,40,128]{3,2,1,0:T(8,128)S(1)}) custom-call(f32[512,128]{1,0:T(8,128)S(1)} %get-tuple-element.33.refs_0_, f32[512,128]{1,0:T(8,128)S(1)} %get-tuple-element.34.refs_1_, f32[512,128]{1,0:T(8,128)S(1)} %get-tuple-element.35.refs_2_.mask.refs_7_, ...), custom_call_target="tpu_custom_call" | custom-call | tf_op jit(solution)/shard_map/boundary/pallas_call | solution.py:1071
  9.3 3.7 %collective-permute-start.3 = (f32[184,128]{1,0:T(8,128)S(1)}, f32[184,128]{1,0:T(8,128)S(1)}, u32[]{:S(2)}, u32[]{:S(2)}) collective-permute-start(f32[184,128]{1,0:T(8,128)S(1)} %get-tuple-element.41), channel_id=1, source_target_pairs={{0,12},{4,0},{8,4},{12,8},{1,13},{5,1},{9,5},{13,9},{2,14},{6,2},{... | collective-permute-start | bytes 282632 | tf_op jit(solution)/shard_map/ppermute | solution.py:1009
  12.9 0.0 copy-start.1
  12.9 0.0 collective-permute-start.4
  12.9 0.7 %copy-done.1 = s32[32]{0:T(128)S(1)} copy-done((s32[32]{0:T(128)S(1)}, s32[32]{0:T(128)}, u32[]{:S(2)}) %copy-start.1) | copy-done | bytes 152
  13.6 0.0 copy-start
  13.6 5.4 %sector.1 = (f32[640,128]{1,0:T(8,128)S(1)}, f32[640,128]{1,0:T(8,128)S(1)}, f32[640,128]{1,0:T(8,128)S(1)}, f32[64,128]{1,0:T(8,128)S(1)}, f32[16,128]{1,0:T(8,128)S(1)}, /*index=5*/f32[8,128]{1,0:T(8,128)S(1)}) custom-call(f32[512,128]{1,0:T(8,128)S(1)} %get-tuple-element.33.refs_0_, f32[512,128]{1,0:T(8,128)S(1)} %get-tuple-element.34.refs_1_, ...), custom_call_target="tpu_custom_call" | custom-call | flops 16000000 | bytes 16000000 | tf_op jit(solution)/shard_map/sector/pallas_call | solution.py:1080
  19.0 0.0 collective-permute-done.3.from_next
  19.0 0.3 collective-permute-done.4.from_prev
  19.3 0.0 copy-done
  19.3 0.7 %correct.1 = (f32[8,40,128]{2,1,0:T(8,128)S(1)}, f32[8,40,128]{2,1,0:T(8,128)S(1)}, f32[88,128]{1,0:T(8,128)S(1)}) custom-call(f32[2,6,40,128]{3,2,1,0:T(8,128)S(1)} %get-tuple-element.40.own_rows, f32[184,128]{1,0:T(8,128)S(1)} %collective-permute-done.3.from_next, f32[184,128]{1,0:T(8,128)S(1)} %collective-permute-done.4.from_prev, ...), custom_call_target="tpu_custom_call" | custom-call | tf_op jit(solution)/shard_map/correct/pallas_call | solution.py:1092
  20.1 2.9 %collective-permute-start.7 = (f32[88,128]{1,0:T(8,128)S(1)}, f32[88,128]{1,0:T(8,128)S(1)}, u32[]{:S(2)}, u32[]{:S(2)}) collective-permute-start(f32[88,128]{1,0:T(8,128)S(1)} %get-tuple-element.45), channel_id=1, source_target_pairs={{0,12},{4,0},{8,4},{12,8},{1,13},{5,1},{9,5},{13,9},{2,14},{6,2},{... | collective-permute-start | bytes 135176 | tf_op jit(solution)/shard_map/ppermute | solution.py:1009
  23.0 0.0 collective-permute-start.6
  23.0 0.6 %collective-permute-start.5 = (f32[88,128]{1,0:T(8,128)S(1)}, f32[88,128]{1,0:T(8,128)S(1)}, u32[]{:S(2)}, u32[]{:S(2)}) collective-permute-start(f32[88,128]{1,0:T(8,128)S(1)} %get-tuple-element.45), channel_id=1, source_target_pairs={{0,4},{4,8},{8,12},{12,0},{1,5},{5,9},{9,13},{13,1},{2,6},{6,10},{... | collective-permute-start | bytes 135176 | tf_op jit(solution)/shard_map/ppermute | solution.py:1009
  23.6 3.2 %source_part.1 = (f32[512,128]{1,0:T(8,128)S(1)}, f32[512,128]{1,0:T(8,128)S(1)}) custom-call(f32[640,128]{1,0:T(8,128)S(1)} %get-tuple-element.46.bm, f32[640,128]{1,0:T(8,128)S(1)} %get-tuple-element.47.be, f32[8,40,128]{2,1,0:T(8,128)S(1)} %get-tuple-element.48.rows_n, f32[8,40,128]{2,1,0:T(8,128)S(1)} %get-tuple-element.49.rows_p, ...), custom_call_target="tpu_custom_call" | custom-call | flops 12000000 | bytes 12000000 | tf_op jit(solution)/shard_map/source_part/pallas_call | solution.py:1102
  26.8 0.0 collective-permute-done.7
  26.8 1.1 %collective-permute-done.6 = f32[88,128]{1,0:T(8,128)S(1)} collective-permute-done((f32[88,128]{1,0:T(8,128)S(1)}, f32[88,128]{1,0:T(8,128)S(1)}, u32[]{:S(2)}, u32[]{:S(2)}) %collective-permute-start.6) | collective-permute-done | bytes 45088 | tf_op jit(solution)/shard_map/ppermute | solution.py:1009
  27.9 0.9 %collective-permute-done.5 = f32[88,128]{1,0:T(8,128)S(1)} collective-permute-done((f32[88,128]{1,0:T(8,128)S(1)}, f32[88,128]{1,0:T(8,128)S(1)}, u32[]{:S(2)}, u32[]{:S(2)}) %collective-permute-start.5) | collective-permute-done | bytes 45088 | tf_op jit(solution)/shard_map/ppermute | solution.py:1009
  28.9 0.3 compact.1
  29.2 0.9 %collective-permute-start.8 = (f32[168,128]{1,0:T(8,128)S(1)}, f32[168,128]{1,0:T(8,128)S(1)}, u32[]{:S(2)}, u32[]{:S(2)}) collective-permute-start(f32[168,128]{1,0:T(8,128)S(1)} %get-tuple-element.55.refs_4_), channel_id=1, source_target_pairs={{0,2},{2,0},{1,3},{3,1},{4,6},{6,4},{5,7},{7,5},{8,10},{10,8},{9,1... | collective-permute-start | bytes 258056 | tf_op jit(solution)/shard_map/ppermute | solution.py:1009
  30.1 0.0 collective-permute-start.9
  30.1 3.6 %collective-permute-done.8.refs_1_ = f32[168,128]{1,0:T(8,128)S(1)} collective-permute-done((f32[168,128]{1,0:T(8,128)S(1)}, f32[168,128]{1,0:T(8,128)S(1)}, u32[]{:S(2)}, u32[]{:S(2)}) %collective-permute-start.8) | collective-permute-done | bytes 86048 | tf_op jit(solution)/shard_map/ppermute | solution.py:1009
  33.7 0.0 collective-permute-start.10
  33.7 0.0 collective-permute-done.9.refs_2_
  33.7 1.3 %collective-permute-done.10.refs_3_ = f32[168,128]{1,0:T(8,128)S(1)} collective-permute-done((f32[168,128]{1,0:T(8,128)S(1)}, f32[168,128]{1,0:T(8,128)S(1)}, u32[]{:S(2)}, u32[]{:S(2)}) %collective-permute-start.10) | collective-permute-done | bytes 86048 | tf_op jit(solution)/shard_map/ppermute | solution.py:1009
  35.0 4.5 %solve.1 = (f32[512,128]{1,0:T(8,128)}, f32[512,128]{1,0:T(8,128)}, f32[1,2]{1,0:T(1,128)}) custom-call(f32[4,88,128]{2,1,0:T(8,128)S(1)} %pad_maximum_fusion.blocks.refs_0_, f32[168,128]{1,0:T(8,128)S(1)} %collective-permute-done.8.refs_1_, f32[200,128]{1,0:T(8,128)S(1)} %collective-permute-done.9.refs_2_, f32[168,128]{1,0:T(8,128)S(1)} %collective-permute-done.10.refs_3_, ...), custom_call_target="tpu_custom_call" | custom-call | tf_op jit(solution)/shard_map/solve/pallas_call | solution.py:1139
  (1 shorter events, 0.0 us)
Async XLA Ops:
  2.3 6.2 %collective-permute-start = (f32[12,16,128]{2,1,0:T(8,128)S(1)}, f32[12,16,128]{2,1,0:T(8,128)S(1)}, u32[]{:S(2)}, u32[]{:S(2)}) collective-permute-start(f32[12,16,128]{2,1,0:T(8,128)S(1)} %get-tuple-element.37), channel_id=1, source_target_pairs={{0,1},{1,0},{2,3},{3,2},{4,5},{5,4},{6,7},{7,6},{8,9},{9,8},{10,11... | collective-permute-start | bytes 294920 | tf_op jit(solution)/shard_map/ppermute | solution.py:1009
  2.8 5.6 %collective-permute-start.1 = (f32[4,16,128]{2,1,0:T(8,128)S(1)}, f32[4,16,128]{2,1,0:T(8,128)S(1)}, u32[]{:S(2)}, u32[]{:S(2)}) collective-permute-start(f32[4,16,128]{2,1,0:T(8,128)S(1)} %get-tuple-element.38), channel_id=1, source_target_pairs={{0,2},{2,0},{1,3},{3,1},{4,6},{6,4},{5,7},{7,5},{8,10},{10,8},{9,1... | collective-permute-start | bytes 98312 | tf_op jit(solution)/shard_map/ppermute | solution.py:1009
  5.4 3.1 %collective-permute-start.2 = (f32[16,128]{1,0:T(8,128)S(1)}, f32[16,128]{1,0:T(8,128)S(1)}, u32[]{:S(2)}, u32[]{:S(2)}) collective-permute-start(f32[16,128]{1,0:T(8,128)S(1)} %get-tuple-element.39), channel_id=1, source_target_pairs={{0,3},{1,2},{2,1},{3,0},{4,7},{5,6},{6,5},{7,4},{8,11},{9,10},{10,... | collective-permute-start | bytes 24584 | tf_op jit(solution)/shard_map/ppermute | solution.py:1015
  9.3 9.7 %collective-permute-start.3 = (f32[184,128]{1,0:T(8,128)S(1)}, f32[184,128]{1,0:T(8,128)S(1)}, u32[]{:S(2)}, u32[]{:S(2)}) collective-permute-start(f32[184,128]{1,0:T(8,128)S(1)} %get-tuple-element.41), channel_id=1, source_target_pairs={{0,12},{4,0},{8,4},{12,8},{1,13},{5,1},{9,5},{13,9},{2,14},{6,2},{... | collective-permute-start | bytes 282632 | tf_op jit(solution)/shard_map/ppermute | solution.py:1009
  12.9 0.7 %copy-start.1 = (s32[32]{0:T(128)S(1)}, s32[32]{0:T(128)}, u32[]{:S(2)}) copy-start(s32[32]{0:T(128)} %param.11) | copy-start | bytes 388
  12.9 6.4 %collective-permute-start.4 = (f32[184,128]{1,0:T(8,128)S(1)}, f32[184,128]{1,0:T(8,128)S(1)}, u32[]{:S(2)}, u32[]{:S(2)}) collective-permute-start(f32[184,128]{1,0:T(8,128)S(1)} %get-tuple-element.42), channel_id=1, source_target_pairs={{0,4},{4,8},{8,12},{12,0},{1,5},{5,9},{9,13},{13,1},{2,6},{6,10},{... | collective-permute-start | bytes 282632 | tf_op jit(solution)/shard_map/ppermute | solution.py:1009
  13.6 5.7 %copy-start = (s32[1,16,128]{2,1,0:T(8,128)S(1)}, s32[1,16,128]{2,1,0:T(8,128)}, u32[]{:S(2)}) copy-start(s32[1,16,128]{2,1,0:T(8,128)} %ids.1) | copy-start | bytes 24580
  20.1 6.8 %collective-permute-start.7 = (f32[88,128]{1,0:T(8,128)S(1)}, f32[88,128]{1,0:T(8,128)S(1)}, u32[]{:S(2)}, u32[]{:S(2)}) collective-permute-start(f32[88,128]{1,0:T(8,128)S(1)} %get-tuple-element.45), channel_id=1, source_target_pairs={{0,12},{4,0},{8,4},{12,8},{1,13},{5,1},{9,5},{13,9},{2,14},{6,2},{... | collective-permute-start | bytes 135176 | tf_op jit(solution)/shard_map/ppermute | solution.py:1009
  23.0 4.9 %collective-permute-start.6 = (f32[88,128]{1,0:T(8,128)S(1)}, f32[88,128]{1,0:T(8,128)S(1)}, u32[]{:S(2)}, u32[]{:S(2)}) collective-permute-start(f32[88,128]{1,0:T(8,128)S(1)} %get-tuple-element.45), channel_id=1, source_target_pairs={{0,8},{4,12},{8,0},{12,4},{1,9},{5,13},{9,1},{13,5},{2,10},{6,14},... | collective-permute-start | bytes 135176 | tf_op jit(solution)/shard_map/ppermute | solution.py:1009
  23.0 5.8 %collective-permute-start.5 = (f32[88,128]{1,0:T(8,128)S(1)}, f32[88,128]{1,0:T(8,128)S(1)}, u32[]{:S(2)}, u32[]{:S(2)}) collective-permute-start(f32[88,128]{1,0:T(8,128)S(1)} %get-tuple-element.45), channel_id=1, source_target_pairs={{0,4},{4,8},{8,12},{12,0},{1,5},{5,9},{9,13},{13,1},{2,6},{6,10},{... | collective-permute-start | bytes 135176 | tf_op jit(solution)/shard_map/ppermute | solution.py:1009
  29.2 4.6 %collective-permute-start.8 = (f32[168,128]{1,0:T(8,128)S(1)}, f32[168,128]{1,0:T(8,128)S(1)}, u32[]{:S(2)}, u32[]{:S(2)}) collective-permute-start(f32[168,128]{1,0:T(8,128)S(1)} %get-tuple-element.55.refs_4_), channel_id=1, source_target_pairs={{0,2},{2,0},{1,3},{3,1},{4,6},{6,4},{5,7},{7,5},{8,10},{10,8},{9,1... | collective-permute-start | bytes 258056 | tf_op jit(solution)/shard_map/ppermute | solution.py:1009
  30.1 3.6 %collective-permute-start.9 = (f32[200,128]{1,0:T(8,128)S(1)}, f32[200,128]{1,0:T(8,128)S(1)}, u32[]{:S(2)}, u32[]{:S(2)}) collective-permute-start(f32[200,128]{1,0:T(8,128)S(1)} %get-tuple-element.56), channel_id=1, source_target_pairs={{0,1},{1,0},{2,3},{3,2},{4,5},{5,4},{6,7},{7,6},{8,9},{9,8},{10,11... | collective-permute-start | bytes 307208 | tf_op jit(solution)/shard_map/ppermute | solution.py:1009
  33.7 1.3 %collective-permute-start.10 = (f32[168,128]{1,0:T(8,128)S(1)}, f32[168,128]{1,0:T(8,128)S(1)}, u32[]{:S(2)}, u32[]{:S(2)}) collective-permute-start(f32[168,128]{1,0:T(8,128)S(1)} %collective-permute-done.8.refs_1_), channel_id=1, source_target_pairs={{0,1},{1,0},{2,3},{3,2},{4,5},{5,4},{6,7},{7,6},{8,9},{9,8},{10,11... | collective-permute-start | bytes 258056 | tf_op jit(solution)/shard_map/ppermute | solution.py:1009

commit v13 on v12

--- a/solution.py
+++ b/solution.py
@@ -352,7 +352,7 @@
         set_plane(qm, i, C, m - DT * plane(xm[2], i, C) * (dm + plane(xm[1], i, C) * m))
         set_plane(qe, i, C, e - DT * plane(xe[2], i, C) * (de + plane(xe[1], i, C) * e))
 
-    loop(1, N - 1, parabolic, 2)
+    loop(1, N - 1, parabolic, N)
 
     def elliptic_source(i):
         m, e, dm, de = spots(qm, qe, i, C, SI)
@@ -360,7 +360,7 @@
         set_plane(bm, i, C, jnp.where(ok, plane(xm[3], i, C) + dm, 0.0))
         set_plane(be, i, C, jnp.where(jnp.logical_and(rim, ok), plane(xe[3], i, C) + de, 0.0))
 
-    loop(2, N - 2, elliptic_source, 2)
+    loop(2, N - 2, elliptic_source, N)
 
     coef, k0 = level_coef(0), level_step(0)
 
@@ -385,7 +385,7 @@
         def _():
             surface[...] = k0 * (n + second)
 
-    loop(0, W // 2, pair, 2)
+    loop(0, W // 2, pair, W)
 
     half = W * C // 8
     z = pairs[pl.ds(0, 2 * half, stride=2), :] + pairs[pl.ds(1, 2 * half, stride=2), :]
@@ -501,7 +501,7 @@
     def one(e):
         sums[pl.ds(e, 1), :] = jnp.sum(jnp.where(patch == e, y, 0.0), axis=0, keepdims=True)
 
-    loop(0, electrodes, one, 8)
+    loop(0, electrodes, one, 32 if electrodes <= 32 else 8)
     totals = lax.dot_general(
         jnp.ones((8, LANES), F32), sums[...], (((1,), (1,)), ((), ())), precision=HIGHEST, preferred_element_type=F32
     )
@@ -1119,7 +1119,7 @@
             "compact",
         )(sector_blocks)
         len_brief = ring(brief, "len", 1)
-        blocks = [sector_blocks, len_brief, ring(across_wall, "wall", 1), ring(len_brief, "wall", 1), brief]
+        blocks = [sector_blocks, len_brief, ring(across_wall, "wall", 1), across(brief), brief]
     elif n_len == 2:
         here = [sector_blocks, ring(sector_blocks, "len", 1)]
     else:

time: 39.7 us -> 39.6 us (level)
  Pallas kernels: 16.7 us -> 12.7 us
  waiting for transfers between devices: 10.2 us -> 14.2 us
    pallas_call x1, Pallas kernels: 5.41 us -> 1.63 us  [body(): call(functools.partial(sector, n_len, n_wall, C, electrodes), [vmem] * (6...]
    ppermute x1 -> x2, waiting for transfers between devices: 3.01 us -> 5.19 us  [across(): return lax.ppermute(x, ('len', 'wall'), pairs)]
    ppermute x10 -> x9, waiting for transfers between devices: 7.19 us -> 8.99 us  [ring(): return lax.ppermute(x, axis, [(i, (i + by) % count) for i in range(count)])]
    ppermute x10 -> x9, starting transfers between devices: 11.2 us -> 10.1 us  [ring(): return lax.ppermute(x, axis, [(i, (i + by) % count) for i in range(count)])]
    ppermute x1 -> x2, starting transfers between devices: 0.07 us -> 1.02 us  [across(): return lax.ppermute(x, ('len', 'wall'), pairs)]
  transfers between devices with their start and end apart: 11 -> 11, of which waited for: 6 -> 7; matrix products, arithmetic and copies ran while one was open for 0% -> 0% of each run, Pallas kernels for 22% -> 12%
where the time goes in v13:
time: 39.6 us; the launch traced here: 39.4 us
  waiting for transfers between devices  14.2 us (36%)
  Pallas kernels  12.7 us (32%)
  starting transfers between devices  11.1 us (28%)
  between operations  0.7 us (2%)
  local copies, waits for them, and re-layouts  0.66 us (2%)
    ppermute x9, starting transfers between devices, ring(): return lax.ppermute(x, axis, [(i, (i + by) % count) for i in range(count)])  10.1 us
    ppermute x9, waiting for transfers between devices, ring(): return lax.ppermute(x, axis, [(i, (i + by) % count) for i in range(count)])  8.99 us
    ppermute x2, waiting for transfers between devices, across(): return lax.ppermute(x, ('len', 'wall'), pairs)  5.19 us
    pallas_call x1, Pallas kernels, body(): call(functools.partial(solve, (n_blk, n_len, n_wall), relative, compacted...  4.5 us
    pallas_call x1, Pallas kernels, body(): call(functools.partial(source_part, n_len, n_wall, C), [vmem] * 6, [(own,...  3.25 us
    pallas_call x1, Pallas kernels, body(): call(functools.partial(pack_faces, n_len), ['hbm'] * 4, [(own, vmem)] * 4...  1.67 us
    pallas_call x1, Pallas kernels, body(): call(functools.partial(sector, n_len, n_wall, C, electrodes), [vmem] * (6...  1.63 us
    ppermute x2, starting transfers between devices, across(): return lax.ppermute(x, ('len', 'wall'), pairs)  1.02 us
  transfers between devices with their start and end apart: 11, of which 7 were waited for; matrix products, arithmetic and copies ran while one was open for 0% of the time, Pallas kernels for 12%

profile of v13, /device:TPU:0, one launch (start us, length us, event | category | flops | bytes accessed | tf_op | source)
XLA Modules:
  0.0 39.4 jit_solution(11273165052848392343)
XLA Ops:
  0.6 1.7 %faces.1 = (f32[512,128]{1,0:T(8,128)S(1)}, f32[512,128]{1,0:T(8,128)S(1)}, f32[512,128]{1,0:T(8,128)S(1)}, f32[512,128]{1,0:T(8,128)S(1)}, f32[12,16,128]{2,1,0...) custom-call(f32[512,128]{1,0:T(8,128)} %bitcast.13, f32[512,128]{1,0:T(8,128)} %bitcast.14, ...), custom_call_target="tpu_custom_call" | custom-call | tf_op jit(solution)/shard_map/faces/pallas_call | solution.py:1049
  2.3 0.5 %collective-permute-start = (f32[12,16,128]{2,1,0:T(8,128)S(1)}, f32[12,16,128]{2,1,0:T(8,128)S(1)}, u32[]{:S(2)}, u32[]{:S(2)}) collective-permute-start(f32[12,16,128]{2,1,0:T(8,128)S(1)} %get-tuple-element.37), channel_id=1, source_target_pairs={{0,1},{1,0},{2,3},{3,2},{4,5},{5,4},{6,7},{7,6},{8,9},{9,8},{10,11... | collective-permute-start | bytes 294920 | tf_op jit(solution)/shard_map/ppermute | solution.py:1009
  2.8 2.6 %collective-permute-start.1 = (f32[4,16,128]{2,1,0:T(8,128)S(1)}, f32[4,16,128]{2,1,0:T(8,128)S(1)}, u32[]{:S(2)}, u32[]{:S(2)}) collective-permute-start(f32[4,16,128]{2,1,0:T(8,128)S(1)} %get-tuple-element.38), channel_id=1, source_target_pairs={{0,2},{2,0},{1,3},{3,1},{4,6},{6,4},{5,7},{7,5},{8,10},{10,8},{9,1... | collective-permute-start | bytes 98312 | tf_op jit(solution)/shard_map/ppermute | solution.py:1009
  5.4 0.1 collective-permute-start.2
  5.5 3.0 %collective-permute-done.2.refs_6_ = f32[16,128]{1,0:T(8,128)S(1)} collective-permute-done((f32[16,128]{1,0:T(8,128)S(1)}, f32[16,128]{1,0:T(8,128)S(1)}, u32[]{:S(2)}, u32[]{:S(2)}) %collective-permute-start.2) | collective-permute-done | bytes 8224 | tf_op jit(solution)/shard_map/ppermute | solution.py:1015
  8.5 0.0 collective-permute-done.1.refs_5_
  8.5 0.0 collective-permute-done.refs_4_
  8.5 0.8 %boundary.1 = (f32[184,128]{1,0:T(8,128)S(1)}, f32[184,128]{1,0:T(8,128)S(1)}, f32[2,6,40,128]{3,2,1,0:T(8,128)S(1)}) custom-call(f32[512,128]{1,0:T(8,128)S(1)} %get-tuple-element.33.refs_0_, f32[512,128]{1,0:T(8,128)S(1)} %get-tuple-element.34.refs_1_, f32[512,128]{1,0:T(8,128)S(1)} %get-tuple-element.35.refs_2_.mask.refs_7_, ...), custom_call_target="tpu_custom_call" | custom-call | tf_op jit(solution)/shard_map/boundary/pallas_call | solution.py:1071
  9.3 3.7 %collective-permute-start.3 = (f32[184,128]{1,0:T(8,128)S(1)}, f32[184,128]{1,0:T(8,128)S(1)}, u32[]{:S(2)}, u32[]{:S(2)}) collective-permute-start(f32[184,128]{1,0:T(8,128)S(1)} %get-tuple-element.41), channel_id=1, source_target_pairs={{0,12},{4,0},{8,4},{12,8},{1,13},{5,1},{9,5},{13,9},{2,14},{6,2},{... | collective-permute-start | bytes 282632 | tf_op jit(solution)/shard_map/ppermute | solution.py:1009
  12.9 0.0 copy-start.1
  12.9 0.0 collective-permute-start.4
  12.9 0.7 %copy-done.1 = s32[32]{0:T(128)S(1)} copy-done((s32[32]{0:T(128)S(1)}, s32[32]{0:T(128)}, u32[]{:S(2)}) %copy-start.1) | copy-done | bytes 152
  13.6 0.0 copy-start
  13.6 1.6 %sector.1 = (f32[640,128]{1,0:T(8,128)S(1)}, f32[640,128]{1,0:T(8,128)S(1)}, f32[640,128]{1,0:T(8,128)S(1)}, f32[64,128]{1,0:T(8,128)S(1)}, f32[16,128]{1,0:T(8,128)S(1)}, /*index=5*/f32[8,128]{1,0:T(8,128)S(1)}) custom-call(f32[512,128]{1,0:T(8,128)S(1)} %get-tuple-element.33.refs_0_, f32[512,128]{1,0:T(8,128)S(1)} %get-tuple-element.34.refs_1_, ...), custom_call_target="tpu_custom_call" | custom-call | flops 16000000 | bytes 16000000 | tf_op jit(solution)/shard_map/sector/pallas_call | solution.py:1080
  15.2 0.8 %collective-permute-done.3.from_next = f32[184,128]{1,0:T(8,128)S(1)} collective-permute-done((f32[184,128]{1,0:T(8,128)S(1)}, f32[184,128]{1,0:T(8,128)S(1)}, u32[]{:S(2)}, u32[]{:S(2)}) %collective-permute-start.3) | collective-permute-done | bytes 94240 | tf_op jit(solution)/shard_map/ppermute | solution.py:1009
  16.1 3.3 %collective-permute-done.4.from_prev = f32[184,128]{1,0:T(8,128)S(1)} collective-permute-done((f32[184,128]{1,0:T(8,128)S(1)}, f32[184,128]{1,0:T(8,128)S(1)}, u32[]{:S(2)}, u32[]{:S(2)}) %collective-permute-start.4) | collective-permute-done | bytes 94240 | tf_op jit(solution)/shard_map/ppermute | solution.py:1009
  19.3 0.0 copy-done
  19.3 0.6 %correct.1 = (f32[8,40,128]{2,1,0:T(8,128)S(1)}, f32[8,40,128]{2,1,0:T(8,128)S(1)}, f32[88,128]{1,0:T(8,128)S(1)}) custom-call(f32[2,6,40,128]{3,2,1,0:T(8,128)S(1)} %get-tuple-element.40.own_rows, f32[184,128]{1,0:T(8,128)S(1)} %collective-permute-done.3.from_next, f32[184,128]{1,0:T(8,128)S(1)} %collective-permute-done.4.from_prev, ...), custom_call_target="tpu_custom_call" | custom-call | tf_op jit(solution)/shard_map/correct/pallas_call | solution.py:1092
  19.9 1.1 %collective-permute-start.7 = (f32[88,128]{1,0:T(8,128)S(1)}, f32[88,128]{1,0:T(8,128)S(1)}, u32[]{:S(2)}, u32[]{:S(2)}) collective-permute-start(f32[88,128]{1,0:T(8,128)S(1)} %get-tuple-element.45), channel_id=1, source_target_pairs={{0,12},{4,0},{8,4},{12,8},{1,13},{5,1},{9,5},{13,9},{2,14},{6,2},{... | collective-permute-start | bytes 135176 | tf_op jit(solution)/shard_map/ppermute | solution.py:1009
  21.0 0.9 %collective-permute-start.6 = (f32[88,128]{1,0:T(8,128)S(1)}, f32[88,128]{1,0:T(8,128)S(1)}, u32[]{:S(2)}, u32[]{:S(2)}) collective-permute-start(f32[88,128]{1,0:T(8,128)S(1)} %get-tuple-element.45), channel_id=1, source_target_pairs={{0,8},{4,12},{8,0},{12,4},{1,9},{5,13},{9,1},{13,5},{2,10},{6,14},... | collective-permute-start | bytes 135176 | tf_op jit(solution)/shard_map/ppermute | solution.py:1009
  21.9 0.1 collective-permute-start.5
  22.0 3.2 %source_part.1 = (f32[512,128]{1,0:T(8,128)S(1)}, f32[512,128]{1,0:T(8,128)S(1)}) custom-call(f32[640,128]{1,0:T(8,128)S(1)} %get-tuple-element.46.bm, f32[640,128]{1,0:T(8,128)S(1)} %get-tuple-element.47.be, f32[8,40,128]{2,1,0:T(8,128)S(1)} %get-tuple-element.48.rows_n, f32[8,40,128]{2,1,0:T(8,128)S(1)} %get-tuple-element.49.rows_p, ...), custom_call_target="tpu_custom_call" | custom-call | flops 12000000 | bytes 12000000 | tf_op jit(solution)/shard_map/source_part/pallas_call | solution.py:1102
  25.2 0.0 collective-permute-done.7
  25.2 1.3 %collective-permute-done.6 = f32[88,128]{1,0:T(8,128)S(1)} collective-permute-done((f32[88,128]{1,0:T(8,128)S(1)}, f32[88,128]{1,0:T(8,128)S(1)}, u32[]{:S(2)}, u32[]{:S(2)}) %collective-permute-start.6) | collective-permute-done | bytes 45088 | tf_op jit(solution)/shard_map/ppermute | solution.py:1009
  26.5 1.2 %collective-permute-done.5 = f32[88,128]{1,0:T(8,128)S(1)} collective-permute-done((f32[88,128]{1,0:T(8,128)S(1)}, f32[88,128]{1,0:T(8,128)S(1)}, u32[]{:S(2)}, u32[]{:S(2)}) %collective-permute-start.5) | collective-permute-done | bytes 45088 | tf_op jit(solution)/shard_map/ppermute | solution.py:1009
  27.7 0.3 compact.1
  28.1 0.1 collective-permute-start.9
  28.1 0.9 %collective-permute-start.10 = (f32[168,128]{1,0:T(8,128)S(1)}, f32[168,128]{1,0:T(8,128)S(1)}, u32[]{:S(2)}, u32[]{:S(2)}) collective-permute-start(f32[168,128]{1,0:T(8,128)S(1)} %get-tuple-element.55.refs_4_), channel_id=1, source_target_pairs={{0,3},{1,2},{2,1},{3,0},{4,7},{5,6},{6,5},{7,4},{8,11},{9,10},{10,... | collective-permute-start | bytes 258056 | tf_op jit(solution)/shard_map/ppermute | solution.py:1015
  29.1 1.2 %collective-permute-start.8 = (f32[168,128]{1,0:T(8,128)S(1)}, f32[168,128]{1,0:T(8,128)S(1)}, u32[]{:S(2)}, u32[]{:S(2)}) collective-permute-start(f32[168,128]{1,0:T(8,128)S(1)} %get-tuple-element.55.refs_4_), channel_id=1, source_target_pairs={{0,2},{2,0},{1,3},{3,1},{4,6},{6,4},{5,7},{7,5},{8,10},{10,8},{9,1... | collective-permute-start | bytes 258056 | tf_op jit(solution)/shard_map/ppermute | solution.py:1009
  30.3 2.2 %collective-permute-done.10.refs_3_ = f32[168,128]{1,0:T(8,128)S(1)} collective-permute-done((f32[168,128]{1,0:T(8,128)S(1)}, f32[168,128]{1,0:T(8,128)S(1)}, u32[]{:S(2)}, u32[]{:S(2)}) %collective-permute-start.10) | collective-permute-done | bytes 86048 | tf_op jit(solution)/shard_map/ppermute | solution.py:1015
  32.5 2.4 %collective-permute-done.8.refs_1_ = f32[168,128]{1,0:T(8,128)S(1)} collective-permute-done((f32[168,128]{1,0:T(8,128)S(1)}, f32[168,128]{1,0:T(8,128)S(1)}, u32[]{:S(2)}, u32[]{:S(2)}) %collective-permute-start.8) | collective-permute-done | bytes 86048 | tf_op jit(solution)/shard_map/ppermute | solution.py:1009
  34.9 0.0 collective-permute-done.9.refs_2_
  34.9 4.5 %solve.1 = (f32[512,128]{1,0:T(8,128)}, f32[512,128]{1,0:T(8,128)}, f32[1,2]{1,0:T(1,128)}) custom-call(f32[4,88,128]{2,1,0:T(8,128)S(1)} %pad_maximum_fusion.blocks.refs_0_, f32[168,128]{1,0:T(8,128)S(1)} %collective-permute-done.8.refs_1_, f32[200,128]{1,0:T(8,128)S(1)} %collective-permute-done.9.refs_2_, f32[168,128]{1,0:T(8,128)S(1)} %collective-permute-done.10.refs_3_, ...), custom_call_target="tpu_custom_call" | custom-call | tf_op jit(solution)/shard_map/solve/pallas_call | solution.py:1139
  (1 shorter events, 0.0 us)
Async XLA Ops:
  2.3 6.2 %collective-permute-start = (f32[12,16,128]{2,1,0:T(8,128)S(1)}, f32[12,16,128]{2,1,0:T(8,128)S(1)}, u32[]{:S(2)}, u32[]{:S(2)}) collective-permute-start(f32[12,16,128]{2,1,0:T(8,128)S(1)} %get-tuple-element.37), channel_id=1, source_target_pairs={{0,1},{1,0},{2,3},{3,2},{4,5},{5,4},{6,7},{7,6},{8,9},{9,8},{10,11... | collective-permute-start | bytes 294920 | tf_op jit(solution)/shard_map/ppermute | solution.py:1009
  2.8 5.6 %collective-permute-start.1 = (f32[4,16,128]{2,1,0:T(8,128)S(1)}, f32[4,16,128]{2,1,0:T(8,128)S(1)}, u32[]{:S(2)}, u32[]{:S(2)}) collective-permute-start(f32[4,16,128]{2,1,0:T(8,128)S(1)} %get-tuple-element.38), channel_id=1, source_target_pairs={{0,2},{2,0},{1,3},{3,1},{4,6},{6,4},{5,7},{7,5},{8,10},{10,8},{9,1... | collective-permute-start | bytes 98312 | tf_op jit(solution)/shard_map/ppermute | solution.py:1009
  5.4 3.1 %collective-permute-start.2 = (f32[16,128]{1,0:T(8,128)S(1)}, f32[16,128]{1,0:T(8,128)S(1)}, u32[]{:S(2)}, u32[]{:S(2)}) collective-permute-start(f32[16,128]{1,0:T(8,128)S(1)} %get-tuple-element.39), channel_id=1, source_target_pairs={{0,3},{1,2},{2,1},{3,0},{4,7},{5,6},{6,5},{7,4},{8,11},{9,10},{10,... | collective-permute-start | bytes 24584 | tf_op jit(solution)/shard_map/ppermute | solution.py:1015
  9.3 6.8 %collective-permute-start.3 = (f32[184,128]{1,0:T(8,128)S(1)}, f32[184,128]{1,0:T(8,128)S(1)}, u32[]{:S(2)}, u32[]{:S(2)}) collective-permute-start(f32[184,128]{1,0:T(8,128)S(1)} %get-tuple-element.41), channel_id=1, source_target_pairs={{0,12},{4,0},{8,4},{12,8},{1,13},{5,1},{9,5},{13,9},{2,14},{6,2},{... | collective-permute-start | bytes 282632 | tf_op jit(solution)/shard_map/ppermute | solution.py:1009
  12.9 0.7 %copy-start.1 = (s32[32]{0:T(128)S(1)}, s32[32]{0:T(128)}, u32[]{:S(2)}) copy-start(s32[32]{0:T(128)} %param.11) | copy-start | bytes 388
  12.9 6.4 %collective-permute-start.4 = (f32[184,128]{1,0:T(8,128)S(1)}, f32[184,128]{1,0:T(8,128)S(1)}, u32[]{:S(2)}, u32[]{:S(2)}) collective-permute-start(f32[184,128]{1,0:T(8,128)S(1)} %get-tuple-element.42), channel_id=1, source_target_pairs={{0,4},{4,8},{8,12},{12,0},{1,5},{5,9},{9,13},{13,1},{2,6},{6,10},{... | collective-permute-start | bytes 282632 | tf_op jit(solution)/shard_map/ppermute | solution.py:1009
  13.6 5.7 %copy-start = (s32[1,16,128]{2,1,0:T(8,128)S(1)}, s32[1,16,128]{2,1,0:T(8,128)}, u32[]{:S(2)}) copy-start(s32[1,16,128]{2,1,0:T(8,128)} %ids.1) | copy-start | bytes 24580
  19.9 5.3 %collective-permute-start.7 = (f32[88,128]{1,0:T(8,128)S(1)}, f32[88,128]{1,0:T(8,128)S(1)}, u32[]{:S(2)}, u32[]{:S(2)}) collective-permute-start(f32[88,128]{1,0:T(8,128)S(1)} %get-tuple-element.45), channel_id=1, source_target_pairs={{0,12},{4,0},{8,4},{12,8},{1,13},{5,1},{9,5},{13,9},{2,14},{6,2},{... | collective-permute-start | bytes 135176 | tf_op jit(solution)/shard_map/ppermute | solution.py:1009
  21.0 5.5 %collective-permute-start.6 = (f32[88,128]{1,0:T(8,128)S(1)}, f32[88,128]{1,0:T(8,128)S(1)}, u32[]{:S(2)}, u32[]{:S(2)}) collective-permute-start(f32[88,128]{1,0:T(8,128)S(1)} %get-tuple-element.45), channel_id=1, source_target_pairs={{0,8},{4,12},{8,0},{12,4},{1,9},{5,13},{9,1},{13,5},{2,10},{6,14},... | collective-permute-start | bytes 135176 | tf_op jit(solution)/shard_map/ppermute | solution.py:1009
  21.9 5.8 %collective-permute-start.5 = (f32[88,128]{1,0:T(8,128)S(1)}, f32[88,128]{1,0:T(8,128)S(1)}, u32[]{:S(2)}, u32[]{:S(2)}) collective-permute-start(f32[88,128]{1,0:T(8,128)S(1)} %get-tuple-element.45), channel_id=1, source_target_pairs={{0,4},{4,8},{8,12},{12,0},{1,5},{5,9},{9,13},{13,1},{2,6},{6,10},{... | collective-permute-start | bytes 135176 | tf_op jit(solution)/shard_map/ppermute | solution.py:1009
  28.1 6.8 %collective-permute-start.9 = (f32[200,128]{1,0:T(8,128)S(1)}, f32[200,128]{1,0:T(8,128)S(1)}, u32[]{:S(2)}, u32[]{:S(2)}) collective-permute-start(f32[200,128]{1,0:T(8,128)S(1)} %get-tuple-element.56), channel_id=1, source_target_pairs={{0,1},{1,0},{2,3},{3,2},{4,5},{5,4},{6,7},{7,6},{8,9},{9,8},{10,11... | collective-permute-start | bytes 307208 | tf_op jit(solution)/shard_map/ppermute | solution.py:1009
  28.1 4.3 %collective-permute-start.10 = (f32[168,128]{1,0:T(8,128)S(1)}, f32[168,128]{1,0:T(8,128)S(1)}, u32[]{:S(2)}, u32[]{:S(2)}) collective-permute-start(f32[168,128]{1,0:T(8,128)S(1)} %get-tuple-element.55.refs_4_), channel_id=1, source_target_pairs={{0,3},{1,2},{2,1},{3,0},{4,7},{5,6},{6,5},{7,4},{8,11},{9,10},{10,... | collective-permute-start | bytes 258056 | tf_op jit(solution)/shard_map/ppermute | solution.py:1015
  29.1 5.8 %collective-permute-start.8 = (f32[168,128]{1,0:T(8,128)S(1)}, f32[168,128]{1,0:T(8,128)S(1)}, u32[]{:S(2)}, u32[]{:S(2)}) collective-permute-start(f32[168,128]{1,0:T(8,128)S(1)} %get-tuple-element.55.refs_4_), channel_id=1, source_target_pairs={{0,2},{2,0},{1,3},{3,1},{4,6},{6,4},{5,7},{7,5},{8,10},{10,8},{9,1... | collective-permute-start | bytes 258056 | tf_op jit(solution)/shard_map/ppermute | solution.py:1009

commit v14 on v13

--- a/solution.py
+++ b/solution.py
@@ -537,7 +537,7 @@
         set_plane(tm, i, C, jnp.where(inside(i, wall, W, n_wall), pm, 0.0))
         set_plane(te, i, C, jnp.where(rim, pe, 0.0))
 
-    loop(H - 1, N - H + 1, part, 2)
+    loop(H - 1, N - H + 1, part, N)
     for side, (rows, at) in enumerate(((rows_n, C - 1), (rows_p, 0))):
         m = rows[0]
         total = (
@@ -561,7 +561,7 @@
         set_plane(base_adj, w, C, lam - DT * plane(mask, w, C) * moved)
         set_plane(base_pot, w, C, m)
 
-    loop(0, W, finish, 2)
+    loop(0, W, finish, W)
 
 
 def halves(shape):
@@ -1119,7 +1119,7 @@
             "compact",
         )(sector_blocks)
         len_brief = ring(brief, "len", 1)
-        blocks = [sector_blocks, len_brief, ring(across_wall, "wall", 1), across(brief), brief]
+        blocks = [sector_blocks, len_brief, ring(across_wall, "wall", 1), ring(len_brief, "wall", 1), brief]
     elif n_len == 2:
         here = [sector_blocks, ring(sector_blocks, "len", 1)]
     else:

time: 39.6 us -> 38.6 us (0.975)
  waiting for transfers between devices: 14.2 us -> 17 us
  Pallas kernels: 12.7 us -> 10.3 us
  starting transfers between devices: 11.1 us -> 9.79 us
    ppermute x9 -> x10, waiting for transfers between devices: 8.99 us -> 14 us  [ring(): return lax.ppermute(x, axis, [(i, (i + by) % count) for i in range(count)])]
    pallas_call x1, Pallas kernels: 3.25 us -> 0.78 us  [body(): call(functools.partial(source_part, n_len, n_wall, C), [vmem] * 6, [(own,...]
    ppermute x2 -> x1, waiting for transfers between devices: 5.19 us -> 3.01 us  [across(): return lax.ppermute(x, ('len', 'wall'), pairs)]
    ppermute x2 -> x1, starting transfers between devices: 1.02 us -> 0.07 us  [across(): return lax.ppermute(x, ('len', 'wall'), pairs)]
    ppermute x9 -> x10, starting transfers between devices: 10.1 us -> 9.72 us  [ring(): return lax.ppermute(x, axis, [(i, (i + by) % count) for i in range(count)])]
  transfers between devices with their start and end apart: 11 -> 11, of which waited for: 7 -> 8; matrix products, arithmetic and copies ran while one was open for 0% -> 0% of each run, Pallas kernels for 12% -> 6%
where the time goes in v14:
time: 38.6 us; the launch traced here: 38.4 us
  waiting for transfers between devices  17 us (44%)
  Pallas kernels  10.3 us (27%)
  starting transfers between devices  9.79 us (25%)
  between operations  0.69 us (2%)
  local copies, waits for them, and re-layouts  0.66 us (2%)
    ppermute x10, waiting for transfers between devices, ring(): return lax.ppermute(x, axis, [(i, (i + by) % count) for i in range(count)])  14 us
    ppermute x10, starting transfers between devices, ring(): return lax.ppermute(x, axis, [(i, (i + by) % count) for i in range(count)])  9.72 us
    pallas_call x1, Pallas kernels, body(): call(functools.partial(solve, (n_blk, n_len, n_wall), relative, compacted...  4.5 us
    ppermute x1, waiting for transfers between devices, across(): return lax.ppermute(x, ('len', 'wall'), pairs)  3.01 us
    pallas_call x1, Pallas kernels, body(): call(functools.partial(pack_faces, n_len), ['hbm'] * 4, [(own, vmem)] * 4...  1.67 us
    pallas_call x1, Pallas kernels, body(): call(functools.partial(sector, n_len, n_wall, C, electrodes), [vmem] * (6...  1.63 us
    pallas_call x1, Pallas kernels, body(): call(functools.partial(boundary, n_len, C), [vmem] * (5 + 2 * n_dir), [(n...  0.8 us
    pallas_call x1, Pallas kernels, body(): call(functools.partial(source_part, n_len, n_wall, C), [vmem] * 6, [(own,...  0.78 us
  transfers between devices with their start and end apart: 11, of which 8 were waited for; matrix products, arithmetic and copies ran while one was open for 0% of the time, Pallas kernels for 6%

profile of v14, /device:TPU:0, one launch (start us, length us, event | category | flops | bytes accessed | tf_op | source)
XLA Modules:
  0.0 38.4 jit_solution(9369358710563951766)
XLA Ops:
  0.6 1.7 %faces.1 = (f32[512,128]{1,0:T(8,128)S(1)}, f32[512,128]{1,0:T(8,128)S(1)}, f32[512,128]{1,0:T(8,128)S(1)}, f32[512,128]{1,0:T(8,128)S(1)}, f32[12,16,128]{2,1,0...) custom-call(f32[512,128]{1,0:T(8,128)} %bitcast.13, f32[512,128]{1,0:T(8,128)} %bitcast.14, ...), custom_call_target="tpu_custom_call" | custom-call | tf_op jit(solution)/shard_map/faces/pallas_call | solution.py:1049
  2.3 0.5 %collective-permute-start = (f32[12,16,128]{2,1,0:T(8,128)S(1)}, f32[12,16,128]{2,1,0:T(8,128)S(1)}, u32[]{:S(2)}, u32[]{:S(2)}) collective-permute-start(f32[12,16,128]{2,1,0:T(8,128)S(1)} %get-tuple-element.37), channel_id=1, source_target_pairs={{0,1},{1,0},{2,3},{3,2},{4,5},{5,4},{6,7},{7,6},{8,9},{9,8},{10,11... | collective-permute-start | bytes 294920 | tf_op jit(solution)/shard_map/ppermute | solution.py:1009
  2.8 2.6 %collective-permute-start.1 = (f32[4,16,128]{2,1,0:T(8,128)S(1)}, f32[4,16,128]{2,1,0:T(8,128)S(1)}, u32[]{:S(2)}, u32[]{:S(2)}) collective-permute-start(f32[4,16,128]{2,1,0:T(8,128)S(1)} %get-tuple-element.38), channel_id=1, source_target_pairs={{0,2},{2,0},{1,3},{3,1},{4,6},{6,4},{5,7},{7,5},{8,10},{10,8},{9,1... | collective-permute-start | bytes 98312 | tf_op jit(solution)/shard_map/ppermute | solution.py:1009
  5.4 0.1 collective-permute-start.2
  5.5 3.0 %collective-permute-done.2.refs_6_ = f32[16,128]{1,0:T(8,128)S(1)} collective-permute-done((f32[16,128]{1,0:T(8,128)S(1)}, f32[16,128]{1,0:T(8,128)S(1)}, u32[]{:S(2)}, u32[]{:S(2)}) %collective-permute-start.2) | collective-permute-done | bytes 8224 | tf_op jit(solution)/shard_map/ppermute | solution.py:1015
  8.5 0.0 collective-permute-done.1.refs_5_
  8.5 0.0 collective-permute-done.refs_4_
  8.5 0.8 %boundary.1 = (f32[184,128]{1,0:T(8,128)S(1)}, f32[184,128]{1,0:T(8,128)S(1)}, f32[2,6,40,128]{3,2,1,0:T(8,128)S(1)}) custom-call(f32[512,128]{1,0:T(8,128)S(1)} %get-tuple-element.33.refs_0_, f32[512,128]{1,0:T(8,128)S(1)} %get-tuple-element.34.refs_1_, f32[512,128]{1,0:T(8,128)S(1)} %get-tuple-element.35.refs_2_.mask.refs_7_, ...), custom_call_target="tpu_custom_call" | custom-call | tf_op jit(solution)/shard_map/boundary/pallas_call | solution.py:1071
  9.3 3.7 %collective-permute-start.3 = (f32[184,128]{1,0:T(8,128)S(1)}, f32[184,128]{1,0:T(8,128)S(1)}, u32[]{:S(2)}, u32[]{:S(2)}) collective-permute-start(f32[184,128]{1,0:T(8,128)S(1)} %get-tuple-element.41), channel_id=1, source_target_pairs={{0,12},{4,0},{8,4},{12,8},{1,13},{5,1},{9,5},{13,9},{2,14},{6,2},{... | collective-permute-start | bytes 282632 | tf_op jit(solution)/shard_map/ppermute | solution.py:1009
  12.9 0.0 copy-start.1
  12.9 0.0 collective-permute-start.4
  12.9 0.7 %copy-done.1 = s32[32]{0:T(128)S(1)} copy-done((s32[32]{0:T(128)S(1)}, s32[32]{0:T(128)}, u32[]{:S(2)}) %copy-start.1) | copy-done | bytes 152
  13.6 0.0 copy-start
  13.6 1.6 %sector.1 = (f32[640,128]{1,0:T(8,128)S(1)}, f32[640,128]{1,0:T(8,128)S(1)}, f32[640,128]{1,0:T(8,128)S(1)}, f32[64,128]{1,0:T(8,128)S(1)}, f32[16,128]{1,0:T(8,128)S(1)}, /*index=5*/f32[8,128]{1,0:T(8,128)S(1)}) custom-call(f32[512,128]{1,0:T(8,128)S(1)} %get-tuple-element.33.refs_0_, f32[512,128]{1,0:T(8,128)S(1)} %get-tuple-element.34.refs_1_, ...), custom_call_target="tpu_custom_call" | custom-call | flops 16000000 | bytes 16000000 | tf_op jit(solution)/shard_map/sector/pallas_call | solution.py:1080
  15.2 0.8 %collective-permute-done.3.from_next = f32[184,128]{1,0:T(8,128)S(1)} collective-permute-done((f32[184,128]{1,0:T(8,128)S(1)}, f32[184,128]{1,0:T(8,128)S(1)}, u32[]{:S(2)}, u32[]{:S(2)}) %collective-permute-start.3) | collective-permute-done | bytes 94240 | tf_op jit(solution)/shard_map/ppermute | solution.py:1009
  16.1 3.3 %collective-permute-done.4.from_prev = f32[184,128]{1,0:T(8,128)S(1)} collective-permute-done((f32[184,128]{1,0:T(8,128)S(1)}, f32[184,128]{1,0:T(8,128)S(1)}, u32[]{:S(2)}, u32[]{:S(2)}) %collective-permute-start.4) | collective-permute-done | bytes 94240 | tf_op jit(solution)/shard_map/ppermute | solution.py:1009
  19.3 0.0 copy-done
  19.3 0.6 %correct.1 = (f32[8,40,128]{2,1,0:T(8,128)S(1)}, f32[8,40,128]{2,1,0:T(8,128)S(1)}, f32[88,128]{1,0:T(8,128)S(1)}) custom-call(f32[2,6,40,128]{3,2,1,0:T(8,128)S(1)} %get-tuple-element.40.own_rows, f32[184,128]{1,0:T(8,128)S(1)} %collective-permute-done.3.from_next, f32[184,128]{1,0:T(8,128)S(1)} %collective-permute-done.4.from_prev, ...), custom_call_target="tpu_custom_call" | custom-call | tf_op jit(solution)/shard_map/correct/pallas_call | solution.py:1092
  19.9 1.1 %collective-permute-start.7 = (f32[88,128]{1,0:T(8,128)S(1)}, f32[88,128]{1,0:T(8,128)S(1)}, u32[]{:S(2)}, u32[]{:S(2)}) collective-permute-start(f32[88,128]{1,0:T(8,128)S(1)} %get-tuple-element.45), channel_id=1, source_target_pairs={{0,12},{4,0},{8,4},{12,8},{1,13},{5,1},{9,5},{13,9},{2,14},{6,2},{... | collective-permute-start | bytes 135176 | tf_op jit(solution)/shard_map/ppermute | solution.py:1009
  21.0 0.9 %collective-permute-start.6 = (f32[88,128]{1,0:T(8,128)S(1)}, f32[88,128]{1,0:T(8,128)S(1)}, u32[]{:S(2)}, u32[]{:S(2)}) collective-permute-start(f32[88,128]{1,0:T(8,128)S(1)} %get-tuple-element.45), channel_id=1, source_target_pairs={{0,8},{4,12},{8,0},{12,4},{1,9},{5,13},{9,1},{13,5},{2,10},{6,14},... | collective-permute-start | bytes 135176 | tf_op jit(solution)/shard_map/ppermute | solution.py:1009
  21.9 0.1 collective-permute-start.5
  22.0 0.8 %source_part.1 = (f32[512,128]{1,0:T(8,128)S(1)}, f32[512,128]{1,0:T(8,128)S(1)}) custom-call(f32[640,128]{1,0:T(8,128)S(1)} %get-tuple-element.46.bm, f32[640,128]{1,0:T(8,128)S(1)} %get-tuple-element.47.be, f32[8,40,128]{2,1,0:T(8,128)S(1)} %get-tuple-element.48.rows_n, f32[8,40,128]{2,1,0:T(8,128)S(1)} %get-tuple-element.49.rows_p, ...), custom_call_target="tpu_custom_call" | custom-call | flops 12000000 | bytes 12000000 | tf_op jit(solution)/shard_map/source_part/pallas_call | solution.py:1102
  22.8 1.2 %collective-permute-done.7 = f32[88,128]{1,0:T(8,128)S(1)} collective-permute-done((f32[88,128]{1,0:T(8,128)S(1)}, f32[88,128]{1,0:T(8,128)S(1)}, u32[]{:S(2)}, u32[]{:S(2)}) %collective-permute-start.7) | collective-permute-done | bytes 45088 | tf_op jit(solution)/shard_map/ppermute | solution.py:1009
  24.0 2.5 %collective-permute-done.6 = f32[88,128]{1,0:T(8,128)S(1)} collective-permute-done((f32[88,128]{1,0:T(8,128)S(1)}, f32[88,128]{1,0:T(8,128)S(1)}, u32[]{:S(2)}, u32[]{:S(2)}) %collective-permute-start.6) | collective-permute-done | bytes 45088 | tf_op jit(solution)/shard_map/ppermute | solution.py:1009
  26.5 1.2 %collective-permute-done.5 = f32[88,128]{1,0:T(8,128)S(1)} collective-permute-done((f32[88,128]{1,0:T(8,128)S(1)}, f32[88,128]{1,0:T(8,128)S(1)}, u32[]{:S(2)}, u32[]{:S(2)}) %collective-permute-start.5) | collective-permute-done | bytes 45088 | tf_op jit(solution)/shard_map/ppermute | solution.py:1009
  27.7 0.3 compact.1
  28.1 0.9 %collective-permute-start.8 = (f32[168,128]{1,0:T(8,128)S(1)}, f32[168,128]{1,0:T(8,128)S(1)}, u32[]{:S(2)}, u32[]{:S(2)}) collective-permute-start(f32[168,128]{1,0:T(8,128)S(1)} %get-tuple-element.55.refs_4_), channel_id=1, source_target_pairs={{0,2},{2,0},{1,3},{3,1},{4,6},{6,4},{5,7},{7,5},{8,10},{10,8},{9,1... | collective-permute-start | bytes 258056 | tf_op jit(solution)/shard_map/ppermute | solution.py:1009
  29.0 0.0 collective-permute-start.9
  29.0 3.6 %collective-permute-done.8.refs_1_ = f32[168,128]{1,0:T(8,128)S(1)} collective-permute-done((f32[168,128]{1,0:T(8,128)S(1)}, f32[168,128]{1,0:T(8,128)S(1)}, u32[]{:S(2)}, u32[]{:S(2)}) %collective-permute-start.8) | collective-permute-done | bytes 86048 | tf_op jit(solution)/shard_map/ppermute | solution.py:1009
  32.6 0.0 collective-permute-start.10
  32.6 0.0 collective-permute-done.9.refs_2_
  32.6 1.3 %collective-permute-done.10.refs_3_ = f32[168,128]{1,0:T(8,128)S(1)} collective-permute-done((f32[168,128]{1,0:T(8,128)S(1)}, f32[168,128]{1,0:T(8,128)S(1)}, u32[]{:S(2)}, u32[]{:S(2)}) %collective-permute-start.10) | collective-permute-done | bytes 86048 | tf_op jit(solution)/shard_map/ppermute | solution.py:1009
  33.9 4.5 %solve.1 = (f32[512,128]{1,0:T(8,128)}, f32[512,128]{1,0:T(8,128)}, f32[1,2]{1,0:T(1,128)}) custom-call(f32[4,88,128]{2,1,0:T(8,128)S(1)} %pad_maximum_fusion.blocks.refs_0_, f32[168,128]{1,0:T(8,128)S(1)} %collective-permute-done.8.refs_1_, f32[200,128]{1,0:T(8,128)S(1)} %collective-permute-done.9.refs_2_, f32[168,128]{1,0:T(8,128)S(1)} %collective-permute-done.10.refs_3_, ...), custom_call_target="tpu_custom_call" | custom-call | tf_op jit(solution)/shard_map/solve/pallas_call | solution.py:1139
  (1 shorter events, 0.0 us)
Async XLA Ops:
  2.3 6.2 %collective-permute-start = (f32[12,16,128]{2,1,0:T(8,128)S(1)}, f32[12,16,128]{2,1,0:T(8,128)S(1)}, u32[]{:S(2)}, u32[]{:S(2)}) collective-permute-start(f32[12,16,128]{2,1,0:T(8,128)S(1)} %get-tuple-element.37), channel_id=1, source_target_pairs={{0,1},{1,0},{2,3},{3,2},{4,5},{5,4},{6,7},{7,6},{8,9},{9,8},{10,11... | collective-permute-start | bytes 294920 | tf_op jit(solution)/shard_map/ppermute | solution.py:1009
  2.8 5.6 %collective-permute-start.1 = (f32[4,16,128]{2,1,0:T(8,128)S(1)}, f32[4,16,128]{2,1,0:T(8,128)S(1)}, u32[]{:S(2)}, u32[]{:S(2)}) collective-permute-start(f32[4,16,128]{2,1,0:T(8,128)S(1)} %get-tuple-element.38), channel_id=1, source_target_pairs={{0,2},{2,0},{1,3},{3,1},{4,6},{6,4},{5,7},{7,5},{8,10},{10,8},{9,1... | collective-permute-start | bytes 98312 | tf_op jit(solution)/shard_map/ppermute | solution.py:1009
  5.4 3.1 %collective-permute-start.2 = (f32[16,128]{1,0:T(8,128)S(1)}, f32[16,128]{1,0:T(8,128)S(1)}, u32[]{:S(2)}, u32[]{:S(2)}) collective-permute-start(f32[16,128]{1,0:T(8,128)S(1)} %get-tuple-element.39), channel_id=1, source_target_pairs={{0,3},{1,2},{2,1},{3,0},{4,7},{5,6},{6,5},{7,4},{8,11},{9,10},{10,... | collective-permute-start | bytes 24584 | tf_op jit(solution)/shard_map/ppermute | solution.py:1015
  9.3 6.8 %collective-permute-start.3 = (f32[184,128]{1,0:T(8,128)S(1)}, f32[184,128]{1,0:T(8,128)S(1)}, u32[]{:S(2)}, u32[]{:S(2)}) collective-permute-start(f32[184,128]{1,0:T(8,128)S(1)} %get-tuple-element.41), channel_id=1, source_target_pairs={{0,12},{4,0},{8,4},{12,8},{1,13},{5,1},{9,5},{13,9},{2,14},{6,2},{... | collective-permute-start | bytes 282632 | tf_op jit(solution)/shard_map/ppermute | solution.py:1009
  12.9 0.7 %copy-start.1 = (s32[32]{0:T(128)S(1)}, s32[32]{0:T(128)}, u32[]{:S(2)}) copy-start(s32[32]{0:T(128)} %param.11) | copy-start | bytes 388
  12.9 6.4 %collective-permute-start.4 = (f32[184,128]{1,0:T(8,128)S(1)}, f32[184,128]{1,0:T(8,128)S(1)}, u32[]{:S(2)}, u32[]{:S(2)}) collective-permute-start(f32[184,128]{1,0:T(8,128)S(1)} %get-tuple-element.42), channel_id=1, source_target_pairs={{0,4},{4,8},{8,12},{12,0},{1,5},{5,9},{9,13},{13,1},{2,6},{6,10},{... | collective-permute-start | bytes 282632 | tf_op jit(solution)/shard_map/ppermute | solution.py:1009
  13.6 5.7 %copy-start = (s32[1,16,128]{2,1,0:T(8,128)S(1)}, s32[1,16,128]{2,1,0:T(8,128)}, u32[]{:S(2)}) copy-start(s32[1,16,128]{2,1,0:T(8,128)} %ids.1) | copy-start | bytes 24580
  19.9 4.1 %collective-permute-start.7 = (f32[88,128]{1,0:T(8,128)S(1)}, f32[88,128]{1,0:T(8,128)S(1)}, u32[]{:S(2)}, u32[]{:S(2)}) collective-permute-start(f32[88,128]{1,0:T(8,128)S(1)} %get-tuple-element.45), channel_id=1, source_target_pairs={{0,12},{4,0},{8,4},{12,8},{1,13},{5,1},{9,5},{13,9},{2,14},{6,2},{... | collective-permute-start | bytes 135176 | tf_op jit(solution)/shard_map/ppermute | solution.py:1009
  21.0 5.5 %collective-permute-start.6 = (f32[88,128]{1,0:T(8,128)S(1)}, f32[88,128]{1,0:T(8,128)S(1)}, u32[]{:S(2)}, u32[]{:S(2)}) collective-permute-start(f32[88,128]{1,0:T(8,128)S(1)} %get-tuple-element.45), channel_id=1, source_target_pairs={{0,8},{4,12},{8,0},{12,4},{1,9},{5,13},{9,1},{13,5},{2,10},{6,14},... | collective-permute-start | bytes 135176 | tf_op jit(solution)/shard_map/ppermute | solution.py:1009
  21.9 5.8 %collective-permute-start.5 = (f32[88,128]{1,0:T(8,128)S(1)}, f32[88,128]{1,0:T(8,128)S(1)}, u32[]{:S(2)}, u32[]{:S(2)}) collective-permute-start(f32[88,128]{1,0:T(8,128)S(1)} %get-tuple-element.45), channel_id=1, source_target_pairs={{0,4},{4,8},{8,12},{12,0},{1,5},{5,9},{9,13},{13,1},{2,6},{6,10},{... | collective-permute-start | bytes 135176 | tf_op jit(solution)/shard_map/ppermute | solution.py:1009
  28.1 4.6 %collective-permute-start.8 = (f32[168,128]{1,0:T(8,128)S(1)}, f32[168,128]{1,0:T(8,128)S(1)}, u32[]{:S(2)}, u32[]{:S(2)}) collective-permute-start(f32[168,128]{1,0:T(8,128)S(1)} %get-tuple-element.55.refs_4_), channel_id=1, source_target_pairs={{0,2},{2,0},{1,3},{3,1},{4,6},{6,4},{5,7},{7,5},{8,10},{10,8},{9,1... | collective-permute-start | bytes 258056 | tf_op jit(solution)/shard_map/ppermute | solution.py:1009
  29.0 3.7 %collective-permute-start.9 = (f32[200,128]{1,0:T(8,128)S(1)}, f32[200,128]{1,0:T(8,128)S(1)}, u32[]{:S(2)}, u32[]{:S(2)}) collective-permute-start(f32[200,128]{1,0:T(8,128)S(1)} %get-tuple-element.56), channel_id=1, source_target_pairs={{0,1},{1,0},{2,3},{3,2},{4,5},{5,4},{6,7},{7,6},{8,9},{9,8},{10,11... | collective-permute-start | bytes 307208 | tf_op jit(solution)/shard_map/ppermute | solution.py:1009
  32.6 1.3 %collective-permute-start.10 = (f32[168,128]{1,0:T(8,128)S(1)}, f32[168,128]{1,0:T(8,128)S(1)}, u32[]{:S(2)}, u32[]{:S(2)}) collective-permute-start(f32[168,128]{1,0:T(8,128)S(1)} %collective-permute-done.8.refs_1_), channel_id=1, source_target_pairs={{0,1},{1,0},{2,3},{3,2},{4,5},{5,4},{6,7},{7,6},{8,9},{9,8},{10,11... | collective-permute-start | bytes 258056 | tf_op jit(solution)/shard_map/ppermute | solution.py:1009

commit v15 on v14

--- a/solution.py
+++ b/solution.py
@@ -189,7 +189,7 @@
     n_dir = 1 if n_len == 2 else 2
     raw, wall_in, refs = refs[:4], refs[4], refs[5:]
     strips, corners, refs = refs[:n_dir], refs[n_dir : 2 * n_dir], refs[2 * n_dir :]
-    to_next, to_prev, own_rows, build = refs
+    first_out, second_out, own_rows, build, to_next, to_prev = refs
     W = raw[0].shape[0] // C
     N = W + 2 * H
     wall, length = lax.axis_index("wall"), lax.axis_index("len")
@@ -250,6 +250,9 @@
         for k, pair in enumerate((adj[0], mask[0], q[0])):
             own_rows[side, 2 * k] = pair[0]
             own_rows[side, 2 * k + 1] = pair[1]
+    even = lax.rem(lax.axis_index("blk"), 2) == 0
+    first_out[...] = jnp.where(even, to_prev[...], to_next[...])
+    second_out[...] = jnp.where(even, to_next[...], to_prev[...])
 
 
 def spots(m_ref, e_ref, i, rows, coef):
@@ -440,9 +443,12 @@
     return near, second, halo, halo_second, delta_o[0]
 
 
-def correct(electrodes, n_len, n_wall, own_rows, from_next, from_prev, coarse, surface, ids, *rest):
+def correct(electrodes, n_len, n_wall, own_rows, first_in, second_in, coarse, surface, ids, *rest):
     rows_n, rows_p, message = rest[:3]
-    lines, sums = rest[3:]
+    lines, sums, from_next, from_prev = rest[3:]
+    even = lax.rem(lax.axis_index("blk"), 2) == 0
+    from_next[...] = jnp.where(even, second_in[...], first_in[...])
+    from_prev[...] = jnp.where(even, first_in[...], second_in[...])
     _, C, L = ids.shape
     N = own_rows.shape[2]
     W = N - 2 * H
@@ -576,7 +582,7 @@
     blk, length, wall = lax.axis_index("blk"), lax.axis_index("len"), lax.axis_index("wall")
     sums = jnp.zeros((8, LANES), F32)
     for d in range(n_blk):
-        b = lax.rem(blk - d + n_blk, n_blk)
+        b = blk ^ d
         for i in range(half):
             sheet1[i, pl.ds(pl.multiple_of(C1 * b, C1), C1), :] = blocks[d, i * C1 : (i + 1) * C1, :]
         out[pl.ds(pl.multiple_of(96 + C * b, C), C), :] = blocks[d, start : start + C, :]
@@ -668,7 +674,7 @@
     often = 40 if NC1 * NL1 <= 4096 else 1
 
     def blk_of(d):
-        return lax.rem(blk - d + n_blk, n_blk) if relative else d
+        return blk ^ d if relative else d
 
     def length_of(j):
         return (length + j) % n_len if n_len == 2 else j
@@ -1009,6 +1015,16 @@
     return lax.ppermute(x, axis, [(i, (i + by) % count) for i in range(count)])
 
 
+def paired(x, by):
+    return lax.ppermute(x, "blk", [(i, i ^ by) for i in range(lax.axis_size("blk"))])
+
+
+def neighbour_pairs(x, odd_first):
+    count = lax.axis_size("blk")
+    assert count % 2 == 0
+    return lax.ppermute(x, "blk", [(i, (i + (1 if i % 2 == odd_first else -1)) % count) for i in range(count)])
+
+
 def across(x):
     n_wall = lax.axis_size("wall")
     pairs = [(l * n_wall + w, (1 - l) * n_wall + (w + 1) % n_wall) for l in range(2) for w in range(n_wall)]
@@ -1068,15 +1084,15 @@
 
     near = (sum(near_rows(n_dir, W)[-1][::2]), L)
     halos = [wall_in, *strips, *corners]
-    to_next, to_prev, own_rows = call(
+    first_out, second_out, own_rows = call(
         functools.partial(boundary, n_len, C),
         [vmem] * (5 + 2 * n_dir),
         [(near, vmem)] * 2 + [((2, 6, N, L), vmem)],
-        [(48, N, L)],
+        [(48, N, L), near, near],
         "boundary",
     )(*fields, *halos)
-    from_next = ring(to_prev, "blk", -1)
-    from_prev = ring(to_next, "blk", 1)
+    first_in = neighbour_pairs(first_out, 1)
+    second_in = neighbour_pairs(second_out, 0)
     qm, bm, be, coarse, surface, patches = call(
         functools.partial(sector, n_len, n_wall, C, electrodes),
         [vmem] * (6 + 2 * n_dir),
@@ -1093,12 +1109,12 @@
         functools.partial(correct, electrodes, n_len, n_wall),
         [vmem] * 6,
         [(rows, vmem), (rows, vmem), (message, vmem)],
-        [(1, N, L), (wide, L)],
+        [(1, N, L), (wide, L), near, near],
         "correct",
-    )(own_rows, from_next, from_prev, coarse, surface, patch_ids)
-
-    relative = n_blk <= 4
-    moved = [ring(mine, "blk", d) for d in range(1, n_blk)] if relative else [lax.all_gather(mine, "blk")]
+    )(own_rows, first_in, second_in, coarse, surface, patch_ids)
+
+    relative = n_blk in (2, 4)
+    moved = [paired(mine, d) for d in range(1, n_blk)] if relative else [lax.all_gather(mine, "blk")]
     base_adj, base_pot = call(
         functools.partial(source_part, n_len, n_wall, C),
         [vmem] * 6,

time: 38.6 us -> 37.4 us (0.969)
  waiting for transfers between devices: 17 us -> 13.4 us
  starting transfers between devices: 9.79 us -> 12.2 us
    ppermute x10 -> x5, waiting for transfers between devices: 14 us -> 4.95 us  [ring(): return lax.ppermute(x, axis, [(i, (i + by) % count) for i in range(count)])]
    ppermute x0 -> x5, starting transfers between devices: none -> 8.12 us  [the longest x3 4.45 us: paired(): lax.ppermute(x, 'blk', [(i, i ^ by) for i in range(lax.axis_size('blk'))])]
    ppermute x10 -> x5, starting transfers between devices: 9.72 us -> 3.97 us  [ring(): return lax.ppermute(x, axis, [(i, (i + by) % count) for i in range(count)])]
    ppermute x0 -> x5, waiting for transfers between devices: none -> 5.41 us  [the longest x2 2.87 us: neighbour_pairs(): lax.ppermute(x, 'blk', [(i, (i + (1 if i % 2 == odd_first else -1)) % cou...]
where the time goes in v15:
time: 37.4 us; the launch traced here: 37.2 us
  waiting for transfers between devices  13.4 us (36%)
  starting transfers between devices  12.2 us (33%)
  Pallas kernels  10.3 us (28%)
  between operations  0.69 us (2%)
  local copies, waits for them, and re-layouts  0.66 us (2%)
    ppermute x5, waiting for transfers between devices, ring(): return lax.ppermute(x, axis, [(i, (i + by) % count) for i in range(count)])  4.95 us
    pallas_call x1, Pallas kernels, body(): call(functools.partial(solve, (n_blk, n_len, n_wall), relative, compacted...  4.49 us
    ppermute x3, starting transfers between devices, paired(): lax.ppermute(x, 'blk', [(i, i ^ by) for i in range(lax.axis_size('blk'))])  4.45 us
    ppermute x5, starting transfers between devices, ring(): return lax.ppermute(x, axis, [(i, (i + by) % count) for i in range(count)])  3.97 us
    ppermute x2, starting transfers between devices, neighbour_pairs(): lax.ppermute(x, 'blk', [(i, (i + (1 if i % 2 == odd_first else -1)) % cou...  3.67 us
    ppermute x1, waiting for transfers between devices, across(): return lax.ppermute(x, ('len', 'wall'), pairs)  3.01 us
    ppermute x2, waiting for transfers between devices, neighbour_pairs(): lax.ppermute(x, 'blk', [(i, (i + (1 if i % 2 == odd_first else -1)) % cou...  2.87 us
    ppermute x3, waiting for transfers between devices, paired(): lax.ppermute(x, 'blk', [(i, i ^ by) for i in range(lax.axis_size('blk'))])  2.54 us
  transfers between devices with their start and end apart: 11, of which 8 were waited for; matrix products, arithmetic and copies ran while one was open for 0% of the time, Pallas kernels for 6%

profile of v15, /device:TPU:0, one launch (start us, length us, event | category | flops | bytes accessed | tf_op | source)
XLA Modules:
  0.0 37.2 jit_solution(14035386101445734258)
XLA Ops:
  0.6 1.7 %faces.1 = (f32[512,128]{1,0:T(8,128)S(1)}, f32[512,128]{1,0:T(8,128)S(1)}, f32[512,128]{1,0:T(8,128)S(1)}, f32[512,128]{1,0:T(8,128)S(1)}, f32[12,16,128]{2,1,0...) custom-call(f32[512,128]{1,0:T(8,128)} %bitcast.13, f32[512,128]{1,0:T(8,128)} %bitcast.14, ...), custom_call_target="tpu_custom_call" | custom-call | tf_op jit(solution)/shard_map/faces/pallas_call | solution.py:1065
  2.3 0.5 %collective-permute-start = (f32[12,16,128]{2,1,0:T(8,128)S(1)}, f32[12,16,128]{2,1,0:T(8,128)S(1)}, u32[]{:S(2)}, u32[]{:S(2)}) collective-permute-start(f32[12,16,128]{2,1,0:T(8,128)S(1)} %get-tuple-element.37), channel_id=1, source_target_pairs={{0,1},{1,0},{2,3},{3,2},{4,5},{5,4},{6,7},{7,6},{8,9},{9,8},{10,11... | collective-permute-start | bytes 294920 | tf_op jit(solution)/shard_map/ppermute | solution.py:1015
  2.8 2.6 %collective-permute-start.1 = (f32[4,16,128]{2,1,0:T(8,128)S(1)}, f32[4,16,128]{2,1,0:T(8,128)S(1)}, u32[]{:S(2)}, u32[]{:S(2)}) collective-permute-start(f32[4,16,128]{2,1,0:T(8,128)S(1)} %get-tuple-element.38), channel_id=1, source_target_pairs={{0,2},{2,0},{1,3},{3,1},{4,6},{6,4},{5,7},{7,5},{8,10},{10,8},{9,1... | collective-permute-start | bytes 98312 | tf_op jit(solution)/shard_map/ppermute | solution.py:1015
  5.4 0.1 collective-permute-start.2
  5.5 3.0 %collective-permute-done.2.refs_6_ = f32[16,128]{1,0:T(8,128)S(1)} collective-permute-done((f32[16,128]{1,0:T(8,128)S(1)}, f32[16,128]{1,0:T(8,128)S(1)}, u32[]{:S(2)}, u32[]{:S(2)}) %collective-permute-start.2) | collective-permute-done | bytes 8224 | tf_op jit(solution)/shard_map/ppermute | solution.py:1031
  8.5 0.0 collective-permute-done.1.refs_5_
  8.5 0.0 collective-permute-done.refs_4_
  8.5 0.8 %boundary.1 = (f32[184,128]{1,0:T(8,128)S(1)}, f32[184,128]{1,0:T(8,128)S(1)}, f32[2,6,40,128]{3,2,1,0:T(8,128)S(1)}) custom-call(f32[512,128]{1,0:T(8,128)S(1)} %get-tuple-element.33.refs_0_, f32[512,128]{1,0:T(8,128)S(1)} %get-tuple-element.34.refs_1_, f32[512,128]{1,0:T(8,128)S(1)} %get-tuple-element.35.refs_2_.mask.refs_7_, ...), custom_call_target="tpu_custom_call" | custom-call | tf_op jit(solution)/shard_map/boundary/pallas_call | solution.py:1087
  9.3 3.7 %collective-permute-start.3 = (f32[184,128]{1,0:T(8,128)S(1)}, f32[184,128]{1,0:T(8,128)S(1)}, u32[]{:S(2)}, u32[]{:S(2)}) collective-permute-start(f32[184,128]{1,0:T(8,128)S(1)} %get-tuple-element.41), channel_id=1, source_target_pairs={{0,12},{4,8},{8,4},{12,0},{1,13},{5,9},{9,5},{13,1},{2,14},{6,10},... | collective-permute-start | bytes 282632 | tf_op jit(solution)/shard_map/ppermute | solution.py:1025
  13.0 0.0 copy-start.1
  13.0 0.0 collective-permute-start.4
  13.0 0.7 %copy-done.1 = s32[32]{0:T(128)S(1)} copy-done((s32[32]{0:T(128)S(1)}, s32[32]{0:T(128)}, u32[]{:S(2)}) %copy-start.1) | copy-done | bytes 152
  13.6 0.0 copy-start
  13.6 1.6 %sector.1 = (f32[640,128]{1,0:T(8,128)S(1)}, f32[640,128]{1,0:T(8,128)S(1)}, f32[640,128]{1,0:T(8,128)S(1)}, f32[64,128]{1,0:T(8,128)S(1)}, f32[16,128]{1,0:T(8,128)S(1)}, /*index=5*/f32[8,128]{1,0:T(8,128)S(1)}) custom-call(f32[512,128]{1,0:T(8,128)S(1)} %get-tuple-element.33.refs_0_, f32[512,128]{1,0:T(8,128)S(1)} %get-tuple-element.34.refs_1_, ...), custom_call_target="tpu_custom_call" | custom-call | flops 16000000 | bytes 16000000 | tf_op jit(solution)/shard_map/sector/pallas_call | solution.py:1096
  15.3 1.5 %collective-permute-done.3.first_in = f32[184,128]{1,0:T(8,128)S(1)} collective-permute-done((f32[184,128]{1,0:T(8,128)S(1)}, f32[184,128]{1,0:T(8,128)S(1)}, u32[]{:S(2)}, u32[]{:S(2)}) %collective-permute-start.3) | collective-permute-done | bytes 94240 | tf_op jit(solution)/shard_map/ppermute | solution.py:1025
  16.7 1.4 %collective-permute-done.4.second_in = f32[184,128]{1,0:T(8,128)S(1)} collective-permute-done((f32[184,128]{1,0:T(8,128)S(1)}, f32[184,128]{1,0:T(8,128)S(1)}, u32[]{:S(2)}, u32[]{:S(2)}) %collective-permute-start.4) | collective-permute-done | bytes 94240 | tf_op jit(solution)/shard_map/ppermute | solution.py:1025
  18.1 0.0 copy-done
  18.1 0.6 %correct.1 = (f32[8,40,128]{2,1,0:T(8,128)S(1)}, f32[8,40,128]{2,1,0:T(8,128)S(1)}, f32[88,128]{1,0:T(8,128)S(1)}) custom-call(f32[2,6,40,128]{3,2,1,0:T(8,128)S(1)} %get-tuple-element.40.own_rows, f32[184,128]{1,0:T(8,128)S(1)} %collective-permute-done.3.first_in, f32[184,128]{1,0:T(8,128)S(1)} %collective-permute-done.4.second_in, ...), custom_call_target="tpu_custom_call" | custom-call | tf_op jit(solution)/shard_map/correct/pallas_call | solution.py:1108
  18.7 2.3 %collective-permute-start.7 = (f32[88,128]{1,0:T(8,128)S(1)}, f32[88,128]{1,0:T(8,128)S(1)}, u32[]{:S(2)}, u32[]{:S(2)}) collective-permute-start(f32[88,128]{1,0:T(8,128)S(1)} %get-tuple-element.45), channel_id=1, source_target_pairs={{0,12},{4,8},{8,4},{12,0},{1,13},{5,9},{9,5},{13,1},{2,14},{6,10},... | collective-permute-start | bytes 135176 | tf_op jit(solution)/shard_map/ppermute | solution.py:1019
  21.0 0.9 %collective-permute-start.6 = (f32[88,128]{1,0:T(8,128)S(1)}, f32[88,128]{1,0:T(8,128)S(1)}, u32[]{:S(2)}, u32[]{:S(2)}) collective-permute-start(f32[88,128]{1,0:T(8,128)S(1)} %get-tuple-element.45), channel_id=1, source_target_pairs={{0,8},{4,12},{8,0},{12,4},{1,9},{5,13},{9,1},{13,5},{2,10},{6,14},... | collective-permute-start | bytes 135176 | tf_op jit(solution)/shard_map/ppermute | solution.py:1019
  21.9 1.2 %collective-permute-start.5 = (f32[88,128]{1,0:T(8,128)S(1)}, f32[88,128]{1,0:T(8,128)S(1)}, u32[]{:S(2)}, u32[]{:S(2)}) collective-permute-start(f32[88,128]{1,0:T(8,128)S(1)} %get-tuple-element.45), channel_id=1, source_target_pairs={{0,4},{4,0},{8,12},{12,8},{1,5},{5,1},{9,13},{13,9},{2,6},{6,2},{1... | collective-permute-start | bytes 135176 | tf_op jit(solution)/shard_map/ppermute | solution.py:1019
  23.1 0.8 %source_part.1 = (f32[512,128]{1,0:T(8,128)S(1)}, f32[512,128]{1,0:T(8,128)S(1)}) custom-call(f32[640,128]{1,0:T(8,128)S(1)} %get-tuple-element.46.bm, f32[640,128]{1,0:T(8,128)S(1)} %get-tuple-element.47.be, f32[8,40,128]{2,1,0:T(8,128)S(1)} %get-tuple-element.48.rows_n, f32[8,40,128]{2,1,0:T(8,128)S(1)} %get-tuple-element.49.rows_p, ...), custom_call_target="tpu_custom_call" | custom-call | flops 12000000 | bytes 12000000 | tf_op jit(solution)/shard_map/source_part/pallas_call | solution.py:1118
  23.9 1.0 %collective-permute-done.7 = f32[88,128]{1,0:T(8,128)S(1)} collective-permute-done((f32[88,128]{1,0:T(8,128)S(1)}, f32[88,128]{1,0:T(8,128)S(1)}, u32[]{:S(2)}, u32[]{:S(2)}) %collective-permute-start.7) | collective-permute-done | bytes 45088 | tf_op jit(solution)/shard_map/ppermute | solution.py:1019
  24.9 1.3 %collective-permute-done.6 = f32[88,128]{1,0:T(8,128)S(1)} collective-permute-done((f32[88,128]{1,0:T(8,128)S(1)}, f32[88,128]{1,0:T(8,128)S(1)}, u32[]{:S(2)}, u32[]{:S(2)}) %collective-permute-start.6) | collective-permute-done | bytes 45088 | tf_op jit(solution)/shard_map/ppermute | solution.py:1019
  26.2 0.3 collective-permute-done.5
  26.5 0.3 compact.1
  26.8 0.9 %collective-permute-start.8 = (f32[168,128]{1,0:T(8,128)S(1)}, f32[168,128]{1,0:T(8,128)S(1)}, u32[]{:S(2)}, u32[]{:S(2)}) collective-permute-start(f32[168,128]{1,0:T(8,128)S(1)} %get-tuple-element.55.refs_4_), channel_id=1, source_target_pairs={{0,2},{2,0},{1,3},{3,1},{4,6},{6,4},{5,7},{7,5},{8,10},{10,8},{9,1... | collective-permute-start | bytes 258056 | tf_op jit(solution)/shard_map/ppermute | solution.py:1015
  27.7 0.0 collective-permute-start.9
  27.7 3.7 %collective-permute-done.8.refs_1_ = f32[168,128]{1,0:T(8,128)S(1)} collective-permute-done((f32[168,128]{1,0:T(8,128)S(1)}, f32[168,128]{1,0:T(8,128)S(1)}, u32[]{:S(2)}, u32[]{:S(2)}) %collective-permute-start.8) | collective-permute-done | bytes 86048 | tf_op jit(solution)/shard_map/ppermute | solution.py:1015
  31.4 0.0 collective-permute-start.10
  31.4 0.0 collective-permute-done.9.refs_2_
  31.4 1.3 %collective-permute-done.10.refs_3_ = f32[168,128]{1,0:T(8,128)S(1)} collective-permute-done((f32[168,128]{1,0:T(8,128)S(1)}, f32[168,128]{1,0:T(8,128)S(1)}, u32[]{:S(2)}, u32[]{:S(2)}) %collective-permute-start.10) | collective-permute-done | bytes 86048 | tf_op jit(solution)/shard_map/ppermute | solution.py:1015
  32.7 4.5 %solve.1 = (f32[512,128]{1,0:T(8,128)}, f32[512,128]{1,0:T(8,128)}, f32[1,2]{1,0:T(1,128)}) custom-call(f32[4,88,128]{2,1,0:T(8,128)S(1)} %pad_maximum_fusion.blocks.refs_0_, f32[168,128]{1,0:T(8,128)S(1)} %collective-permute-done.8.refs_1_, f32[200,128]{1,0:T(8,128)S(1)} %collective-permute-done.9.refs_2_, f32[168,128]{1,0:T(8,128)S(1)} %collective-permute-done.10.refs_3_, ...), custom_call_target="tpu_custom_call" | custom-call | tf_op jit(solution)/shard_map/solve/pallas_call | solution.py:1155
  (1 shorter events, 0.0 us)
Async XLA Ops:
  2.3 6.2 %collective-permute-start = (f32[12,16,128]{2,1,0:T(8,128)S(1)}, f32[12,16,128]{2,1,0:T(8,128)S(1)}, u32[]{:S(2)}, u32[]{:S(2)}) collective-permute-start(f32[12,16,128]{2,1,0:T(8,128)S(1)} %get-tuple-element.37), channel_id=1, source_target_pairs={{0,1},{1,0},{2,3},{3,2},{4,5},{5,4},{6,7},{7,6},{8,9},{9,8},{10,11... | collective-permute-start | bytes 294920 | tf_op jit(solution)/shard_map/ppermute | solution.py:1015
  2.8 5.6 %collective-permute-start.1 = (f32[4,16,128]{2,1,0:T(8,128)S(1)}, f32[4,16,128]{2,1,0:T(8,128)S(1)}, u32[]{:S(2)}, u32[]{:S(2)}) collective-permute-start(f32[4,16,128]{2,1,0:T(8,128)S(1)} %get-tuple-element.38), channel_id=1, source_target_pairs={{0,2},{2,0},{1,3},{3,1},{4,6},{6,4},{5,7},{7,5},{8,10},{10,8},{9,1... | collective-permute-start | bytes 98312 | tf_op jit(solution)/shard_map/ppermute | solution.py:1015
  5.4 3.1 %collective-permute-start.2 = (f32[16,128]{1,0:T(8,128)S(1)}, f32[16,128]{1,0:T(8,128)S(1)}, u32[]{:S(2)}, u32[]{:S(2)}) collective-permute-start(f32[16,128]{1,0:T(8,128)S(1)} %get-tuple-element.39), channel_id=1, source_target_pairs={{0,3},{1,2},{2,1},{3,0},{4,7},{5,6},{6,5},{7,4},{8,11},{9,10},{10,... | collective-permute-start | bytes 24584 | tf_op jit(solution)/shard_map/ppermute | solution.py:1031
  9.3 7.4 %collective-permute-start.3 = (f32[184,128]{1,0:T(8,128)S(1)}, f32[184,128]{1,0:T(8,128)S(1)}, u32[]{:S(2)}, u32[]{:S(2)}) collective-permute-start(f32[184,128]{1,0:T(8,128)S(1)} %get-tuple-element.41), channel_id=1, source_target_pairs={{0,12},{4,8},{8,4},{12,0},{1,13},{5,9},{9,5},{13,1},{2,14},{6,10},... | collective-permute-start | bytes 282632 | tf_op jit(solution)/shard_map/ppermute | solution.py:1025
  13.0 0.7 %copy-start.1 = (s32[32]{0:T(128)S(1)}, s32[32]{0:T(128)}, u32[]{:S(2)}) copy-start(s32[32]{0:T(128)} %param.11) | copy-start | bytes 388
  13.0 5.2 %collective-permute-start.4 = (f32[184,128]{1,0:T(8,128)S(1)}, f32[184,128]{1,0:T(8,128)S(1)}, u32[]{:S(2)}, u32[]{:S(2)}) collective-permute-start(f32[184,128]{1,0:T(8,128)S(1)} %get-tuple-element.42), channel_id=1, source_target_pairs={{0,4},{4,0},{8,12},{12,8},{1,5},{5,1},{9,13},{13,9},{2,6},{6,2},{1... | collective-permute-start | bytes 282632 | tf_op jit(solution)/shard_map/ppermute | solution.py:1025
  13.6 4.5 %copy-start = (s32[1,16,128]{2,1,0:T(8,128)S(1)}, s32[1,16,128]{2,1,0:T(8,128)}, u32[]{:S(2)}) copy-start(s32[1,16,128]{2,1,0:T(8,128)} %ids.1) | copy-start | bytes 24580
  18.7 6.2 %collective-permute-start.7 = (f32[88,128]{1,0:T(8,128)S(1)}, f32[88,128]{1,0:T(8,128)S(1)}, u32[]{:S(2)}, u32[]{:S(2)}) collective-permute-start(f32[88,128]{1,0:T(8,128)S(1)} %get-tuple-element.45), channel_id=1, source_target_pairs={{0,12},{4,8},{8,4},{12,0},{1,13},{5,9},{9,5},{13,1},{2,14},{6,10},... | collective-permute-start | bytes 135176 | tf_op jit(solution)/shard_map/ppermute | solution.py:1019
  21.0 5.2 %collective-permute-start.6 = (f32[88,128]{1,0:T(8,128)S(1)}, f32[88,128]{1,0:T(8,128)S(1)}, u32[]{:S(2)}, u32[]{:S(2)}) collective-permute-start(f32[88,128]{1,0:T(8,128)S(1)} %get-tuple-element.45), channel_id=1, source_target_pairs={{0,8},{4,12},{8,0},{12,4},{1,9},{5,13},{9,1},{13,5},{2,10},{6,14},... | collective-permute-start | bytes 135176 | tf_op jit(solution)/shard_map/ppermute | solution.py:1019
  21.9 4.6 %collective-permute-start.5 = (f32[88,128]{1,0:T(8,128)S(1)}, f32[88,128]{1,0:T(8,128)S(1)}, u32[]{:S(2)}, u32[]{:S(2)}) collective-permute-start(f32[88,128]{1,0:T(8,128)S(1)} %get-tuple-element.45), channel_id=1, source_target_pairs={{0,4},{4,0},{8,12},{12,8},{1,5},{5,1},{9,13},{13,9},{2,6},{6,2},{1... | collective-permute-start | bytes 135176 | tf_op jit(solution)/shard_map/ppermute | solution.py:1019
  26.8 4.6 %collective-permute-start.8 = (f32[168,128]{1,0:T(8,128)S(1)}, f32[168,128]{1,0:T(8,128)S(1)}, u32[]{:S(2)}, u32[]{:S(2)}) collective-permute-start(f32[168,128]{1,0:T(8,128)S(1)} %get-tuple-element.55.refs_4_), channel_id=1, source_target_pairs={{0,2},{2,0},{1,3},{3,1},{4,6},{6,4},{5,7},{7,5},{8,10},{10,8},{9,1... | collective-permute-start | bytes 258056 | tf_op jit(solution)/shard_map/ppermute | solution.py:1015
  27.7 3.7 %collective-permute-start.9 = (f32[200,128]{1,0:T(8,128)S(1)}, f32[200,128]{1,0:T(8,128)S(1)}, u32[]{:S(2)}, u32[]{:S(2)}) collective-permute-start(f32[200,128]{1,0:T(8,128)S(1)} %get-tuple-element.56), channel_id=1, source_target_pairs={{0,1},{1,0},{2,3},{3,2},{4,5},{5,4},{6,7},{7,6},{8,9},{9,8},{10,11... | collective-permute-start | bytes 307208 | tf_op jit(solution)/shard_map/ppermute | solution.py:1015
  31.4 1.3 %collective-permute-start.10 = (f32[168,128]{1,0:T(8,128)S(1)}, f32[168,128]{1,0:T(8,128)S(1)}, u32[]{:S(2)}, u32[]{:S(2)}) collective-permute-start(f32[168,128]{1,0:T(8,128)S(1)} %collective-permute-done.8.refs_1_), channel_id=1, source_target_pairs={{0,1},{1,0},{2,3},{3,2},{4,5},{5,4},{6,7},{7,6},{8,9},{9,8},{10,11... | collective-permute-start | bytes 258056 | tf_op jit(solution)/shard_map/ppermute | solution.py:1015

commit v16 on v15

--- a/solution.py
+++ b/solution.py
@@ -101,9 +101,9 @@
 
 def pack_faces(n_len, adj, ion, mask, mis, *rest):
     n_dir = 1 if n_len == 2 else 2
-    fields, wall_out, rest = rest[:4], rest[4], rest[5:]
-    strips, corners = rest[:n_dir], rest[n_dir : 2 * n_dir]
-    whole_mask, sems = rest[2 * n_dir :]
+    fields, rest = rest[:4], rest[4:]
+    corners, strips = rest[:n_dir], rest[n_dir : 2 * n_dir]
+    wall_out, whole_mask, sems = rest[2 * n_dir :]
     cells = adj.shape[0]
     C = wall_out.shape[1]
     W = cells // C
@@ -187,8 +187,9 @@
 
 def boundary(n_len, C, *refs):
     n_dir = 1 if n_len == 2 else 2
-    raw, wall_in, refs = refs[:4], refs[4], refs[5:]
-    strips, corners, refs = refs[:n_dir], refs[n_dir : 2 * n_dir], refs[2 * n_dir :]
+    raw, refs = refs[:4], refs[4:]
+    corners, strips, wall_in = refs[:n_dir], refs[n_dir : 2 * n_dir], refs[2 * n_dir]
+    refs = refs[2 * n_dir + 1 :]
     first_out, second_out, own_rows, build, to_next, to_prev = refs
     W = raw[0].shape[0] // C
     N = W + 2 * H
@@ -333,8 +334,9 @@
 
 def sector(n_len, n_wall, C, electrodes, *refs):
     n_dir = 1 if n_len == 2 else 2
-    raw, wall_in, refs = refs[:4], refs[4], refs[5:]
-    strips, corners, refs = refs[:n_dir], refs[n_dir : 2 * n_dir], refs[2 * n_dir :]
+    raw, refs = refs[:4], refs[4:]
+    corners, strips, wall_in = refs[:n_dir], refs[n_dir : 2 * n_dir], refs[2 * n_dir]
+    refs = refs[2 * n_dir + 1 :]
     owner, qm, bm, be, coarse, surface, patches, qe, pairs = refs[:9]
     xm, xe = refs[9:13], refs[13:17]
     assemble(n_len, C, raw, wall_in, strips, corners, xm, xe)
@@ -943,7 +945,7 @@
         set_plane(adj_out, w, C, plane(base_adj, w, C) - DT * plane(mask, w, C) * moved)
         set_plane(pot_out, w, C, plane(base_pot, w, C) + m)
 
-    parts = 2
+    parts = 4
     size = W // parts
     copies = []
     for k in range(parts):
@@ -1062,28 +1064,28 @@
     field, own = (N * C, L), (cells, L)
     raw = [x.reshape(cells, L) for x in (adj_next, ion_slope, tissue_mask, misfit)]
 
-    *fields, wall_out = (faces := call(
+    faces = call(
         functools.partial(pack_faces, n_len),
         ["hbm"] * 4,
         [(own, vmem)] * 4
-        + [((sum(FACES), C, L), vmem)]
+        + [((C, L), vmem)] * n_dir
         + [((4, C, L), vmem)] * n_dir
-        + [((C, L), vmem)] * n_dir,
+        + [((sum(FACES), C, L), vmem)],
         [pltpu.VMEM(own, jnp.int32), pltpu.SemaphoreType.DMA((4, 4))],
         "faces",
         room=52.75,
-    )(*raw))[:5]
-    strip_out, corner_out = faces[5 : 5 + n_dir], faces[5 + n_dir :]
-    wall_in = ring(wall_out, "wall", 1)
+    )(*raw)
+    fields, corner_out, strip_out, wall_out = faces[:4], faces[4 : 4 + n_dir], faces[4 + n_dir : -1], faces[-1]
     if n_dir == 1:
+        corners = [across(corner_out[0])]
         strips = [ring(strip_out[0], "len", 1)]
-        corners = [across(corner_out[0])]
     else:
         strips = [ring(strip_out[1], "len", -1), ring(strip_out[0], "len", 1)]
         corners = [ring(ring(corner_out[1], "wall", 1), "len", -1), ring(ring(corner_out[0], "wall", 1), "len", 1)]
+    wall_in = ring(wall_out, "wall", 1)
 
     near = (sum(near_rows(n_dir, W)[-1][::2]), L)
-    halos = [wall_in, *strips, *corners]
+    halos = [*corners, *strips, wall_in]
     first_out, second_out, own_rows = call(
         functools.partial(boundary, n_len, C),
         [vmem] * (5 + 2 * n_dir),
@@ -1151,7 +1153,7 @@
     tall = (Q * (C + 8) + 16, L)
     taller = ((W + 2) * (C + 8) + 16, L)
     scratch = grids + [(Q * C, NL1), tall, tall, taller, taller, own, own]
-    scratch += [(2, n_blk * C, n_len * L), (2, 2, 64, L), pltpu.SemaphoreType.DMA((2, 2))]
+    scratch += [(2, n_blk * C, n_len * L), (2, 2, 64, L), pltpu.SemaphoreType.DMA((2, 4))]
     adj_prev, potential, patch_grad = call(
         functools.partial(solve, (n_blk, n_len, n_wall), relative, compacted, C, W),
         [vmem] * (len(blocks) + 4),

time: 37.4 us -> 37.3 us (level)
  no operation moved by 1% of the time
where the time goes in v16:
time: 37.3 us; the launch traced here: 37.1 us
  waiting for transfers between devices  13.4 us (36%)
  starting transfers between devices  12.2 us (33%)
  Pallas kernels  10.3 us (28%)
  between operations  0.68 us (2%)
  local copies, waits for them, and re-layouts  0.66 us (2%)
    ppermute x5, waiting for transfers between devices, ring(): return lax.ppermute(x, axis, [(i, (i + by) % count) for i in range(count)])  4.95 us
    pallas_call x1, Pallas kernels, body(): call(functools.partial(solve, (n_blk, n_len, n_wall), relative, compacted...  4.49 us
    ppermute x3, starting transfers between devices, paired(): lax.ppermute(x, 'blk', [(i, i ^ by) for i in range(lax.axis_size('blk'))])  4.45 us
    ppermute x5, starting transfers between devices, ring(): return lax.ppermute(x, axis, [(i, (i + by) % count) for i in range(count)])  3.97 us
    ppermute x2, starting transfers between devices, neighbour_pairs(): lax.ppermute(x, 'blk', [(i, (i + (1 if i % 2 == odd_first else -1)) % cou...  3.67 us
    ppermute x1, waiting for transfers between devices, across(): return lax.ppermute(x, ('len', 'wall'), pairs)  3.01 us
    ppermute x2, waiting for transfers between devices, neighbour_pairs(): lax.ppermute(x, 'blk', [(i, (i + (1 if i % 2 == odd_first else -1)) % cou...  2.88 us
    ppermute x3, waiting for transfers between devices, paired(): lax.ppermute(x, 'blk', [(i, i ^ by) for i in range(lax.axis_size('blk'))])  2.54 us
  transfers between devices with their start and end apart: 11, of which 8 were waited for; matrix products, arithmetic and copies ran while one was open for 0% of the time, Pallas kernels for 6%

profile of v16, /device:TPU:0, one launch (start us, length us, event | category | flops | bytes accessed | tf_op | source)
XLA Modules:
  0.0 37.1 jit_solution(5644207750530740070)
XLA Ops:
  0.6 1.7 %faces.1 = (f32[512,128]{1,0:T(8,128)S(1)}, f32[512,128]{1,0:T(8,128)S(1)}, f32[512,128]{1,0:T(8,128)S(1)}, f32[512,128]{1,0:T(8,128)S(1)}, f32[16,128]{1,0:T(8,...) custom-call(f32[512,128]{1,0:T(8,128)} %bitcast.13, f32[512,128]{1,0:T(8,128)} %bitcast.14, ...), custom_call_target="tpu_custom_call" | custom-call | tf_op jit(solution)/shard_map/faces/pallas_call | solution.py:1067
  2.3 0.5 %collective-permute-start.2 = (f32[12,16,128]{2,1,0:T(8,128)S(1)}, f32[12,16,128]{2,1,0:T(8,128)S(1)}, u32[]{:S(2)}, u32[]{:S(2)}) collective-permute-start(f32[12,16,128]{2,1,0:T(8,128)S(1)} %get-tuple-element.39), channel_id=1, source_target_pairs={{0,1},{1,0},{2,3},{3,2},{4,5},{5,4},{6,7},{7,6},{8,9},{9,8},{10,11... | collective-permute-start | bytes 294920 | tf_op jit(solution)/shard_map/ppermute | solution.py:1017
  2.8 2.6 %collective-permute-start.1 = (f32[4,16,128]{2,1,0:T(8,128)S(1)}, f32[4,16,128]{2,1,0:T(8,128)S(1)}, u32[]{:S(2)}, u32[]{:S(2)}) collective-permute-start(f32[4,16,128]{2,1,0:T(8,128)S(1)} %get-tuple-element.38), channel_id=1, source_target_pairs={{0,2},{2,0},{1,3},{3,1},{4,6},{6,4},{5,7},{7,5},{8,10},{10,8},{9,1... | collective-permute-start | bytes 98312 | tf_op jit(solution)/shard_map/ppermute | solution.py:1017
  5.4 0.1 collective-permute-start
  5.5 3.0 %collective-permute-done.refs_4_ = f32[16,128]{1,0:T(8,128)S(1)} collective-permute-done((f32[16,128]{1,0:T(8,128)S(1)}, f32[16,128]{1,0:T(8,128)S(1)}, u32[]{:S(2)}, u32[]{:S(2)}) %collective-permute-start) | collective-permute-done | bytes 8224 | tf_op jit(solution)/shard_map/ppermute | solution.py:1033
  8.5 0.0 collective-permute-done.1.refs_5_
  8.5 0.0 collective-permute-done.2.refs_6_
  8.5 0.8 %boundary.1 = (f32[184,128]{1,0:T(8,128)S(1)}, f32[184,128]{1,0:T(8,128)S(1)}, f32[2,6,40,128]{3,2,1,0:T(8,128)S(1)}) custom-call(f32[512,128]{1,0:T(8,128)S(1)} %get-tuple-element.33.refs_0_, f32[512,128]{1,0:T(8,128)S(1)} %get-tuple-element.34.refs_1_, f32[512,128]{1,0:T(8,128)S(1)} %get-tuple-element.35.refs_2_.mask.refs_7_, ...), custom_call_target="tpu_custom_call" | custom-call | tf_op jit(solution)/shard_map/boundary/pallas_call | solution.py:1089
  9.3 3.7 %collective-permute-start.3 = (f32[184,128]{1,0:T(8,128)S(1)}, f32[184,128]{1,0:T(8,128)S(1)}, u32[]{:S(2)}, u32[]{:S(2)}) collective-permute-start(f32[184,128]{1,0:T(8,128)S(1)} %get-tuple-element.41), channel_id=1, source_target_pairs={{0,12},{4,8},{8,4},{12,0},{1,13},{5,9},{9,5},{13,1},{2,14},{6,10},... | collective-permute-start | bytes 282632 | tf_op jit(solution)/shard_map/ppermute | solution.py:1027
  12.9 0.0 copy-start.1
  13.0 0.0 collective-permute-start.4
  13.0 0.7 %copy-done.1 = s32[32]{0:T(128)S(1)} copy-done((s32[32]{0:T(128)S(1)}, s32[32]{0:T(128)}, u32[]{:S(2)}) %copy-start.1) | copy-done | bytes 152
  13.6 0.0 copy-start
  13.6 1.6 %sector.1 = (f32[640,128]{1,0:T(8,128)S(1)}, f32[640,128]{1,0:T(8,128)S(1)}, f32[640,128]{1,0:T(8,128)S(1)}, f32[64,128]{1,0:T(8,128)S(1)}, f32[16,128]{1,0:T(8,128)S(1)}, /*index=5*/f32[8,128]{1,0:T(8,128)S(1)}) custom-call(f32[512,128]{1,0:T(8,128)S(1)} %get-tuple-element.33.refs_0_, f32[512,128]{1,0:T(8,128)S(1)} %get-tuple-element.34.refs_1_, ...), custom_call_target="tpu_custom_call" | custom-call | flops 16000000 | bytes 16000000 | tf_op jit(solution)/shard_map/sector/pallas_call | solution.py:1098
  15.2 1.5 %collective-permute-done.3.first_in = f32[184,128]{1,0:T(8,128)S(1)} collective-permute-done((f32[184,128]{1,0:T(8,128)S(1)}, f32[184,128]{1,0:T(8,128)S(1)}, u32[]{:S(2)}, u32[]{:S(2)}) %collective-permute-start.3) | collective-permute-done | bytes 94240 | tf_op jit(solution)/shard_map/ppermute | solution.py:1027
  16.7 1.4 %collective-permute-done.4.second_in = f32[184,128]{1,0:T(8,128)S(1)} collective-permute-done((f32[184,128]{1,0:T(8,128)S(1)}, f32[184,128]{1,0:T(8,128)S(1)}, u32[]{:S(2)}, u32[]{:S(2)}) %collective-permute-start.4) | collective-permute-done | bytes 94240 | tf_op jit(solution)/shard_map/ppermute | solution.py:1027
  18.1 0.0 copy-done
  18.1 0.6 %correct.1 = (f32[8,40,128]{2,1,0:T(8,128)S(1)}, f32[8,40,128]{2,1,0:T(8,128)S(1)}, f32[88,128]{1,0:T(8,128)S(1)}) custom-call(f32[2,6,40,128]{3,2,1,0:T(8,128)S(1)} %get-tuple-element.40.own_rows, f32[184,128]{1,0:T(8,128)S(1)} %collective-permute-done.3.first_in, f32[184,128]{1,0:T(8,128)S(1)} %collective-permute-done.4.second_in, ...), custom_call_target="tpu_custom_call" | custom-call | tf_op jit(solution)/shard_map/correct/pallas_call | solution.py:1110
  18.7 2.3 %collective-permute-start.7 = (f32[88,128]{1,0:T(8,128)S(1)}, f32[88,128]{1,0:T(8,128)S(1)}, u32[]{:S(2)}, u32[]{:S(2)}) collective-permute-start(f32[88,128]{1,0:T(8,128)S(1)} %get-tuple-element.45), channel_id=1, source_target_pairs={{0,12},{4,8},{8,4},{12,0},{1,13},{5,9},{9,5},{13,1},{2,14},{6,10},... | collective-permute-start | bytes 135176 | tf_op jit(solution)/shard_map/ppermute | solution.py:1021
  21.0 0.9 %collective-permute-start.6 = (f32[88,128]{1,0:T(8,128)S(1)}, f32[88,128]{1,0:T(8,128)S(1)}, u32[]{:S(2)}, u32[]{:S(2)}) collective-permute-start(f32[88,128]{1,0:T(8,128)S(1)} %get-tuple-element.45), channel_id=1, source_target_pairs={{0,8},{4,12},{8,0},{12,4},{1,9},{5,13},{9,1},{13,5},{2,10},{6,14},... | collective-permute-start | bytes 135176 | tf_op jit(solution)/shard_map/ppermute | solution.py:1021
  21.9 1.2 %collective-permute-start.5 = (f32[88,128]{1,0:T(8,128)S(1)}, f32[88,128]{1,0:T(8,128)S(1)}, u32[]{:S(2)}, u32[]{:S(2)}) collective-permute-start(f32[88,128]{1,0:T(8,128)S(1)} %get-tuple-element.45), channel_id=1, source_target_pairs={{0,4},{4,0},{8,12},{12,8},{1,5},{5,1},{9,13},{13,9},{2,6},{6,2},{1... | collective-permute-start | bytes 135176 | tf_op jit(solution)/shard_map/ppermute | solution.py:1021
  23.1 0.8 %source_part.1 = (f32[512,128]{1,0:T(8,128)S(1)}, f32[512,128]{1,0:T(8,128)S(1)}) custom-call(f32[640,128]{1,0:T(8,128)S(1)} %get-tuple-element.46.bm, f32[640,128]{1,0:T(8,128)S(1)} %get-tuple-element.47.be, f32[8,40,128]{2,1,0:T(8,128)S(1)} %get-tuple-element.48.rows_n, f32[8,40,128]{2,1,0:T(8,128)S(1)} %get-tuple-element.49.rows_p, ...), custom_call_target="tpu_custom_call" | custom-call | flops 12000000 | bytes 12000000 | tf_op jit(solution)/shard_map/source_part/pallas_call | solution.py:1120
  23.9 1.0 %collective-permute-done.7 = f32[88,128]{1,0:T(8,128)S(1)} collective-permute-done((f32[88,128]{1,0:T(8,128)S(1)}, f32[88,128]{1,0:T(8,128)S(1)}, u32[]{:S(2)}, u32[]{:S(2)}) %collective-permute-start.7) | collective-permute-done | bytes 45088 | tf_op jit(solution)/shard_map/ppermute | solution.py:1021
  24.9 1.3 %collective-permute-done.6 = f32[88,128]{1,0:T(8,128)S(1)} collective-permute-done((f32[88,128]{1,0:T(8,128)S(1)}, f32[88,128]{1,0:T(8,128)S(1)}, u32[]{:S(2)}, u32[]{:S(2)}) %collective-permute-start.6) | collective-permute-done | bytes 45088 | tf_op jit(solution)/shard_map/ppermute | solution.py:1021
  26.2 0.3 collective-permute-done.5
  26.5 0.3 compact.1
  26.8 0.9 %collective-permute-start.8 = (f32[168,128]{1,0:T(8,128)S(1)}, f32[168,128]{1,0:T(8,128)S(1)}, u32[]{:S(2)}, u32[]{:S(2)}) collective-permute-start(f32[168,128]{1,0:T(8,128)S(1)} %get-tuple-element.55.refs_4_), channel_id=1, source_target_pairs={{0,2},{2,0},{1,3},{3,1},{4,6},{6,4},{5,7},{7,5},{8,10},{10,8},{9,1... | collective-permute-start | bytes 258056 | tf_op jit(solution)/shard_map/ppermute | solution.py:1017
  27.7 0.0 collective-permute-start.9
  27.7 3.7 %collective-permute-done.8.refs_1_ = f32[168,128]{1,0:T(8,128)S(1)} collective-permute-done((f32[168,128]{1,0:T(8,128)S(1)}, f32[168,128]{1,0:T(8,128)S(1)}, u32[]{:S(2)}, u32[]{:S(2)}) %collective-permute-start.8) | collective-permute-done | bytes 86048 | tf_op jit(solution)/shard_map/ppermute | solution.py:1017
  31.4 0.0 collective-permute-start.10
  31.4 0.0 collective-permute-done.9.refs_2_
  31.4 1.3 %collective-permute-done.10.refs_3_ = f32[168,128]{1,0:T(8,128)S(1)} collective-permute-done((f32[168,128]{1,0:T(8,128)S(1)}, f32[168,128]{1,0:T(8,128)S(1)}, u32[]{:S(2)}, u32[]{:S(2)}) %collective-permute-start.10) | collective-permute-done | bytes 86048 | tf_op jit(solution)/shard_map/ppermute | solution.py:1017
  32.7 4.5 %solve.1 = (f32[512,128]{1,0:T(8,128)}, f32[512,128]{1,0:T(8,128)}, f32[1,2]{1,0:T(1,128)}) custom-call(f32[4,88,128]{2,1,0:T(8,128)S(1)} %pad_maximum_fusion.blocks.refs_0_, f32[168,128]{1,0:T(8,128)S(1)} %collective-permute-done.8.refs_1_, f32[200,128]{1,0:T(8,128)S(1)} %collective-permute-done.9.refs_2_, f32[168,128]{1,0:T(8,128)S(1)} %collective-permute-done.10.refs_3_, ...), custom_call_target="tpu_custom_call" | custom-call | tf_op jit(solution)/shard_map/solve/pallas_call | solution.py:1157
  (1 shorter events, 0.0 us)
Async XLA Ops:
  2.3 6.2 %collective-permute-start.2 = (f32[12,16,128]{2,1,0:T(8,128)S(1)}, f32[12,16,128]{2,1,0:T(8,128)S(1)}, u32[]{:S(2)}, u32[]{:S(2)}) collective-permute-start(f32[12,16,128]{2,1,0:T(8,128)S(1)} %get-tuple-element.39), channel_id=1, source_target_pairs={{0,1},{1,0},{2,3},{3,2},{4,5},{5,4},{6,7},{7,6},{8,9},{9,8},{10,11... | collective-permute-start | bytes 294920 | tf_op jit(solution)/shard_map/ppermute | solution.py:1017
  2.8 5.6 %collective-permute-start.1 = (f32[4,16,128]{2,1,0:T(8,128)S(1)}, f32[4,16,128]{2,1,0:T(8,128)S(1)}, u32[]{:S(2)}, u32[]{:S(2)}) collective-permute-start(f32[4,16,128]{2,1,0:T(8,128)S(1)} %get-tuple-element.38), channel_id=1, source_target_pairs={{0,2},{2,0},{1,3},{3,1},{4,6},{6,4},{5,7},{7,5},{8,10},{10,8},{9,1... | collective-permute-start | bytes 98312 | tf_op jit(solution)/shard_map/ppermute | solution.py:1017
  5.4 3.1 %collective-permute-start = (f32[16,128]{1,0:T(8,128)S(1)}, f32[16,128]{1,0:T(8,128)S(1)}, u32[]{:S(2)}, u32[]{:S(2)}) collective-permute-start(f32[16,128]{1,0:T(8,128)S(1)} %get-tuple-element.37), channel_id=1, source_target_pairs={{0,3},{1,2},{2,1},{3,0},{4,7},{5,6},{6,5},{7,4},{8,11},{9,10},{10,... | collective-permute-start | bytes 24584 | tf_op jit(solution)/shard_map/ppermute | solution.py:1033
  9.3 7.4 %collective-permute-start.3 = (f32[184,128]{1,0:T(8,128)S(1)}, f32[184,128]{1,0:T(8,128)S(1)}, u32[]{:S(2)}, u32[]{:S(2)}) collective-permute-start(f32[184,128]{1,0:T(8,128)S(1)} %get-tuple-element.41), channel_id=1, source_target_pairs={{0,12},{4,8},{8,4},{12,0},{1,13},{5,9},{9,5},{13,1},{2,14},{6,10},... | collective-permute-start | bytes 282632 | tf_op jit(solution)/shard_map/ppermute | solution.py:1027
  12.9 0.7 %copy-start.1 = (s32[32]{0:T(128)S(1)}, s32[32]{0:T(128)}, u32[]{:S(2)}) copy-start(s32[32]{0:T(128)} %param.11) | copy-start | bytes 388
  13.0 5.2 %collective-permute-start.4 = (f32[184,128]{1,0:T(8,128)S(1)}, f32[184,128]{1,0:T(8,128)S(1)}, u32[]{:S(2)}, u32[]{:S(2)}) collective-permute-start(f32[184,128]{1,0:T(8,128)S(1)} %get-tuple-element.42), channel_id=1, source_target_pairs={{0,4},{4,0},{8,12},{12,8},{1,5},{5,1},{9,13},{13,9},{2,6},{6,2},{1... | collective-permute-start | bytes 282632 | tf_op jit(solution)/shard_map/ppermute | solution.py:1027
  13.6 4.5 %copy-start = (s32[1,16,128]{2,1,0:T(8,128)S(1)}, s32[1,16,128]{2,1,0:T(8,128)}, u32[]{:S(2)}) copy-start(s32[1,16,128]{2,1,0:T(8,128)} %ids.1) | copy-start | bytes 24580
  18.7 6.2 %collective-permute-start.7 = (f32[88,128]{1,0:T(8,128)S(1)}, f32[88,128]{1,0:T(8,128)S(1)}, u32[]{:S(2)}, u32[]{:S(2)}) collective-permute-start(f32[88,128]{1,0:T(8,128)S(1)} %get-tuple-element.45), channel_id=1, source_target_pairs={{0,12},{4,8},{8,4},{12,0},{1,13},{5,9},{9,5},{13,1},{2,14},{6,10},... | collective-permute-start | bytes 135176 | tf_op jit(solution)/shard_map/ppermute | solution.py:1021
  21.0 5.2 %collective-permute-start.6 = (f32[88,128]{1,0:T(8,128)S(1)}, f32[88,128]{1,0:T(8,128)S(1)}, u32[]{:S(2)}, u32[]{:S(2)}) collective-permute-start(f32[88,128]{1,0:T(8,128)S(1)} %get-tuple-element.45), channel_id=1, source_target_pairs={{0,8},{4,12},{8,0},{12,4},{1,9},{5,13},{9,1},{13,5},{2,10},{6,14},... | collective-permute-start | bytes 135176 | tf_op jit(solution)/shard_map/ppermute | solution.py:1021
  21.9 4.6 %collective-permute-start.5 = (f32[88,128]{1,0:T(8,128)S(1)}, f32[88,128]{1,0:T(8,128)S(1)}, u32[]{:S(2)}, u32[]{:S(2)}) collective-permute-start(f32[88,128]{1,0:T(8,128)S(1)} %get-tuple-element.45), channel_id=1, source_target_pairs={{0,4},{4,0},{8,12},{12,8},{1,5},{5,1},{9,13},{13,9},{2,6},{6,2},{1... | collective-permute-start | bytes 135176 | tf_op jit(solution)/shard_map/ppermute | solution.py:1021
  26.8 4.6 %collective-permute-start.8 = (f32[168,128]{1,0:T(8,128)S(1)}, f32[168,128]{1,0:T(8,128)S(1)}, u32[]{:S(2)}, u32[]{:S(2)}) collective-permute-start(f32[168,128]{1,0:T(8,128)S(1)} %get-tuple-element.55.refs_4_), channel_id=1, source_target_pairs={{0,2},{2,0},{1,3},{3,1},{4,6},{6,4},{5,7},{7,5},{8,10},{10,8},{9,1... | collective-permute-start | bytes 258056 | tf_op jit(solution)/shard_map/ppermute | solution.py:1017
  27.7 3.7 %collective-permute-start.9 = (f32[200,128]{1,0:T(8,128)S(1)}, f32[200,128]{1,0:T(8,128)S(1)}, u32[]{:S(2)}, u32[]{:S(2)}) collective-permute-start(f32[200,128]{1,0:T(8,128)S(1)} %get-tuple-element.56), channel_id=1, source_target_pairs={{0,1},{1,0},{2,3},{3,2},{4,5},{5,4},{6,7},{7,6},{8,9},{9,8},{10,11... | collective-permute-start | bytes 307208 | tf_op jit(solution)/shard_map/ppermute | solution.py:1017
  31.4 1.3 %collective-permute-start.10 = (f32[168,128]{1,0:T(8,128)S(1)}, f32[168,128]{1,0:T(8,128)S(1)}, u32[]{:S(2)}, u32[]{:S(2)}) collective-permute-start(f32[168,128]{1,0:T(8,128)S(1)} %collective-permute-done.8.refs_1_), channel_id=1, source_target_pairs={{0,1},{1,0},{2,3},{3,2},{4,5},{5,4},{6,7},{7,6},{8,9},{9,8},{10,11... | collective-permute-start | bytes 258056 | tf_op jit(solution)/shard_map/ppermute | solution.py:1017

commit v17 on v15

--- a/solution.py
+++ b/solution.py
@@ -511,7 +511,6 @@
     totals = lax.dot_general(
         jnp.ones((8, LANES), F32), sums[...], (((1,), (1,)), ((), ())), precision=HIGHEST, preferred_element_type=F32
     )
-    message[half + C : half + C + 8, :] = jnp.zeros((8, LANES), F32)
     for t in range(wide // LANES):
         message[half + C + t : half + C + t + 1, :] = totals[0:1, t * LANES : (t + 1) * LANES]
 
@@ -580,14 +579,15 @@
     W1, C1 = W // 2, C // 2
     half, start, middle = W1 // 2, W1 // 2 * C1, LANES // 2
     blk, length, wall = lax.axis_index("blk"), lax.axis_index("len"), lax.axis_index("wall")
-    sums = jnp.zeros((8, LANES), F32)
+    sums = jnp.zeros((1, LANES), F32)
     for d in range(n_blk):
         b = blk ^ d
         for i in range(half):
             sheet1[i, pl.ds(pl.multiple_of(C1 * b, C1), C1), :] = blocks[d, i * C1 : (i + 1) * C1, :]
         out[pl.ds(pl.multiple_of(96 + C * b, C), C), :] = blocks[d, start : start + C, :]
-        sums = sums + blocks[d, start + C : start + C + 8, :]
-    out[160:168, :] = sums
+        sums = sums + blocks[d, start + C : start + C + 1, :]
+    out[160:168, :] = jnp.zeros((8, LANES), F32)
+    out[160:161, :] = sums
     NC1 = sheet1.shape[1]
     lane, at = halves((NC1, LANES))
     low = lane < middle
@@ -980,6 +980,8 @@
     start = half * C1
     totals = [jnp.zeros((C, LANES), F32) for _ in owned]
     small = [jnp.zeros((8, LANES), F32) for _ in owned]
+    lines = blocks[0].shape[1] - start - C
+    thin = [jnp.zeros((lines, LANES), F32) for _ in owned]
     for v in range(n_wall):
         wall_s = wall_of(v)
         for j in range(n_len):
@@ -997,15 +999,15 @@
                 big, little = carry
                 values = sheet[wall_s, pl.ds(pl.multiple_of(blk_of(d) * C, C), C), at_l]
                 ids = ref[d, start : start + C, :]
-                parts = ref[d, start + C : start + C + 8, :]
+                parts = ref[d, start + C : start + C + lines, :]
                 big = [x + jnp.where(ids == e, values, 0.0) for x, e in zip(big, owned)]
-                little = [x + jnp.where(spot == e, parts, 0.0) for x, e in zip(little, owned)]
+                little = [x + jnp.where(spot[:lines] == e, parts, 0.0) for x, e in zip(little, owned)]
                 return big, little
 
-            totals, small = lax.fori_loop(0, n_blk, add, (totals, small), unroll=min(4, n_blk))
+            totals, thin = lax.fori_loop(0, n_blk, add, (totals, thin), unroll=min(4, n_blk))
     factor = 1.0 / (2.0 * C * L / 2) ** 0.5
     for r in range(2):
-        patch_grad[0, r] = (jnp.sum(totals[r]) + jnp.sum(small[r])) * factor
+        patch_grad[0, r] = (jnp.sum(totals[r]) + jnp.sum(small[r]) + jnp.sum(thin[r])) * factor
     for copy in copies:
         copy.wait()
 
@@ -1104,7 +1106,7 @@
 
     rows = (8, N, L)
     wide = LANES * ((electrodes + LANES - 1) // LANES)
-    message = (cells // 8 + C + 8, L)
+    message = (cells // 8 + C + wide // LANES, L)
     rows_n, rows_p, mine = call(
         functools.partial(correct, electrodes, n_len, n_wall),
         [vmem] * 6,

time: 37.4 us -> 37.4 us (level)
  no operation moved by 1% of the time
where the time goes in v17:
time: 37.4 us; the launch traced here: 37.2 us
  waiting for transfers between devices  13.4 us (36%)
  starting transfers between devices  12.2 us (33%)
  Pallas kernels  10.3 us (28%)
  between operations  0.69 us (2%)
  local copies, waits for them, and re-layouts  0.66 us (2%)
    ppermute x5, waiting for transfers between devices, ring(): return lax.ppermute(x, axis, [(i, (i + by) % count) for i in range(count)])  4.95 us
    pallas_call x1, Pallas kernels, body(): call(functools.partial(solve, (n_blk, n_len, n_wall), relative, compacted...  4.5 us
    ppermute x3, starting transfers between devices, paired(): lax.ppermute(x, 'blk', [(i, i ^ by) for i in range(lax.axis_size('blk'))])  4.45 us
    ppermute x5, starting transfers between devices, ring(): return lax.ppermute(x, axis, [(i, (i + by) % count) for i in range(count)])  3.97 us
    ppermute x2, starting transfers between devices, neighbour_pairs(): lax.ppermute(x, 'blk', [(i, (i + (1 if i % 2 == odd_first else -1)) % cou...  3.67 us
    ppermute x1, waiting for transfers between devices, across(): return lax.ppermute(x, ('len', 'wall'), pairs)  3.01 us
    ppermute x2, waiting for transfers between devices, neighbour_pairs(): lax.ppermute(x, 'blk', [(i, (i + (1 if i % 2 == odd_first else -1)) % cou...  2.87 us
    ppermute x3, waiting for transfers between devices, paired(): lax.ppermute(x, 'blk', [(i, i ^ by) for i in range(lax.axis_size('blk'))])  2.54 us
  transfers between devices with their start and end apart: 11, of which 8 were waited for; matrix products, arithmetic and copies ran while one was open for 0% of the time, Pallas kernels for 6%

profile of v17, /device:TPU:0, one launch (start us, length us, event | category | flops | bytes accessed | tf_op | source)
XLA Modules:
  0.0 37.2 jit_solution(17545227657978975144)
XLA Ops:
  0.6 1.7 %faces.1 = (f32[512,128]{1,0:T(8,128)S(1)}, f32[512,128]{1,0:T(8,128)S(1)}, f32[512,128]{1,0:T(8,128)S(1)}, f32[512,128]{1,0:T(8,128)S(1)}, f32[12,16,128]{2,1,0...) custom-call(f32[512,128]{1,0:T(8,128)} %bitcast.13, f32[512,128]{1,0:T(8,128)} %bitcast.14, ...), custom_call_target="tpu_custom_call" | custom-call | tf_op jit(solution)/shard_map/faces/pallas_call | solution.py:1067
  2.3 0.5 %collective-permute-start = (f32[12,16,128]{2,1,0:T(8,128)S(1)}, f32[12,16,128]{2,1,0:T(8,128)S(1)}, u32[]{:S(2)}, u32[]{:S(2)}) collective-permute-start(f32[12,16,128]{2,1,0:T(8,128)S(1)} %get-tuple-element.37), channel_id=1, source_target_pairs={{0,1},{1,0},{2,3},{3,2},{4,5},{5,4},{6,7},{7,6},{8,9},{9,8},{10,11... | collective-permute-start | bytes 294920 | tf_op jit(solution)/shard_map/ppermute | solution.py:1017
  2.8 2.6 %collective-permute-start.1 = (f32[4,16,128]{2,1,0:T(8,128)S(1)}, f32[4,16,128]{2,1,0:T(8,128)S(1)}, u32[]{:S(2)}, u32[]{:S(2)}) collective-permute-start(f32[4,16,128]{2,1,0:T(8,128)S(1)} %get-tuple-element.38), channel_id=1, source_target_pairs={{0,2},{2,0},{1,3},{3,1},{4,6},{6,4},{5,7},{7,5},{8,10},{10,8},{9,1... | collective-permute-start | bytes 98312 | tf_op jit(solution)/shard_map/ppermute | solution.py:1017
  5.4 0.1 collective-permute-start.2
  5.5 3.0 %collective-permute-done.2.refs_6_ = f32[16,128]{1,0:T(8,128)S(1)} collective-permute-done((f32[16,128]{1,0:T(8,128)S(1)}, f32[16,128]{1,0:T(8,128)S(1)}, u32[]{:S(2)}, u32[]{:S(2)}) %collective-permute-start.2) | collective-permute-done | bytes 8224 | tf_op jit(solution)/shard_map/ppermute | solution.py:1033
  8.5 0.0 collective-permute-done.1.refs_5_
  8.5 0.0 collective-permute-done.refs_4_
  8.5 0.8 %boundary.1 = (f32[184,128]{1,0:T(8,128)S(1)}, f32[184,128]{1,0:T(8,128)S(1)}, f32[2,6,40,128]{3,2,1,0:T(8,128)S(1)}) custom-call(f32[512,128]{1,0:T(8,128)S(1)} %get-tuple-element.33.refs_0_, f32[512,128]{1,0:T(8,128)S(1)} %get-tuple-element.34.refs_1_, f32[512,128]{1,0:T(8,128)S(1)} %get-tuple-element.35.refs_2_.mask.refs_7_, ...), custom_call_target="tpu_custom_call" | custom-call | tf_op jit(solution)/shard_map/boundary/pallas_call | solution.py:1089
  9.3 3.7 %collective-permute-start.3 = (f32[184,128]{1,0:T(8,128)S(1)}, f32[184,128]{1,0:T(8,128)S(1)}, u32[]{:S(2)}, u32[]{:S(2)}) collective-permute-start(f32[184,128]{1,0:T(8,128)S(1)} %get-tuple-element.41), channel_id=1, source_target_pairs={{0,12},{4,8},{8,4},{12,0},{1,13},{5,9},{9,5},{13,1},{2,14},{6,10},... | collective-permute-start | bytes 282632 | tf_op jit(solution)/shard_map/ppermute | solution.py:1027
  13.0 0.0 copy-start.1
  13.0 0.0 collective-permute-start.4
  13.0 0.7 %copy-done.1 = s32[32]{0:T(128)S(1)} copy-done((s32[32]{0:T(128)S(1)}, s32[32]{0:T(128)}, u32[]{:S(2)}) %copy-start.1) | copy-done | bytes 152
  13.6 0.0 copy-start
  13.6 1.6 %sector.1 = (f32[640,128]{1,0:T(8,128)S(1)}, f32[640,128]{1,0:T(8,128)S(1)}, f32[640,128]{1,0:T(8,128)S(1)}, f32[64,128]{1,0:T(8,128)S(1)}, f32[16,128]{1,0:T(8,128)S(1)}, /*index=5*/f32[8,128]{1,0:T(8,128)S(1)}) custom-call(f32[512,128]{1,0:T(8,128)S(1)} %get-tuple-element.33.refs_0_, f32[512,128]{1,0:T(8,128)S(1)} %get-tuple-element.34.refs_1_, ...), custom_call_target="tpu_custom_call" | custom-call | flops 16000000 | bytes 16000000 | tf_op jit(solution)/shard_map/sector/pallas_call | solution.py:1098
  15.3 1.5 %collective-permute-done.3.first_in = f32[184,128]{1,0:T(8,128)S(1)} collective-permute-done((f32[184,128]{1,0:T(8,128)S(1)}, f32[184,128]{1,0:T(8,128)S(1)}, u32[]{:S(2)}, u32[]{:S(2)}) %collective-permute-start.3) | collective-permute-done | bytes 94240 | tf_op jit(solution)/shard_map/ppermute | solution.py:1027
  16.7 1.4 %collective-permute-done.4.second_in = f32[184,128]{1,0:T(8,128)S(1)} collective-permute-done((f32[184,128]{1,0:T(8,128)S(1)}, f32[184,128]{1,0:T(8,128)S(1)}, u32[]{:S(2)}, u32[]{:S(2)}) %collective-permute-start.4) | collective-permute-done | bytes 94240 | tf_op jit(solution)/shard_map/ppermute | solution.py:1027
  18.1 0.0 copy-done
  18.1 0.6 %correct.1 = (f32[8,40,128]{2,1,0:T(8,128)S(1)}, f32[8,40,128]{2,1,0:T(8,128)S(1)}, f32[81,128]{1,0:T(8,128)S(1)}) custom-call(f32[2,6,40,128]{3,2,1,0:T(8,128)S(1)} %get-tuple-element.40.own_rows, f32[184,128]{1,0:T(8,128)S(1)} %collective-permute-done.3.first_in, f32[184,128]{1,0:T(8,128)S(1)} %collective-permute-done.4.second_in, ...), custom_call_target="tpu_custom_call" | custom-call | tf_op jit(solution)/shard_map/correct/pallas_call | solution.py:1110
  18.7 2.3 %collective-permute-start.7 = (f32[81,128]{1,0:T(8,128)S(1)}, f32[81,128]{1,0:T(8,128)S(1)}, u32[]{:S(2)}, u32[]{:S(2)}) collective-permute-start(f32[81,128]{1,0:T(8,128)S(1)} %get-tuple-element.45), channel_id=1, source_target_pairs={{0,12},{4,8},{8,4},{12,0},{1,13},{5,9},{9,5},{13,1},{2,14},{6,10},... | collective-permute-start | bytes 124424 | tf_op jit(solution)/shard_map/ppermute | solution.py:1021
  21.0 0.9 %collective-permute-start.6 = (f32[81,128]{1,0:T(8,128)S(1)}, f32[81,128]{1,0:T(8,128)S(1)}, u32[]{:S(2)}, u32[]{:S(2)}) collective-permute-start(f32[81,128]{1,0:T(8,128)S(1)} %get-tuple-element.45), channel_id=1, source_target_pairs={{0,8},{4,12},{8,0},{12,4},{1,9},{5,13},{9,1},{13,5},{2,10},{6,14},... | collective-permute-start | bytes 124424 | tf_op jit(solution)/shard_map/ppermute | solution.py:1021
  21.9 1.2 %collective-permute-start.5 = (f32[81,128]{1,0:T(8,128)S(1)}, f32[81,128]{1,0:T(8,128)S(1)}, u32[]{:S(2)}, u32[]{:S(2)}) collective-permute-start(f32[81,128]{1,0:T(8,128)S(1)} %get-tuple-element.45), channel_id=1, source_target_pairs={{0,4},{4,0},{8,12},{12,8},{1,5},{5,1},{9,13},{13,9},{2,6},{6,2},{1... | collective-permute-start | bytes 124424 | tf_op jit(solution)/shard_map/ppermute | solution.py:1021
  23.1 0.8 %source_part.1 = (f32[512,128]{1,0:T(8,128)S(1)}, f32[512,128]{1,0:T(8,128)S(1)}) custom-call(f32[640,128]{1,0:T(8,128)S(1)} %get-tuple-element.46.bm, f32[640,128]{1,0:T(8,128)S(1)} %get-tuple-element.47.be, f32[8,40,128]{2,1,0:T(8,128)S(1)} %get-tuple-element.48.rows_n, f32[8,40,128]{2,1,0:T(8,128)S(1)} %get-tuple-element.49.rows_p, ...), custom_call_target="tpu_custom_call" | custom-call | flops 12000000 | bytes 12000000 | tf_op jit(solution)/shard_map/source_part/pallas_call | solution.py:1120
  23.9 1.0 %collective-permute-done.7 = f32[81,128]{1,0:T(8,128)S(1)} collective-permute-done((f32[81,128]{1,0:T(8,128)S(1)}, f32[81,128]{1,0:T(8,128)S(1)}, u32[]{:S(2)}, u32[]{:S(2)}) %collective-permute-start.7) | collective-permute-done | bytes 41504 | tf_op jit(solution)/shard_map/ppermute | solution.py:1021
  24.9 1.3 %collective-permute-done.6 = f32[81,128]{1,0:T(8,128)S(1)} collective-permute-done((f32[81,128]{1,0:T(8,128)S(1)}, f32[81,128]{1,0:T(8,128)S(1)}, u32[]{:S(2)}, u32[]{:S(2)}) %collective-permute-start.6) | collective-permute-done | bytes 41504 | tf_op jit(solution)/shard_map/ppermute | solution.py:1021
  26.2 0.3 collective-permute-done.5
  26.5 0.3 compact.1
  26.8 0.9 %collective-permute-start.8 = (f32[168,128]{1,0:T(8,128)S(1)}, f32[168,128]{1,0:T(8,128)S(1)}, u32[]{:S(2)}, u32[]{:S(2)}) collective-permute-start(f32[168,128]{1,0:T(8,128)S(1)} %get-tuple-element.55.refs_4_), channel_id=1, source_target_pairs={{0,2},{2,0},{1,3},{3,1},{4,6},{6,4},{5,7},{7,5},{8,10},{10,8},{9,1... | collective-permute-start | bytes 258056 | tf_op jit(solution)/shard_map/ppermute | solution.py:1017
  27.7 0.0 collective-permute-start.9
  27.7 3.7 %collective-permute-done.8.refs_1_ = f32[168,128]{1,0:T(8,128)S(1)} collective-permute-done((f32[168,128]{1,0:T(8,128)S(1)}, f32[168,128]{1,0:T(8,128)S(1)}, u32[]{:S(2)}, u32[]{:S(2)}) %collective-permute-start.8) | collective-permute-done | bytes 86048 | tf_op jit(solution)/shard_map/ppermute | solution.py:1017
  31.4 0.0 collective-permute-start.10
  31.4 0.0 collective-permute-done.9.refs_2_
  31.4 1.3 %collective-permute-done.10.refs_3_ = f32[168,128]{1,0:T(8,128)S(1)} collective-permute-done((f32[168,128]{1,0:T(8,128)S(1)}, f32[168,128]{1,0:T(8,128)S(1)}, u32[]{:S(2)}, u32[]{:S(2)}) %collective-permute-start.10) | collective-permute-done | bytes 86048 | tf_op jit(solution)/shard_map/ppermute | solution.py:1017
  32.7 4.5 %solve.1 = (f32[512,128]{1,0:T(8,128)}, f32[512,128]{1,0:T(8,128)}, f32[1,2]{1,0:T(1,128)}) custom-call(f32[4,81,128]{2,1,0:T(8,128)S(1)} %pad_maximum_fusion.blocks.refs_0_, f32[168,128]{1,0:T(8,128)S(1)} %collective-permute-done.8.refs_1_, f32[200,128]{1,0:T(8,128)S(1)} %collective-permute-done.9.refs_2_, f32[168,128]{1,0:T(8,128)S(1)} %collective-permute-done.10.refs_3_, ...), custom_call_target="tpu_custom_call" | custom-call | tf_op jit(solution)/shard_map/solve/pallas_call | solution.py:1157
  (1 shorter events, 0.0 us)
Async XLA Ops:
  2.3 6.2 %collective-permute-start = (f32[12,16,128]{2,1,0:T(8,128)S(1)}, f32[12,16,128]{2,1,0:T(8,128)S(1)}, u32[]{:S(2)}, u32[]{:S(2)}) collective-permute-start(f32[12,16,128]{2,1,0:T(8,128)S(1)} %get-tuple-element.37), channel_id=1, source_target_pairs={{0,1},{1,0},{2,3},{3,2},{4,5},{5,4},{6,7},{7,6},{8,9},{9,8},{10,11... | collective-permute-start | bytes 294920 | tf_op jit(solution)/shard_map/ppermute | solution.py:1017
  2.8 5.6 %collective-permute-start.1 = (f32[4,16,128]{2,1,0:T(8,128)S(1)}, f32[4,16,128]{2,1,0:T(8,128)S(1)}, u32[]{:S(2)}, u32[]{:S(2)}) collective-permute-start(f32[4,16,128]{2,1,0:T(8,128)S(1)} %get-tuple-element.38), channel_id=1, source_target_pairs={{0,2},{2,0},{1,3},{3,1},{4,6},{6,4},{5,7},{7,5},{8,10},{10,8},{9,1... | collective-permute-start | bytes 98312 | tf_op jit(solution)/shard_map/ppermute | solution.py:1017
  5.4 3.1 %collective-permute-start.2 = (f32[16,128]{1,0:T(8,128)S(1)}, f32[16,128]{1,0:T(8,128)S(1)}, u32[]{:S(2)}, u32[]{:S(2)}) collective-permute-start(f32[16,128]{1,0:T(8,128)S(1)} %get-tuple-element.39), channel_id=1, source_target_pairs={{0,3},{1,2},{2,1},{3,0},{4,7},{5,6},{6,5},{7,4},{8,11},{9,10},{10,... | collective-permute-start | bytes 24584 | tf_op jit(solution)/shard_map/ppermute | solution.py:1033
  9.3 7.4 %collective-permute-start.3 = (f32[184,128]{1,0:T(8,128)S(1)}, f32[184,128]{1,0:T(8,128)S(1)}, u32[]{:S(2)}, u32[]{:S(2)}) collective-permute-start(f32[184,128]{1,0:T(8,128)S(1)} %get-tuple-element.41), channel_id=1, source_target_pairs={{0,12},{4,8},{8,4},{12,0},{1,13},{5,9},{9,5},{13,1},{2,14},{6,10},... | collective-permute-start | bytes 282632 | tf_op jit(solution)/shard_map/ppermute | solution.py:1027
  13.0 0.7 %copy-start.1 = (s32[32]{0:T(128)S(1)}, s32[32]{0:T(128)}, u32[]{:S(2)}) copy-start(s32[32]{0:T(128)} %param.11) | copy-start | bytes 388
  13.0 5.2 %collective-permute-start.4 = (f32[184,128]{1,0:T(8,128)S(1)}, f32[184,128]{1,0:T(8,128)S(1)}, u32[]{:S(2)}, u32[]{:S(2)}) collective-permute-start(f32[184,128]{1,0:T(8,128)S(1)} %get-tuple-element.42), channel_id=1, source_target_pairs={{0,4},{4,0},{8,12},{12,8},{1,5},{5,1},{9,13},{13,9},{2,6},{6,2},{1... | collective-permute-start | bytes 282632 | tf_op jit(solution)/shard_map/ppermute | solution.py:1027
  13.6 4.5 %copy-start = (s32[1,16,128]{2,1,0:T(8,128)S(1)}, s32[1,16,128]{2,1,0:T(8,128)}, u32[]{:S(2)}) copy-start(s32[1,16,128]{2,1,0:T(8,128)} %ids.1) | copy-start | bytes 24580
  18.7 6.2 %collective-permute-start.7 = (f32[81,128]{1,0:T(8,128)S(1)}, f32[81,128]{1,0:T(8,128)S(1)}, u32[]{:S(2)}, u32[]{:S(2)}) collective-permute-start(f32[81,128]{1,0:T(8,128)S(1)} %get-tuple-element.45), channel_id=1, source_target_pairs={{0,12},{4,8},{8,4},{12,0},{1,13},{5,9},{9,5},{13,1},{2,14},{6,10},... | collective-permute-start | bytes 124424 | tf_op jit(solution)/shard_map/ppermute | solution.py:1021
  21.0 5.2 %collective-permute-start.6 = (f32[81,128]{1,0:T(8,128)S(1)}, f32[81,128]{1,0:T(8,128)S(1)}, u32[]{:S(2)}, u32[]{:S(2)}) collective-permute-start(f32[81,128]{1,0:T(8,128)S(1)} %get-tuple-element.45), channel_id=1, source_target_pairs={{0,8},{4,12},{8,0},{12,4},{1,9},{5,13},{9,1},{13,5},{2,10},{6,14},... | collective-permute-start | bytes 124424 | tf_op jit(solution)/shard_map/ppermute | solution.py:1021
  21.9 4.6 %collective-permute-start.5 = (f32[81,128]{1,0:T(8,128)S(1)}, f32[81,128]{1,0:T(8,128)S(1)}, u32[]{:S(2)}, u32[]{:S(2)}) collective-permute-start(f32[81,128]{1,0:T(8,128)S(1)} %get-tuple-element.45), channel_id=1, source_target_pairs={{0,4},{4,0},{8,12},{12,8},{1,5},{5,1},{9,13},{13,9},{2,6},{6,2},{1... | collective-permute-start | bytes 124424 | tf_op jit(solution)/shard_map/ppermute | solution.py:1021
  26.8 4.6 %collective-permute-start.8 = (f32[168,128]{1,0:T(8,128)S(1)}, f32[168,128]{1,0:T(8,128)S(1)}, u32[]{:S(2)}, u32[]{:S(2)}) collective-permute-start(f32[168,128]{1,0:T(8,128)S(1)} %get-tuple-element.55.refs_4_), channel_id=1, source_target_pairs={{0,2},{2,0},{1,3},{3,1},{4,6},{6,4},{5,7},{7,5},{8,10},{10,8},{9,1... | collective-permute-start | bytes 258056 | tf_op jit(solution)/shard_map/ppermute | solution.py:1017
  27.7 3.7 %collective-permute-start.9 = (f32[200,128]{1,0:T(8,128)S(1)}, f32[200,128]{1,0:T(8,128)S(1)}, u32[]{:S(2)}, u32[]{:S(2)}) collective-permute-start(f32[200,128]{1,0:T(8,128)S(1)} %get-tuple-element.56), channel_id=1, source_target_pairs={{0,1},{1,0},{2,3},{3,2},{4,5},{5,4},{6,7},{7,6},{8,9},{9,8},{10,11... | collective-permute-start | bytes 307208 | tf_op jit(solution)/shard_map/ppermute | solution.py:1017
  31.4 1.3 %collective-permute-start.10 = (f32[168,128]{1,0:T(8,128)S(1)}, f32[168,128]{1,0:T(8,128)S(1)}, u32[]{:S(2)}, u32[]{:S(2)}) collective-permute-start(f32[168,128]{1,0:T(8,128)S(1)} %collective-permute-done.8.refs_1_), channel_id=1, source_target_pairs={{0,1},{1,0},{2,3},{3,2},{4,5},{5,4},{6,7},{7,6},{8,9},{9,8},{10,11... | collective-permute-start | bytes 258056 | tf_op jit(solution)/shard_map/ppermute | solution.py:1017
